TPU v7x, 32 devices: a whole 2x2x4 slice. The times are simulated.
32 devices in a mesh: section: 2 (over x), fsdp: 4 (over y, core), rep: 4 (over z).
Axes of the slice: x: 2, y: 2, z: 4, core: 2. Of those that a mesh axis runs over, the one named last changes fastest.
Arguments:
- inputs: bfloat16 [64, 256, 1024], P(('fsdp', 'rep')), may hold values from -6 to 6
- teacher: bfloat16 [64, 256, 1024], P(('fsdp', 'rep')), may hold values from -6 to 6
- lengths: int32 [64], replicated, may hold values from 1 to 256, as said below
- order: int32 [64], replicated, may hold values from 0 to 63, as said below
- loss_scale: float32 [], replicated, may hold values from 131072 to 524288
- norm_gain1: bfloat16 [2, 1024], P('section', 'fsdp'), may hold values from 0.5 to 1.5
- w_query: bfloat16 [2, 1024, 512], P('section', 'fsdp'), may hold values from -0.1875 to 0.1875
- w_key: bfloat16 [2, 1024, 128], P('section', 'fsdp'), may hold values from -0.1875 to 0.1875
- w_value: bfloat16 [2, 1024, 128], P('section', 'fsdp'), may hold values from -0.1875 to 0.1875
- w_attn_out: bfloat16 [2, 512, 1024], P('section', 'fsdp'), may hold values from -1 to 1
- w_ssm_gate: bfloat16 [2, 1024, 1536], P('section', 'fsdp'), may hold values from -0.1875 to 0.1875
- w_conv_in: bfloat16 [2, 1024, 1792], P('section', 'fsdp'), may hold values from -0.1875 to 0.1875
- w_step: bfloat16 [2, 1024, 24], P('section', 'fsdp'), may hold values from -0.046875 to 0.046875
- conv_kernel: bfloat16 [2, 4, 1792], P('section', None, 'fsdp'), may hold values from -3 to 3
- conv_bias: bfloat16 [2, 1792], P('section', 'fsdp'), may hold values from -3 to 3
- step_bias: float32 [2, 24], P('section'), may hold values from -6 to -2.5
- decay_log: float32 [2, 24], P('section'), may hold values from 0 to 1.4
- skip_gain: float32 [2, 24], P('section'), may hold values from 0.5 to 1.5
- ssm_norm_gain: bfloat16 [2, 1536], P('section', 'fsdp'), may hold values from 0.5 to 1.5
- w_ssm_out: bfloat16 [2, 1536, 1024], P('section', 'fsdp'), may hold values from -0.15625 to 0.15625
- norm_gain2: bfloat16 [2, 1024], P('section', 'fsdp'), may hold values from 0.5 to 1.5
- w_gate: bfloat16 [2, 1024, 2048], P('section', 'fsdp'), may hold values from -0.1875 to 0.1875
- w_up: bfloat16 [2, 1024, 2048], P('section', 'fsdp'), may hold values from -0.1875 to 0.1875
- w_down: bfloat16 [2, 2048, 1024], P('section', 'fsdp'), may hold values from -0.125 to 0.125
Outputs:
- activations: bfloat16 [2, 64, 256, 1024], P('section', ('fsdp', 'rep'))
- gradients: bfloat16 [2, 64, 256, 1024], P('section', ('fsdp', 'rep'))
- loss: float32 [], replicated
- grad_norm_gain1: float32 [2, 1024], P('section', 'fsdp')
- grad_w_query: float32 [2, 1024, 512], P('section', 'fsdp')
- grad_w_key: float32 [2, 1024, 128], P('section', 'fsdp')
- grad_w_value: float32 [2, 1024, 128], P('section', 'fsdp')
- grad_w_attn_out: float32 [2, 512, 1024], P('section', 'fsdp')
- grad_w_ssm_gate: float32 [2, 1024, 1536], P('section', 'fsdp')
- grad_w_conv_in: float32 [2, 1024, 1792], P('section', 'fsdp')
- grad_w_step: float32 [2, 1024, 24], P('section', 'fsdp')
- grad_conv_kernel: float32 [2, 4, 1792], P('section', None, 'fsdp')
- grad_conv_bias: float32 [2, 1792], P('section', 'fsdp')
- grad_step_bias: float32 [2, 24], P('section')
- grad_decay_log: float32 [2, 24], P('section')
- grad_skip_gain: float32 [2, 24], P('section')
- grad_ssm_norm_gain: float32 [2, 1536], P('section', 'fsdp')
- grad_w_ssm_out: float32 [2, 1536, 1024], P('section', 'fsdp')
- grad_norm_gain2: float32 [2, 1024], P('section', 'fsdp')
- grad_w_gate: float32 [2, 1024, 2048], P('section', 'fsdp')
- grad_w_up: float32 [2, 1024, 2048], P('section', 'fsdp')
- grad_w_down: float32 [2, 2048, 1024], P('section', 'fsdp')
Inputs may be any that keep to these rules, and one draw needn't show every extreme that they name: `lengths`: valid tokens fill the first positions of a sequence; the last sequence holds 256. `order`: A permutation; dealt positions are numbered as the rows of the sharded layout, 4 to a device. A sequence stays among the 4 devices that share its fsdp index, and each device sends exactly one of its sequences to each of them.
All inputs are finite; a program needn't handle non-finite values.
Results may differ from a plain program's by a relative error of at most 0.022.
Values may be sent and summed in bfloat16 or wider, within the bound.
No kernel may reach another device: no remote copies, remote signals or barrier semaphores. Data moves between devices by JAX's collectives and lax.ppermute only.
A program may use at most 448 MiB of HBM per device.

v0:
```python
import math

import jax
import jax.numpy as jnp
from jax import lax
from jax.sharding import PartitionSpec as P

HD = 64


EPSILON = 1e-05
ROPE_BASE = 100000000000.0
MASKED = -1e30
HIGHEST = lax.Precision.HIGHEST


def passed_along(block, axis, distance):
    devices = range(lax.axis_size(axis))
    route = [(i - distance, i) for i in devices if i - distance in devices]
    return lax.ppermute(block, axis, route)


def matmul(left_side, right_side):
    return jnp.dot(left_side, right_side, preferred_element_type=jnp.float32)


def left_product(left_side, right_side):
    return lax.dot_general(
        left_side, right_side, (((0,), (0,)), ((), ())), preferred_element_type=jnp.float32
    )


def right_product(left_side, right_side):
    return lax.dot_general(
        left_side, right_side, (((1,), (1,)), ((), ())), preferred_element_type=jnp.float32
    )


def norm_rows(values, gain_row):
    return (
        values * lax.rsqrt(jnp.mean(values * values, axis=-1, keepdims=True) + EPSILON) * gain_row
    )


def rope_tables(length, head_size):
    halves = head_size // 2
    inverse = jnp.exp(
        jnp.arange(halves, dtype=jnp.float32) * (-2.0 * math.log(ROPE_BASE) / head_size)
    )
    angles = jnp.arange(length, dtype=jnp.float32)[:, None] * inverse[None, :]
    return (jnp.cos(angles)[:, None, :], jnp.sin(angles)[:, None, :])


def rotate(values, cosine, sine_table):
    halves = values.shape[-1] // 2
    former = values[..., :halves]
    latter = values[..., halves:]
    return jnp.concatenate(
        [former * cosine - latter * sine_table, latter * cosine + former * sine_table], axis=-1
    )


def soft_plus(values):
    return jnp.log1p(jnp.exp(values))


def swish(values):
    return values * jax.nn.sigmoid(values)


def swiglu(gate_value, up_value):
    return swish(gate_value) * up_value


def mixer_core(
    gate_raw, conv_raw, step_raw, kernel, conv_bias, step_bias, decay_log, skip_gain, gain_row
):
    length = conv_raw.shape[0]
    kernel_taps = kernel.shape[0]
    head_count = step_raw.shape[1]
    inner_width = gate_raw.shape[1]
    state_width = (conv_raw.shape[1] - inner_width) // 2
    padded = jnp.pad(conv_raw, ((kernel_taps - 1, 0), (0, 0)))
    convolved = conv_bias[None, :]
    for offset in range(kernel_taps):
        convolved = convolved + kernel[offset][None, :] * padded[offset : offset + length]
    convolved = swish(convolved)
    states_in = convolved[:, :inner_width].reshape(length, head_count, inner_width // head_count)
    inputs_b = convolved[:, inner_width : inner_width + state_width]
    inputs_c = convolved[:, inner_width + state_width :]
    step_size = soft_plus(step_raw + step_bias[None, :])
    running = jnp.cumsum(-step_size * jnp.exp(decay_log)[None, :], axis=0).T
    row_index = lax.broadcasted_iota(jnp.int32, (length, length), 0)
    col_index = lax.broadcasted_iota(jnp.int32, (length, length), 1)
    causal = (col_index <= row_index)[None]
    decay_matrix = jnp.exp(jnp.where(causal, running[:, :, None] - running[:, None, :], MASKED))
    intersection = jnp.dot(
        inputs_c, inputs_b.T, precision=HIGHEST, preferred_element_type=jnp.float32
    )
    weights = decay_matrix * intersection[None]
    scaled = step_size[:, :, None] * states_in
    mixed_heads = jnp.einsum(
        "hts,shp->thp", weights, scaled, precision=HIGHEST, preferred_element_type=jnp.float32
    )
    mixed_heads = mixed_heads + skip_gain[None, :, None] * states_in
    gated_rows = mixed_heads.reshape(length, inner_width) * swish(gate_raw)
    return norm_rows(gated_rows, gain_row)


def layer_forward(seq_in, full_layer, heads_in, valid_rows, tables):
    (
        gain_one,
        w_query,
        w_key,
        w_value,
        w_attn_out,
        w_ssm_gate,
        w_conv_in,
        w_step,
        conv_kernel,
        conv_bias,
        ssm_gain,
        w_ssm_out,
        gain_two,
        w_gate,
        w_up,
        w_down,
    ) = full_layer
    step_bias, decay_log, skip_gain = heads_in
    cosine, sine_table, causal = tables
    length = seq_in.shape[0]
    head_count = w_query.shape[1] // HD
    key_heads = w_key.shape[1] // HD
    residual = seq_in.astype(jnp.float32)
    normed, norm_one_back = jax.vjp(norm_rows, residual, gain_one.astype(jnp.float32))
    normed = normed.astype(jnp.bfloat16)
    query_pre = matmul(normed, w_query).reshape(length, head_count, HD)
    key_pre = matmul(normed, w_key).reshape(length, key_heads, HD)
    values_low = matmul(normed, w_value).astype(jnp.bfloat16).reshape(length, key_heads, HD)
    query_low = rotate(query_pre, cosine, sine_table).astype(jnp.bfloat16)
    query_low = query_low.reshape(length, key_heads, head_count // key_heads, HD)
    keys_low = rotate(key_pre, cosine, sine_table).astype(jnp.bfloat16)
    scores = jnp.einsum(
        "qgrd,kgd->grqk", query_low, keys_low, preferred_element_type=jnp.float32
    ) * HD ** (-0.5)
    scores = jnp.where(causal, scores, MASKED)
    row_top = jnp.max(scores, axis=-1, keepdims=True)
    exp_scores = jnp.exp(scores - row_top)
    attn_probs = exp_scores / jnp.sum(exp_scores, axis=-1, keepdims=True)
    probs_low = attn_probs.astype(jnp.bfloat16)
    attn_mixed = jnp.einsum(
        "grqk,kgd->qgrd", probs_low, values_low, preferred_element_type=jnp.float32
    )
    attn_mixed = attn_mixed.reshape(length, head_count * HD).astype(jnp.bfloat16)
    attention = matmul(attn_mixed, w_attn_out)
    ssm_inputs = (
        matmul(normed, w_ssm_gate),
        matmul(normed, w_conv_in),
        matmul(normed, w_step),
        conv_kernel.astype(jnp.float32),
        conv_bias.astype(jnp.float32),
        step_bias,
        decay_log,
        skip_gain,
        ssm_gain.astype(jnp.float32),
    )
    ssm_out, ssm_back = jax.vjp(jax.checkpoint(mixer_core), *ssm_inputs)
    ssm_low = ssm_out.astype(jnp.bfloat16)
    hidden = residual + attention + matmul(ssm_low, w_ssm_out)
    normed_two, norm_two_back = jax.vjp(norm_rows, hidden, gain_two.astype(jnp.float32))
    normed_two = normed_two.astype(jnp.bfloat16)
    act_value, swiglu_back = jax.vjp(swiglu, matmul(normed_two, w_gate), matmul(normed_two, w_up))
    act_low = act_value.astype(jnp.bfloat16)
    output = (hidden + matmul(act_low, w_down)) * valid_rows[:, None]
    stored = (
        valid_rows,
        normed,
        norm_one_back,
        values_low,
        query_low,
        keys_low,
        attn_probs,
        probs_low,
        attn_mixed,
        ssm_back,
        ssm_low,
        norm_two_back,
        normed_two,
        swiglu_back,
        act_low,
        output,
    )
    return (output, stored)


def layer_backward(grad_out, stored, full_layer, tables):
    (
        gain_one,
        w_query,
        w_key,
        w_value,
        w_attn_out,
        w_ssm_gate,
        w_conv_in,
        w_step,
        conv_kernel,
        conv_bias,
        ssm_gain,
        w_ssm_out,
        gain_two,
        w_gate,
        w_up,
        w_down,
    ) = full_layer
    (
        valid_rows,
        normed,
        norm_one_back,
        values_low,
        query_low,
        keys_low,
        attn_probs,
        probs_low,
        attn_mixed,
        ssm_back,
        ssm_low,
        norm_two_back,
        normed_two,
        swiglu_back,
        act_low,
        output,
    ) = stored
    cosine, sine_table, causal = tables
    length = normed.shape[0]
    score_scale = HD ** (-0.5)
    d_sum = grad_out * valid_rows[:, None]
    d_mlp = d_sum.astype(jnp.bfloat16)
    grad_down = left_product(act_low, d_mlp)
    d_gate, d_up = swiglu_back(right_product(d_mlp, w_down))
    d_gate = d_gate.astype(jnp.bfloat16)
    d_up = d_up.astype(jnp.bfloat16)
    grad_gate = left_product(normed_two, d_gate)
    grad_upper = left_product(normed_two, d_up)
    d_normed_two = right_product(d_gate, w_gate) + right_product(d_up, w_up)
    d_hidden_norm, grad_gain_two = norm_two_back(d_normed_two)
    d_hidden = d_sum + d_hidden_norm
    d_branch = d_hidden.astype(jnp.bfloat16)
    grad_attn_out = left_product(attn_mixed, d_branch)
    d_mixed = right_product(d_branch, w_attn_out).astype(jnp.bfloat16).reshape(query_low.shape)
    d_probs = jnp.einsum("qgrd,kgd->grqk", d_mixed, values_low, preferred_element_type=jnp.float32)
    d_values = jnp.einsum("grqk,qgrd->kgd", probs_low, d_mixed, preferred_element_type=jnp.float32)
    d_values = d_values.reshape(length, -1).astype(jnp.bfloat16)
    d_scores = attn_probs * (d_probs - jnp.sum(attn_probs * d_probs, axis=-1, keepdims=True))
    d_scores = d_scores.astype(jnp.bfloat16)
    d_query = (
        jnp.einsum("grqk,kgd->qgrd", d_scores, keys_low, preferred_element_type=jnp.float32)
        * score_scale
    )
    d_keys = (
        jnp.einsum("grqk,qgrd->kgd", d_scores, query_low, preferred_element_type=jnp.float32)
        * score_scale
    )
    d_query = (
        rotate(d_query.reshape(length, -1, HD), cosine, -sine_table)
        .reshape(length, -1)
        .astype(jnp.bfloat16)
    )
    d_keys = rotate(d_keys, cosine, -sine_table).reshape(length, -1).astype(jnp.bfloat16)
    grad_ssm_out = left_product(ssm_low, d_branch)
    ssm_grads = ssm_back(right_product(d_branch, w_ssm_out))
    d_gate_raw = ssm_grads[0].astype(jnp.bfloat16)
    d_conv_raw = ssm_grads[1].astype(jnp.bfloat16)
    d_step_raw = ssm_grads[2].astype(jnp.bfloat16)
    projections = (
        (d_query, w_query),
        (d_keys, w_key),
        (d_values, w_value),
        (d_gate_raw, w_ssm_gate),
        (d_conv_raw, w_conv_in),
        (d_step_raw, w_step),
    )
    grad_inputs = [left_product(normed, grad_low) for grad_low, weight in projections]
    d_normed = sum((right_product(grad_low, weight) for grad_low, weight in projections))
    d_input_norm, grad_gain_one = norm_one_back(d_normed)
    d_input = d_hidden + d_input_norm
    weight_grads = (
        grad_gain_one,
        grad_inputs[0],
        grad_inputs[1],
        grad_inputs[2],
        grad_attn_out,
        grad_inputs[3],
        grad_inputs[4],
        grad_inputs[5],
        ssm_grads[3],
        ssm_grads[4],
        ssm_grads[8],
        grad_ssm_out,
        grad_gain_two,
        grad_gate,
        grad_upper,
        grad_down,
    )
    head_grads = (ssm_grads[5], ssm_grads[6], ssm_grads[7])
    return (d_input, weight_grads, head_grads)


def body(
    inputs,
    teacher,
    lengths,
    order,
    loss_scale,
    norm_gain1,
    w_query,
    w_key,
    w_value,
    w_attn_out,
    w_ssm_gate,
    w_conv_in,
    w_step,
    conv_kernel,
    conv_bias,
    step_bias,
    decay_log,
    skip_gain,
    ssm_norm_gain,
    w_ssm_out,
    norm_gain2,
    w_gate,
    w_up,
    w_down,
):
    group_size = lax.axis_size("rep")
    section_index = lax.axis_index("section")
    first_section = section_index == 0
    device = lax.axis_index("fsdp") * group_size + lax.axis_index("rep")
    length = inputs.shape[1]
    model_width = inputs.shape[2]
    inverse_order = jnp.argsort(order)
    own_order = lax.dynamic_slice_in_dim(order, device * group_size, group_size)
    target = own_order // group_size % group_size
    sources = lax.dynamic_slice_in_dim(inverse_order, device * group_size, group_size)
    anchor = sources // group_size % group_size
    dealt_lengths = jnp.take(lengths, sources)
    own_data = jnp.where(first_section, inputs, teacher)
    outgoing = jnp.take(own_data, jnp.argsort(target), axis=0)
    arrived = lax.all_to_all(outgoing, "rep", split_axis=0, concat_axis=0, tiled=True)
    dealt_rows = jnp.take(arrived, anchor, axis=0)
    cosine, sine_table = rope_tables(length, HD)
    causal = lax.broadcasted_iota(jnp.int32, (length, length), 1) <= lax.broadcasted_iota(
        jnp.int32, (length, length), 0
    )
    tables = (cosine, sine_table, causal)
    positions = jnp.arange(length, dtype=jnp.int32)
    valid_count = jnp.sum(lengths).astype(jnp.float32)
    factor = loss_scale / (valid_count * model_width)
    gathered = (
        lax.all_gather(norm_gain1, "fsdp", axis=1, tiled=True),
        lax.all_gather(w_query, "fsdp", axis=1, tiled=True),
        lax.all_gather(w_key, "fsdp", axis=1, tiled=True),
        lax.all_gather(w_value, "fsdp", axis=1, tiled=True),
        lax.all_gather(w_attn_out, "fsdp", axis=1, tiled=True),
        lax.all_gather(w_ssm_gate, "fsdp", axis=1, tiled=True),
        lax.all_gather(w_conv_in, "fsdp", axis=1, tiled=True),
        lax.all_gather(w_step, "fsdp", axis=1, tiled=True),
        lax.all_gather(conv_kernel, "fsdp", axis=2, tiled=True),
        lax.all_gather(conv_bias, "fsdp", axis=1, tiled=True),
        lax.all_gather(ssm_norm_gain, "fsdp", axis=1, tiled=True),
        lax.all_gather(w_ssm_out, "fsdp", axis=1, tiled=True),
        lax.all_gather(norm_gain2, "fsdp", axis=1, tiled=True),
        lax.all_gather(w_gate, "fsdp", axis=1, tiled=True),
        lax.all_gather(w_up, "fsdp", axis=1, tiled=True),
        lax.all_gather(w_down, "fsdp", axis=1, tiled=True),
    )
    full_layer = tuple((piece[0] for piece in gathered))
    heads_in = (step_bias[0], decay_log[0], skip_gain[0])
    received = jnp.zeros((length, model_width), jnp.bfloat16)
    saved_list = []
    out_list = []
    for tick_index in range(group_size + 1):
        micro = jnp.clip(tick_index - section_index, 0, group_size - 1)
        seq_in = jnp.where(first_section, dealt_rows[min(tick_index, group_size - 1)], received)
        valid_rows = (positions < jnp.take(dealt_lengths, micro)).astype(jnp.float32)
        output, stored = layer_forward(seq_in, full_layer, heads_in, valid_rows, tables)
        out_low = output.astype(jnp.bfloat16)
        out_list.append(out_low)
        saved_list.append(stored)
        if tick_index < group_size:
            received = passed_along(out_low, "section", 1)
    out_stack = jnp.stack(out_list)
    held = lax.optimization_barrier(
        (
            (
                norm_gain1,
                w_query,
                w_key,
                w_value,
                w_attn_out,
                w_ssm_gate,
                w_conv_in,
                w_step,
                conv_kernel,
                conv_bias,
                ssm_norm_gain,
                w_ssm_out,
                norm_gain2,
                w_gate,
                w_up,
                w_down,
            ),
            out_stack,
        )
    )
    shards_again = held[0]
    out_stack = held[1]
    regathered = (
        lax.all_gather(shards_again[0], "fsdp", axis=1, tiled=True),
        lax.all_gather(shards_again[1], "fsdp", axis=1, tiled=True),
        lax.all_gather(shards_again[2], "fsdp", axis=1, tiled=True),
        lax.all_gather(shards_again[3], "fsdp", axis=1, tiled=True),
        lax.all_gather(shards_again[4], "fsdp", axis=1, tiled=True),
        lax.all_gather(shards_again[5], "fsdp", axis=1, tiled=True),
        lax.all_gather(shards_again[6], "fsdp", axis=1, tiled=True),
        lax.all_gather(shards_again[7], "fsdp", axis=1, tiled=True),
        lax.all_gather(shards_again[8], "fsdp", axis=2, tiled=True),
        lax.all_gather(shards_again[9], "fsdp", axis=1, tiled=True),
        lax.all_gather(shards_again[10], "fsdp", axis=1, tiled=True),
        lax.all_gather(shards_again[11], "fsdp", axis=1, tiled=True),
        lax.all_gather(shards_again[12], "fsdp", axis=1, tiled=True),
        lax.all_gather(shards_again[13], "fsdp", axis=1, tiled=True),
        lax.all_gather(shards_again[14], "fsdp", axis=1, tiled=True),
        lax.all_gather(shards_again[15], "fsdp", axis=1, tiled=True),
    )
    full_back = tuple((piece[0] for piece in regathered))
    accum = tuple((jnp.zeros(piece.shape, jnp.float32) for piece in full_back))
    head_accum = tuple((jnp.zeros(piece.shape, jnp.float32) for piece in heads_in))
    loss_part = jnp.zeros((), jnp.float32)
    incoming = jnp.zeros((length, model_width), jnp.bfloat16)
    grad_list = []
    for turn_index in range(group_size + 1):
        stored = saved_list[group_size - turn_index]
        valid_rows = stored[0]
        output = stored[-1]
        later_micro = max(group_size - 1 - turn_index, 0)
        later_flag = 1.0 if turn_index < group_size else 0.0
        first_flag = 1.0 if turn_index >= 1 else 0.0
        misfit = output - dealt_rows[later_micro].astype(jnp.float32)
        squares = later_flag * jnp.sum(valid_rows[:, None] * misfit * misfit)
        loss_part = loss_part + jnp.where(first_section, 0.0, squares)
        grad_seed = jnp.where(
            first_section,
            incoming.astype(jnp.float32) * first_flag,
            2.0 * later_flag * factor * valid_rows[:, None] * misfit,
        )
        d_input, weight_grads, head_grads = layer_backward(grad_seed, stored, full_back, tables)
        accum = tuple((total + extra for total, extra in zip(accum, weight_grads)))
        head_accum = tuple((total + extra for total, extra in zip(head_accum, head_grads)))
        grad_low = d_input.astype(jnp.bfloat16)
        grad_list.append(grad_low)
        if turn_index < group_size:
            incoming = passed_along(grad_low, "section", -1)
    acts_mine = lax.dynamic_slice_in_dim(out_stack, section_index, group_size, 0)
    grads_mine = lax.dynamic_slice_in_dim(jnp.stack(grad_list[::-1]), section_index, group_size, 0)
    back_data = jnp.where(first_section, grads_mine, acts_mine)
    outgoing_back = jnp.take(back_data, jnp.argsort(anchor), axis=0)
    returned = lax.all_to_all(outgoing_back, "rep", split_axis=0, concat_axis=0, tiled=True)
    restored = jnp.take(returned, target, axis=0)
    activations = jnp.where(first_section, acts_mine, restored)[None]
    gradients = jnp.where(first_section, restored, grads_mine)[None]
    (
        grad_gain_one,
        grad_query,
        grad_key,
        grad_value,
        grad_attn_out,
        grad_ssm_gate,
        grad_conv_in,
        grad_step,
        grad_kernel,
        grad_conv_bias,
        grad_ssm_gain,
        grad_ssm_out,
        grad_gain_two,
        grad_gate,
        grad_upper,
        grad_down,
    ) = accum
    pieces = (
        lax.psum_scatter(
            grad_gain_one[None].astype(jnp.bfloat16), "fsdp", scatter_dimension=1, tiled=True
        ).astype(jnp.float32),
        lax.psum_scatter(
            grad_query[None].astype(jnp.bfloat16), "fsdp", scatter_dimension=1, tiled=True
        ).astype(jnp.float32),
        lax.psum_scatter(
            grad_key[None].astype(jnp.bfloat16), "fsdp", scatter_dimension=1, tiled=True
        ).astype(jnp.float32),
        lax.psum_scatter(
            grad_value[None].astype(jnp.bfloat16), "fsdp", scatter_dimension=1, tiled=True
        ).astype(jnp.float32),
        lax.psum_scatter(
            grad_attn_out[None].astype(jnp.bfloat16), "fsdp", scatter_dimension=1, tiled=True
        ).astype(jnp.float32),
        lax.psum_scatter(
            grad_ssm_gate[None].astype(jnp.bfloat16), "fsdp", scatter_dimension=1, tiled=True
        ).astype(jnp.float32),
        lax.psum_scatter(
            grad_conv_in[None].astype(jnp.bfloat16), "fsdp", scatter_dimension=1, tiled=True
        ).astype(jnp.float32),
        lax.psum_scatter(
            grad_step[None].astype(jnp.bfloat16), "fsdp", scatter_dimension=1, tiled=True
        ).astype(jnp.float32),
        lax.psum_scatter(
            grad_kernel[None].astype(jnp.bfloat16), "fsdp", scatter_dimension=2, tiled=True
        ).astype(jnp.float32),
        lax.psum_scatter(
            grad_conv_bias[None].astype(jnp.bfloat16), "fsdp", scatter_dimension=1, tiled=True
        ).astype(jnp.float32),
        lax.psum_scatter(
            grad_ssm_gain[None].astype(jnp.bfloat16), "fsdp", scatter_dimension=1, tiled=True
        ).astype(jnp.float32),
        lax.psum_scatter(
            grad_ssm_out[None].astype(jnp.bfloat16), "fsdp", scatter_dimension=1, tiled=True
        ).astype(jnp.float32),
        lax.psum_scatter(
            grad_gain_two[None].astype(jnp.bfloat16), "fsdp", scatter_dimension=1, tiled=True
        ).astype(jnp.float32),
        lax.psum_scatter(
            grad_gate[None].astype(jnp.bfloat16), "fsdp", scatter_dimension=1, tiled=True
        ).astype(jnp.float32),
        lax.psum_scatter(
            grad_upper[None].astype(jnp.bfloat16), "fsdp", scatter_dimension=1, tiled=True
        ).astype(jnp.float32),
        lax.psum_scatter(
            grad_down[None].astype(jnp.bfloat16), "fsdp", scatter_dimension=1, tiled=True
        ).astype(jnp.float32),
    )
    shards = (
        lax.psum(pieces[0].astype(jnp.bfloat16), "rep").astype(jnp.float32),
        lax.psum(pieces[1].astype(jnp.bfloat16), "rep").astype(jnp.float32),
        lax.psum(pieces[2].astype(jnp.bfloat16), "rep").astype(jnp.float32),
        lax.psum(pieces[3].astype(jnp.bfloat16), "rep").astype(jnp.float32),
        lax.psum(pieces[4].astype(jnp.bfloat16), "rep").astype(jnp.float32),
        lax.psum(pieces[5].astype(jnp.bfloat16), "rep").astype(jnp.float32),
        lax.psum(pieces[6].astype(jnp.bfloat16), "rep").astype(jnp.float32),
        lax.psum(pieces[7].astype(jnp.bfloat16), "rep").astype(jnp.float32),
        lax.psum(pieces[8].astype(jnp.bfloat16), "rep").astype(jnp.float32),
        lax.psum(pieces[9].astype(jnp.bfloat16), "rep").astype(jnp.float32),
        lax.psum(pieces[10].astype(jnp.bfloat16), "rep").astype(jnp.float32),
        lax.psum(pieces[11].astype(jnp.bfloat16), "rep").astype(jnp.float32),
        lax.psum(pieces[12].astype(jnp.bfloat16), "rep").astype(jnp.float32),
        lax.psum(pieces[13].astype(jnp.bfloat16), "rep").astype(jnp.float32),
        lax.psum(pieces[14].astype(jnp.bfloat16), "rep").astype(jnp.float32),
        lax.psum(pieces[15].astype(jnp.bfloat16), "rep").astype(jnp.float32),
    )
    section_slots = (jnp.arange(lax.axis_size("section"), dtype=jnp.int32) == section_index)[
        :, None
    ]
    loss_total, bias_rows, decay_rows, skip_rows = lax.psum(
        (
            loss_part,
            jnp.where(section_slots, head_accum[0][None], 0.0),
            jnp.where(section_slots, head_accum[1][None], 0.0),
            jnp.where(section_slots, head_accum[2][None], 0.0),
        ),
        ("section", "fsdp", "rep"),
    )
    loss_value = loss_total / (valid_count * model_width)
    grad_bias_rows = lax.dynamic_slice_in_dim(bias_rows, section_index, 1, 0)
    grad_decay_rows = lax.dynamic_slice_in_dim(decay_rows, section_index, 1, 0)
    grad_skip_rows = lax.dynamic_slice_in_dim(skip_rows, section_index, 1, 0)
    return (
        activations,
        gradients,
        loss_value,
        shards[0],
        shards[1],
        shards[2],
        shards[3],
        shards[4],
        shards[5],
        shards[6],
        shards[7],
        shards[8],
        shards[9],
        grad_bias_rows,
        grad_decay_rows,
        grad_skip_rows,
        shards[10],
        shards[11],
        shards[12],
        shards[13],
        shards[14],
        shards[15],
    )


def solution(mesh):
    in_specs = (
        P(("fsdp", "rep"), None, None),
        P(("fsdp", "rep"), None, None),
        P(),
        P(),
        P(),
        P("section", "fsdp"),
        P("section", "fsdp", None),
        P("section", "fsdp", None),
        P("section", "fsdp", None),
        P("section", "fsdp", None),
        P("section", "fsdp", None),
        P("section", "fsdp", None),
        P("section", "fsdp", None),
        P("section", None, "fsdp"),
        P("section", "fsdp"),
        P("section", None),
        P("section", None),
        P("section", None),
        P("section", "fsdp"),
        P("section", "fsdp", None),
        P("section", "fsdp"),
        P("section", "fsdp", None),
        P("section", "fsdp", None),
        P("section", "fsdp", None),
    )
    out_specs = (
        P("section", ("fsdp", "rep"), None, None),
        P("section", ("fsdp", "rep"), None, None),
        P(),
        P("section", "fsdp"),
        P("section", "fsdp", None),
        P("section", "fsdp", None),
        P("section", "fsdp", None),
        P("section", "fsdp", None),
        P("section", "fsdp", None),
        P("section", "fsdp", None),
        P("section", "fsdp", None),
        P("section", None, "fsdp"),
        P("section", "fsdp"),
        P("section", None),
        P("section", None),
        P("section", None),
        P("section", "fsdp"),
        P("section", "fsdp", None),
        P("section", "fsdp"),
        P("section", "fsdp", None),
        P("section", "fsdp", None),
        P("section", "fsdp", None),
    )
    return jax.shard_map(body, mesh=mesh, in_specs=in_specs, out_specs=out_specs, check_vma=False)
```

profile of v0, /device:TPU:0, one launch (start us, length us, event | category | flops | bytes accessed | tf_op | source)
XLA Modules:
  0.0 1993.1 jit_solution(13454789998857789368)
XLA Ops:
  46.1 14.4 all_gather.88
  96.6 37.1 %slice_reduce_fusion.3 = (f32[1792]{0:T(1024)S(1)}, f32[1792]{0:T(1024)S(1)}, f32[1792]{0:T(1024)S(1)}, f32[1792]{0:T(1024)S(1)}) fusion(f32[1,4,1792]{1,0,2:T(1,128)S(1)} %convert_element_type.862), kind=kLoop, calls=%fused_computation.869 | loop fusion | bytes 57344 | tf_op jit(solution)/shard_map/jvp()/slice | solution.py:86
  162.0 10.5 bitcast_add_fusion.9
  193.6 25.6 %all-gather.29.cloned.1.call-done = bf16[1,1024,2048]{2,1,0:T(8,128)(2,1)} async-done(((bf16[1,256,2048]{2,1,0:T(8,128)(2,1)}), bf16[1,1024,2048]{2,1,0:T(8,128)(2,1)}) %all-gather.29.cloned.1.call-update) | async-done | bytes 4194320 | tf_op jit(solution)/shard_map/all_gather | solution.py:373
  225.3 30.0 %all-gather.31.cloned.1.call-done = bf16[1,2048,1024]{2,1,0:T(8,128)(2,1)} async-done(((bf16[1,512,1024]{2,1,0:T(8,128)(2,1)}), bf16[1,2048,1024]{2,1,0:T(8,128)(2,1)}) %all-gather.31.cloned.1.call-update) | async-done | bytes 4194320 | tf_op jit(solution)/shard_map/all_gather | solution.py:374
  589.8 29.0 %all-gather.37.cloned.1.call-done = bf16[1,1024,2048]{2,1,0:T(8,128)(2,1)} async-done(((bf16[1,256,2048]{2,1,0:T(8,128)(2,1)}), bf16[1,1024,2048]{2,1,0:T(8,128)(2,1)}) %all-gather.37.cloned.1.call-update) | async-done | bytes 4194320 | tf_op jit(solution)/shard_map/all_gather | solution.py:432
  623.6 31.3 %all-gather.35.cloned.1.call-done = bf16[1,1024,2048]{2,1,0:T(8,128)(2,1)} async-done(((bf16[1,256,2048]{2,1,0:T(8,128)(2,1)}), bf16[1,1024,2048]{2,1,0:T(8,128)(2,1)}) %all-gather.35.cloned.1.call-update) | async-done | bytes 4194320 | tf_op jit(solution)/shard_map/all_gather | solution.py:431
  661.6 23.3 %all-gather.43.cloned.1.call-done = bf16[1,1536,1024]{2,1,0:T(8,128)(2,1)} async-done(((bf16[1,384,1024]{2,1,0:T(8,128)(2,1)}), bf16[1,1536,1024]{2,1,0:T(8,128)(2,1)}) %all-gather.43.cloned.1.call-update) | async-done | bytes 3145744 | tf_op jit(solution)/shard_map/all_gather | solution.py:429
  725.4 11.1 fusion.116
  864.0 11.6 fusion.118
  1000.2 11.1 fusion.120
  1131.8 11.1 fusion.122
  1363.2 11.0 fusion.124
  1382.0 12.3 fusion.145
  1415.1 15.5 fusion.146
  1450.9 14.0 fusion.147
  1485.2 14.2 fusion.148
  1536.8 14.3 reduce-scatter.45.cloned.1.call-done
  1551.2 47.1 %reduce-scatter.47.cloned.1.call-done = bf16[1,512,1024]{2,1,0:T(8,128)(2,1)} async-done(((bf16[1,2048,1024]{2,1,0:T(8,128)(2,1)}), bf16[1,512,1024]{2,1,0:T(8,128)(2,1)}) %reduce-scatter.47.cloned.1.call-update) | async-done | bytes 1048592 | tf_op jit(solution)/shard_map/reduce_scatter | solution.py:535
  1621.8 63.2 %all-reduce.66 = (f32[]{:T(128)}, f32[2,24]{1,0:T(2,128)S(1)}, f32[2,24]{1,0:T(2,128)S(1)}, f32[2,24]{1,0:T(2,128)S(1)}) all-reduce(f32[]{:T(128)S(6)} %add.1646, f32[2,24]{1,0:T(2,128)S(1)} %get-tuple-element.517, f32[2,24]{1,0:T(2,128)S(1)} %get-tuple-element.516, ...), channel_id=1, replica_groups=mesh['section'=2,'fsdp'=4,'rep'=4] {'section','fsdp','rep'}, use_global_device_ids=true, to_apply=%region_109.111 | all-reduce | flops 145 | bytes 1160 | tf_op jit(solution)/shard_map/psum | solution.py:560
  1693.5 23.3 %reduce-scatter.51.cloned.1.call-done = bf16[448,4]{1,0:T(8,128)(2,1)} async-done(((bf16[1792,4]{1,0:T(8,128)(2,1)}), bf16[448,4]{1,0:T(8,128)(2,1)}) %reduce-scatter.51.cloned.1.call-update) | async-done | bytes 3600
  1718.0 21.3 %reduce-scatter.39.cloned.1.call-done = bf16[1,256,24]{1,2,0:T(8,128)(2,1)} async-done(((bf16[1,1024,24]{1,2,0:T(8,128)(2,1)}), bf16[1,256,24]{1,2,0:T(8,128)(2,1)}) %reduce-scatter.39.cloned.1.call-update) | async-done | bytes 12304 | tf_op jit(solution)/shard_map/reduce_scatter | solution.py:511
  1739.3 19.4 all-reduce.67
  1770.5 198.6 %all-reduce.71.cloned.1.call-done = (bf16[1,256,512]{2,1,0:T(8,128)(2,1)}, bf16[1,256,128]{2,1,0:T(8,128)(2,1)}, bf16[1,256,128]{2,1,0:T(8,128)(2,1)}, bf16[1,12...) async-done(((bf16[1,256,512]{2,1,0:T(8,128)(2,1)}, ...) | async-done | bytes 6291472 | tf_op jit(solution)/shard_map/psum | solution.py:541
  (2132 shorter events, 1260.3 us)
Async XLA Ops:
  8.7 166.8 %all-gather.23.cloned.1.call-start = ((), (), s32[]{:S(2)}) async-start(), calls=%async_computation.21 | async-start | bytes 3932160 | tf_op jit(solution)/shard_map/all_gather | solution.py:364
  9.4 171.3 %all-gather.25.cloned.1.call-start = ((), (), s32[]{:S(2)}) async-start(), calls=%async_computation.22 | async-start | bytes 3932160 | tf_op jit(solution)/shard_map/all_gather | solution.py:370
  10.0 175.2 %all-gather.19.cloned.1.call-start = ((), (), s32[]{:S(2)}) async-start(), calls=%async_computation.19 | async-start | bytes 1310720 | tf_op jit(solution)/shard_map/all_gather | solution.py:363
  10.6 177.9 %all-gather.27.cloned.1.call-start = ((), (), s32[]{:S(2)}) async-start(), calls=%async_computation.23 | async-start | bytes 5242880 | tf_op jit(solution)/shard_map/all_gather | solution.py:372
  11.2 208.0 %all-gather.29.cloned.1.call-start = ((), (), s32[]{:S(2)}) async-start(), calls=%async_computation.24 | async-start | bytes 5242880 | tf_op jit(solution)/shard_map/all_gather | solution.py:373
  30.8 224.5 %all-gather.31.cloned.1.call-start = ((), (), s32[]{:S(2)}) async-start(), calls=%async_computation.25 | async-start | bytes 5242880 | tf_op jit(solution)/shard_map/all_gather | solution.py:374
  31.6 551.3 %all-gather.33.cloned.1.call-start = ((), (), s32[]{:S(2)}) async-start(), calls=%async_computation.26 | async-start | bytes 5242880 | tf_op jit(solution)/shard_map/all_gather | solution.py:433
  546.2 200.7 %all-gather.39.cloned.1.call-start = ((), (), s32[]{:S(2)}) async-start(), calls=%async_computation.29 | async-start | bytes 1310720 | tf_op jit(solution)/shard_map/all_gather | solution.py:422
  547.0 229.4 %all-gather.41.cloned.1.call-start = ((), (), s32[]{:S(2)}) async-start(), calls=%async_computation.30 | async-start | bytes 1310720 | tf_op jit(solution)/shard_map/all_gather | solution.py:419
  547.6 234.0 %all-gather.47.cloned.1.call-start = ((), (), s32[]{:S(2)}) async-start(), calls=%async_computation.33 | async-start | bytes 4587520 | tf_op jit(solution)/shard_map/all_gather | solution.py:424
  548.2 237.9 %all-gather.45.cloned.1.call-start = ((), (), s32[]{:S(2)}) async-start(), calls=%async_computation.32 | async-start | bytes 3932160 | tf_op jit(solution)/shard_map/all_gather | solution.py:423
  572.6 964.0 %reduce-scatter.29.cloned.1.call-start = ((), (), s32[]{:S(2)}) async-start(), calls=%async_computation.35 | async-start | bytes 327680 | tf_op jit(solution)/shard_map/reduce_scatter | solution.py:496
  1235.2 301.4 %reduce-scatter.31.cloned.1.call-start = ((), (), s32[]{:S(2)}) async-start(), calls=%async_computation.36 | async-start | bytes 327680 | tf_op jit(solution)/shard_map/reduce_scatter | solution.py:499
  1245.4 291.3 %reduce-scatter.27.cloned.1.call-start = ((), (), s32[]{:S(2)}) async-start(), calls=%async_computation.34 | async-start | bytes 1310720 | tf_op jit(solution)/shard_map/reduce_scatter | solution.py:493
  1252.1 284.6 %reduce-scatter.33.cloned.1.call-start = ((), (), s32[]{:S(2)}) async-start(), calls=%async_computation.37 | async-start | bytes 1310720 | tf_op jit(solution)/shard_map/reduce_scatter | solution.py:502
  1286.1 250.7 %reduce-scatter.35.cloned.1.call-start = ((), (), s32[]{:S(2)}) async-start(), calls=%async_computation.38 | async-start | bytes 3932160 | tf_op jit(solution)/shard_map/reduce_scatter | solution.py:505
  1307.5 229.3 %reduce-scatter.41.cloned.1.call-start = ((), (), s32[]{:S(2)}) async-start(), calls=%async_computation.41 | async-start | bytes 3932160 | tf_op jit(solution)/shard_map/reduce_scatter | solution.py:523
  1329.3 207.5 %reduce-scatter.37.cloned.1.call-start = ((), (), s32[]{:S(2)}) async-start(), calls=%async_computation.39 | async-start | bytes 4587520 | tf_op jit(solution)/shard_map/reduce_scatter | solution.py:508
  1499.6 187.5 %reduce-scatter.49.cloned.1.call-start = ((), (), s32[]{:S(2)}) async-start(), calls=%async_computation.45 | async-start | bytes 327680
  1529.8 158.3 %reduce-scatter.57.cloned.1.call-start = ((), (), s32[]{:S(2)}) async-start(), calls=%async_computation.49 | async-start | bytes 327680
  1532.0 160.6 %reduce-scatter.53.cloned.1.call-start = ((), (), s32[]{:S(2)}) async-start(), calls=%async_computation.47 | async-start | bytes 573440
  1533.3 183.6 %reduce-scatter.51.cloned.1.call-start = ((), (), s32[]{:S(2)}) async-start(), calls=%async_computation.46 | async-start | bytes 573440
  1535.5 203.8 %reduce-scatter.39.cloned.1.call-start = ((), (), s32[]{:S(2)}) async-start(), calls=%async_computation.40 | async-start | bytes 61440 | tf_op jit(solution)/shard_map/reduce_scatter | solution.py:511
  1536.6 432.5 %all-reduce.71.cloned.1.call-start = ((), (), s32[]{:S(2)}) async-start(), calls=%async_computation.50 | async-start | bytes 12582912 | tf_op jit(solution)/shard_map/psum | solution.py:541
  (701 other events, 6341.4 us)
Sparse Core Ops, SparseCore 0:
  30.6 36.5 all-gather.20
  68.8 30.1 all-gather.22
  100.4 28.5 all-gather.24
  148.6 34.4 all-gather.26
  184.7 34.4 all-gather.28
  220.8 34.4 all-gather.30
  544.4 38.4 all-gather.32
  584.3 34.4 all-gather.36
  620.4 34.4 all-gather.34
  656.3 28.5 all-gather.42
  722.8 31.4 all-gather.46
  755.8 28.5 all-gather.44
  1279.5 24.8 reduce-scatter.26
  1307.0 24.8 reduce-scatter.32
  1334.5 37.9 reduce-scatter.34
  1375.1 37.9 reduce-scatter.40
  1415.6 41.2 reduce-scatter.36
  1459.5 44.5 reduce-scatter.42
  1506.6 44.5 reduce-scatter.44
  1553.7 44.5 reduce-scatter.46
  1647.5 20.7 reduce-scatter.54
  1671.3 21.1 reduce-scatter.52
  1695.6 21.1 reduce-scatter.50
  1742.7 226.3 all-reduce.70
  (9 shorter events, 167.7 us)
where the time goes:
time: 2000 us; the launch traced here: 1990 us
  matrix products  729 us (36%)
  waiting for transfers between devices  528 us (26%)
  local copies, waits for them, and re-layouts  260 us (13%)
  other arithmetic  243 us (12%)
  blocking collectives  162 us (8%)
  starting transfers between devices  39.1 us (2%)
  between operations  32.4 us (2%)
    dot_general x55, matrix products, left_product(): lax.dot_general(left_side, right_side, (((0,), (0,)), ((), ())), preferre...  225 us
    psum x1, waiting for transfers between devices, body(): lax.psum(pieces[1].astype(jnp.bfloat16), 'rep').astype(jnp.float32)  199 us
    dot_general x20, matrix products, mixer_core(): jnp.einsum('hts,shp->thp', weights, scaled, precision=HIGHEST, preferred_...  197 us
    dot_general x55, matrix products, matmul(): return jnp.dot(left_side, right_side, preferred_element_type=jnp.float32)  125 us
    dot_general x55, matrix products, right_product(): lax.dot_general(left_side, right_side, (((1,), (1,)), ((), ())), preferre...  95.9 us
    unnamed x1381, local copies, waits for them, and re-layouts  74.1 us
    psum x1, blocking collectives, body(): lax.psum((loss_part, jnp.where(section_slots, head_accum[0][None], 0.0),...  63.2 us
    ppermute x8, waiting for transfers between devices, passed_along(): return lax.ppermute(block, axis, route)  62.1 us
  transfers between devices with their start and end apart: 43, of which 20 were waited for; matrix products, arithmetic and copies ran while one was open for 29% of the time, Pallas kernels for 0%

commit v1 on v0

v1 whole, which is shorter than its diff:
```python
import math
import functools

import jax
import jax.numpy as jnp
from jax import lax
from jax.experimental import pallas as pl
from jax.experimental.pallas import tpu as pltpu
from jax.sharding import PartitionSpec as P

HD = 64
EPSILON = 1e-05
ROPE_BASE = 100000000000.0
MASKED = -1e30
F32 = jnp.float32
BF = jnp.bfloat16
TILE = 256
HALF = 128
ANY = pl.BlockSpec(memory_space=pl.ANY)
VM = pl.BlockSpec(memory_space=pltpu.VMEM)
SM = pl.BlockSpec(memory_space=pltpu.SMEM)


def dot(a, b):
    return jnp.dot(a, b, preferred_element_type=F32)


def dot_nt(a, b):
    return lax.dot_general(a, b, (((1,), (1,)), ((), ())), preferred_element_type=F32)


def dot_tn(a, b):
    return lax.dot_general(a, b, (((0,), (0,)), ((), ())), preferred_element_type=F32)


def sigmoid(v):
    return 0.5 * jnp.tanh(0.5 * v) + 0.5


def lanes(i, width=TILE):
    return pl.ds(pl.multiple_of(i * width, width), width)


def iota(shape, axis):
    return lax.broadcasted_iota(jnp.int32, shape, axis)


def split2(v):
    hi = v.astype(BF)
    return hi, (v - hi.astype(F32)).astype(BF)


def split3(v):
    hi = v.astype(BF)
    rest = v - hi.astype(F32)
    mid = rest.astype(BF)
    return hi, mid, (rest - mid.astype(F32)).astype(BF)


def expand_matrix(tile):
    row = jnp.bitwise_and(iota((TILE, TILE), 0), HALF - 1)
    col = jnp.right_shift(iota((TILE, TILE), 1), 6) + tile * (TILE // HD)
    return jnp.where(row == col, 1.0, 0.0).astype(BF)


def reduce_matrix(tile):
    row = jnp.right_shift(iota((TILE, HALF), 0), 6) + tile * (TILE // HD)
    col = iota((TILE, HALF), 1)
    return jnp.where(row == col, 1.0, 0.0).astype(BF)


def both(v):
    return jnp.concatenate(split2(v), axis=1)


def rope(v, cosine, sine, first):
    turned = jnp.where(first, pltpu.roll(v, HALF - HD // 2, 1), pltpu.roll(v, HD // 2, 1))
    return v * cosine + turned * sine


def copies_in(pairs, sems):
    copies = [pltpu.make_async_copy(a, b, sems.at[i]) for i, (a, b) in enumerate(pairs)]
    for copy in copies:
        copy.start()
    return copies


V_TAP, V_CBIAS, V_GS, V_SKIP, V_G1, V_G2, V_SBIAS, V_DECAY = 0, 4, 5, 6, 7, 8, 9, 10


def scan_terms(step_raw, vec_ref, heads):
    lane = iota(step_raw.shape, 1)
    pre = step_raw + vec_ref[V_SBIAS : V_SBIAS + 1, :HALF]
    soft = jnp.maximum(pre, 0.0) + jnp.log1p(jnp.exp(-jnp.abs(pre)))
    step = jnp.where(lane < heads, soft, 0.0)
    change = step * vec_ref[V_DECAY : V_DECAY + 1, :HALF]
    length = step.shape[0]
    lower = jnp.where(
        iota((length, length), 0) >= iota((length, length), 1), 1.0, 0.0
    ).astype(BF)
    run = sum(dot(lower, part) for part in split3(change))
    middle = run[HALF - 1 : HALF, :]
    bend = jnp.where(iota(run.shape, 0) < HALF, middle - run, run - middle)
    bend = jnp.exp(jnp.minimum(bend, 0.0))
    return pre, step, change, run, bend


def broadcast_runs(run, run_wide, heads):
    for h in range(heads):
        run_wide[:, h * HALF : (h + 1) * HALF] = jnp.broadcast_to(
            run[:, h : h + 1], (run.shape[0], HALF)
        )


def mix_forward(
    slot_ref, x_ref, vec_ref, cos_ref, sin_ref, win_hbm, wout_hbm, *rest, n_stack, widths
):
    ci, mi, qw, kw, heads = widths
    outs = rest[n_stack : 2 * n_stack + 1]
    stacks, hidden_ref = outs[:n_stack], outs[n_stack]
    (win, wout, normed, conv_raw, z, xbc, gate_raw, qkv, step_raw, probs, branch, y, gated,
     run_wide, run_row, step_two, bend_two, in_sem, out_sem) = rest[2 * n_stack + 1 :]
    (s_normed, s_conv, s_z, s_gate, s_qkv, s_step, s_probs, s_branch, s_y, s_hidden, s_x) = stacks
    slot, active = slot_ref[0], slot_ref[1] > 0
    g0 = ci
    q0 = ci + mi
    total = win.shape[1]
    load = copies_in(
        [
            (win_hbm.at[:, q0:total], win.at[:, q0:total]),
            (win_hbm.at[:, 0:ci], win.at[:, 0:ci]),
            (win_hbm.at[:, g0:q0], win.at[:, g0:q0]),
            (wout_hbm, wout),
        ],
        in_sem,
    )
    stores = []

    def save(buffer, stack):
        copy = pltpu.make_async_copy(buffer, stack.at[slot], out_sem.at[len(stores)])
        pl.when(active)(copy.start)
        stores.append(copy)

    length = x_ref.shape[0]
    x = x_ref[...].astype(F32)
    rate = lax.rsqrt(jnp.mean(x * x, axis=-1, keepdims=True) + EPSILON)
    normed[...] = (x * rate * vec_ref[V_G1 : V_G1 + 1, : x.shape[1]]).astype(BF)
    save(normed, s_normed)
    lane_first = jnp.bitwise_and(iota((length, HALF), 1), HD - 1) < HD // 2
    half_low = iota((length, HALF), 1) < HD

    load[0].wait()
    cosine, sine = cos_ref[...], sin_ref[...]
    n_rope = (qw + kw) // HALF
    for t in range((total - q0) // HALF // 2):
        raw = dot(normed[...], win[:, q0 + t * TILE : q0 + (t + 1) * TILE])
        for part in range(2):
            c = 2 * t + part
            piece = raw[:, part * HALF : (part + 1) * HALF]
            if c < n_rope:
                piece = rope(piece, cosine, sine, lane_first)
            if c < n_rope + kw // HALF:
                qkv[:, c * HALF : (c + 1) * HALF] = piece.astype(BF)
            else:
                step_raw[...] = piece
    if ((total - q0) // HALF) % 2:
        step_raw[...] = dot(normed[...], win[:, total - HALF : total])
    save(qkv, s_qkv)
    save(step_raw, s_step)

    load[1].wait()
    row = iota((length, TILE), 0)

    def conv_tile(t, carry):
        cols = lanes(t)
        raw = dot(normed[...], win[:, cols])
        conv_raw[:, cols] = raw.astype(BF)
        total_z = vec_ref[V_CBIAS : V_CBIAS + 1, cols] + raw * vec_ref[3:4, cols]
        for back in range(1, 4):
            moved = jnp.where(row >= back, pltpu.roll(raw, back, 0), 0.0)
            total_z = total_z + moved * vec_ref[3 - back : 4 - back, cols]
        z[:, cols] = total_z.astype(BF)
        xbc[:, cols] = (total_z * sigmoid(total_z)).astype(BF)
        return carry

    lax.fori_loop(0, ci // TILE, conv_tile, 0)
    save(conv_raw, s_conv)
    save(z, s_z)

    load[2].wait()

    def gate_tile(t, carry):
        raw = dot(normed[...], win[:, pl.ds(pl.multiple_of(g0 + t * TILE, TILE), TILE)])
        gate_raw[:, lanes(t)] = raw.astype(BF)
        return carry

    lax.fori_loop(0, mi // TILE, gate_tile, 0)
    save(gate_raw, s_gate)

    keys, values = qkv[:, qw : qw + kw], qkv[:, qw + kw : qw + 2 * kw]
    keys_far, values_far = pltpu.roll(keys.astype(F32), HD, 1).astype(BF), pltpu.roll(
        values.astype(F32), HD, 1
    ).astype(BF)
    causal_top = iota((HALF, HALF), 1) <= iota((HALF, HALF), 0)
    causal_low = iota((HALF, length), 1) <= iota((HALF, length), 0) + HALF
    pairs = qw // HALF
    groups = kw // HD
    probs_zero = jnp.zeros((HALF, HALF), BF)
    for pair in range(pairs):
        group = pair // (pairs // groups)
        keep = half_low if group == 0 else jnp.logical_not(half_low)
        keys_two = jnp.where(keep, keys, keys_far)
        values_two = jnp.where(keep, values, values_far)
        query = qkv[:, pair * HALF : (pair + 1) * HALF] * jnp.asarray(HD ** (-0.5), BF)
        results = []
        for side in range(2):
            own = half_low if side == 0 else jnp.logical_not(half_low)
            q = jnp.where(own, query, jnp.zeros_like(query))
            at = (2 * pair + side) * length
            out = []
            for lo, causal in ((0, causal_top), (1, causal_low)):
                width = HALF if lo == 0 else length
                scores = dot_nt(q[lo * HALF : (lo + 1) * HALF], keys_two[:width])
                scores = jnp.where(causal, scores, MASKED)
                top = jnp.max(scores, axis=-1, keepdims=True)
                weights = jnp.exp(scores - top)
                weights = weights / jnp.sum(weights, axis=-1, keepdims=True)
                weights = weights.astype(BF)
                if lo == 0:
                    probs[at : at + HALF, :HALF] = weights
                    probs[at : at + HALF, HALF:] = probs_zero
                else:
                    probs[at + HALF : at + length, :] = weights
                out.append(dot(weights, values_two[:width]))
            results.append(jnp.concatenate(out, axis=0))
        mixed = jnp.where(half_low, results[0], results[1])
        branch[:, mi + pair * HALF : mi + (pair + 1) * HALF] = mixed.astype(BF)
    save(probs, s_probs)

    pre, step, change, run, bend = scan_terms(step_raw[...], vec_ref, heads)
    turned = run.T
    run_row[:HALF, :] = turned[:, :HALF]
    run_row[HALF:, :] = turned[:, HALF:]
    broadcast_runs(run, run_wide, heads)
    step_two[...] = both(step)
    bend_two[...] = both(bend)
    b_in, c_in = xbc[:, mi : mi + HALF], xbc[:, mi + HALF : mi + 2 * HALF]
    tops = [dot_nt(c_in[c * HALF : (c + 1) * HALF], b_in[c * HALF : (c + 1) * HALF]) for c in (0, 1)]
    cross = dot_nt(c_in[HALF:], b_in[:HALF]).astype(BF)
    pair_low = iota((HALF, HALF), 1) < HD
    tops = [jnp.where(causal_top, t, 0.0) for t in tops]

    def mix_tile(t, squares):
        cols = lanes(t)
        spread = expand_matrix(t)
        x_in = xbc[:, cols].astype(F32)
        scaled = (dot(step_two[...], spread) * x_in).astype(BF)
        bends = dot(bend_two[...], spread)
        u = (bends[:HALF] * scaled[:HALF].astype(F32)).astype(BF)
        far = dot(cross, u) * bends[HALF:]
        parts = []
        for p in range(TILE // HALF):
            block = []
            for c in range(2):
                rows = slice(c * HALF, (c + 1) * HALF)
                weights = []
                for side in range(2):
                    h = t * (TILE // HD) + 2 * p + side
                    wide = run_wide[rows, lanes(h, HALF)]
                    line = run_row[pl.ds(c * HALF + h, 1), :]
                    decay = jnp.exp(jnp.minimum(wide - line, 0.0))
                    weights.append((decay * tops[c]).astype(BF))
                xs = scaled[rows, p * HALF : (p + 1) * HALF]
                zero = jnp.zeros_like(xs)
                right = jnp.concatenate(
                    [jnp.where(pair_low, xs, zero), jnp.where(pair_low, zero, xs)], axis=0
                )
                block.append(dot(jnp.concatenate(weights, axis=1), right))
            parts.append(jnp.concatenate(block, axis=0))
        out = jnp.concatenate(parts, axis=1)
        out = out + jnp.concatenate([jnp.zeros_like(far), far], axis=0)
        out = out + vec_ref[V_SKIP : V_SKIP + 1, cols] * x_in
        y[:, cols] = out.astype(BF)
        g = gate_raw[:, cols].astype(F32)
        out = out * (g * sigmoid(g))
        gated[:, cols] = out
        return squares + jnp.sum(out * out, axis=-1, keepdims=True)

    squares = lax.fori_loop(0, mi // TILE, mix_tile, jnp.zeros((length, 1), F32))
    save(y, s_y)
    rate = lax.rsqrt(squares * (1.0 / mi) + EPSILON)
    branch[:, :mi] = (gated[...] * rate * vec_ref[V_GS : V_GS + 1, :mi]).astype(BF)
    save(branch, s_branch)

    load[3].wait()

    def out_tile(t, carry):
        cols = lanes(t)
        hidden_ref[:, cols] = x_ref[:, cols].astype(F32) + dot(branch[...], wout[:, cols])
        return carry

    lax.fori_loop(0, wout.shape[1] // TILE, out_tile, 0)
    save(hidden_ref, s_hidden)
    save(x_ref, s_x)
    for copy in stores:
        pl.when(active)(copy.wait)


def mixer_forward_call(slot, x, vec, cosine, sine, win, wout, stacks, widths):
    ci, mi, qw, kw, heads = widths
    length, width = x.shape
    n_stack = len(stacks)
    scratch = [
        pltpu.VMEM(win.shape, BF),
        pltpu.VMEM(wout.shape, BF),
        pltpu.VMEM((length, width), BF),
        pltpu.VMEM((length, ci), BF),
        pltpu.VMEM((length, ci), BF),
        pltpu.VMEM((length, ci), BF),
        pltpu.VMEM((length, mi), BF),
        pltpu.VMEM((length, qw + 2 * kw), BF),
        pltpu.VMEM((length, HALF), F32),
        pltpu.VMEM((qw // HD * length, length), BF),
        pltpu.VMEM((length, mi + qw), BF),
        pltpu.VMEM((length, mi), BF),
        pltpu.VMEM((length, mi), F32),
        pltpu.VMEM((length, heads * HALF), F32),
        pltpu.VMEM((length, HALF), F32),
        pltpu.VMEM((length, 2 * HALF), BF),
        pltpu.VMEM((length, 2 * HALF), BF),
        pltpu.SemaphoreType.DMA((4,)),
        pltpu.SemaphoreType.DMA((n_stack,)),
    ]
    out = pl.pallas_call(
        functools.partial(mix_forward, n_stack=n_stack, widths=widths),
        out_shape=[jax.ShapeDtypeStruct(s.shape, s.dtype) for s in stacks]
        + [jax.ShapeDtypeStruct((length, width), F32)],
        in_specs=[SM, VM, VM, VM, VM, ANY, ANY] + [ANY] * n_stack,
        out_specs=[ANY] * n_stack + [VM],
        scratch_shapes=scratch,
        input_output_aliases={7 + i: i for i in range(n_stack)},
        compiler_params=pltpu.CompilerParams(vmem_limit_bytes=44 * 1024 * 1024),
        cost_estimate=pl.CostEstimate(
            flops=2 * length * (win.size + wout.size), bytes_accessed=24000000, transcendentals=0
        ),
        name="mixer_forward",
    )(slot, x, vec, cosine, sine, win, wout, *stacks)
    return list(out[:n_stack]), out[n_stack]


def mlp_forward(slot_ref, hidden_ref, valid_ref, vec_ref, wgu_hbm, wdown_hbm, *rest, n_stack):
    outs = rest[n_stack : 2 * n_stack + 1]
    stacks, low_ref = outs[:n_stack], outs[n_stack]
    wgu, wdown, normed, gu, act, final, in_sem, out_sem = rest[2 * n_stack + 1 :]
    s_normed, s_gu, s_act, s_final, s_low = stacks
    slot, active = slot_ref[0], slot_ref[1] > 0
    ff = wdown.shape[0]
    parts = 4
    step = ff // parts
    pairs = []
    for i in range(parts):
        a = slice(i * step, (i + 1) * step)
        b = slice(ff + i * step, ff + (i + 1) * step)
        pairs += [(wgu_hbm.at[:, a], wgu.at[:, a]), (wgu_hbm.at[:, b], wgu.at[:, b])]
    pairs.append((wdown_hbm, wdown))
    load = copies_in(pairs, in_sem)
    stores = []

    def save(buffer, stack):
        copy = pltpu.make_async_copy(buffer, stack.at[slot], out_sem.at[len(stores)])
        pl.when(active)(copy.start)
        stores.append(copy)

    hidden = hidden_ref[...]
    rate = lax.rsqrt(jnp.mean(hidden * hidden, axis=-1, keepdims=True) + EPSILON)
    normed[...] = (hidden * rate * vec_ref[V_G2 : V_G2 + 1, : hidden.shape[1]]).astype(BF)
    save(normed, s_normed)
    for i in range(parts):
        load[2 * i].wait()
        load[2 * i + 1].wait()

        def up_tile(t, carry):
            a = pl.ds(pl.multiple_of(i * step + t * TILE, TILE), TILE)
            b = pl.ds(pl.multiple_of(ff + i * step + t * TILE, TILE), TILE)
            gate = dot(normed[...], wgu[:, a])
            up = dot(normed[...], wgu[:, b])
            gu[:, a] = gate.astype(BF)
            gu[:, b] = up.astype(BF)
            act[:, a] = (gate * sigmoid(gate) * up).astype(BF)
            return carry

        lax.fori_loop(0, step // TILE, up_tile, 0)
    save(gu, s_gu)
    save(act, s_act)
    load[2 * parts].wait()

    def down_tile(t, carry):
        cols = lanes(t)
        out = (hidden_ref[:, cols] + dot(act[...], wdown[:, cols])) * valid_ref[...]
        final[:, cols] = out
        low_ref[:, cols] = out.astype(BF)
        return carry

    lax.fori_loop(0, wdown.shape[1] // TILE, down_tile, 0)
    save(final, s_final)
    save(low_ref, s_low)
    for copy in stores:
        pl.when(active)(copy.wait)


def mlp_forward_call(slot, hidden, valid, vec, wgu, wdown, stacks):
    length, width = hidden.shape
    ff = wdown.shape[0]
    n_stack = len(stacks)
    scratch = [
        pltpu.VMEM(wgu.shape, BF),
        pltpu.VMEM(wdown.shape, BF),
        pltpu.VMEM((length, width), BF),
        pltpu.VMEM((length, 2 * ff), BF),
        pltpu.VMEM((length, ff), BF),
        pltpu.VMEM((length, width), F32),
        pltpu.SemaphoreType.DMA((9,)),
        pltpu.SemaphoreType.DMA((n_stack,)),
    ]
    out = pl.pallas_call(
        functools.partial(mlp_forward, n_stack=n_stack),
        out_shape=[jax.ShapeDtypeStruct(s.shape, s.dtype) for s in stacks]
        + [jax.ShapeDtypeStruct((length, width), BF)],
        in_specs=[SM, VM, VM, VM, ANY, ANY] + [ANY] * n_stack,
        out_specs=[ANY] * n_stack + [VM],
        scratch_shapes=scratch,
        input_output_aliases={6 + i: i for i in range(n_stack)},
        compiler_params=pltpu.CompilerParams(vmem_limit_bytes=32 * 1024 * 1024),
        cost_estimate=pl.CostEstimate(
            flops=2 * length * (wgu.size + wdown.size), bytes_accessed=19000000, transcendentals=0
        ),
        name="mlp_forward",
    )(slot, hidden, valid, vec, wgu, wdown, *stacks)
    return list(out[:n_stack]), out[n_stack]


def mlp_backward(
    slot_ref, mix_ref, target_ref, valid_ref, vec_ref, wgu_hbm, wdown_hbm, s_final, s_hidden, s_gu,
    *rest, n_stack
):
    outs = rest[n_stack : 2 * n_stack + 1]
    stacks, d_hidden_ref = outs[:n_stack], outs[n_stack]
    (wgu, wdown, final, hidden, gu, d_mlp, d_gu, d_sum, d_normed, small, in_sem, out_sem) = rest[
        2 * n_stack + 1 :
    ]
    s_dmlp, s_dgu, s_small = stacks
    slot, active = slot_ref[0], slot_ref[1] > 0
    ff = wdown.shape[0]
    load = copies_in(
        [
            (s_final.at[slot], final),
            (s_gu.at[slot], gu),
            (wdown_hbm, wdown),
            (wgu_hbm, wgu),
            (s_hidden.at[slot], hidden),
        ],
        in_sem,
    )
    stores = []

    def save(buffer, stack):
        copy = pltpu.make_async_copy(buffer, stack.at[slot], out_sem.at[len(stores)])
        pl.when(active)(copy.start)
        stores.append(copy)

    load[0].wait()
    target = target_ref[...].astype(F32)
    valid = valid_ref[...]
    misfit = final[...] - target
    loss = jnp.sum(valid * misfit * misfit, axis=0, keepdims=True)
    seed = valid * jnp.where(mix_ref[0] > 0.5, target, mix_ref[1] * misfit)
    d_sum[...] = seed
    d_mlp[...] = seed.astype(BF)
    save(d_mlp, s_dmlp)
    load[1].wait()
    load[2].wait()

    def act_tile(t, carry):
        a = lanes(t)
        b = pl.ds(pl.multiple_of(ff + t * TILE, TILE), TILE)
        d_act = dot_nt(d_mlp[...], wdown[a, :])
        gate, up = gu[:, a].astype(F32), gu[:, b].astype(F32)
        s = sigmoid(gate)
        swish = gate * s
        d_gu[:, a] = (d_act * up * (s + swish - swish * s)).astype(BF)
        d_gu[:, b] = (d_act * swish).astype(BF)
        return carry

    lax.fori_loop(0, ff // TILE, act_tile, 0)
    save(d_gu, s_dgu)
    load[3].wait()

    def back_tile(t, carry):
        rows = lanes(t)
        d_normed[:, rows] = dot_nt(d_gu[...], wgu[rows, :])
        return carry

    lax.fori_loop(0, wgu.shape[0] // TILE, back_tile, 0)
    load[4].wait()
    h = hidden[...]
    width = h.shape[1]
    rate = lax.rsqrt(jnp.mean(h * h, axis=-1, keepdims=True) + EPSILON)
    unit = h * rate
    d_n = d_normed[...]
    small[...] = jnp.zeros_like(small)
    small[0:1, :width] = jnp.sum(d_n * unit, axis=0, keepdims=True)
    small[1:2, :width] = loss
    save(small, s_small)
    d_n = d_n * vec_ref[V_G2 : V_G2 + 1, :width]
    d_hidden_ref[...] = d_sum[...] + rate * (
        d_n - unit * jnp.mean(d_n * unit, axis=-1, keepdims=True)
    )
    for copy in stores:
        pl.when(active)(copy.wait)


def mlp_backward_call(slot, mix, target, valid, vec, wgu, wdown, reads, stacks):
    length, width = target.shape
    ff = wdown.shape[0]
    n_stack = len(stacks)
    scratch = [
        pltpu.VMEM(wgu.shape, BF),
        pltpu.VMEM(wdown.shape, BF),
        pltpu.VMEM((length, width), F32),
        pltpu.VMEM((length, width), F32),
        pltpu.VMEM((length, 2 * ff), BF),
        pltpu.VMEM((length, width), BF),
        pltpu.VMEM((length, 2 * ff), BF),
        pltpu.VMEM((length, width), F32),
        pltpu.VMEM((length, width), F32),
        pltpu.VMEM(stacks[2].shape[1:], F32),
        pltpu.SemaphoreType.DMA((5,)),
        pltpu.SemaphoreType.DMA((n_stack,)),
    ]
    out = pl.pallas_call(
        functools.partial(mlp_backward, n_stack=n_stack),
        out_shape=[jax.ShapeDtypeStruct(s.shape, s.dtype) for s in stacks]
        + [jax.ShapeDtypeStruct((length, width), F32)],
        in_specs=[SM, SM, VM, VM, VM, ANY, ANY, ANY, ANY, ANY] + [ANY] * n_stack,
        out_specs=[ANY] * n_stack + [VM],
        scratch_shapes=scratch,
        input_output_aliases={10 + i: i for i in range(n_stack)},
        compiler_params=pltpu.CompilerParams(vmem_limit_bytes=40 * 1024 * 1024),
        cost_estimate=pl.CostEstimate(
            flops=2 * length * (wgu.size + wdown.size), bytes_accessed=20000000, transcendentals=0
        ),
        name="mlp_backward",
    )(slot, mix, target, valid, vec, wgu, wdown, *reads, *stacks)
    return list(out[:n_stack]), out[n_stack]


def column_sum(v):
    return jnp.sum(v, axis=0, keepdims=True)


def mix_backward(
    slot_ref, d_hidden_ref, vec_ref, cos_ref, sin_ref, win_hbm, wout_hbm,
    s_conv, s_z, s_gate, s_qkv, s_step, s_probs, s_y, s_x, *rest, n_stack, widths
):
    ci, mi, qw, kw, heads = widths
    outs = rest[n_stack : 2 * n_stack + 1]
    stacks, d_input_ref = outs[:n_stack], outs[n_stack]
    (win, wout, conv_raw, z, gate_raw, qkv, step_raw, probs, y, x_low, d_branch, d_proj, d_mixed,
     d_ssm, d_z, d_normed, run_wide, run_row, step_two, bend_two, tops, d_tops, run_acc, step_acc,
     small, in_sem, out_sem) = rest[2 * n_stack + 1 :]
    s_dbranch, s_dproj, s_small = stacks
    slot, active = slot_ref[0], slot_ref[1] > 0
    g0, q0 = ci, ci + mi
    s0 = q0 + qw + 2 * kw
    total = win.shape[1]
    length, width = d_hidden_ref.shape
    load = copies_in(
        [
            (wout_hbm, wout),
            (s_probs.at[slot], probs),
            (s_qkv.at[slot], qkv),
            (s_step.at[slot], step_raw),
            (s_gate.at[slot], gate_raw),
            (s_y.at[slot], y),
            (s_z.at[slot], z),
            (s_conv.at[slot], conv_raw),
            (win_hbm, win),
            (s_x.at[slot], x_low),
        ],
        in_sem,
    )
    stores = []

    def save(buffer, stack):
        copy = pltpu.make_async_copy(buffer, stack.at[slot], out_sem.at[len(stores)])
        pl.when(active)(copy.start)
        stores.append(copy)

    small[...] = jnp.zeros_like(small)
    d_branch[...] = d_hidden_ref[...].astype(BF)
    save(d_branch, s_dbranch)
    load[0].wait()
    for t in range(qw // TILE):
        rows = slice(mi + t * TILE, mi + (t + 1) * TILE)
        d_mixed[:, t * TILE : (t + 1) * TILE] = dot_nt(d_branch[...], wout[rows, :]).astype(BF)

    lane_first = jnp.bitwise_and(iota((length, HALF), 1), HD - 1) < HD // 2
    half_low = iota((length, HALF), 1) < HD
    cosine, sine = cos_ref[...], -sin_ref[...]
    load[1].wait()
    load[2].wait()
    keys, values = qkv[:, qw : qw + kw], qkv[:, qw + kw : qw + 2 * kw]
    keys_far, values_far = pltpu.roll(keys.astype(F32), HD, 1).astype(BF), pltpu.roll(
        values.astype(F32), HD, 1
    ).astype(BF)
    pairs = qw // HALF
    groups = kw // HD
    scale = HD ** (-0.5)
    d_keys = [jnp.zeros((length, HALF), F32) for _ in range(groups)]
    d_values = [jnp.zeros((length, HALF), F32) for _ in range(groups)]
    for pair in range(pairs):
        group = pair // (pairs // groups)
        keep = half_low if group == 0 else jnp.logical_not(half_low)
        keys_two = jnp.where(keep, keys, keys_far)
        values_two = jnp.where(keep, values, values_far)
        cols = slice(pair * HALF, (pair + 1) * HALF)
        query, d_out = qkv[:, cols], d_mixed[:, cols]
        results = []
        for side in range(2):
            own = half_low if side == 0 else jnp.logical_not(half_low)
            q = jnp.where(own, query, jnp.zeros_like(query))
            d_o = jnp.where(own, d_out, jnp.zeros_like(d_out))
            at = (2 * pair + side) * length
            weights = probs[at : at + length, :]
            wide = weights.astype(F32)
            d_weights = dot_nt(d_o, values_two)
            inner = wide * d_weights
            d_scores = (inner - wide * jnp.sum(inner, axis=-1, keepdims=True)).astype(BF)
            results.append(dot(d_scores, keys_two))
            d_keys[group] = d_keys[group] + dot_tn(d_scores, q)
            d_values[group] = d_values[group] + dot_tn(weights, d_o)
        d_q = jnp.where(half_low, results[0], results[1]) * scale
        d_proj[:, q0 + pair * HALF : q0 + (pair + 1) * HALF] = rope(
            d_q, cosine, sine, lane_first
        ).astype(BF)
    folded = [v + pltpu.roll(v, HD, 1) for v in d_keys]
    d_k = jnp.where(half_low, folded[0], folded[1]) * scale
    d_proj[:, q0 + qw : q0 + qw + kw] = rope(d_k, cosine, sine, lane_first).astype(BF)
    folded = [v + pltpu.roll(v, HD, 1) for v in d_values]
    d_proj[:, q0 + qw + kw : s0] = jnp.where(half_low, folded[0], folded[1]).astype(BF)

    load[3].wait()
    load[4].wait()
    load[5].wait()

    def norm_tile(t, sums):
        cols = lanes(t)
        d_s = dot_nt(d_branch[...], wout[cols, :])
        d_ssm[:, cols] = d_s
        g = gate_raw[:, cols].astype(F32)
        gated = y[:, cols].astype(F32) * (g * sigmoid(g))
        d_n = d_s * vec_ref[V_GS : V_GS + 1, cols]
        return (
            sums[0] + jnp.sum(gated * gated, axis=-1, keepdims=True),
            sums[1] + jnp.sum(gated * d_n, axis=-1, keepdims=True),
        )

    zero_col = jnp.zeros((length, 1), F32)
    squares, along = lax.fori_loop(0, mi // TILE, norm_tile, (zero_col, zero_col))
    rate = lax.rsqrt(squares * (1.0 / mi) + EPSILON)
    along = along * (rate * rate) * (1.0 / mi)

    pre, step, change, run, bend = scan_terms(step_raw[...], vec_ref, heads)
    turned = run.T
    run_row[:HALF, :] = turned[:, :HALF]
    run_row[HALF:, :] = turned[:, HALF:]
    broadcast_runs(run, run_wide, heads)
    step_two[...] = both(step)
    bend_two[...] = both(bend)
    load[6].wait()
    zb = z[:, mi : mi + 2 * HALF].astype(F32)
    sb = sigmoid(zb)
    bc = (zb * sb).astype(BF)
    b_in, c_in = bc[:, :HALF], bc[:, HALF:]
    causal = iota((HALF, HALF), 1) <= iota((HALF, HALF), 0)
    for c in range(2):
        rows = slice(c * HALF, (c + 1) * HALF)
        tops[rows, :] = jnp.where(causal, dot_nt(c_in[rows], b_in[rows]), 0.0)
    cross = dot_nt(c_in[HALF:], b_in[:HALF])
    cross_turned = cross.T.astype(BF)
    cross = cross.astype(BF)
    pair_low = iota((HALF, HALF), 1) < HD
    d_tops[...] = jnp.zeros_like(d_tops)
    run_acc[...] = jnp.zeros_like(run_acc)
    step_acc[...] = jnp.zeros_like(step_acc)

    def mix_tile(t, carry):
        cols = lanes(t)
        g = gate_raw[:, cols].astype(F32)
        s = sigmoid(g)
        swish = g * s
        y_in = y[:, cols].astype(F32)
        gated = y_in * swish
        d_s = d_ssm[:, cols]
        small[V_GS : V_GS + 1, cols] = column_sum(d_s * gated * rate)
        d_gated = rate * (d_s * vec_ref[V_GS : V_GS + 1, cols]) - gated * (along * rate)
        d_proj[:, pl.ds(pl.multiple_of(g0 + t * TILE, TILE), TILE)] = (
            d_gated * y_in * (s + swish - swish * s)
        ).astype(BF)
        d_y = d_gated * swish
        z_in = z[:, cols].astype(F32)
        s = sigmoid(z_in)
        x_in = z_in * s
        slope = s + x_in - x_in * s
        spread = expand_matrix(t)
        steps = dot(step_two[...], spread)
        bends = dot(bend_two[...], spread)
        scaled = (steps * x_in).astype(BF)
        d_low = d_y.astype(BF)
        u = (bends[:HALF] * scaled[:HALF].astype(F32)).astype(BF)
        v = (bends[HALF:] * d_y[HALF:]).astype(BF)
        far = dot(cross, u)
        back = dot(cross_turned, v)
        d_tops[2 * HALF :, :] += dot_nt(v, u)
        mixed_parts, back_parts = [], []
        for p in range(TILE // HALF):
            mixed_block, back_block = [], []
            for c in range(2):
                rows = slice(c * HALF, (c + 1) * HALF)
                xs = scaled[rows, p * HALF : (p + 1) * HALF]
                dy = d_low[rows, p * HALF : (p + 1) * HALF]
                zero = jnp.zeros_like(xs)
                xs_two = [jnp.where(pair_low, xs, zero), jnp.where(pair_low, zero, xs)]
                dy_two = [jnp.where(pair_low, dy, zero), jnp.where(pair_low, zero, dy)]
                weights = []
                d_top = jnp.zeros((HALF, HALF), F32)
                for side in range(2):
                    h = t * (TILE // HD) + 2 * p + side
                    wide = run_wide[rows, lanes(h, HALF)]
                    line = run_row[pl.ds(c * HALF + h, 1), :]
                    decay = jnp.exp(jnp.minimum(wide - line, 0.0))
                    weights.append((decay * tops[rows, :]).astype(BF))
                    d_top = d_top + decay * dot_nt(dy_two[side], xs)
                d_tops[rows, :] += d_top
                mixed_block.append(
                    dot(jnp.concatenate(weights, axis=1), jnp.concatenate(xs_two, axis=0))
                )
                back_block.append(
                    dot_tn(jnp.concatenate(weights, axis=0), jnp.concatenate(dy_two, axis=0))
                )
            mixed_parts.append(jnp.concatenate(mixed_block, axis=0))
            back_parts.append(jnp.concatenate(back_block, axis=0))
        mixed = jnp.concatenate(mixed_parts, axis=1)
        d_scaled = jnp.concatenate(back_parts, axis=1)
        crossing = jnp.concatenate(
            [-(u.astype(F32) * back), v.astype(F32) * far], axis=0
        )
        runs = d_low.astype(F32) * mixed - scaled.astype(F32) * d_scaled + crossing
        d_scaled = d_scaled + jnp.concatenate([bends[:HALF] * back, jnp.zeros_like(back)], axis=0)
        gather = reduce_matrix(t)
        run_acc[...] += sum(dot(part, gather) for part in split2(runs))
        step_acc[...] += sum(dot(part, gather) for part in split2(x_in * d_scaled))
        small[V_SKIP : V_SKIP + 1, cols] = column_sum(d_y * x_in)
        d_x = steps * d_scaled + vec_ref[V_SKIP : V_SKIP + 1, cols] * d_y
        d_z[:, cols] = d_x * slope
        return carry

    lax.fori_loop(0, mi // TILE, mix_tile, 0)
    d_top = [
        jnp.where(causal, d_tops[c * HALF : (c + 1) * HALF, :], 0.0).astype(BF) for c in range(2)
    ]
    d_cross = d_tops[2 * HALF :, :].astype(BF)
    d_c = jnp.concatenate(
        [dot(d_top[0], b_in[:HALF]), dot(d_cross, b_in[:HALF]) + dot(d_top[1], b_in[HALF:])], axis=0
    )
    d_b = jnp.concatenate(
        [dot_tn(d_top[0], c_in[:HALF]) + dot_tn(d_cross, c_in[HALF:]), dot_tn(d_top[1], c_in[HALF:])],
        axis=0,
    )
    xb = zb * sb
    d_z[:, mi : mi + 2 * HALF] = jnp.concatenate([d_b, d_c], axis=1) * (sb + xb - xb * sb)
    upper = jnp.where(
        iota((length, length), 0) <= iota((length, length), 1), 1.0, 0.0
    ).astype(BF)
    d_change = sum(dot(upper, part) for part in split3(run_acc[...]))
    d_pre = (step_acc[...] + d_change * vec_ref[V_DECAY : V_DECAY + 1, :HALF]) * sigmoid(pre)
    d_pre = jnp.where(iota(d_pre.shape, 1) < heads, d_pre, 0.0)
    d_proj[:, s0:total] = d_pre.astype(BF)
    small[V_SBIAS : V_SBIAS + 1, :HALF] = column_sum(d_pre)
    small[V_DECAY : V_DECAY + 1, :HALF] = column_sum(d_change * change)

    load[7].wait()
    row = iota((length, TILE), 0)

    def conv_tile(t, carry):
        cols = lanes(t)
        d = d_z[:, cols]
        raw = conv_raw[:, cols].astype(F32)
        small[V_CBIAS : V_CBIAS + 1, cols] = column_sum(d)
        small[3:4, cols] = column_sum(d * raw)
        out = d * vec_ref[3:4, cols]
        for ahead in range(1, 4):
            moved = jnp.where(row < length - ahead, pltpu.roll(d, length - ahead, 0), 0.0)
            small[3 - ahead : 4 - ahead, cols] = column_sum(moved * raw)
            out = out + moved * vec_ref[3 - ahead : 4 - ahead, cols]
        d_proj[:, cols] = out.astype(BF)
        return carry

    lax.fori_loop(0, ci // TILE, conv_tile, 0)
    save(d_proj, s_dproj)

    load[8].wait()

    def back_tile(t, carry):
        rows = lanes(t)
        d_normed[:, rows] = dot_nt(d_proj[...], win[rows, :])
        return carry

    lax.fori_loop(0, width // TILE, back_tile, 0)
    load[9].wait()
    x = x_low[...].astype(F32)
    rate_one = lax.rsqrt(jnp.mean(x * x, axis=-1, keepdims=True) + EPSILON)
    unit = x * rate_one
    d_n = d_normed[...]
    small[V_G1 : V_G1 + 1, :width] = column_sum(d_n * unit)
    save(small, s_small)
    d_n = d_n * vec_ref[V_G1 : V_G1 + 1, :width]
    d_input_ref[...] = (
        d_hidden_ref[...]
        + rate_one * (d_n - unit * jnp.mean(d_n * unit, axis=-1, keepdims=True))
    ).astype(BF)
    for copy in stores:
        pl.when(active)(copy.wait)


def mixer_backward_call(slot, d_hidden, vec, cosine, sine, win, wout, reads, stacks, widths):
    ci, mi, qw, kw, heads = widths
    length, width = d_hidden.shape
    n_stack = len(stacks)
    n_read = len(reads)
    scratch = [
        pltpu.VMEM(win.shape, BF),
        pltpu.VMEM(wout.shape, BF),
        pltpu.VMEM((length, ci), BF),
        pltpu.VMEM((length, ci), BF),
        pltpu.VMEM((length, mi), BF),
        pltpu.VMEM((length, qw + 2 * kw), BF),
        pltpu.VMEM((length, HALF), F32),
        pltpu.VMEM((qw // HD * length, length), BF),
        pltpu.VMEM((length, mi), BF),
        pltpu.VMEM((length, width), BF),
        pltpu.VMEM((length, width), BF),
        pltpu.VMEM((length, win.shape[1]), BF),
        pltpu.VMEM((length, qw), BF),
        pltpu.VMEM((length, mi), F32),
        pltpu.VMEM((length, ci), F32),
        pltpu.VMEM((length, width), F32),
        pltpu.VMEM((length, heads * HALF), F32),
        pltpu.VMEM((length, HALF), F32),
        pltpu.VMEM((length, 2 * HALF), BF),
        pltpu.VMEM((length, 2 * HALF), BF),
        pltpu.VMEM((2 * HALF, HALF), F32),
        pltpu.VMEM((3 * HALF, HALF), F32),
        pltpu.VMEM((length, HALF), F32),
        pltpu.VMEM((length, HALF), F32),
        pltpu.VMEM(stacks[2].shape[1:], F32),
        pltpu.SemaphoreType.DMA((10,)),
        pltpu.SemaphoreType.DMA((n_stack,)),
    ]
    out = pl.pallas_call(
        functools.partial(mix_backward, n_stack=n_stack, widths=widths),
        out_shape=[jax.ShapeDtypeStruct(s.shape, s.dtype) for s in stacks]
        + [jax.ShapeDtypeStruct((length, width), BF)],
        in_specs=[SM, VM, VM, VM, VM, ANY, ANY] + [ANY] * (n_read + n_stack),
        out_specs=[ANY] * n_stack + [VM],
        scratch_shapes=scratch,
        input_output_aliases={7 + n_read + i: i for i in range(n_stack)},
        compiler_params=pltpu.CompilerParams(vmem_limit_bytes=48 * 1024 * 1024),
        cost_estimate=pl.CostEstimate(
            flops=2 * length * (win.size + wout.size), bytes_accessed=24000000, transcendentals=0
        ),
        name="mixer_backward",
    )(slot, d_hidden, vec, cosine, sine, win, wout, *reads, *stacks)
    return list(out[:n_stack]), out[n_stack]


def rope_tables(length):
    halves = HD // 2
    inverse = jnp.exp(jnp.arange(halves, dtype=F32) * (-2.0 * math.log(ROPE_BASE) / HD))
    angles = jnp.arange(length, dtype=F32)[:, None] * inverse[None, :]
    cosine, sine = jnp.cos(angles), jnp.sin(angles)
    return (
        jnp.concatenate([cosine] * 4, axis=1),
        jnp.concatenate([-sine, sine, -sine, sine], axis=1),
    )


def swap(block, axis, bit):
    return lax.ppermute(block, axis, [(i, i ^ bit) for i in range(lax.axis_size(axis))])


def place(full, piece, row):
    return lax.dynamic_update_slice(full, piece, (row, 0))


def quick_links():
    return lax.axis_size("fsdp") == 4 and lax.axis_size("rep") == 4


def gather_rows(shard):
    if not quick_links():
        return lax.all_gather(shard, "fsdp", axis=0, tiled=True)
    me = lax.axis_index("fsdp")
    parity = lax.axis_index("rep") % 2
    rows = shard.shape[0]
    half = rows // 2
    first = lax.dynamic_slice_in_dim(shard, parity * half, half, 0)
    far_one = swap(first, "fsdp", 2)
    far_two = swap(far_one, "rep", 1)
    near = swap(shard, "fsdp", 1)
    full = jnp.zeros((rows * 4, shard.shape[1]), shard.dtype)
    full = place(full, shard, me * rows)
    full = place(full, near, (me ^ 1) * rows)
    for piece, at in ((far_one, parity * half), (far_two, (1 - parity) * half)):
        full = place(full, piece, (me ^ 2) * rows + at)
        full = place(full, swap(piece, "fsdp", 1), (me ^ 3) * rows + at)
    return full


def plus(a, b):
    return (a.astype(F32) + b.astype(F32)).astype(BF)


def reduce_rows(grad):
    n = lax.axis_size("fsdp")
    if not quick_links():
        own = lax.psum_scatter(grad, "fsdp", scatter_dimension=0, tiled=True)
        return lax.psum(own, "rep").astype(F32)
    me, rank = lax.axis_index("fsdp"), lax.axis_index("rep")
    core, chip = me % 2, me // 2
    rows = grad.shape[0] // n
    blocks = grad.reshape(2, 2, rows, grad.shape[1])
    away = lax.dynamic_index_in_dim(blocks, 1 - core, 1, keepdims=False)
    stay = lax.dynamic_index_in_dim(blocks, core, 1, keepdims=False)
    pair = plus(stay, swap(away, "fsdp", 1))
    away = lax.dynamic_index_in_dim(pair, 1 - chip, 0, keepdims=False)
    stay = lax.dynamic_index_in_dim(pair, chip, 0, keepdims=False)
    own = plus(stay, swap(away, "fsdp", 2))
    inner = jnp.logical_or(rank == 1, rank == 2)
    own = plus(own, lax.ppermute(own, "rep", [(0, 1), (3, 2)]))
    total = plus(own, lax.ppermute(own, "rep", [(1, 2), (2, 1)]))
    outer = lax.ppermute(total, "rep", [(1, 0), (2, 3)])
    return jnp.where(inner, total, outer).astype(F32)


def weight_grad(left, right):
    return lax.dot_general(
        left, right, (((0, 1), (0, 1)), ((), ())), preferred_element_type=F32
    ).astype(BF)


def body(
    inputs,
    teacher,
    lengths,
    order,
    loss_scale,
    norm_gain1,
    w_query,
    w_key,
    w_value,
    w_attn_out,
    w_ssm_gate,
    w_conv_in,
    w_step,
    conv_kernel,
    conv_bias,
    step_bias,
    decay_log,
    skip_gain,
    ssm_norm_gain,
    w_ssm_out,
    norm_gain2,
    w_gate,
    w_up,
    w_down,
):
    n_rep = lax.axis_size("rep")
    n_fsdp = lax.axis_size("fsdp")
    rank = lax.axis_index("rep")
    section = lax.axis_index("section")
    first = section == 0
    device = lax.axis_index("fsdp") * n_rep + rank
    count, length, width = inputs.shape
    ci, mi, qw, kw = (w.shape[2] for w in (w_conv_in, w_ssm_gate, w_query, w_key))
    heads = w_step.shape[2]
    ff = w_up.shape[2]
    widths = (ci, mi, qw, kw, heads)
    taps = conv_kernel.shape[1]
    rows = width // n_fsdp

    def columns(flat):
        wide = -(-flat.size // rows)
        return jnp.pad(flat, (0, wide * rows - flat.size)).reshape(rows, wide)

    convs = jnp.concatenate([conv_kernel[0], conv_bias], axis=0)
    riders = [norm_gain1[0][:, None], norm_gain2[0][:, None], columns(convs.reshape(-1)), columns(ssm_norm_gain[0])]
    used = sum(r.shape[1] for r in riders)
    shard_in = jnp.concatenate(
        [w_conv_in[0], w_ssm_gate[0], w_query[0], w_key[0], w_value[0], w_step[0]]
        + riders
        + [jnp.zeros((rows, HALF - heads - used), BF)],
        axis=1,
    )
    win = gather_rows(shard_in)
    wout = jnp.concatenate([gather_rows(w_ssm_out[0]), gather_rows(w_attn_out[0])], axis=0)
    wgu = gather_rows(jnp.concatenate([w_gate[0], w_up[0]], axis=1))
    wdown = gather_rows(w_down[0])

    at = ci + mi + qw + 2 * kw + heads
    ridden = win[:, at : at + used].reshape(n_fsdp, rows, used)
    wide = riders[2].shape[1]
    conv_all = ridden[:, :, 2 : 2 + wide].reshape(n_fsdp, -1)[:, : (taps + 1) * ci // n_fsdp]
    conv_all = conv_all.reshape(n_fsdp, taps + 1, ci // n_fsdp).transpose(1, 0, 2).reshape(taps + 1, ci)
    ssm_gain = ridden[:, :, 2 + wide :].reshape(n_fsdp, -1)[:, : mi // n_fsdp].reshape(1, mi)

    def table_row(v):
        v = v.astype(F32)
        return jnp.pad(v, ((0, 0), (0, ci - v.shape[1])))

    vec = jnp.concatenate(
        [
            table_row(v)
            for v in (
                conv_all,
                ssm_gain,
                jnp.repeat(skip_gain, HD, axis=1),
                ridden[:, :, 0].reshape(1, width),
                ridden[:, :, 1].reshape(1, width),
                step_bias,
                -jnp.exp(decay_log),
                jnp.zeros((16 - taps - 7, 1), F32),
            )
        ],
        axis=0,
    )
    cosine, sine = rope_tables(length)

    inverse_order = jnp.argsort(order)
    target = lax.dynamic_slice_in_dim(order, device * count, count) // count % n_rep
    sources = lax.dynamic_slice_in_dim(inverse_order, device * count, count)
    anchor = sources // count % n_rep
    own_data = jnp.where(first, inputs, teacher)
    turns = jnp.arange(count, dtype=jnp.int32)
    send_at = jnp.argsort(target ^ rank)
    keep_at = jnp.argsort(anchor ^ rank)
    dealt = []
    for j in range(count):
        piece = lax.dynamic_index_in_dim(own_data, send_at[j], 0, keepdims=False)
        dealt.append(swap(piece, "rep", j) if j else piece)
    own_lengths = jnp.take(lengths, jnp.take(sources, keep_at))
    positions = jnp.arange(length, dtype=jnp.int32)
    valid_all = (positions[None, :] < own_lengths[:, None]).astype(F32)[:, :, None]
    valid_count = jnp.sum(lengths).astype(F32)
    factor = loss_scale / (valid_count * width)

    def stack(*shape, kind=BF):
        return jnp.zeros((count,) + shape, kind)

    mix_stacks = [
        stack(length, width),
        stack(length, ci),
        stack(length, ci),
        stack(length, mi),
        stack(length, qw + 2 * kw),
        stack(length, HALF, kind=F32),
        stack(qw // HD * length, length),
        stack(length, mi + qw),
        stack(length, mi),
        stack(length, width, kind=F32),
        stack(length, width),
    ]
    mlp_stacks = [
        stack(length, width),
        stack(length, 2 * ff),
        stack(length, ff),
        stack(length, width, kind=F32),
        stack(length, width),
    ]
    skew = 2

    def slot_of(raw):
        inside = jnp.logical_and(raw >= 0, raw < count).astype(jnp.int32)
        return jnp.clip(raw, 0, count - 1), inside

    received = []
    for tick in range(count + skew):
        slot, inside = slot_of(tick - skew * section)
        if tick < skew:
            seq_in = dealt[tick]
        elif tick < count:
            seq_in = jnp.where(first, dealt[tick], received[tick - skew])
        else:
            seq_in = received[tick - skew]
        slots = jnp.stack([slot, inside])
        mix_stacks, hidden = mixer_forward_call(
            slots, seq_in, vec, cosine, sine, win, wout, mix_stacks, widths
        )
        valid = lax.dynamic_index_in_dim(valid_all, slot, 0, keepdims=False)
        mlp_stacks, low = mlp_forward_call(slots, hidden, valid, vec, wgu, wdown, mlp_stacks)
        if tick < count:
            received.append(lax.ppermute(low, "section", [(0, 1)]))

    (s_normed, s_conv, s_z, s_gate, s_qkv, s_step, s_probs, s_branch, s_y, s_hidden, s_x) = mix_stacks
    s_normed2, s_gu, s_act, s_final, s_low = mlp_stacks
    mlp_grads = [stack(length, width), stack(length, 2 * ff), stack(8, width, kind=F32)]
    mix_grads = [stack(length, width), stack(length, win.shape[1]), stack(16, ci, kind=F32)]
    mix = jnp.stack([jnp.where(first, 1.0, 0.0), 2.0 * factor])
    incoming, returned, d_inputs = [], [None] * count, [None] * count
    for turn in range(count + skew):
        slot, inside = slot_of(count - 1 - turn + skew * (1 - section))
        if turn < skew:
            seed = dealt[count - 1 - turn]
        elif turn < count:
            seed = jnp.where(first, incoming[turn - skew], dealt[count - 1 - turn])
        else:
            seed = incoming[turn - skew]
        slots = jnp.stack([slot, inside])
        valid = lax.dynamic_index_in_dim(valid_all, slot, 0, keepdims=False)
        mlp_grads, d_hidden = mlp_backward_call(
            slots, mix, seed, valid, vec, wgu, wdown, [s_final, s_hidden, s_gu], mlp_grads
        )
        mix_grads, d_input = mixer_backward_call(
            slots,
            d_hidden,
            vec,
            cosine,
            sine,
            win,
            wout,
            [s_conv, s_z, s_gate, s_qkv, s_step, s_probs, s_y, s_x],
            mix_grads,
            widths,
        )
        if turn < count:
            incoming.append(lax.ppermute(d_input, "section", [(1, 0)]))
            d_inputs[count - 1 - turn] = d_input
        if turn >= skew:
            j = count - 1 - turn + skew
            back = jnp.where(first, d_input, s_low[j])
            returned[j] = swap(back, "rep", j) if j else back

    s_dmlp, s_dgu, small_mlp = mlp_grads
    s_dbranch, s_dproj, small_mix = mix_grads
    grad_gu = reduce_rows(weight_grad(s_normed2, s_dgu))
    grad_down = reduce_rows(weight_grad(s_act, s_dmlp))
    grad_out = weight_grad(s_branch, s_dbranch)
    grad_ssm_out = reduce_rows(grad_out[:mi])
    grad_attn_out = reduce_rows(grad_out[mi:])
    grad_in = reduce_rows(weight_grad(s_normed, s_dproj))

    mix_sum = jnp.sum(small_mix, axis=0)
    mlp_sum = jnp.sum(small_mlp, axis=0)
    loss_part = jnp.where(first, 0.0, jnp.sum(mlp_sum[1]))
    flat = jnp.concatenate(
        [
            mix_sum[:5].reshape(-1),
            mix_sum[V_GS, :mi],
            mix_sum[V_G1, :width],
            mlp_sum[0],
            mix_sum[V_SBIAS, :heads],
            mix_sum[V_DECAY, :heads],
            jnp.sum(mix_sum[V_SKIP, :mi].reshape(heads, HD), axis=1),
        ]
    )
    slots = jnp.arange(lax.axis_size("section"), dtype=jnp.int32) == section
    flat = jnp.where(slots[:, None], flat[None], 0.0)
    loss_total, flat = lax.psum((loss_part, flat), ("section", "fsdp", "rep"))
    flat = lax.dynamic_index_in_dim(flat, section, 0, keepdims=False)
    cuts = [taps * ci, ci, mi, width, width, heads, heads, heads]
    parts, begin = [], 0
    for cut in cuts:
        parts.append(flat[begin : begin + cut])
        begin += cut
    fsdp = lax.axis_index("fsdp")

    def own(v):
        size = v.shape[-1] // n_fsdp
        return lax.dynamic_slice_in_dim(v, fsdp * size, size, v.ndim - 1)[None]

    returned = jnp.stack(returned)
    restored = jnp.take(returned, target ^ rank, axis=0)
    dealt_acts = jnp.take(s_low, anchor ^ rank, axis=0)
    dealt_grads = jnp.take(jnp.stack(d_inputs), anchor ^ rank, axis=0)
    activations = jnp.where(first, dealt_acts, restored)[None]
    gradients = jnp.where(first, restored, dealt_grads)[None]
    q0 = ci + mi
    s0 = q0 + qw + 2 * kw
    return (
        activations,
        gradients,
        loss_total / (valid_count * width),
        own(parts[3]),
        grad_in[None, :, q0 : q0 + qw],
        grad_in[None, :, q0 + qw : q0 + qw + kw],
        grad_in[None, :, q0 + qw + kw : s0],
        grad_attn_out[None],
        grad_in[None, :, ci:q0],
        grad_in[None, :, :ci],
        grad_in[None, :, s0 : s0 + heads],
        own(parts[0].reshape(taps, ci)),
        own(parts[1]),
        parts[5][None],
        parts[6][None],
        parts[7][None],
        own(parts[2]),
        grad_ssm_out[None],
        own(parts[4]),
        grad_gu[None, :, :ff],
        grad_gu[None, :, ff:],
        grad_down[None],
    )


def solution(mesh):
    rows3 = P("section", "fsdp", None)
    pair = P("section", "fsdp")
    one = P("section", None)
    data = P(("fsdp", "rep"), None, None)
    taps = P("section", None, "fsdp")
    in_specs = (data, data, P(), P(), P(), pair) + (rows3,) * 7
    in_specs += (taps, pair, one, one, one, pair, rows3, pair, rows3, rows3, rows3)
    placed = P("section", ("fsdp", "rep"), None, None)
    out_specs = (placed, placed, P(), pair) + (rows3,) * 7
    out_specs += (taps, pair, one, one, one, pair, rows3, pair, rows3, rows3, rows3)
    return jax.shard_map(body, mesh=mesh, in_specs=in_specs, out_specs=out_specs, check_vma=False)
```

time: 2000 us -> 1270 us (0.64)
  matrix products: 729 us -> 37.1 us
  Pallas kernels: 0 us -> 375 us
  other arithmetic: 243 us -> 68.2 us
  blocking collectives: 162 us -> 42.3 us
  waiting for transfers between devices: 528 us -> 437 us
  local copies, waits for them, and re-layouts: 260 us -> 203 us
  starting transfers between devices: 39.1 us -> 75.6 us
    dot_general x230 -> x4, matrix products: 716 us -> 37.1 us  [weight_grad(): lax.dot_general(left, right, (((0, 1), (0, 1)), ((), ())), preferred_elem...]
    pallas_call x0 -> x24, Pallas kernels: none -> 375 us  [the longest x6 145 us: mixer_backward_call(): pl.pallas_call(functools.partial(mix_backward, n_stack=n_stack, widths=wi...]
    ppermute x8 -> x64, waiting for transfers between devices: 62.1 us -> 362 us  [the longest x41 183 us: swap(): lax.ppermute(block, axis, [(i, i ^ bit) for i in range(lax.axis_size(axis...]
    all_gather x16 -> x0, waiting for transfers between devices: 150 us -> none  [the longest x1 31.3 us: body(): lax.all_gather(shards_again[13], 'fsdp', axis=1, tiled=True)]
    psum x1, waiting for transfers between devices: 199 us -> 74.7 us  [body(): loss_total, flat = lax.psum((loss_part, flat), ('section', 'fsdp', 'rep'))]
    reduce_sum x37 -> x4, other arithmetic: 85.9 us -> 0.78 us  [the longest x1 0.63 us: body(): valid_count = jnp.sum(lengths).astype(F32)]
    reduce_scatter x11 -> x0, waiting for transfers between devices: 82.9 us -> none  [the longest x1 47.1 us: body(): lax.psum_scatter(grad_down[None].astype(jnp.bfloat16), 'fsdp', scatter_di...]
    slice x28 -> x15, local copies, waits for them, and re-layouts: 85.3 us -> 7.55 us  [the longest x2 2.27 us: body(): parts.append(flat[begin:begin + cut])]
  transfers between devices with their start and end apart: 43 -> 65, of which waited for: 20 -> 17; matrix products, arithmetic and copies ran while one was open for 29% -> 17% of each run, Pallas kernels for 0% -> 22%
where the time goes in v1:
time: 1270 us
  waiting for transfers between devices  437 us (34%)
  Pallas kernels  375 us (30%)
  local copies, waits for them, and re-layouts  203 us (16%)
  starting transfers between devices  75.6 us (6%)
  other arithmetic  68.2 us (5%)
  blocking collectives  42.3 us (3%)
  matrix products  37.1 us (3%)
  between operations  28.1 us (2%)
    ppermute x41, waiting for transfers between devices, swap(): lax.ppermute(block, axis, [(i, i ^ bit) for i in range(lax.axis_size(axis...  183 us
    pallas_call x6, Pallas kernels, mixer_backward_call(): pl.pallas_call(functools.partial(mix_backward, n_stack=n_stack, widths=wi...  145 us
    ppermute x5, waiting for transfers between devices, reduce_rows(): outer = lax.ppermute(total, 'rep', [(1, 0), (2, 3)])  128 us
    pallas_call x6, Pallas kernels, mixer_forward_call(): pl.pallas_call(functools.partial(mix_forward, n_stack=n_stack, widths=wid...  116 us
    psum x1, waiting for transfers between devices, body(): loss_total, flat = lax.psum((loss_part, flat), ('section', 'fsdp', 'rep'))  74.7 us
    pallas_call x6, Pallas kernels, mlp_backward_call(): pl.pallas_call(functools.partial(mlp_backward, n_stack=n_stack), out_shap...  62.4 us
    unnamed x226, local copies, waits for them, and re-layouts  58 us
    pallas_call x6, Pallas kernels, mlp_forward_call(): pl.pallas_call(functools.partial(mlp_forward, n_stack=n_stack), out_shape...  51.9 us
  transfers between devices with their start and end apart: 65, of which 17 were waited for; matrix products, arithmetic and copies ran while one was open for 17% of the time, Pallas kernels for 22%

profile of v1, /device:TPU:0, one launch (start us, length us, event | category | flops | bytes accessed | tf_op | source)
XLA Modules:
  0.0 1266.9 jit_solution(4806849163263333573)
XLA Ops:
  164.1 13.5 %collective-permute-done.20 = bf16[128,4096]{1,0:T(8,128)(2,1)S(1)} collective-permute-done((bf16[128,4096]{1,0:T(8,128)(2,1)S(1)}, bf16[128,4096]{1,0:T(8,128)(2,1)S(1)}, u32[]{:S(2)}, u32[]{:S(2)}) %collective-permute-start.20) | collective-permute-done | bytes 1048608 | tf_op jit(solution)/shard_map/ppermute | solution.py:899
  183.2 39.8 %collective-permute-done.5 = bf16[128,4224]{1,0:T(8,128)(2,1)S(1)} collective-permute-done((bf16[128,4224]{1,0:T(8,128)(2,1)S(1)}, bf16[128,4224]{1,0:T(8,128)(2,1)S(1)}, u32[]{:S(2)}, u32[]{:S(2)}) %collective-permute-start.5) | collective-permute-done | bytes 1081376 | tf_op jit(solution)/shard_map/ppermute | solution.py:899
  247.9 19.3 %mixer_forward.6 = (bf16[4,256,1024]{2,1,0:T(8,128)(2,1)S(1)}, bf16[4,256,1792]{2,1,0:T(8,128)(2,1)}, bf16[4,256,1792]{2,1,0:T(8,128)(2,1)}, bf16[4,256,1536]{2,...) custom-call(s32[2]{0:T(128)S(1)} %pad_add_fusion.3.slot_ref, ...), custom_call_target="tpu_custom_call", output_to_operand_aliasing={{0}: (7, {}), {1}: (8, {}), {2}: (9, {}), {3}: (10, {}), {4... | custom-call | flops 3288334336 | bytes 24000000 | tf_op jit(solution)/shard_map/mixer_forward/pallas_call | solution.py:334
  287.9 20.2 %mixer_forward.7 = (bf16[4,256,1024]{2,1,0:T(8,128)(2,1)S(1)}, bf16[4,256,1792]{2,1,0:T(8,128)(2,1)}, bf16[4,256,1792]{2,1,0:T(8,128)(2,1)}, bf16[4,256,1536]{2,...) custom-call(s32[2]{0:T(128)S(1)} %pad_add_fusion.2.slot_ref, ...), custom_call_target="tpu_custom_call", output_to_operand_aliasing={{0}: (7, {}), {1}: (8, {}), {2}: (9, {}), {3}: (10, {}), {4... | custom-call | flops 3288334336 | bytes 24000000 | tf_op jit(solution)/shard_map/mixer_forward/pallas_call | solution.py:334
  325.5 19.4 %mixer_forward.8 = (bf16[4,256,1024]{2,1,0:T(8,128)(2,1)S(1)}, bf16[4,256,1792]{2,1,0:T(8,128)(2,1)}, bf16[4,256,1792]{2,1,0:T(8,128)(2,1)}, bf16[4,256,1536]{2,...) custom-call(s32[2]{0:T(128)S(1)} %pad_add_fusion.4.slot_ref, ...), custom_call_target="tpu_custom_call", output_to_operand_aliasing={{0}: (7, {}), {1}: (8, {}), {2}: (9, {}), {3}: (10, {}), {4... | custom-call | flops 3288334336 | bytes 24000000 | tf_op jit(solution)/shard_map/mixer_forward/pallas_call | solution.py:334
  362.3 19.5 %mixer_forward.9 = (bf16[4,256,1024]{2,1,0:T(8,128)(2,1)S(1)}, bf16[4,256,1792]{2,1,0:T(8,128)(2,1)}, bf16[4,256,1792]{2,1,0:T(8,128)(2,1)}, bf16[4,256,1536]{2,...) custom-call(s32[2]{0:T(128)S(1)} %pad_add_fusion.1.slot_ref, ...), custom_call_target="tpu_custom_call", output_to_operand_aliasing={{0}: (7, {}), {1}: (8, {}), {2}: (9, {}), {3}: (10, {}), {4... | custom-call | flops 3288334336 | bytes 24000000 | tf_op jit(solution)/shard_map/mixer_forward/pallas_call | solution.py:334
  397.3 18.5 %mixer_forward.10 = (bf16[4,256,1024]{2,1,0:T(8,128)(2,1)S(1)}, bf16[4,256,1792]{2,1,0:T(8,128)(2,1)}, bf16[4,256,1792]{2,1,0:T(8,128)(2,1)}, bf16[4,256,1536]{2...) custom-call(s32[2]{0:T(128)S(1)} %pad_add_fusion.5.slot_ref, ...), custom_call_target="tpu_custom_call", output_to_operand_aliasing={{0}: (7, {}), {1}: (8, {}), {2}: (9, {}), {3}: (10, {}), {4... | custom-call | flops 3288334336 | bytes 24000000 | tf_op jit(solution)/shard_map/mixer_forward/pallas_call | solution.py:334
  430.6 18.7 %mixer_forward.11 = (bf16[4,256,1024]{2,1,0:T(8,128)(2,1)S(1)}, bf16[4,256,1792]{2,1,0:T(8,128)(2,1)}, bf16[4,256,1792]{2,1,0:T(8,128)(2,1)}, bf16[4,256,1536]{2...) custom-call(s32[2]{0:T(128)S(1)} %pad_add_fusion.slot_ref, ...), custom_call_target="tpu_custom_call", output_to_operand_aliasing={{0}: (7, {}), {1}: (8, {}), {2}: (9, {}), {3}: (10, {}), {4... | custom-call | flops 3288334336 | bytes 24000000 | tf_op jit(solution)/shard_map/mixer_forward/pallas_call | solution.py:334
  468.9 10.8 mlp_backward.6
  485.5 24.2 %mixer_backward.6 = (bf16[4,256,1024]{2,1,0:T(8,128)(2,1)}, bf16[4,256,4224]{2,1,0:T(8,128)(2,1)}, f32[4,16,1792]{2,1,0:T(8,128)S(1)}, bf16[256,1024]{1,0:T(8,128)(2,1)}) custom-call(s32[2]{0:T(128)S(1)} %pad_add_fusion.9.slot_ref, f32[256,1024]{1,0:T(8,128)S(1)} %get-tuple-element.289.d_hidden_ref, ...), custom_call_target="tpu_custom_call", output_to_operand_aliasing={{0}: (15, {}), {1}: (16, {}), {2}: (17, {})} | custom-call | flops 3288334336 | bytes 24000000 | tf_op jit(solution)/shard_map/mixer_backward/pallas_call | solution.py:870
  521.5 24.2 %mixer_backward.7 = (bf16[4,256,1024]{2,1,0:T(8,128)(2,1)}, bf16[4,256,4224]{2,1,0:T(8,128)(2,1)}, f32[4,16,1792]{2,1,0:T(8,128)S(1)}, bf16[256,1024]{1,0:T(8,128)(2,1)}) custom-call(s32[2]{0:T(128)S(1)} %pad_add_fusion.8.slot_ref, f32[256,1024]{1,0:T(8,128)S(1)} %get-tuple-element.280.d_hidden_ref, ...), custom_call_target="tpu_custom_call", output_to_operand_aliasing={{0}: (15, {}), {1}: (16, {}), {2}: (17, {})} | custom-call | flops 3288334336 | bytes 24000000 | tf_op jit(solution)/shard_map/mixer_backward/pallas_call | solution.py:870
  567.9 24.7 %mixer_backward.8 = (bf16[4,256,1024]{2,1,0:T(8,128)(2,1)}, bf16[4,256,4224]{2,1,0:T(8,128)(2,1)}, f32[4,16,1792]{2,1,0:T(8,128)S(1)}, bf16[256,1024]{1,0:T(8,128)(2,1)}) custom-call(s32[2]{0:T(128)S(1)} %pad_add_fusion.10.slot_ref, f32[256,1024]{1,0:T(8,128)S(1)} %get-tuple-element.302.d_hidden_ref, ...), custom_call_target="tpu_custom_call", output_to_operand_aliasing={{0}: (15, {}), {1}: (16, {}), {2}: (17, {})} | custom-call | flops 3288334336 | bytes 24000000 | tf_op jit(solution)/shard_map/mixer_backward/pallas_call | solution.py:870
  605.1 24.6 %mixer_backward.9 = (bf16[4,256,1024]{2,1,0:T(8,128)(2,1)}, bf16[4,256,4224]{2,1,0:T(8,128)(2,1)}, f32[4,16,1792]{2,1,0:T(8,128)S(1)}, bf16[256,1024]{1,0:T(8,128)(2,1)}) custom-call(s32[2]{0:T(128)S(1)} %pad_add_fusion.7.slot_ref, f32[256,1024]{1,0:T(8,128)S(1)} %get-tuple-element.301.d_hidden_ref, ...), custom_call_target="tpu_custom_call", output_to_operand_aliasing={{0}: (15, {}), {1}: (16, {}), {2}: (17, {})} | custom-call | flops 3288334336 | bytes 24000000 | tf_op jit(solution)/shard_map/mixer_backward/pallas_call | solution.py:870
  653.5 23.9 %mixer_backward.10 = (bf16[4,256,1024]{2,1,0:T(8,128)(2,1)}, bf16[4,256,4224]{2,1,0:T(8,128)(2,1)}, f32[4,16,1792]{2,1,0:T(8,128)S(1)}, bf16[256,1024]{1,0:T(8,128)(2,1)S(1)}) custom-call(s32[2]{0:T(128)S(1)} %pad_add_fusion.11.slot_ref, ...), custom_call_target="tpu_custom_call", output_to_operand_aliasing={{0}: (15, {}), {1}: (16, {}), {2}: (17, {})} | custom-call | flops 3288334336 | bytes 24000000 | tf_op jit(solution)/shard_map/mixer_backward/pallas_call | solution.py:870
  688.1 23.8 %mixer_backward.11 = (bf16[4,256,1024]{2,1,0:T(8,128)(2,1)}, bf16[4,256,4224]{2,1,0:T(8,128)(2,1)}, f32[4,16,1792]{2,1,0:T(8,128)S(1)}, bf16[256,1024]{1,0:T(8,128)(2,1)S(1)}) custom-call(s32[2]{0:T(128)S(1)} %pad_add_fusion.6.slot_ref, ...), custom_call_target="tpu_custom_call", output_to_operand_aliasing={{0}: (15, {}), {1}: (16, {}), {2}: (17, {})} | custom-call | flops 3288334336 | bytes 24000000 | tf_op jit(solution)/shard_map/mixer_backward/pallas_call | solution.py:870
  733.1 12.2 bitcast_convert_fusion.1
  771.5 42.3 %psum.14 = f32[]{:T(128)} all-reduce(f32[]{:T(128)S(6)} %select_n.416), channel_id=1, replica_groups=mesh['section'=2,'fsdp'=4,'rep'=4] {'section','fsdp','rep'}, use_global_device_ids=true, to_apply=%region_6.8 | all-reduce | flops 1 | bytes 8 | tf_op jit(solution)/shard_map/psum | solution.py:1178
  821.0 74.7 %all-reduce.10.cloned.1.call-done = f32[2,12616]{1,0:T(2,128)} async-done(((f32[2,12616]{1,0:T(2,128)}), f32[2,12616]{1,0:T(2,128)}) %all-reduce.10.cloned.1.call-update) | async-done | bytes 100944 | tf_op jit(solution)/shard_map/psum | solution.py:1178
  930.2 14.3 %collective-permute-done.37 = bf16[256,1024]{1,0:T(8,128)(2,1)S(1)} collective-permute-done((bf16[256,1024]{1,0:T(8,128)(2,1)}, bf16[256,1024]{1,0:T(8,128)(2,1)S(1)}, u32[]{:S(2)}, u32[]{:S(2)}) %collective-permute-start.37) | collective-permute-done | bytes 524320 | tf_op jit(solution)/shard_map/ppermute | solution.py:899
  955.0 31.6 %collective-permute-done.50 = bf16[384,1024]{1,0:T(8,128)(2,1)S(1)} collective-permute-done((bf16[384,1024]{1,0:T(8,128)(2,1)}, bf16[384,1024]{1,0:T(8,128)(2,1)S(1)}, u32[]{:S(2)}, u32[]{:S(2)}) %collective-permute-start.50) | collective-permute-done | bytes 786464 | tf_op jit(solution)/shard_map/ppermute | solution.py:899
  993.9 39.1 %collective-permute-done.40 = bf16[256,4224]{1,0:T(8,128)(2,1)} collective-permute-done((bf16[256,4224]{1,0:T(8,128)(2,1)}, bf16[256,4224]{1,0:T(8,128)(2,1)}, u32[]{:S(2)}, u32[]{:S(2)}) %collective-permute-start.40) | collective-permute-done | bytes 2162720 | tf_op jit(solution)/shard_map/ppermute | solution.py:899
  1058.0 40.9 %collective-permute-done.41 = bf16[256,4224]{1,0:T(8,128)(2,1)S(1)} collective-permute-done((bf16[256,4224]{1,0:T(8,128)(2,1)S(1)}, bf16[256,4224]{1,0:T(8,128)(2,1)S(1)}, u32[]{:S(2)}, u32[]{:S(2)}) %collective-permute-start.41) | collective-permute-done | bytes 2162720 | tf_op jit(solution)/shard_map/ppermute | solution.py:950
  1121.4 90.8 %collective-permute-done.63 = bf16[512,1024]{1,0:T(8,128)(2,1)S(1)} collective-permute-done((bf16[512,1024]{1,0:T(8,128)(2,1)S(1)}, bf16[512,1024]{1,0:T(8,128)(2,1)S(1)}, u32[]{:S(2)}, u32[]{:S(2)}) %collective-permute-start.63) | collective-permute-done | bytes 1048608 | tf_op jit(solution)/shard_map/ppermute | solution.py:952
  1216.2 37.2 %collective-permute-done.43 = bf16[256,4224]{1,0:T(8,128)(2,1)S(1)} collective-permute-done((bf16[256,4224]{1,0:T(8,128)(2,1)S(1)}, bf16[256,4224]{1,0:T(8,128)(2,1)S(1)}, u32[]{:S(2)}, u32[]{:S(2)}) %collective-permute-start.43) | collective-permute-done | bytes 2162720 | tf_op jit(solution)/shard_map/ppermute | solution.py:952
  (587 shorter events, 530.5 us)
Async XLA Ops:
  7.2 888.5 %all-reduce.10.cloned.1.call-start = ((), (), s32[]{:S(2)}) async-start(), calls=%async_computation | async-start | bytes 202752 | tf_op jit(solution)/shard_map/psum | solution.py:1178
  9.0 84.5 %collective-permute-start.8 = (bf16[192,1024]{1,0:T(8,128)(2,1)}, bf16[192,1024]{1,0:T(8,128)(2,1)}, u32[]{:S(2)}, u32[]{:S(2)}) collective-permute-start(bf16[192,1024]{1,0:T(8,128)(2,1)} %dynamic-slice_bitcast_fusion.14), channel_id=1, source_target_pairs={{0,8},{4,12},{8,0},{12,4},{1,9},{5,13},{9,1},{13,5},{2,10},{6,14},... | collective-permute-start | bytes 1179656 | tf_op jit(solution)/shard_map/ppermute | solution.py:899
  12.0 93.8 %collective-permute-start.7 = (bf16[384,1024]{1,0:T(8,128)(2,1)}, bf16[384,1024]{1,0:T(8,128)(2,1)}, u32[]{:S(2)}, u32[]{:S(2)}) collective-permute-start(bf16[384,1024]{1,0:T(8,128)(2,1)} %bitcast.259), channel_id=1, source_target_pairs={{0,4},{4,0},{8,12},{12,8},{1,5},{5,1},{9,13},{13,9},{2,6},{6,2},{1... | collective-permute-start | bytes 2359304 | tf_op jit(solution)/shard_map/ppermute | solution.py:899
  13.6 74.4 %collective-permute-start.12 = (bf16[128,1024]{1,0:T(8,128)(2,1)}, bf16[128,1024]{1,0:T(8,128)(2,1)}, u32[]{:S(2)}, u32[]{:S(2)}) collective-permute-start(bf16[128,1024]{1,0:T(8,128)(2,1)} %bitcast.262), channel_id=1, source_target_pairs={{0,4},{4,0},{8,12},{12,8},{1,5},{5,1},{9,13},{13,9},{2,6},{6,2},{1... | collective-permute-start | bytes 786440 | tf_op jit(solution)/shard_map/ppermute | solution.py:899
  140.8 181.9 %collective-permute-start.28 = (bf16[256,1024]{1,0:T(8,128)(2,1)}, bf16[256,1024]{1,0:T(8,128)(2,1)}, u32[]{:S(2)}, u32[]{:S(2)}) collective-permute-start(bf16[256,1024]{1,0:T(8,128)(2,1)} %get-tuple-element.398), channel_id=1, source_target_pairs={{0,2},{1,3},{2,0},{3,1},{4,6},{5,7},{6,4},{7,5},{8,10},{9,11},{10,... | collective-permute-start | bytes 1572872 | tf_op jit(solution)/shard_map/ppermute | solution.py:899
  148.5 137.8 %collective-permute-start.1 = (bf16[256,1024]{1,0:T(8,128)(2,1)}, bf16[256,1024]{1,0:T(8,128)(2,1)}, u32[]{:S(2)}, u32[]{:S(2)}) collective-permute-start(bf16[256,1024]{1,0:T(8,128)(2,1)} %get-tuple-element.400), channel_id=1, source_target_pairs={{0,1},{1,0},{2,3},{3,2},{4,5},{5,4},{6,7},{7,6},{8,9},{9,8},{10,11... | collective-permute-start | bytes 1572872 | tf_op jit(solution)/shard_map/ppermute | solution.py:899
  160.3 199.2 %collective-permute-start = (bf16[256,1024]{1,0:T(8,128)(2,1)}, bf16[256,1024]{1,0:T(8,128)(2,1)}, u32[]{:S(2)}, u32[]{:S(2)}) collective-permute-start(bf16[256,1024]{1,0:T(8,128)(2,1)} %get-tuple-element.401), channel_id=1, source_target_pairs={{0,3},{1,2},{2,1},{3,0},{4,7},{5,6},{6,5},{7,4},{8,11},{9,10},{10,... | collective-permute-start | bytes 1572872 | tf_op jit(solution)/shard_map/ppermute | solution.py:899
  731.5 218.4 %collective-permute-start.59 = (bf16[2,512,1024]{2,1,0:T(8,128)(2,1)}, bf16[2,512,1024]{2,1,0:T(8,128)(2,1)}, u32[]{:S(2)}, u32[]{:S(2)}) collective-permute-start(bf16[2,512,1024]{2,1,0:T(8,128)(2,1)} %dynamic-slice_bitcast_fusion.3), channel_id=1, source_target_pairs={{0,4},{4,0},{8,12},{12,8},{1,5},{5,1},{9,13},{13,9},{2,6},{6,2},{1... | collective-permute-start | bytes 6291464 | tf_op jit(solution)/shard_map/ppermute | solution.py:899
  750.5 160.6 %collective-permute-start.54 = (bf16[2,256,4096]{2,1,0:T(8,128)(2,1)}, bf16[2,256,4096]{2,1,0:T(8,128)(2,1)}, u32[]{:S(2)}, u32[]{:S(2)}) collective-permute-start(bf16[2,256,4096]{2,1,0:T(8,128)(2,1)} %dynamic-slice_bitcast_fusion.1), channel_id=1, source_target_pairs={{0,4},{4,0},{8,12},{12,8},{1,5},{5,1},{9,13},{13,9},{2,6},{6,2},{1... | collective-permute-start | bytes 12582920 | tf_op jit(solution)/shard_map/ppermute | solution.py:899
  752.0 154.1 %collective-permute-start.49 = (bf16[2,384,1024]{2,1,0:T(8,128)(2,1)}, bf16[2,384,1024]{2,1,0:T(8,128)(2,1)}, u32[]{:S(2)}, u32[]{:S(2)}) collective-permute-start(bf16[2,384,1024]{2,1,0:T(8,128)(2,1)} %dynamic-slice_bitcast_fusion.5), channel_id=1, source_target_pairs={{0,4},{4,0},{8,12},{12,8},{1,5},{5,1},{9,13},{13,9},{2,6},{6,2},{1... | collective-permute-start | bytes 4718600 | tf_op jit(solution)/shard_map/ppermute | solution.py:899
  753.1 64.1 %collective-permute-start.44 = (bf16[2,128,1024]{2,1,0:T(8,128)(2,1)}, bf16[2,128,1024]{2,1,0:T(8,128)(2,1)}, u32[]{:S(2)}, u32[]{:S(2)}) collective-permute-start(bf16[2,128,1024]{2,1,0:T(8,128)(2,1)} %dynamic-slice_bitcast_fusion.8), channel_id=1, source_target_pairs={{0,4},{4,0},{8,12},{12,8},{1,5},{5,1},{9,13},{13,9},{2,6},{6,2},{1... | collective-permute-start | bytes 1572872 | tf_op jit(solution)/shard_map/ppermute | solution.py:899
  769.0 150.8 %collective-permute-start.39 = (bf16[2,256,4224]{2,1,0:T(8,128)(2,1)}, bf16[2,256,4224]{2,1,0:T(8,128)(2,1)}, u32[]{:S(2)}, u32[]{:S(2)}) collective-permute-start(bf16[2,256,4224]{2,1,0:T(8,128)(2,1)} %dynamic-slice_bitcast_fusion), channel_id=1, source_target_pairs={{0,4},{4,0},{8,12},{12,8},{1,5},{5,1},{9,13},{13,9},{2,6},{6,2},{1... | collective-permute-start | bytes 12976136 | tf_op jit(solution)/shard_map/ppermute | solution.py:899
  818.5 84.2 %collective-permute-start.45 = (bf16[128,1024]{1,0:T(8,128)(2,1)S(1)}, bf16[128,1024]{1,0:T(8,128)(2,1)S(1)}, u32[]{:S(2)}, u32[]{:S(2)}) collective-permute-start(bf16[128,1024]{1,0:T(8,128)(2,1)S(1)} %dynamic-slice_bitcast_fusion.15), channel_id=1, source_target_pairs={{0,8},{4,12},{8,0},{12,4},{1,9},{5,13},{9,1},{13,5},{2,10},{6,14},... | collective-permute-start | bytes 786440 | tf_op jit(solution)/shard_map/ppermute | solution.py:899
  920.9 68.8 %collective-permute-start.55 = (bf16[256,4096]{1,0:T(8,128)(2,1)}, bf16[256,4096]{1,0:T(8,128)(2,1)}, u32[]{:S(2)}, u32[]{:S(2)}) collective-permute-start(bf16[256,4096]{1,0:T(8,128)(2,1)} %dynamic-slice_bitcast_fusion.4), channel_id=1, source_target_pairs={{0,8},{4,12},{8,0},{12,4},{1,9},{5,13},{9,1},{13,5},{2,10},{6,14},... | collective-permute-start | bytes 6291464 | tf_op jit(solution)/shard_map/ppermute | solution.py:899
  946.1 86.9 %collective-permute-start.40 = (bf16[256,4224]{1,0:T(8,128)(2,1)}, bf16[256,4224]{1,0:T(8,128)(2,1)}, u32[]{:S(2)}, u32[]{:S(2)}) collective-permute-start(bf16[256,4224]{1,0:T(8,128)(2,1)} %dynamic-slice_bitcast_fusion.2), channel_id=1, source_target_pairs={{0,8},{4,12},{8,0},{12,4},{1,9},{5,13},{9,1},{13,5},{2,10},{6,14},... | collective-permute-start | bytes 6488072 | tf_op jit(solution)/shard_map/ppermute | solution.py:899
  949.1 91.6 %collective-permute-start.47 = (bf16[128,1024]{1,0:T(8,128)(2,1)S(1)}, bf16[128,1024]{1,0:T(8,128)(2,1)S(1)}, u32[]{:S(2)}, u32[]{:S(2)}) collective-permute-start(bf16[128,1024]{1,0:T(8,128)(2,1)S(1)} %add_convert_fusion.9), channel_id=1, source_target_pairs={{1,2},{2,1},{5,6},{6,5},{9,10},{10,9},{13,14},{14,13},{17,18},{18,... | collective-permute-start | bytes 786440 | tf_op jit(solution)/shard_map/ppermute | solution.py:951
  953.4 98.4 %collective-permute-start.60 = (bf16[512,1024]{1,0:T(8,128)(2,1)S(1)}, bf16[512,1024]{1,0:T(8,128)(2,1)S(1)}, u32[]{:S(2)}, u32[]{:S(2)}) collective-permute-start(bf16[512,1024]{1,0:T(8,128)(2,1)S(1)} %dynamic-slice_bitcast_fusion.6), channel_id=1, source_target_pairs={{0,8},{4,12},{8,0},{12,4},{1,9},{5,13},{9,1},{13,5},{2,10},{6,14},... | collective-permute-start | bytes 3145736 | tf_op jit(solution)/shard_map/ppermute | solution.py:899
  986.9 68.2 %collective-permute-start.51 = (bf16[384,1024]{1,0:T(8,128)(2,1)S(1)}, bf16[384,1024]{1,0:T(8,128)(2,1)S(1)}, u32[]{:S(2)}, u32[]{:S(2)}) collective-permute-start(bf16[384,1024]{1,0:T(8,128)(2,1)S(1)} %fusion.9), channel_id=1, source_target_pairs={{0,1},{3,2},{4,5},{7,6},{8,9},{11,10},{12,13},{15,14},{16,17},{19,... | collective-permute-start | bytes 2359304 | tf_op jit(solution)/shard_map/ppermute | solution.py:950
  992.1 64.2 %collective-permute-start.56 = (bf16[256,4096]{1,0:T(8,128)(2,1)S(1)}, bf16[256,4096]{1,0:T(8,128)(2,1)S(1)}, u32[]{:S(2)}, u32[]{:S(2)}) collective-permute-start(bf16[256,4096]{1,0:T(8,128)(2,1)S(1)} %fusion.4), channel_id=1, source_target_pairs={{0,1},{3,2},{4,5},{7,6},{8,9},{11,10},{12,13},{15,14},{16,17},{19,... | collective-permute-start | bytes 6291464 | tf_op jit(solution)/shard_map/ppermute | solution.py:950
  1035.1 63.8 %collective-permute-start.41 = (bf16[256,4224]{1,0:T(8,128)(2,1)S(1)}, bf16[256,4224]{1,0:T(8,128)(2,1)S(1)}, u32[]{:S(2)}, u32[]{:S(2)}) collective-permute-start(bf16[256,4224]{1,0:T(8,128)(2,1)S(1)} %fusion.2), channel_id=1, source_target_pairs={{0,1},{3,2},{4,5},{7,6},{8,9},{11,10},{12,13},{15,14},{16,17},{19,... | collective-permute-start | bytes 6488072 | tf_op jit(solution)/shard_map/ppermute | solution.py:950
  1052.3 61.1 %collective-permute-start.61 = (bf16[512,1024]{1,0:T(8,128)(2,1)S(1)}, bf16[512,1024]{1,0:T(8,128)(2,1)S(1)}, u32[]{:S(2)}, u32[]{:S(2)}) collective-permute-start(bf16[512,1024]{1,0:T(8,128)(2,1)S(1)} %fusion.6), channel_id=1, source_target_pairs={{0,1},{3,2},{4,5},{7,6},{8,9},{11,10},{12,13},{15,14},{16,17},{19,... | collective-permute-start | bytes 3145736 | tf_op jit(solution)/shard_map/ppermute | solution.py:950
  1115.3 98.3 %collective-permute-start.58 = (bf16[256,4096]{1,0:T(8,128)(2,1)S(1)}, bf16[256,4096]{1,0:T(8,128)(2,1)S(1)}, u32[]{:S(2)}, u32[]{:S(2)}) collective-permute-start(bf16[256,4096]{1,0:T(8,128)(2,1)S(1)} %add_convert_fusion.2), channel_id=1, source_target_pairs={{1,0},{2,3},{5,4},{6,7},{9,8},{10,11},{13,12},{14,15},{17,16},{18,... | collective-permute-start | bytes 6291464 | tf_op jit(solution)/shard_map/ppermute | solution.py:952
  1117.0 95.1 %collective-permute-start.63 = (bf16[512,1024]{1,0:T(8,128)(2,1)S(1)}, bf16[512,1024]{1,0:T(8,128)(2,1)S(1)}, u32[]{:S(2)}, u32[]{:S(2)}) collective-permute-start(bf16[512,1024]{1,0:T(8,128)(2,1)S(1)} %add_convert_fusion.4), channel_id=1, source_target_pairs={{1,0},{2,3},{5,4},{6,7},{9,8},{10,11},{13,12},{14,15},{17,16},{18,... | collective-permute-start | bytes 3145736 | tf_op jit(solution)/shard_map/ppermute | solution.py:952
  1118.8 134.5 %collective-permute-start.43 = (bf16[256,4224]{1,0:T(8,128)(2,1)S(1)}, bf16[256,4224]{1,0:T(8,128)(2,1)S(1)}, u32[]{:S(2)}, u32[]{:S(2)}) collective-permute-start(bf16[256,4224]{1,0:T(8,128)(2,1)S(1)} %add_convert_fusion), channel_id=1, source_target_pairs={{1,0},{2,3},{5,4},{6,7},{9,8},{10,11},{13,12},{14,15},{17,16},{18,... | collective-permute-start | bytes 6488072 | tf_op jit(solution)/shard_map/ppermute | solution.py:952
  (151 other events, 3052.7 us)
Sparse Core Ops, SparseCore 0:
  771.7 124.0 all-reduce.9

commit v2 on v1

v2 whole, which is shorter than its diff:
```python
import math
import functools

import jax
import jax.numpy as jnp
from jax import lax
from jax.experimental import pallas as pl
from jax.experimental.pallas import tpu as pltpu
from jax.sharding import PartitionSpec as P

HD = 64
EPSILON = 1e-05
ROPE_BASE = 100000000000.0
MASKED = -1e30
F32 = jnp.float32
BF = jnp.bfloat16
TILE = 256
HALF = 128
HB = pl.BlockSpec(memory_space=pltpu.HBM)
VM = pl.BlockSpec(memory_space=pltpu.VMEM)
SM = pl.BlockSpec(memory_space=pltpu.SMEM)


def dot(a, b):
    return jnp.dot(a, b, preferred_element_type=F32)


def dot_nt(a, b):
    return lax.dot_general(a, b, (((1,), (1,)), ((), ())), preferred_element_type=F32)


def dot_tn(a, b):
    return lax.dot_general(a, b, (((0,), (0,)), ((), ())), preferred_element_type=F32)


def sigmoid(v):
    return 0.5 * jnp.tanh(0.5 * v) + 0.5


def lanes(i, width=TILE):
    return pl.ds(pl.multiple_of(i * width, width), width)


def iota(shape, axis):
    return lax.broadcasted_iota(jnp.int32, shape, axis)


def split2(v):
    hi = v.astype(BF)
    return hi, (v - hi.astype(F32)).astype(BF)


def split3(v):
    hi = v.astype(BF)
    rest = v - hi.astype(F32)
    mid = rest.astype(BF)
    return hi, mid, (rest - mid.astype(F32)).astype(BF)


def expand_matrix(tile):
    row = jnp.bitwise_and(iota((TILE, TILE), 0), HALF - 1)
    col = jnp.right_shift(iota((TILE, TILE), 1), 6) + tile * (TILE // HD)
    return jnp.where(row == col, 1.0, 0.0).astype(BF)


def reduce_matrix(tile):
    row = jnp.right_shift(iota((TILE, HALF), 0), 6) + tile * (TILE // HD)
    col = iota((TILE, HALF), 1)
    return jnp.where(row == col, 1.0, 0.0).astype(BF)


def both(v):
    return jnp.concatenate(split2(v), axis=1)


def rope(v, cosine, sine, first):
    turned = jnp.where(first, pltpu.roll(v, HALF - HD // 2, 1), pltpu.roll(v, HD // 2, 1))
    return v * cosine + turned * sine


def start_all(groups, sems):
    waits, at = [], 0
    for group in groups:
        copies = []
        for source, target in group:
            copies.append(pltpu.make_async_copy(source, target, sems.at[at]))
            at += 1
        for copy in copies:
            copy.start()
        waits.append(copies)

    def wait(i):
        for copy in waits[i]:
            copy.wait()

    return wait


def row_pieces(pieces, spots, scratch, columns):
    if len(pieces) == 1:
        return [(pieces[0].at[:, a], scratch.at[:, b]) for a, b in columns]
    unit = pieces[-1].shape[0]
    if len(pieces) == 4:
        places = [jnp.right_shift(spots[i], 1) for i in (0, 1, 2, 4)]
    else:
        places = [spots[i] for i in range(6)]
    out = []
    for a, b in columns:
        for place, piece in zip(places, pieces):
            rows = pl.ds(pl.multiple_of(place * unit, unit), piece.shape[0])
            out.append((piece.at[:, a], scratch.at[rows, b]))
    return out


def out_pieces(pieces, spots, scratch, inner):
    if len(pieces) == 1:
        return [(pieces[0], scratch)]
    total, width = scratch.shape
    n = total // pieces[0].shape[0]
    cut, rest = inner // n, (total - inner) // n
    out = []
    for i, piece in enumerate(pieces):
        block, side = jnp.right_shift(spots[i], 1), jnp.bitwise_and(spots[i], 1)
        span = piece.shape[1]
        cols = slice(0, width)
        if span < width:
            cols = pl.ds(pl.multiple_of(side * span, span), span)
        upper = pl.ds(pl.multiple_of(block * cut, cut), cut)
        lower = pl.ds(pl.multiple_of(inner + block * rest, rest), rest)
        out.append((piece.at[:cut, :], scratch.at[upper, cols]))
        out.append((piece.at[cut:, :], scratch.at[lower, cols]))
    return out


def saver(slot, active, sems):
    stores = []

    def save(buffer, stack, at=slot):
        copy = pltpu.make_async_copy(buffer, stack.at[at], sems.at[len(stores)])
        pl.when(active)(copy.start)
        stores.append(copy)

    def finish():
        for copy in stores:
            pl.when(active)(copy.wait)

    return save, finish


def in_hbm(a):
    return pltpu.with_memory_space_constraint(a, pltpu.HBM)


def call(body, name, scalars, spots, ordinary, weights, reads, stacks, result, scratch, limit, work):
    fresh = isinstance(stacks[0], jax.ShapeDtypeStruct)
    flat = [piece for group in weights for piece in group]
    counts = [len(group) for group in weights]
    kept = [] if fresh else list(stacks)
    ahead = len(scalars) + 1 + len(ordinary) + len(flat) + len(reads)
    n = len(stacks)
    cuts = [len(scalars), 1, len(ordinary), len(flat), len(reads), len(kept), n, 1]

    def kernel(*refs):
        parts, at = [], 0
        for cut in cuts:
            parts.append(refs[at : at + cut])
            at += cut
        groups, begin = [], 0
        for c in counts:
            groups.append(parts[3][begin : begin + c])
            begin += c
        for _ in body(
            parts[0], parts[1][0], parts[2], groups, parts[4], parts[6], parts[7][0], refs[at:]
        ):
            pass

    out = pl.pallas_call(
        kernel,
        out_shape=[pltpu.HBM(s.shape, s.dtype) for s in stacks] + [result],
        in_specs=[SM] * (len(scalars) + 1)
        + [VM] * len(ordinary)
        + [HB] * (len(flat) + len(reads) + len(kept)),
        out_specs=[HB] * n + [VM],
        scratch_shapes=scratch,
        input_output_aliases={} if fresh else {ahead + i: i for i in range(n)},
        compiler_params=pltpu.CompilerParams(vmem_limit_bytes=limit * 1024 * 1024),
        cost_estimate=pl.CostEstimate(
            flops=work * 100000000, bytes_accessed=1000000, transcendentals=0
        ),
        name=name,
    )(*scalars, spots, *ordinary, *(in_hbm(a) for a in flat + list(reads) + kept))
    return list(out[:n]), out[n]


V_TAP, V_CBIAS, V_GS, V_SKIP, V_G1, V_G2, V_SBIAS, V_DECAY = 0, 4, 5, 6, 7, 8, 9, 10


def scan_terms(step_raw, vec_ref, heads):
    lane = iota(step_raw.shape, 1)
    pre = step_raw + vec_ref[V_SBIAS : V_SBIAS + 1, :HALF]
    soft = jnp.maximum(pre, 0.0) + jnp.log1p(jnp.exp(-jnp.abs(pre)))
    step = jnp.where(lane < heads, soft, 0.0)
    change = step * vec_ref[V_DECAY : V_DECAY + 1, :HALF]
    length = step.shape[0]
    lower = jnp.where(
        iota((length, length), 0) >= iota((length, length), 1), 1.0, 0.0
    ).astype(BF)
    run = sum(dot(lower, part) for part in split3(change))
    middle = run[HALF - 1 : HALF, :]
    bend = jnp.where(iota(run.shape, 0) < HALF, middle - run, run - middle)
    bend = jnp.exp(jnp.minimum(bend, 0.0))
    return pre, step, change, run, bend


def broadcast_runs(run, run_wide, heads):
    for h in range(heads):
        run_wide[:, h * HALF : (h + 1) * HALF] = jnp.broadcast_to(
            run[:, h : h + 1], (run.shape[0], HALF)
        )


def mix_forward(widths, scalars, spots, ordinary, weights, reads, stacks, hidden_ref, scratch):
    ci, mi, qw, kw, heads = widths
    index_ref, slot_ref = scalars
    base = 4 * index_ref[0]
    x_ref, vec_ref, cos_ref, sin_ref, _ = ordinary
    w_first, w_conv, w_gate, w_out = weights
    (win, wout, normed, conv_raw, z, xbc, gate_raw, qkv, step_raw, probs, branch, mixed_all, y,
     gated, run_wide, run_row, step_two, bend_two, in_sem, out_sem) = scratch
    (s_normed, s_conv, s_z, s_gate, s_qkv, s_step, s_probs, s_ssm, s_mixed, s_y, s_hidden,
     s_x) = stacks
    g0 = ci
    q0 = ci + mi
    total = win.shape[1]
    tail = total - q0
    wait = start_all(
        [
            row_pieces(w_first, spots, win, [(slice(0, tail), slice(q0, total))]),
            row_pieces(w_conv, spots, win, [(slice(0, ci), slice(0, ci))]),
            row_pieces(w_gate, spots, win, [(slice(0, mi), slice(g0, q0))]),
            out_pieces(w_out, spots, wout, mi),
        ],
        in_sem,
    )
    save, finish = saver(slot_ref[base], slot_ref[base + 1] > 0, out_sem)
    yield

    length = x_ref.shape[0]
    x = x_ref[...].astype(F32)
    rate = lax.rsqrt(jnp.mean(x * x, axis=-1, keepdims=True) + EPSILON)
    normed[...] = (x * rate * vec_ref[V_G1 : V_G1 + 1, : x.shape[1]]).astype(BF)
    save(normed, s_normed)
    lane_first = jnp.bitwise_and(iota((length, HALF), 1), HD - 1) < HD // 2
    half_low = iota((length, HALF), 1) < HD

    wait(0)
    cosine, sine = cos_ref[...], sin_ref[...]
    n_rope = (qw + kw) // HALF
    for t in range((total - q0) // HALF // 2):
        raw = dot(normed[...], win[:, q0 + t * TILE : q0 + (t + 1) * TILE])
        for part in range(2):
            c = 2 * t + part
            piece = raw[:, part * HALF : (part + 1) * HALF]
            if c < n_rope:
                piece = rope(piece, cosine, sine, lane_first)
            if c < n_rope + kw // HALF:
                qkv[:, c * HALF : (c + 1) * HALF] = piece.astype(BF)
            else:
                step_raw[...] = piece
    if ((total - q0) // HALF) % 2:
        step_raw[...] = dot(normed[...], win[:, total - HALF : total])
    save(qkv, s_qkv)
    save(step_raw, s_step)

    wait(1)
    row = iota((length, TILE), 0)

    def conv_tile(t, carry):
        cols = lanes(t)
        raw = dot(normed[...], win[:, cols])
        conv_raw[:, cols] = raw.astype(BF)
        total_z = vec_ref[V_CBIAS : V_CBIAS + 1, cols] + raw * vec_ref[3:4, cols]
        for back in range(1, 4):
            moved = jnp.where(row >= back, pltpu.roll(raw, back, 0), 0.0)
            total_z = total_z + moved * vec_ref[3 - back : 4 - back, cols]
        z[:, cols] = total_z.astype(BF)
        xbc[:, cols] = (total_z * sigmoid(total_z)).astype(BF)
        return carry

    lax.fori_loop(0, ci // TILE, conv_tile, 0, unroll=True)
    save(conv_raw, s_conv)
    save(z, s_z)

    wait(2)

    def gate_tile(t, carry):
        raw = dot(normed[...], win[:, pl.ds(pl.multiple_of(g0 + t * TILE, TILE), TILE)])
        gate_raw[:, lanes(t)] = raw.astype(BF)
        return carry

    lax.fori_loop(0, mi // TILE, gate_tile, 0, unroll=True)
    save(gate_raw, s_gate)

    yield

    keys, values = qkv[:, qw : qw + kw], qkv[:, qw + kw : qw + 2 * kw]
    keys_far, values_far = pltpu.roll(keys.astype(F32), HD, 1).astype(BF), pltpu.roll(
        values.astype(F32), HD, 1
    ).astype(BF)
    causal_top = iota((HALF, HALF), 1) <= iota((HALF, HALF), 0)
    causal_low = iota((HALF, length), 1) <= iota((HALF, length), 0) + HALF
    pairs = qw // HALF
    groups = kw // HD
    probs_zero = jnp.zeros((HALF, HALF), BF)
    for pair in range(pairs):
        group = pair // (pairs // groups)
        keep = half_low if group == 0 else jnp.logical_not(half_low)
        keys_two = jnp.where(keep, keys, keys_far)
        values_two = jnp.where(keep, values, values_far)
        query = qkv[:, pair * HALF : (pair + 1) * HALF] * jnp.asarray(HD ** (-0.5), BF)
        results = []
        for side in range(2):
            own = half_low if side == 0 else jnp.logical_not(half_low)
            q = jnp.where(own, query, jnp.zeros_like(query))
            at = (2 * pair + side) * length
            out = []
            for lo, causal in ((0, causal_top), (1, causal_low)):
                width = HALF if lo == 0 else length
                scores = dot_nt(q[lo * HALF : (lo + 1) * HALF], keys_two[:width])
                scores = jnp.where(causal, scores, MASKED)
                top = jnp.max(scores, axis=-1, keepdims=True)
                weights = jnp.exp(scores - top)
                weights = weights / jnp.sum(weights, axis=-1, keepdims=True)
                weights = weights.astype(BF)
                if lo == 0:
                    probs[at : at + HALF, :HALF] = weights
                    probs[at : at + HALF, HALF:] = probs_zero
                else:
                    probs[at + HALF : at + length, :] = weights
                out.append(dot(weights, values_two[:width]))
            results.append(jnp.concatenate(out, axis=0))
        mixed = jnp.where(half_low, results[0], results[1])
        mixed_all[:, pair * HALF : (pair + 1) * HALF] = mixed.astype(BF)
    save(probs, s_probs)
    save(mixed_all, s_mixed)

    pre, step, change, run, bend = scan_terms(step_raw[...], vec_ref, heads)
    turned = run.T
    run_row[:HALF, :] = turned[:, :HALF]
    run_row[HALF:, :] = turned[:, HALF:]
    broadcast_runs(run, run_wide, heads)
    step_two[...] = both(step)
    bend_two[...] = both(bend)
    b_in, c_in = xbc[:, mi : mi + HALF], xbc[:, mi + HALF : mi + 2 * HALF]
    tops = [dot_nt(c_in[c * HALF : (c + 1) * HALF], b_in[c * HALF : (c + 1) * HALF]) for c in (0, 1)]
    cross = dot_nt(c_in[HALF:], b_in[:HALF]).astype(BF)
    pair_low = iota((HALF, HALF), 1) < HD
    tops = [jnp.where(causal_top, t, 0.0) for t in tops]

    def mix_tile(t, squares):
        cols = lanes(t)
        spread = expand_matrix(t)
        x_in = xbc[:, cols].astype(F32)
        scaled = (dot(step_two[...], spread) * x_in).astype(BF)
        bends = dot(bend_two[...], spread)
        u = (bends[:HALF] * scaled[:HALF].astype(F32)).astype(BF)
        far = dot(cross, u) * bends[HALF:]
        parts = []
        for p in range(TILE // HALF):
            block = []
            for c in range(2):
                rows = slice(c * HALF, (c + 1) * HALF)
                weights = []
                for side in range(2):
                    h = t * (TILE // HD) + 2 * p + side
                    wide = run_wide[rows, lanes(h, HALF)]
                    line = run_row[pl.ds(c * HALF + h, 1), :]
                    decay = jnp.exp(jnp.minimum(wide - line, 0.0))
                    weights.append((decay * tops[c]).astype(BF))
                xs = scaled[rows, p * HALF : (p + 1) * HALF]
                zero = jnp.zeros_like(xs)
                right = jnp.concatenate(
                    [jnp.where(pair_low, xs, zero), jnp.where(pair_low, zero, xs)], axis=0
                )
                block.append(dot(jnp.concatenate(weights, axis=1), right))
            parts.append(jnp.concatenate(block, axis=0))
        out = jnp.concatenate(parts, axis=1)
        out = out + jnp.concatenate([jnp.zeros_like(far), far], axis=0)
        out = out + vec_ref[V_SKIP : V_SKIP + 1, cols] * x_in
        y[:, cols] = out.astype(BF)
        g = gate_raw[:, cols].astype(F32)
        out = out * (g * sigmoid(g))
        gated[:, cols] = out
        return squares + jnp.sum(out * out, axis=-1, keepdims=True)

    squares = lax.fori_loop(0, mi // TILE, mix_tile, jnp.zeros((length, 1), F32), unroll=True)
    save(y, s_y)
    rate = lax.rsqrt(squares * (1.0 / mi) + EPSILON)
    branch[...] = (gated[...] * rate * vec_ref[V_GS : V_GS + 1, :mi]).astype(BF)
    save(branch, s_ssm)

    wait(3)

    def out_tile(t, carry):
        cols = lanes(t)
        hidden_ref[:, cols] = (
            x_ref[:, cols].astype(F32)
            + dot(branch[...], wout[:mi, cols])
            + dot(mixed_all[...], wout[mi:, cols])
        )
        return carry

    lax.fori_loop(0, wout.shape[1] // TILE, out_tile, 0, unroll=True)
    save(hidden_ref, s_hidden)
    save(x_ref, s_x)
    yield
    finish()


def mixer_forward_scratch(length, width, widths, total):
    ci, mi, qw, kw, heads = widths
    return [
        pltpu.VMEM((width, total), BF),
        pltpu.VMEM((mi + qw, width), BF),
        pltpu.VMEM((length, width), BF),
        pltpu.VMEM((length, ci), BF),
        pltpu.VMEM((length, ci), BF),
        pltpu.VMEM((length, ci), BF),
        pltpu.VMEM((length, mi), BF),
        pltpu.VMEM((length, qw + 2 * kw), BF),
        pltpu.VMEM((length, HALF), F32),
        pltpu.VMEM((qw // HD * length, length), BF),
        pltpu.VMEM((length, mi), BF),
        pltpu.VMEM((length, qw), BF),
        pltpu.VMEM((length, mi), BF),
        pltpu.VMEM((length, mi), F32),
        pltpu.VMEM((length, heads * HALF), F32),
        pltpu.VMEM((length, HALF), F32),
        pltpu.VMEM((length, 2 * HALF), BF),
        pltpu.VMEM((length, 2 * HALF), BF),
        pltpu.SemaphoreType.DMA((32,)),
        pltpu.SemaphoreType.DMA((12,)),
    ]


def mixer_forward_call(
    index, slot, spots, x, vec, cosine, sine, turn, weights, stacks, widths, total
):
    ci, mi, qw, kw, heads = widths
    length, width = x.shape
    scratch = mixer_forward_scratch(length, width, widths, total)
    return call(
        functools.partial(mix_forward, widths),
        "mixer_forward",
        [index, slot],
        spots,
        [x, vec, cosine, sine, turn],
        weights,
        [],
        stacks,
        jax.ShapeDtypeStruct((length, width), F32),
        scratch,
        44,
        200,
    )


def mlp_forward(scalars, spots, ordinary, weights, reads, stacks, low_ref, scratch):
    index_ref, slot_ref = scalars
    base = 4 * index_ref[0]
    hidden_ref, vec_ref = ordinary
    w_g, w_u, w_down = weights
    wgu, wdown, normed, gate_low, up_low, act, final, in_sem, out_sem = scratch
    s_normed, s_gate, s_up, s_act, s_final, s_low = stacks
    ff = wdown.shape[0]
    parts = 2
    step = ff // parts
    groups = []
    for i in range(parts):
        a = slice(i * step, (i + 1) * step)
        b = slice(ff + i * step, ff + (i + 1) * step)
        groups.append(
            row_pieces(w_g, spots, wgu, [(a, a)]) + row_pieces(w_u, spots, wgu, [(a, b)])
        )
    groups.append(row_pieces(w_down, spots, wdown, [(slice(0, wdown.shape[1]),) * 2]))
    wait = start_all(groups, in_sem)
    save, finish = saver(slot_ref[base], slot_ref[base + 1] > 0, out_sem)
    yield
    valid = jnp.where(iota((hidden_ref.shape[0], 1), 0) < slot_ref[base + 2], 1.0, 0.0)

    hidden = hidden_ref[...]
    rate = lax.rsqrt(jnp.mean(hidden * hidden, axis=-1, keepdims=True) + EPSILON)
    normed[...] = (hidden * rate * vec_ref[V_G2 : V_G2 + 1, : hidden.shape[1]]).astype(BF)
    save(normed, s_normed)
    for i in range(parts):
        wait(i)

        def up_tile(t, carry):
            a = pl.ds(pl.multiple_of(i * step + t * TILE, TILE), TILE)
            b = pl.ds(pl.multiple_of(ff + i * step + t * TILE, TILE), TILE)
            gate = dot(normed[...], wgu[:, a])
            up = dot(normed[...], wgu[:, b])
            gate_low[:, a] = gate.astype(BF)
            up_low[:, a] = up.astype(BF)
            act[:, a] = (gate * sigmoid(gate) * up).astype(BF)
            return carry

        lax.fori_loop(0, step // TILE, up_tile, 0, unroll=True)
    save(gate_low, s_gate)
    save(up_low, s_up)
    save(act, s_act)
    wait(parts)

    def down_tile(t, carry):
        cols = lanes(t)
        out = (hidden_ref[:, cols] + dot(act[...], wdown[:, cols])) * valid
        final[:, cols] = out
        low_ref[:, cols] = out.astype(BF)
        return carry

    lax.fori_loop(0, wdown.shape[1] // TILE, down_tile, 0, unroll=True)
    save(final, s_final)
    save(low_ref, s_low, slot_ref[base + 3])
    yield
    finish()


def mlp_forward_scratch(length, width, ff):
    return [
        pltpu.VMEM((width, 2 * ff), BF),
        pltpu.VMEM((ff, width), BF),
        pltpu.VMEM((length, width), BF),
        pltpu.VMEM((length, ff), BF),
        pltpu.VMEM((length, ff), BF),
        pltpu.VMEM((length, ff), BF),
        pltpu.VMEM((length, width), F32),
        pltpu.SemaphoreType.DMA((32,)),
        pltpu.SemaphoreType.DMA((6,)),
    ]


def mlp_forward_call(index, slot, spots, hidden, vec, weights, stacks, ff):
    length, width = hidden.shape
    scratch = mlp_forward_scratch(length, width, ff)
    return call(
        mlp_forward,
        "mlp_forward",
        [index, slot],
        spots,
        [hidden, vec],
        weights,
        [],
        stacks,
        jax.ShapeDtypeStruct((length, width), BF),
        scratch,
        32,
        3,
    )


def mlp_backward(scalars, spots, ordinary, weights, reads, stacks, d_hidden_ref, scratch):
    index_ref, slot_ref, mix_ref = scalars
    base = 4 * index_ref[0]
    target_ref, vec_ref, _ = ordinary
    w_g, w_u, w_down = weights
    s_final, s_hidden, s_gate, s_up = reads
    (wgu, wdown, final, hidden, gate_low, up_low, d_mlp, d_gu, d_sum, d_normed, small, in_sem,
     out_sem) = scratch
    s_dmlp, s_dgate, s_dup, s_small = stacks
    slot = slot_ref[base]
    ff = wdown.shape[0]
    wait = start_all(
        [
            [(s_final.at[slot], final)],
            [(s_gate.at[slot], gate_low), (s_up.at[slot], up_low)]
            + row_pieces(w_down, spots, wdown, [(slice(0, wdown.shape[1]),) * 2]),
            row_pieces(w_g, spots, wgu, [(slice(0, ff), slice(0, ff))])
            + row_pieces(w_u, spots, wgu, [(slice(0, ff), slice(ff, 2 * ff))]),
            [(s_hidden.at[slot], hidden)],
        ],
        in_sem,
    )
    save, finish = saver(slot, slot_ref[base + 1] > 0, out_sem)
    yield
    wait(0)
    target = target_ref[...].astype(F32)
    valid = jnp.where(iota((target_ref.shape[0], 1), 0) < slot_ref[base + 2], 1.0, 0.0)
    misfit = final[...] - target
    loss = jnp.sum(valid * misfit * misfit, axis=0, keepdims=True)
    seed = valid * jnp.where(mix_ref[0] > 0.5, target, mix_ref[1] * misfit)
    d_sum[...] = seed
    d_mlp[...] = seed.astype(BF)
    save(d_mlp, s_dmlp)
    wait(1)

    def act_tile(t, carry):
        a = lanes(t)
        b = pl.ds(pl.multiple_of(ff + t * TILE, TILE), TILE)
        d_act = dot_nt(d_mlp[...], wdown[a, :])
        gate, up = gate_low[:, a].astype(F32), up_low[:, a].astype(F32)
        s = sigmoid(gate)
        swish = gate * s
        d_gu[:, a] = (d_act * up * (s + swish - swish * s)).astype(BF)
        d_gu[:, b] = (d_act * swish).astype(BF)
        return carry

    lax.fori_loop(0, ff // TILE, act_tile, 0, unroll=True)
    save(d_gu.at[:, :ff], s_dgate)
    save(d_gu.at[:, ff:], s_dup)
    wait(2)
    yield

    def back_tile(t, carry):
        rows = lanes(t)
        d_normed[:, rows] = dot_nt(d_gu[...], wgu[rows, :])
        return carry

    lax.fori_loop(0, wgu.shape[0] // TILE, back_tile, 0, unroll=True)
    wait(3)
    h = hidden[...]
    width = h.shape[1]
    rate = lax.rsqrt(jnp.mean(h * h, axis=-1, keepdims=True) + EPSILON)
    unit = h * rate
    d_n = d_normed[...]
    small[...] = jnp.zeros_like(small)
    small[0:1, :width] = jnp.sum(d_n * unit, axis=0, keepdims=True)
    small[1:2, :width] = loss
    save(small, s_small)
    d_n = d_n * vec_ref[V_G2 : V_G2 + 1, :width]
    d_hidden_ref[...] = d_sum[...] + rate * (
        d_n - unit * jnp.mean(d_n * unit, axis=-1, keepdims=True)
    )
    yield
    finish()


def mlp_backward_scratch(length, width, ff, small):
    return [
        pltpu.VMEM((width, 2 * ff), BF),
        pltpu.VMEM((ff, width), BF),
        pltpu.VMEM((length, width), F32),
        pltpu.VMEM((length, width), F32),
        pltpu.VMEM((length, ff), BF),
        pltpu.VMEM((length, ff), BF),
        pltpu.VMEM((length, width), BF),
        pltpu.VMEM((length, 2 * ff), BF),
        pltpu.VMEM((length, width), F32),
        pltpu.VMEM((length, width), F32),
        pltpu.VMEM(small, F32),
        pltpu.SemaphoreType.DMA((32,)),
        pltpu.SemaphoreType.DMA((4,)),
    ]


def mlp_backward_call(index, slot, mix, spots, target, vec, turn, weights, reads, stacks, ff):
    length, width = target.shape
    scratch = mlp_backward_scratch(length, width, ff, stacks[-1].shape[1:])
    return call(
        mlp_backward,
        "mlp_backward",
        [index, slot, mix],
        spots,
        [target, vec, turn],
        weights,
        reads,
        stacks,
        jax.ShapeDtypeStruct((length, width), F32),
        scratch,
        40,
        3,
    )


def column_sum(v):
    return jnp.sum(v, axis=0, keepdims=True)


def mix_backward(
    widths, scalars, spots, ordinary, weights, reads, stacks, d_input_ref, scratch
):
    ci, mi, qw, kw, heads = widths
    index_ref, slot_ref = scalars
    base = 4 * index_ref[0]
    d_hidden_ref, vec_ref, cos_ref, sin_ref, _ = ordinary
    w_first, w_conv, w_gate, w_out = weights
    s_conv, s_z, s_gate, s_qkv, s_step, s_probs, s_y, s_x = reads
    (win, wout, conv_raw, z, gate_raw, qkv, step_raw, probs, y, x_low, d_branch, d_proj, d_mixed,
     d_ssm, d_z, d_normed, run_wide, run_row, step_two, bend_two, tops, d_tops, run_acc, step_acc,
     small, in_sem, out_sem) = scratch
    s_dbranch, s_dfirst, s_dconv, s_dgate, s_dinput, s_small = stacks
    slot = slot_ref[base]
    g0, q0 = ci, ci + mi
    s0 = q0 + qw + 2 * kw
    total = win.shape[1]
    tail = total - q0
    length, width = d_hidden_ref.shape
    wait = start_all(
        [
            out_pieces(w_out, spots, wout, mi),
            [(s_probs.at[slot], probs), (s_qkv.at[slot], qkv)],
            [(s_step.at[slot], step_raw), (s_gate.at[slot], gate_raw), (s_y.at[slot], y)],
            [(s_z.at[slot], z)],
            [(s_conv.at[slot], conv_raw)],
            row_pieces(w_first, spots, win, [(slice(0, tail), slice(q0, total))])
            + row_pieces(w_conv, spots, win, [(slice(0, ci), slice(0, ci))])
            + row_pieces(w_gate, spots, win, [(slice(0, mi), slice(g0, q0))]),
            [(s_x.at[slot], x_low)],
        ],
        in_sem,
    )
    save, finish = saver(slot, slot_ref[base + 1] > 0, out_sem)
    yield
    small[...] = jnp.zeros_like(small)
    d_branch[...] = d_hidden_ref[...].astype(BF)
    save(d_branch, s_dbranch)
    wait(0)
    for t in range(qw // TILE):
        rows = slice(mi + t * TILE, mi + (t + 1) * TILE)
        d_mixed[:, t * TILE : (t + 1) * TILE] = dot_nt(d_branch[...], wout[rows, :]).astype(BF)

    lane_first = jnp.bitwise_and(iota((length, HALF), 1), HD - 1) < HD // 2
    half_low = iota((length, HALF), 1) < HD
    cosine, sine = cos_ref[...], -sin_ref[...]
    wait(1)
    keys, values = qkv[:, qw : qw + kw], qkv[:, qw + kw : qw + 2 * kw]
    keys_far, values_far = pltpu.roll(keys.astype(F32), HD, 1).astype(BF), pltpu.roll(
        values.astype(F32), HD, 1
    ).astype(BF)
    pairs = qw // HALF
    groups = kw // HD
    scale = HD ** (-0.5)
    d_keys = [jnp.zeros((length, HALF), F32) for _ in range(groups)]
    d_values = [jnp.zeros((length, HALF), F32) for _ in range(groups)]
    for pair in range(pairs):
        group = pair // (pairs // groups)
        keep = half_low if group == 0 else jnp.logical_not(half_low)
        keys_two = jnp.where(keep, keys, keys_far)
        values_two = jnp.where(keep, values, values_far)
        cols = slice(pair * HALF, (pair + 1) * HALF)
        query, d_out = qkv[:, cols], d_mixed[:, cols]
        results = []
        for side in range(2):
            own = half_low if side == 0 else jnp.logical_not(half_low)
            q = jnp.where(own, query, jnp.zeros_like(query))
            d_o = jnp.where(own, d_out, jnp.zeros_like(d_out))
            at = (2 * pair + side) * length
            weights = probs[at : at + length, :]
            wide = weights.astype(F32)
            d_weights = dot_nt(d_o, values_two)
            inner = wide * d_weights
            d_scores = (inner - wide * jnp.sum(inner, axis=-1, keepdims=True)).astype(BF)
            results.append(dot(d_scores, keys_two))
            d_keys[group] = d_keys[group] + dot_tn(d_scores, q)
            d_values[group] = d_values[group] + dot_tn(weights, d_o)
        d_q = jnp.where(half_low, results[0], results[1]) * scale
        d_proj[:, q0 + pair * HALF : q0 + (pair + 1) * HALF] = rope(
            d_q, cosine, sine, lane_first
        ).astype(BF)
    folded = [v + pltpu.roll(v, HD, 1) for v in d_keys]
    d_k = jnp.where(half_low, folded[0], folded[1]) * scale
    d_proj[:, q0 + qw : q0 + qw + kw] = rope(d_k, cosine, sine, lane_first).astype(BF)
    folded = [v + pltpu.roll(v, HD, 1) for v in d_values]
    d_proj[:, q0 + qw + kw : s0] = jnp.where(half_low, folded[0], folded[1]).astype(BF)

    wait(2)

    def norm_tile(t, sums):
        cols = lanes(t)
        d_s = dot_nt(d_branch[...], wout[cols, :])
        d_ssm[:, cols] = d_s
        g = gate_raw[:, cols].astype(F32)
        gated = y[:, cols].astype(F32) * (g * sigmoid(g))
        d_n = d_s * vec_ref[V_GS : V_GS + 1, cols]
        return (
            sums[0] + jnp.sum(gated * gated, axis=-1, keepdims=True),
            sums[1] + jnp.sum(gated * d_n, axis=-1, keepdims=True),
        )

    zero_col = jnp.zeros((length, 1), F32)
    squares, along = lax.fori_loop(0, mi // TILE, norm_tile, (zero_col, zero_col), unroll=True)
    rate = lax.rsqrt(squares * (1.0 / mi) + EPSILON)
    along = along * (rate * rate) * (1.0 / mi)

    pre, step, change, run, bend = scan_terms(step_raw[...], vec_ref, heads)
    turned = run.T
    run_row[:HALF, :] = turned[:, :HALF]
    run_row[HALF:, :] = turned[:, HALF:]
    broadcast_runs(run, run_wide, heads)
    step_two[...] = both(step)
    bend_two[...] = both(bend)
    wait(3)
    zb = z[:, mi : mi + 2 * HALF].astype(F32)
    sb = sigmoid(zb)
    bc = (zb * sb).astype(BF)
    b_in, c_in = bc[:, :HALF], bc[:, HALF:]
    causal = iota((HALF, HALF), 1) <= iota((HALF, HALF), 0)
    for c in range(2):
        rows = slice(c * HALF, (c + 1) * HALF)
        tops[rows, :] = jnp.where(causal, dot_nt(c_in[rows], b_in[rows]), 0.0)
    cross = dot_nt(c_in[HALF:], b_in[:HALF])
    cross_turned = cross.T.astype(BF)
    cross = cross.astype(BF)
    pair_low = iota((HALF, HALF), 1) < HD
    d_tops[...] = jnp.zeros_like(d_tops)
    run_acc[...] = jnp.zeros_like(run_acc)
    step_acc[...] = jnp.zeros_like(step_acc)

    def mix_tile(t, carry):
        cols = lanes(t)
        g = gate_raw[:, cols].astype(F32)
        s = sigmoid(g)
        swish = g * s
        y_in = y[:, cols].astype(F32)
        gated = y_in * swish
        d_s = d_ssm[:, cols]
        small[V_GS : V_GS + 1, cols] = column_sum(d_s * gated * rate)
        d_gated = rate * (d_s * vec_ref[V_GS : V_GS + 1, cols]) - gated * (along * rate)
        d_proj[:, pl.ds(pl.multiple_of(g0 + t * TILE, TILE), TILE)] = (
            d_gated * y_in * (s + swish - swish * s)
        ).astype(BF)
        d_y = d_gated * swish
        z_in = z[:, cols].astype(F32)
        s = sigmoid(z_in)
        x_in = z_in * s
        slope = s + x_in - x_in * s
        spread = expand_matrix(t)
        steps = dot(step_two[...], spread)
        bends = dot(bend_two[...], spread)
        scaled = (steps * x_in).astype(BF)
        d_low = d_y.astype(BF)
        u = (bends[:HALF] * scaled[:HALF].astype(F32)).astype(BF)
        v = (bends[HALF:] * d_y[HALF:]).astype(BF)
        far = dot(cross, u)
        back = dot(cross_turned, v)
        d_tops[2 * HALF :, :] += dot_nt(v, u)
        mixed_parts, back_parts = [], []
        for p in range(TILE // HALF):
            mixed_block, back_block = [], []
            for c in range(2):
                rows = slice(c * HALF, (c + 1) * HALF)
                xs = scaled[rows, p * HALF : (p + 1) * HALF]
                dy = d_low[rows, p * HALF : (p + 1) * HALF]
                zero = jnp.zeros_like(xs)
                xs_two = [jnp.where(pair_low, xs, zero), jnp.where(pair_low, zero, xs)]
                dy_two = [jnp.where(pair_low, dy, zero), jnp.where(pair_low, zero, dy)]
                weights = []
                d_top = jnp.zeros((HALF, HALF), F32)
                for side in range(2):
                    h = t * (TILE // HD) + 2 * p + side
                    wide = run_wide[rows, lanes(h, HALF)]
                    line = run_row[pl.ds(c * HALF + h, 1), :]
                    decay = jnp.exp(jnp.minimum(wide - line, 0.0))
                    weights.append((decay * tops[rows, :]).astype(BF))
                    d_top = d_top + decay * dot_nt(dy_two[side], xs)
                d_tops[rows, :] += d_top
                mixed_block.append(
                    dot(jnp.concatenate(weights, axis=1), jnp.concatenate(xs_two, axis=0))
                )
                back_block.append(
                    dot_tn(jnp.concatenate(weights, axis=0), jnp.concatenate(dy_two, axis=0))
                )
            mixed_parts.append(jnp.concatenate(mixed_block, axis=0))
            back_parts.append(jnp.concatenate(back_block, axis=0))
        mixed = jnp.concatenate(mixed_parts, axis=1)
        d_scaled = jnp.concatenate(back_parts, axis=1)
        crossing = jnp.concatenate(
            [-(u.astype(F32) * back), v.astype(F32) * far], axis=0
        )
        runs = d_low.astype(F32) * mixed - scaled.astype(F32) * d_scaled + crossing
        d_scaled = d_scaled + jnp.concatenate([bends[:HALF] * back, jnp.zeros_like(back)], axis=0)
        gather = reduce_matrix(t)
        run_acc[...] += sum(dot(part, gather) for part in split2(runs))
        step_acc[...] += sum(dot(part, gather) for part in split2(x_in * d_scaled))
        small[V_SKIP : V_SKIP + 1, cols] = column_sum(d_y * x_in)
        d_x = steps * d_scaled + vec_ref[V_SKIP : V_SKIP + 1, cols] * d_y
        d_z[:, cols] = d_x * slope
        return carry

    lax.fori_loop(0, mi // TILE, mix_tile, 0, unroll=True)
    d_top = [
        jnp.where(causal, d_tops[c * HALF : (c + 1) * HALF, :], 0.0).astype(BF) for c in range(2)
    ]
    d_cross = d_tops[2 * HALF :, :].astype(BF)
    d_c = jnp.concatenate(
        [dot(d_top[0], b_in[:HALF]), dot(d_cross, b_in[:HALF]) + dot(d_top[1], b_in[HALF:])], axis=0
    )
    d_b = jnp.concatenate(
        [dot_tn(d_top[0], c_in[:HALF]) + dot_tn(d_cross, c_in[HALF:]), dot_tn(d_top[1], c_in[HALF:])],
        axis=0,
    )
    xb = zb * sb
    d_z[:, mi : mi + 2 * HALF] = jnp.concatenate([d_b, d_c], axis=1) * (sb + xb - xb * sb)
    upper = jnp.where(
        iota((length, length), 0) <= iota((length, length), 1), 1.0, 0.0
    ).astype(BF)
    d_change = sum(dot(upper, part) for part in split3(run_acc[...]))
    d_pre = (step_acc[...] + d_change * vec_ref[V_DECAY : V_DECAY + 1, :HALF]) * sigmoid(pre)
    d_pre = jnp.where(iota(d_pre.shape, 1) < heads, d_pre, 0.0)
    d_proj[:, s0:total] = d_pre.astype(BF)
    small[V_SBIAS : V_SBIAS + 1, :HALF] = column_sum(d_pre)
    small[V_DECAY : V_DECAY + 1, :HALF] = column_sum(d_change * change)

    wait(4)
    row = iota((length, TILE), 0)

    def conv_tile(t, carry):
        cols = lanes(t)
        d = d_z[:, cols]
        raw = conv_raw[:, cols].astype(F32)
        small[V_CBIAS : V_CBIAS + 1, cols] = column_sum(d)
        small[3:4, cols] = column_sum(d * raw)
        out = d * vec_ref[3:4, cols]
        for ahead in range(1, 4):
            moved = jnp.where(row < length - ahead, pltpu.roll(d, length - ahead, 0), 0.0)
            small[3 - ahead : 4 - ahead, cols] = column_sum(moved * raw)
            out = out + moved * vec_ref[3 - ahead : 4 - ahead, cols]
        d_proj[:, cols] = out.astype(BF)
        return carry

    lax.fori_loop(0, ci // TILE, conv_tile, 0, unroll=True)
    save(d_proj.at[:, q0:], s_dfirst)
    save(d_proj.at[:, :ci], s_dconv)
    save(d_proj.at[:, g0:q0], s_dgate)

    wait(5)

    def back_tile(t, carry):
        rows = lanes(t)
        d_normed[:, rows] = dot_nt(d_proj[...], win[rows, :])
        return carry

    lax.fori_loop(0, width // TILE, back_tile, 0, unroll=True)
    wait(6)
    x = x_low[...].astype(F32)
    rate_one = lax.rsqrt(jnp.mean(x * x, axis=-1, keepdims=True) + EPSILON)
    unit = x * rate_one
    d_n = d_normed[...]
    small[V_G1 : V_G1 + 1, :width] = column_sum(d_n * unit)
    save(small, s_small)
    d_n = d_n * vec_ref[V_G1 : V_G1 + 1, :width]
    d_input_ref[...] = (
        d_hidden_ref[...]
        + rate_one * (d_n - unit * jnp.mean(d_n * unit, axis=-1, keepdims=True))
    ).astype(BF)
    save(d_input_ref, s_dinput, slot_ref[base + 3])
    yield
    finish()


def mixer_backward_scratch(length, width, widths, total, small):
    ci, mi, qw, kw, heads = widths
    return [
        pltpu.VMEM((width, total), BF),
        pltpu.VMEM((mi + qw, width), BF),
        pltpu.VMEM((length, ci), BF),
        pltpu.VMEM((length, ci), BF),
        pltpu.VMEM((length, mi), BF),
        pltpu.VMEM((length, qw + 2 * kw), BF),
        pltpu.VMEM((length, HALF), F32),
        pltpu.VMEM((qw // HD * length, length), BF),
        pltpu.VMEM((length, mi), BF),
        pltpu.VMEM((length, width), BF),
        pltpu.VMEM((length, width), BF),
        pltpu.VMEM((length, total), BF),
        pltpu.VMEM((length, qw), BF),
        pltpu.VMEM((length, mi), F32),
        pltpu.VMEM((length, ci), F32),
        pltpu.VMEM((length, width), F32),
        pltpu.VMEM((length, heads * HALF), F32),
        pltpu.VMEM((length, HALF), F32),
        pltpu.VMEM((length, 2 * HALF), BF),
        pltpu.VMEM((length, 2 * HALF), BF),
        pltpu.VMEM((2 * HALF, HALF), F32),
        pltpu.VMEM((3 * HALF, HALF), F32),
        pltpu.VMEM((length, HALF), F32),
        pltpu.VMEM((length, HALF), F32),
        pltpu.VMEM(small, F32),
        pltpu.SemaphoreType.DMA((48,)),
        pltpu.SemaphoreType.DMA((6,)),
    ]


def mixer_backward_call(
    index, slot, spots, d_hidden, vec, cosine, sine, turn, weights, reads, stacks, widths, total
):
    ci, mi, qw, kw, heads = widths
    length, width = d_hidden.shape
    scratch = mixer_backward_scratch(length, width, widths, total, stacks[-1].shape[1:])
    return call(
        functools.partial(mix_backward, widths),
        "mixer_backward",
        [index, slot],
        spots,
        [d_hidden, vec, cosine, sine, turn],
        weights,
        reads,
        stacks,
        jax.ShapeDtypeStruct((length, width), BF),
        scratch,
        48,
        250,
    )


def weight_kernel(core_ref, away_ref, stay_ref, right_ref, out_away, out_stay, turned):
    rows = away_ref.shape[2]
    tokens = away_ref.shape[0] * away_ref.shape[1]

    @pl.when(pl.program_id(1) == 0)
    def _():
        turned[:rows, :] = away_ref[...].reshape(tokens, rows).T
        turned[rows:, :] = stay_ref[...].reshape(tokens, rows).T

    right = right_ref[...].reshape(tokens, right_ref.shape[2])
    out_away[0] = dot(turned[:rows, :], right).astype(BF)
    out_stay[0] = dot(turned[rows:, :], right).astype(BF)


def weight_grad_halves(core, left, right):
    count, length, depth = left.shape
    columns = right.shape[2]
    rows = depth // 4
    tile = max(t for t in (896, 768, 512, 256, 128) if columns % t == 0)
    grid = pltpu.PrefetchScalarGridSpec(
        num_scalar_prefetch=1,
        grid=(2, columns // tile),
        in_specs=[
            pl.BlockSpec((count, length, rows), lambda c, n, core: (0, 0, 2 * c + 1 - core[0])),
            pl.BlockSpec((count, length, rows), lambda c, n, core: (0, 0, 2 * c + core[0])),
            pl.BlockSpec((count, length, tile), lambda c, n, core: (0, 0, n)),
        ],
        out_specs=[pl.BlockSpec((1, rows, tile), lambda c, n, core: (c, 0, n))] * 2,
        scratch_shapes=[pltpu.VMEM((2 * rows, count * length), BF)],
    )
    shape = jax.ShapeDtypeStruct((2, rows, columns), BF)
    return pl.pallas_call(
        weight_kernel,
        out_shape=[shape, shape],
        grid_spec=grid,
        compiler_params=pltpu.CompilerParams(vmem_limit_bytes=40 * 1024 * 1024),
        cost_estimate=pl.CostEstimate(
            flops=100000000, bytes_accessed=1000000, transcendentals=0
        ),
        name="weight_gradient",
    )(core, left, left, right)


def layer_forward_call(
    index, slot, spots, x, vec, cosine, sine, turn, weights, stacks, widths, total, ff
):
    length, width = x.shape
    first = mixer_forward_scratch(length, width, widths, total)
    second = mlp_forward_scratch(length, width, ff)
    n = 12

    def body(scalars, spots, ordinary, weights, reads, stacks, low_ref, scratch):
        hidden = scratch[-1]
        one = mix_forward(
            widths, scalars, spots, ordinary, weights[:4], [], stacks[:n], hidden,
            scratch[: len(first)],
        )
        two = mlp_forward(
            scalars, spots, [hidden, ordinary[1]], weights[4:], [], stacks[n:], low_ref,
            scratch[len(first) : -1],
        )
        for part in (one, one, two, one, two, one, two):
            next(part, None)
        yield

    return call(
        body,
        "layer_forward",
        [index, slot],
        spots,
        [x, vec, cosine, sine, turn],
        weights,
        [],
        stacks,
        jax.ShapeDtypeStruct((length, width), BF),
        first + second + [pltpu.VMEM((length, width), F32)],
        58,
        200,
    )


def layer_backward_call(
    index, slot, mix, spots, target, vec, cosine, sine, turn, weights, reads, stacks, widths, total, ff
):
    length, width = target.shape
    first = mlp_backward_scratch(length, width, ff, stacks[3].shape[1:])
    second = mixer_backward_scratch(length, width, widths, total, stacks[-1].shape[1:])
    n = 4

    def body(scalars, spots, ordinary, weights, reads, stacks, d_input_ref, scratch):
        d_hidden = scratch[-1]
        target_ref, vec_ref, cos_ref, sin_ref, turn_ref = ordinary
        one = mlp_backward(
            scalars, spots, [target_ref, vec_ref, turn_ref], weights[4:], reads[:4],
            stacks[:n], d_hidden, scratch[: len(first)],
        )
        two = mix_backward(
            widths, scalars[:2], spots, [d_hidden, vec_ref, cos_ref, sin_ref, turn_ref],
            weights[:4], reads[4:], stacks[n:], d_input_ref, scratch[len(first) : -1],
        )
        for part in (one, one, two, one, two, one, two):
            next(part, None)
        yield

    return call(
        body,
        "layer_backward",
        [index, slot, mix],
        spots,
        [target, vec, cosine, sine, turn],
        weights,
        reads,
        stacks,
        jax.ShapeDtypeStruct((length, width), BF),
        first + second + [pltpu.VMEM((length, width), F32)],
        60,
        250,
    )


def rope_tables(length):
    halves = HD // 2
    inverse = jnp.exp(jnp.arange(halves, dtype=F32) * (-2.0 * math.log(ROPE_BASE) / HD))
    angles = jnp.arange(length, dtype=F32)[:, None] * inverse[None, :]
    cosine, sine = jnp.cos(angles), jnp.sin(angles)
    return (
        jnp.concatenate([cosine] * 4, axis=1),
        jnp.concatenate([-sine, sine, -sine, sine], axis=1),
    )


def swap(block, axis, bit):
    return lax.ppermute(block, axis, [(i, i ^ bit) for i in range(lax.axis_size(axis))])


def after(value, *others):
    if not others:
        return value
    return lax.optimization_barrier((value,) + others)[0]


def corner(made):
    part = made.reshape(-1, made.shape[-1])[:8, :HALF].astype(BF)
    return jnp.dot(part, jnp.ones((HALF, HALF), BF), preferred_element_type=F32)


def quick_links():
    return lax.axis_size("fsdp") == 4 and lax.axis_size("rep") == 4


def gather_halves(shard, axis, before_y=(), before_z=()):
    parity = lax.axis_index("rep") % 2
    half = shard.shape[axis] // 2
    mine = lax.dynamic_slice_in_dim(shard, parity * half, half, axis)
    near = swap(shard, "fsdp", 1)
    far_one = swap(after(mine, *before_y), "fsdp", 2)
    far_two = swap(after(far_one, *before_z), "rep", 1)
    return [shard, near, far_one, far_two, swap(far_one, "fsdp", 1), swap(far_two, "fsdp", 1)]


def gather_wholes(shard, *before_y):
    far = swap(after(shard, *before_y), "fsdp", 2)
    return [shard, swap(shard, "fsdp", 1), far, swap(far, "fsdp", 1)]


def plus(a, b):
    return (a.astype(F32) + b.astype(F32)).astype(BF)


def weight_grad(left, right):
    return lax.dot_general(
        left, right, (((0, 1), (0, 1)), ((), ())), preferred_element_type=F32
    ).astype(BF)


class Reduction:
    def __init__(self, left, right, riders=None):
        self.left, self.right, self.riders = left, right, riders

    def begin(self, order):
        left, right = order(self.left, self.right)
        core = lax.axis_index("fsdp") % 2
        away, stay = weight_grad_halves(core.astype(jnp.int32)[None], left, right)
        if self.riders is not None:
            blocks, column = self.riders
            away, stay = (
                lax.dynamic_update_slice(
                    grad, lax.dynamic_index_in_dim(blocks, i, 1, keepdims=False), (0, 0, column)
                )
                for grad, i in ((away, 1 - core), (stay, core))
            )
        self.stay = stay
        self.moved = swap(away, "fsdp", 1)
        return stay

    def chips(self, order):
        chip = lax.axis_index("fsdp") // 2
        self.kept = order(self.stay, self.moved)

        def part(i):
            return [lax.dynamic_index_in_dim(v, i, 0, keepdims=False) for v in self.kept]

        away = plus(*part(1 - chip))
        self.moved = swap(away, "fsdp", 2)
        return away

    def line_in(self, order):
        chip = lax.axis_index("fsdp") // 2
        *kept, moved = order(*self.kept, self.moved)
        one, two = (lax.dynamic_index_in_dim(v, chip, 0, keepdims=False) for v in kept)
        self.stay = (one.astype(F32) + two.astype(F32) + moved.astype(F32)).astype(BF)
        self.moved = lax.ppermute(self.stay, "rep", [(0, 1), (3, 2)])
        return self.stay

    def middle(self, order):
        stay, moved = order(self.stay, self.moved)
        self.stay = plus(stay, moved)
        self.moved = lax.ppermute(self.stay, "rep", [(1, 2), (2, 1)])
        return self.stay

    def line_out(self, order):
        stay, moved = order(self.stay, self.moved)
        self.stay = plus(stay, moved)
        self.moved = lax.ppermute(self.stay, "rep", [(1, 0), (2, 3)])
        return self.stay

    def finish(self, order):
        stay, moved = order(self.stay, self.moved)
        rank = lax.axis_index("rep")
        inner = jnp.logical_or(rank == 1, rank == 2)
        self.result = jnp.where(inner, stay, moved).astype(F32)
        return self.result


def body(
    inputs,
    teacher,
    lengths,
    order,
    loss_scale,
    norm_gain1,
    w_query,
    w_key,
    w_value,
    w_attn_out,
    w_ssm_gate,
    w_conv_in,
    w_step,
    conv_kernel,
    conv_bias,
    step_bias,
    decay_log,
    skip_gain,
    ssm_norm_gain,
    w_ssm_out,
    norm_gain2,
    w_gate,
    w_up,
    w_down,
):
    quick = quick_links()
    n_rep = lax.axis_size("rep")
    n_fsdp = lax.axis_size("fsdp")
    rank = lax.axis_index("rep")
    fsdp = lax.axis_index("fsdp")
    section = lax.axis_index("section")
    first = section == 0
    device = fsdp * n_rep + rank
    count, length, width = inputs.shape
    ci, mi, qw, kw = (w.shape[2] for w in (w_conv_in, w_ssm_gate, w_query, w_key))
    heads = w_step.shape[2]
    ff = w_up.shape[2]
    widths = (ci, mi, qw, kw, heads)
    taps = conv_kernel.shape[1]
    rows = width // n_fsdp
    tail = qw + 2 * kw + HALF
    total = ci + mi + tail

    turns = jnp.arange(count, dtype=jnp.int32)
    numbers = jnp.arange(order.shape[0], dtype=jnp.int32)
    mine = device * count + turns
    sources = jnp.sum(jnp.where(order[None, :] == mine[:, None], numbers[None, :], 0), axis=1)
    target = lax.dynamic_slice_in_dim(order, device * count, count) // count % n_rep
    anchor = sources // count % n_rep

    def inverse(key):
        return jnp.sum(jnp.where((key ^ rank)[None, :] == turns[:, None], turns[None, :], 0), axis=1)

    send_at, keep_at = inverse(target), inverse(anchor)
    own_lengths = jnp.take(lengths, jnp.take(sources, keep_at))
    outgoing = [
        jnp.where(
            first,
            lax.dynamic_index_in_dim(inputs, send_at[j], 0, keepdims=False),
            lax.dynamic_index_in_dim(teacher, send_at[j], 0, keepdims=False),
        )
        for j in range(count)
    ]
    dealt = [outgoing[0]]

    def deal(j, *earlier):
        dealt.append(swap(after(outgoing[j], *earlier), "rep", j))

    for j in range(1, count - 1):
        deal(j)

    def columns(flat):
        wide = -(-flat.size // rows)
        return jnp.pad(flat, (0, wide * rows - flat.size)).reshape(rows, wide)

    convs = jnp.concatenate([conv_kernel[0], conv_bias], axis=0)
    riders = jnp.concatenate(
        [
            norm_gain1[0][:, None],
            norm_gain2[0][:, None],
            columns(convs.reshape(-1)),
            columns(ssm_norm_gain[0]),
        ],
        axis=1,
    )
    used = riders.shape[1]
    wide = -(-convs.size // rows)
    shard_first = jnp.concatenate(
        [w_query[0], w_key[0], w_value[0], w_step[0], riders]
        + [jnp.zeros((rows, HALF - heads - used), BF)],
        axis=1,
    )
    at = qw + 2 * kw + heads
    parity = rank % 2
    if quick:
        g_gate = gather_halves(w_ssm_gate[0], 0, (), dealt[1:2])
        g_conv = gather_halves(w_conv_in[0], 0, (), dealt[2:3])
        g_first = gather_halves(shard_first, 0, g_gate[2:3], g_gate[3:4])
        shard_out = jnp.concatenate([w_ssm_out[0], w_attn_out[0]], axis=0)
        g_out = gather_halves(shard_out, 1, g_conv[2:3], g_conv[3:4])
        g_g = gather_halves(w_gate[0], 0, g_first[2:3], g_first[3:4])
        g_u = gather_wholes(w_up[0], g_out[2], g_g[2])
        spots = [2 * fsdp, 2 * (fsdp ^ 1)]
        spots += [2 * (fsdp ^ k) + b for k in (2, 3) for b in (parity, 1 - parity)]
        spots = jnp.stack(spots).astype(jnp.int32)
        cut = [piece[:, at : at + used] for piece in g_first]
        swapped = [jnp.where(parity == 0, cut[i], cut[i + 1]) for i in (2, 4)]
        swapped2 = [jnp.where(parity == 0, cut[i + 1], cut[i]) for i in (2, 4)]
        blocks = jnp.stack(
            [cut[0], cut[1]]
            + [jnp.concatenate([a, b], axis=0) for a, b in zip(swapped, swapped2)]
        )
        ridden = jnp.take(blocks, jnp.arange(4, dtype=jnp.int32) ^ fsdp, axis=0)
    else:

        def whole(shard):
            return lax.all_gather(shard, "fsdp", axis=0, tiled=True)

        g_first, g_conv, g_gate, g_g, g_u, g_down = (
            [whole(w)]
            for w in (shard_first, w_conv_in[0], w_ssm_gate[0], w_gate[0], w_up[0], w_down[0])
        )
        g_out = [jnp.concatenate([whole(w_ssm_out[0]), whole(w_attn_out[0])], axis=0)]
        spots = jnp.zeros((1,), jnp.int32)
        ridden = g_first[0][:, at : at + used].reshape(n_fsdp, rows, used)
    mixer_weights = [g_first, g_conv, g_gate, g_out]
    mlp_weights = None if quick else [g_g, g_u, g_down]

    conv_all = ridden[:, :, 2 : 2 + wide].reshape(n_fsdp, -1)[:, : (taps + 1) * ci // n_fsdp]
    conv_all = conv_all.reshape(n_fsdp, taps + 1, ci // n_fsdp).transpose(1, 0, 2)
    ssm_gain = ridden[:, :, 2 + wide :].reshape(n_fsdp, -1)[:, : mi // n_fsdp].reshape(1, mi)

    def table_row(v):
        v = v.astype(F32)
        return jnp.pad(v, ((0, 0), (0, ci - v.shape[1])))

    vec = jnp.concatenate(
        [
            table_row(v)
            for v in (
                conv_all.reshape(taps + 1, ci),
                ssm_gain,
                jnp.repeat(skip_gain, HD, axis=1),
                ridden[:, :, 0].reshape(1, width),
                ridden[:, :, 1].reshape(1, width),
                step_bias,
                -jnp.exp(decay_log),
                jnp.zeros((16 - taps - 7, 1), F32),
            )
        ],
        axis=0,
    )
    cosine, sine = rope_tables(length)

    valid_count = jnp.sum(lengths).astype(F32)
    factor = loss_scale / (valid_count * width)

    skew = 2
    steps = count + skew
    ticks = jnp.arange(steps, dtype=jnp.int32)
    raw = jnp.concatenate([ticks - skew * section, count - 1 - ticks + skew * (1 - section)])
    inside = jnp.logical_and(raw >= 0, raw < count).astype(jnp.int32)
    slots = jnp.clip(raw, 0, count - 1)
    plan = [slots, inside, jnp.take(own_lengths, slots), jnp.take(keep_at, slots)]
    plan = jnp.stack(plan, axis=1).reshape(-1)
    mix = jnp.stack([jnp.where(first, 1.0, 0.0), 2.0 * factor])

    def stack(*shape, kind=BF):
        return jax.ShapeDtypeStruct((count,) + shape, kind)

    mix_stacks = [
        stack(length, width),
        stack(length, ci),
        stack(length, ci),
        stack(length, mi),
        stack(length, qw + 2 * kw),
        stack(length, HALF, kind=F32),
        stack(qw // HD * length, length),
        stack(length, mi),
        stack(length, qw),
        stack(length, mi),
        stack(length, width, kind=F32),
        stack(length, width),
    ]
    mlp_stacks = [
        stack(length, width),
        stack(length, ff),
        stack(length, ff),
        stack(length, ff),
        stack(length, width, kind=F32),
        stack(length, width),
    ]

    token = []

    def chained(*values):
        if not quick or not token:
            return values
        return lax.optimization_barrier(values + tuple(token))[: len(values)]

    def chain(made):
        token[:] = [made]

    received, hiddens = [], []

    def number(i):
        return jnp.full((1,), i, jnp.int32)

    def mixer_tick(tick, turn, mix_stacks):
        mix_stacks, hidden = mixer_forward_call(
            number(tick),
            plan,
            spots,
            dealt[tick],
            vec,
            cosine,
            sine,
            corner(turn),
            mixer_weights,
            mix_stacks,
            widths,
            total,
        )
        chain(hidden)
        hiddens.append(hidden)
        return mix_stacks

    def mlp_tick(tick, mlp_stacks):
        (hidden,) = chained(hiddens[tick])
        mlp_stacks, low = mlp_forward_call(
            number(tick), plan, spots, hidden, vec, mlp_weights, mlp_stacks, ff
        )
        return mlp_stacks, low

    def layer_tick(tick, turn, stacks):
        if tick < count:
            one, two = chained(dealt[tick], received[tick - skew])
            seq_in = jnp.where(first, one, two)
        else:
            seq_in = received[tick - skew]
        return layer_forward_call(
            number(tick),
            plan,
            spots,
            seq_in,
            vec,
            cosine,
            sine,
            corner(turn),
            mixer_weights + mlp_weights,
            stacks,
            widths,
            total,
            ff,
        )

    mix_stacks = mixer_tick(0, dealt[0], mix_stacks)
    if quick:
        mlp_weights = [g_g, g_u, gather_wholes(w_down[0], hiddens[0])]
    deal(count - 1, hiddens[0])
    mix_stacks = mixer_tick(1, hiddens[0], mix_stacks)
    for tick in range(steps):
        if tick < skew:
            mlp_stacks, low = mlp_tick(tick, mlp_stacks)
        else:
            stacks, low = layer_tick(tick, low, mix_stacks + mlp_stacks)
            mix_stacks, mlp_stacks = stacks[: len(mix_stacks)], stacks[len(mix_stacks) :]
        chain(low)
        if tick < count:
            received.append(lax.ppermute(low, "section", [(0, 1)]))

    (s_normed, s_conv, s_z, s_gate, s_qkv, s_step, s_probs, s_ssm, s_mixed, s_y, s_hidden,
     s_x) = mix_stacks
    s_normed2, s_g, s_u, s_act, s_final, s_low = mlp_stacks
    mlp_grads = [
        stack(length, width),
        stack(length, ff),
        stack(length, ff),
        stack(8, width, kind=F32),
    ]
    mix_grads = [
        stack(length, width),
        stack(length, tail),
        stack(length, ci),
        stack(length, mi),
        stack(length, width),
        stack(16, ci, kind=F32),
    ]
    incoming, returned = [], [None] * count

    hiddens = []

    def mlp_turn(turn, mlp_grads):
        (seed,) = chained(incoming[turn - skew])
        return mlp_backward_call(
            number(steps + turn),
            plan,
            mix,
            spots,
            seed,
            vec,
            corner(hiddens[-1]) if turn > count else jnp.zeros((8, HALF), F32),
            mlp_weights,
            reads,
            mlp_grads,
            ff,
        )

    def mixer_turn(turn, d_hidden, before, mix_grads):
        mix_grads, d_input = mixer_backward_call(
            number(steps + turn),
            plan,
            spots,
            d_hidden,
            vec,
            cosine,
            sine,
            corner(before),
            mixer_weights,
            mix_reads,
            mix_grads,
            widths,
            total,
        )
        send_back(turn, d_input)
        return mix_grads, d_input

    def send_back(turn, d_input):
        if turn < count:
            incoming.append(lax.ppermute(d_input, "section", [(1, 0)]))
        if turn >= skew:
            j = count - 1 - turn + skew
            back = lax.dynamic_index_in_dim(after(s_low, d_input), keep_at[j], 0, keepdims=False)
            back = jnp.where(first, d_input, back)
            returned[j] = swap(back, "rep", j) if j else back

    reads = [s_final, s_hidden, s_g, s_u]
    mix_reads = [s_conv, s_z, s_gate, s_qkv, s_step, s_probs, s_y, s_x]
    d_input = low
    for turn in range(count):
        if turn < skew:
            (seed,) = chained(dealt[count - 1 - turn])
        else:
            one, two = chained(incoming[turn - skew], dealt[count - 1 - turn])
            seed = jnp.where(first, one, two)
        grads, d_input = layer_backward_call(
            number(steps + turn),
            plan,
            mix,
            spots,
            seed,
            vec,
            cosine,
            sine,
            corner(d_input),
            mixer_weights + mlp_weights,
            reads + mix_reads,
            mlp_grads + mix_grads,
            widths,
            total,
            ff,
        )
        mlp_grads, mix_grads = grads[: len(mlp_grads)], grads[len(mlp_grads) :]
        chain(d_input)
        send_back(turn, d_input)

    for turn in range(count, steps):
        mlp_grads, d_hidden = mlp_turn(turn, mlp_grads)
        chain(d_hidden)
        hiddens.append(d_hidden)
    s_dmlp, s_dg, s_du, small_mlp = mlp_grads
    early = [(s_normed2, s_dg), (s_normed2, s_du), (s_act, s_dmlp)]
    chunks = [Reduction(*pair) for pair in early]

    def stages(*words):
        for word in words:
            chain(getattr(chunks[int(word[1])], names[word[0]])(chained))

    names = dict(W="begin", A="chips", L="line_in", M="middle", O="line_out", F="finish")
    if quick:
        stages("W0", "W1", "W2", "A0", "A1", "A2")
    for turn in range(count, steps):
        d_hidden = hiddens[turn - count]
        before = d_hidden
        if quick:
            before = after(token[0], *returned[2:]) if turn > count else token[0]
        mix_grads, d_input = mixer_turn(turn, d_hidden, before, mix_grads)
        if quick:
            chain(d_input)
            if turn == count:
                stages("L0")
    s_dbranch, s_dfirst, s_dconv, s_dgate, s_dinput, small_mix = mix_grads
    late = [
        (s_normed, s_dconv),
        (s_normed, s_dgate),
        (s_ssm, s_dbranch),
        (s_normed, s_dfirst),
        (s_mixed, s_dbranch),
    ]

    mix_sum = jnp.sum(small_mix, axis=0)
    mlp_sum = jnp.sum(small_mlp, axis=0)
    singles = jnp.concatenate(
        [
            mix_sum[V_SBIAS, :heads],
            mix_sum[V_DECAY, :heads],
            jnp.sum(mix_sum[V_SKIP, :mi].reshape(heads, HD), axis=1),
            jnp.sum(mlp_sum[1])[None],
        ]
    )

    def share(v):
        return v.reshape(v.shape[0], n_fsdp, -1).transpose(1, 0, 2).reshape(n_fsdp, -1)

    shares = [
        share(mix_sum[: taps + 1]),
        share(mix_sum[V_GS : V_GS + 1, :mi]),
        share(mix_sum[V_G1 : V_G1 + 1, :width]),
        share(mlp_sum[:1]),
        jnp.broadcast_to(singles[None], (n_fsdp, singles.size)),
    ]
    cuts = [v.shape[1] for v in shares]
    flat = jnp.concatenate(shares, axis=1)

    if quick:
        spare = -(-flat.shape[1] // rows)
        flat = jnp.pad(flat, ((0, 0), (0, spare * rows - flat.shape[1])))
        riders = flat.astype(BF).reshape(2, 2, rows, spare)
        column = tail - HALF + heads
        chunks += [Reduction(*pair) for pair in late]
        chunks[6].riders = (riders, column)
        stages("L1", "M0", "W3", "W4", "W5", "W6", "W7")
        stages("A3", "L2", "M1", "O0")
        stages("A4", "L3", "M2", "O1", "F0")
        token.append(returned[1])
        stages("A5", "L4", "M3", "O2", "F1")
        stages("A6", "L5", "M4", "O3", "F2")
        stages("A7", "L6", "M5", "O4", "F3")
        stages("L7", "M6", "O5", "F4", "M7", "O6", "F5", "O7", "F6", "F7")
        reduced = [chunk.result for chunk in chunks]
        flat = reduced[6][:, column : column + spare].reshape(-1)
        ends = chained(*returned, s_dinput, s_low)
        returned, s_dinput, s_low = ends[:count], ends[-2], ends[-1]
    else:

        def reduce_all(pair):
            grad = weight_grad(*pair)
            own = lax.psum_scatter(grad, "fsdp", scatter_dimension=0, tiled=True)
            return lax.psum(own, "rep").astype(F32)

        reduced = [reduce_all(pair) for pair in early + late]
        flat = lax.psum(lax.psum_scatter(flat, "fsdp", tiled=True), "rep").reshape(-1)
    grad_gate, grad_up, grad_down, grad_conv, grad_sgate, grad_ssm_out, grad_first, grad_attn = reduced

    parts, begin = [], 0
    for cut in cuts[:-1] + [heads] * 3 + [1]:
        parts.append(flat[begin : begin + cut])
        begin += cut
    convs = parts[0].reshape(taps + 1, -1)
    loss = jnp.where(first, lax.ppermute(parts[-1], "section", [(1, 0)]), parts[-1])[0]

    restored = jnp.zeros((count, length, width), BF)
    for j in range(count):
        restored = lax.dynamic_update_index_in_dim(restored, returned[j], send_at[j], 0)
    activations = jnp.where(first, s_low, restored)[None]
    gradients = jnp.where(first, restored, s_dinput)[None]
    s0 = qw + 2 * kw
    return (
        activations,
        gradients,
        loss / (valid_count * width),
        parts[2][None],
        grad_first[None, :, :qw],
        grad_first[None, :, qw : qw + kw],
        grad_first[None, :, qw + kw : s0],
        grad_attn[None],
        grad_sgate[None],
        grad_conv[None],
        grad_first[None, :, s0 : s0 + heads],
        convs[None, :taps],
        convs[None, taps],
        parts[4][None],
        parts[5][None],
        parts[6][None],
        parts[1][None],
        grad_ssm_out[None],
        parts[3][None],
        grad_gate[None],
        grad_up[None],
        grad_down[None],
    )


def solution(mesh):
    rows3 = P("section", "fsdp", None)
    pair = P("section", "fsdp")
    one = P("section", None)
    data = P(("fsdp", "rep"), None, None)
    taps = P("section", None, "fsdp")
    in_specs = (data, data, P(), P(), P(), pair) + (rows3,) * 7
    in_specs += (taps, pair, one, one, one, pair, rows3, pair, rows3, rows3, rows3)
    placed = P("section", ("fsdp", "rep"), None, None)
    out_specs = (placed, placed, P(), pair) + (rows3,) * 7
    out_specs += (taps, pair, one, one, one, pair, rows3, pair, rows3, rows3, rows3)
    return jax.shard_map(body, mesh=mesh, in_specs=in_specs, out_specs=out_specs, check_vma=False)
```

time: 1270 us -> 823 us (0.65)
  waiting for transfers between devices: 437 us -> 200 us
  local copies, waits for them, and re-layouts: 203 us -> 61.2 us
  blocking collectives: 42.3 us -> 0 us
  matrix products: 37.1 us -> 11.2 us
  Pallas kernels: 375 us -> 354 us
  starting transfers between devices: 75.6 us -> 95 us
    ppermute x41 -> x53, waiting for transfers between devices: 183 us -> 95.7 us  [swap(): lax.ppermute(block, axis, [(i, i ^ bit) for i in range(lax.axis_size(axis...]
    ppermute x19 -> x29, waiting for transfers between devices: 180 us -> 104 us  [the longest x8 72.7 us: line_out(): self.moved = lax.ppermute(self.stay, 'rep', [(1, 0), (2, 3)])]
    psum x1 -> x0, waiting for transfers between devices: 74.7 us -> none  [body(): loss_total, flat = lax.psum((loss_part, flat), ('section', 'fsdp', 'rep'))]
    psum x1 -> x0, blocking collectives: 42.3 us -> none  [body(): loss_total, flat = lax.psum((loss_part, flat), ('section', 'fsdp', 'rep'))]
    unnamed x226 -> x203, local copies, waits for them, and re-layouts: 58 us -> 23.6 us
    dynamic_update_slice x29 -> x6, local copies, waits for them, and re-layouts: 35.6 us -> 5.26 us  [the longest x2 3.9 us: begin(): lax.dynamic_update_slice(grad, lax.dynamic_index_in_dim(blocks, i, 1, kee...]
    ppermute x19 -> x29, starting transfers between devices: 28.9 us -> 57.8 us  [the longest x8 32.7 us: line_in(): self.moved = lax.ppermute(self.stay, 'rep', [(0, 1), (3, 2)])]
    dot_general x4 -> x13, matrix products: 37.1 us -> 11.2 us  [corner(): return jnp.dot(part, jnp.ones((HALF, HALF), BF), preferred_element_type=F32)]
  transfers between devices with their start and end apart: 65 -> 86, of which waited for: 17 -> 22; matrix products, arithmetic and copies ran while one was open for 17% -> 13% of each run, Pallas kernels for 22% -> 34%
where the time goes in v2:
time: 823 us; the launch traced here: 811 us
  Pallas kernels  354 us (43%)
  waiting for transfers between devices  200 us (24%)
  starting transfers between devices  95 us (12%)
  other arithmetic  66.5 us (8%)
  local copies, waits for them, and re-layouts  61.2 us (7%)
  between operations  22.5 us (3%)
  matrix products  11.2 us (1%)
    pallas_call x16, Pallas kernels, call(): pl.pallas_call(kernel, out_shape=[pltpu.HBM(s.shape, s.dtype) for s in st...  306 us
    ppermute x53, waiting for transfers between devices, swap(): lax.ppermute(block, axis, [(i, i ^ bit) for i in range(lax.axis_size(axis...  95.7 us
    ppermute x8, waiting for transfers between devices, line_out(): self.moved = lax.ppermute(self.stay, 'rep', [(1, 0), (2, 3)])  72.7 us
    pallas_call x8, Pallas kernels, weight_grad_halves(): pl.pallas_call(weight_kernel, out_shape=[shape, shape], grid_spec=grid, c...  48.6 us
    ppermute x8, starting transfers between devices, line_in(): self.moved = lax.ppermute(self.stay, 'rep', [(0, 1), (3, 2)])  32.7 us
    ppermute x53, starting transfers between devices, swap(): lax.ppermute(block, axis, [(i, i ^ bit) for i in range(lax.axis_size(axis...  30.3 us
    ppermute x8, waiting for transfers between devices, line_in(): self.moved = lax.ppermute(self.stay, 'rep', [(0, 1), (3, 2)])  25.6 us
    unnamed x203, local copies, waits for them, and re-layouts  23.6 us
  transfers between devices with their start and end apart: 86, of which 22 were waited for; matrix products, arithmetic and copies ran while one was open for 13% of the time, Pallas kernels for 34%

profile of v2, /device:TPU:0, one launch (start us, length us, event | category | flops | bytes accessed | tf_op | source)
XLA Modules:
  0.0 811.0 jit_solution(184591856598415966)
XLA Ops:
  88.8 10.3 %collective-permute-done.19.refs_29_.refs_30_ = bf16[512,512]{1,0:T(8,128)(2,1)} collective-permute-done((bf16[512,512]{1,0:T(8,128)(2,1)}, bf16[512,512]{1,0:T(8,128)(2,1)}, u32[]{:S(2)}, u32[]{:S(2)}) %collective-permute-start.19) | collective-permute-done | bytes 524320 | tf_op jit(solution)/shard_map/ppermute | solution.py:1137
  106.6 15.3 %mixer_forward.2 = (bf16[4,256,1024]{2,1,0:T(8,128)(2,1)}, bf16[4,256,1792]{2,1,0:T(8,128)(2,1)}, bf16[4,256,1792]{2,1,0:T(8,128)(2,1)}, bf16[4,256,1536]{2,1,0:...) custom-call(s32[1]{0:T(128)} %constant.355.clone.1.refs_0_, ...), custom_call_target="tpu_custom_call" | custom-call | flops 20000000000 | bytes 1000000 | tf_op jit(solution)/shard_map/mixer_forward/pallas_call | solution.py:177
  124.4 12.6 %collective-permute-done.25.refs_8_.refs_35_.refs_36_.refs_10_ = bf16[128,2048]{1,0:T(8,128)(2,1)S(1)} collective-permute-done((bf16[128,2048]{1,0:T(8,128)(2,1)}, bf16[128,2048]{1,0:T(8,128)(2,1)S(1)}, u32[]{:S(2)}, u32[]{:S(2)}) %collective-permute-start.25) | collective-permute-done | bytes 524320 | tf_op jit(solution)/shard_map/ppermute | solution.py:1137
  137.5 16.1 %collective-permute-done.32.refs_17_.refs_44_.refs_45_.refs_19_ = bf16[512,1024]{1,0:T(8,128)(2,1)S(1)} collective-permute-done((bf16[512,1024]{1,0:T(8,128)(2,1)S(1)}, bf16[512,1024]{1,0:T(8,128)(2,1)S(1)}, u32[]{:S(2)}, u32[]{:S(2)}) %collective-permute-start.32) | collective-permute-done | bytes 1048608 | tf_op jit(solution)/shard_map/ppermute | solution.py:1137
  153.6 15.1 %mixer_forward.3 = (bf16[4,256,1024]{2,1,0:T(8,128)(2,1)}, bf16[4,256,1792]{2,1,0:T(8,128)(2,1)}, bf16[4,256,1792]{2,1,0:T(8,128)(2,1)}, bf16[4,256,1536]{2,1,0:...) custom-call(s32[1]{0:T(128)} %constant.366.clone.1.refs_0_, ...), custom_call_target="tpu_custom_call", output_to_operand_aliasing={{0}: (32, {}), {1}: (33, {}), {2}: (34, {}), {3}: (35, {}),... | custom-call | flops 20000000000 | bytes 1000000 | tf_op jit(solution)/shard_map/mixer_forward/pallas_call | solution.py:177
  197.9 21.3 %layer_forward.4 = (bf16[4,256,1024]{2,1,0:T(8,128)(2,1)}, bf16[4,256,1792]{2,1,0:T(8,128)(2,1)}, bf16[4,256,1792]{2,1,0:T(8,128)(2,1)}, bf16[4,256,1536]{2,1,0:...) custom-call(s32[1]{0:T(128)} %constant.367.clone.1.refs_0_, ...), custom_call_target="tpu_custom_call", output_to_operand_aliasing={{0}: (46, {}), {1}: (47, {}), {2}: (48, {}), {3}: (49, {}),... | custom-call | flops 20000000000 | bytes 1000000 | tf_op jit(solution)/shard_map/layer_forward/pallas_call | solution.py:177
  223.6 21.0 %layer_forward.5 = (bf16[4,256,1024]{2,1,0:T(8,128)(2,1)}, bf16[4,256,1792]{2,1,0:T(8,128)(2,1)}, bf16[4,256,1792]{2,1,0:T(8,128)(2,1)}, bf16[4,256,1536]{2,1,0:...) custom-call(s32[1]{0:T(128)} %constant.365.clone.1.refs_0_, ...), custom_call_target="tpu_custom_call", output_to_operand_aliasing={{0}: (46, {}), {1}: (47, {}), {2}: (48, {}), {3}: (49, {}),... | custom-call | flops 20000000000 | bytes 1000000 | tf_op jit(solution)/shard_map/layer_forward/pallas_call | solution.py:177
  248.2 19.9 %layer_forward.6 = (bf16[4,256,1024]{2,1,0:T(8,128)(2,1)}, bf16[4,256,1792]{2,1,0:T(8,128)(2,1)}, bf16[4,256,1792]{2,1,0:T(8,128)(2,1)}, bf16[4,256,1536]{2,1,0:...) custom-call(s32[1]{0:T(128)} %constant.368.clone.1.refs_0_, ...), custom_call_target="tpu_custom_call", output_to_operand_aliasing={{0}: (46, {}), {1}: (47, {}), {2}: (48, {}), {3}: (49, {}),... | custom-call | flops 20000000000 | bytes 1000000 | tf_op jit(solution)/shard_map/layer_forward/pallas_call | solution.py:177
  270.3 19.7 %layer_forward.7 = (bf16[4,256,1024]{2,1,0:T(8,128)(2,1)}, bf16[4,256,1792]{2,1,0:T(8,128)(2,1)}, bf16[4,256,1792]{2,1,0:T(8,128)(2,1)}, bf16[4,256,1536]{2,1,0:...) custom-call(s32[1]{0:T(128)} %constant.364.clone.1.refs_0_, ...), custom_call_target="tpu_custom_call", output_to_operand_aliasing={{0}: (46, {}), {1}: (47, {}), {2}: (48, {}), {3}: (49, {}),... | custom-call | flops 20000000000 | bytes 1000000 | tf_op jit(solution)/shard_map/layer_forward/pallas_call | solution.py:177
  291.5 27.9 %layer_backward.4 = (bf16[4,256,1024]{2,1,0:T(8,128)(2,1)}, bf16[4,256,2048]{2,1,0:T(8,128)(2,1)}, bf16[4,256,2048]{2,1,0:T(8,128)(2,1)}, f32[4,8,1024]{2,1,0:T(...) custom-call(s32[1]{0:T(128)} %constant.354.clone.1.refs_0_, ...), custom_call_target="tpu_custom_call" | custom-call | flops 24999999488 | bytes 1000000 | tf_op jit(solution)/shard_map/layer_backward/pallas_call | solution.py:177
  322.5 28.0 %layer_backward.5 = (bf16[4,256,1024]{2,1,0:T(8,128)(2,1)}, bf16[4,256,2048]{2,1,0:T(8,128)(2,1)}, bf16[4,256,2048]{2,1,0:T(8,128)(2,1)}, f32[4,8,1024]{2,1,0:T(...) custom-call(s32[1]{0:T(128)} %constant.353.clone.1.refs_0_, ...), custom_call_target="tpu_custom_call", output_to_operand_aliasing={{0}: (59, {}), {1}: (60, {}), {2}: (61, {}), {3}: (62, {}),... | custom-call | flops 24999999488 | bytes 1000000 | tf_op jit(solution)/shard_map/layer_backward/pallas_call | solution.py:177
  354.3 29.1 %layer_backward.6 = (bf16[4,256,1024]{2,1,0:T(8,128)(2,1)}, bf16[4,256,2048]{2,1,0:T(8,128)(2,1)}, bf16[4,256,2048]{2,1,0:T(8,128)(2,1)}, f32[4,8,1024]{2,1,0:T(...) custom-call(s32[1]{0:T(128)} %constant.369.clone.1.refs_0_, ...), custom_call_target="tpu_custom_call", output_to_operand_aliasing={{0}: (59, {}), {1}: (60, {}), {2}: (61, {}), {3}: (62, {}),... | custom-call | flops 24999999488 | bytes 1000000 | tf_op jit(solution)/shard_map/layer_backward/pallas_call | solution.py:177
  387.1 29.1 %layer_backward.7 = (bf16[4,256,1024]{2,1,0:T(8,128)(2,1)}, bf16[4,256,2048]{2,1,0:T(8,128)(2,1)}, bf16[4,256,2048]{2,1,0:T(8,128)(2,1)}, f32[4,8,1024]{2,1,0:T(...) custom-call(s32[1]{0:T(128)} %constant.352.clone.1.refs_0_, ...), custom_call_target="tpu_custom_call", output_to_operand_aliasing={{0}: (59, {}), {1}: (60, {}), {2}: (61, {}), {3}: (62, {}),... | custom-call | flops 24999999488 | bytes 1000000 | tf_op jit(solution)/shard_map/layer_backward/pallas_call | solution.py:177
  418.0 10.1 %mlp_backward.2 = (bf16[4,256,1024]{2,1,0:T(8,128)(2,1)}, bf16[4,256,2048]{2,1,0:T(8,128)(2,1)}, bf16[4,256,2048]{2,1,0:T(8,128)(2,1)}, f32[4,8,1024]{2,1,0:T(8,128)}, f32[256,1024]{1,0:T(8,128)S(1)}) custom-call(s32[1]{0:T(128)} %constant.370.clone.1.refs_0_, ...), custom_call_target="tpu_custom_call", output_to_operand_aliasing={{0}: (25, {}), {1}: (26, {}), {2}: (27, {}), {3}: (28, {})} | custom-call | flops 300000000 | bytes 1000000 | tf_op jit(solution)/shard_map/mlp_backward/pallas_call | solution.py:177
  433.7 10.1 %mlp_backward.3 = (bf16[4,256,1024]{2,1,0:T(8,128)(2,1)}, bf16[4,256,2048]{2,1,0:T(8,128)(2,1)}, bf16[4,256,2048]{2,1,0:T(8,128)(2,1)}, f32[4,8,1024]{2,1,0:T(8,128)}, f32[256,1024]{1,0:T(8,128)S(1)}) custom-call(s32[1]{0:T(128)} %constant.337.clone.1.refs_0_, ...), custom_call_target="tpu_custom_call", output_to_operand_aliasing={{0}: (25, {}), {1}: (26, {}), {2}: (27, {}), {3}: (28, {})} | custom-call | flops 300000000 | bytes 1000000 | tf_op jit(solution)/shard_map/mlp_backward/pallas_call | solution.py:177
  489.7 21.2 %mixer_backward.2 = (bf16[4,256,1024]{2,1,0:T(8,128)(2,1)}, bf16[4,256,896]{2,1,0:T(8,128)(2,1)}, bf16[4,256,1792]{2,1,0:T(8,128)(2,1)}, bf16[4,256,1536]{2,1,0:...) custom-call(s32[1]{0:T(128)} %constant.370.clone.1.refs_0_, ...), custom_call_target="tpu_custom_call", output_to_operand_aliasing={{0}: (40, {}), {1}: (41, {}), {2}: (42, {}), {3}: (43, {}),... | custom-call | flops 24999999488 | bytes 1000000 | tf_op jit(solution)/shard_map/mixer_backward/pallas_call | solution.py:177
  526.8 20.9 %mixer_backward.3 = (bf16[4,256,1024]{2,1,0:T(8,128)(2,1)}, bf16[4,256,896]{2,1,0:T(8,128)(2,1)}, bf16[4,256,1792]{2,1,0:T(8,128)(2,1)}, bf16[4,256,1536]{2,1,0:...) custom-call(s32[1]{0:T(128)} %constant.337.clone.1.refs_0_, ...), custom_call_target="tpu_custom_call", output_to_operand_aliasing={{0}: (40, {}), {1}: (41, {}), {2}: (42, {}), {3}: (43, {}),... | custom-call | flops 24999999488 | bytes 1000000 | tf_op jit(solution)/shard_map/mixer_backward/pallas_call | solution.py:177
  621.8 15.0 %collective-permute-done.55 = bf16[256,1792]{1,0:T(8,128)(2,1)S(1)} collective-permute-done((bf16[256,1792]{1,0:T(8,128)(2,1)S(1)}, bf16[256,1792]{1,0:T(8,128)(2,1)S(1)}, u32[]{:S(2)}, u32[]{:S(2)}) %collective-permute-start.55) | collective-permute-done | bytes 917536 | tf_op jit(solution)/shard_map/ppermute | solution.py:1137
  643.1 20.1 %collective-permute-done.63 = bf16[256,2048]{1,0:T(8,128)(2,1)S(1)} collective-permute-done((bf16[256,2048]{1,0:T(8,128)(2,1)S(1)}, bf16[256,2048]{1,0:T(8,128)(2,1)S(1)}, u32[]{:S(2)}, u32[]{:S(2)}) %collective-permute-start.63) | collective-permute-done | bytes 1048608 | tf_op jit(solution)/shard_map/ppermute | solution.py:1228
  668.8 14.2 %collective-permute-done.60 = bf16[256,1792]{1,0:T(8,128)(2,1)S(1)} collective-permute-done((bf16[256,1792]{1,0:T(8,128)(2,1)S(1)}, bf16[256,1792]{1,0:T(8,128)(2,1)S(1)}, u32[]{:S(2)}, u32[]{:S(2)}) %collective-permute-start.60) | collective-permute-done | bytes 917536 | tf_op jit(solution)/shard_map/ppermute | solution.py:1216
  684.7 10.2 %collective-permute-start.67 = (bf16[256,1536]{1,0:T(8,128)(2,1)S(1)}, bf16[256,1536]{1,0:T(8,128)(2,1)S(1)}, u32[]{:S(2)}, u32[]{:S(2)}) collective-permute-start(bf16[256,1536]{1,0:T(8,128)(2,1)S(1)} %fusion.5), channel_id=1, source_target_pairs={{0,1},{3,2},{4,5},{7,6},{8,9},{11,10},{12,13},{15,14},{16,17},{19,... | collective-permute-start | bytes 2359304 | tf_op jit(solution)/shard_map/ppermute | solution.py:1216
  736.0 13.4 %collective-permute-done.72 = bf16[256,1792]{1,0:T(8,128)(2,1)S(1)} collective-permute-done((bf16[256,1792]{1,0:T(8,128)(2,1)S(1)}, bf16[256,1792]{1,0:T(8,128)(2,1)S(1)}, u32[]{:S(2)}, u32[]{:S(2)}) %collective-permute-start.72) | collective-permute-done | bytes 917536 | tf_op jit(solution)/shard_map/ppermute | solution.py:1228
  754.8 11.5 %collective-permute-done.77 = bf16[256,1536]{1,0:T(8,128)(2,1)S(1)} collective-permute-done((bf16[256,1536]{1,0:T(8,128)(2,1)S(1)}, bf16[256,1536]{1,0:T(8,128)(2,1)S(1)}, u32[]{:S(2)}, u32[]{:S(2)}) %collective-permute-start.77) | collective-permute-done | bytes 786464 | tf_op jit(solution)/shard_map/ppermute | solution.py:1228
  769.7 13.4 %collective-permute-done.81 = bf16[384,1024]{1,0:T(8,128)(2,1)S(1)} collective-permute-done((bf16[384,1024]{1,0:T(8,128)(2,1)S(1)}, bf16[384,1024]{1,0:T(8,128)(2,1)S(1)}, u32[]{:S(2)}, u32[]{:S(2)}) %collective-permute-start.81) | collective-permute-done | bytes 786464 | tf_op jit(solution)/shard_map/ppermute | solution.py:1228
  (570 shorter events, 363.1 us)
Async XLA Ops:
  26.8 36.3 %collective-permute-start.1 = (bf16[256,896]{1,0:T(8,128)(2,1)S(1)}, bf16[256,896]{1,0:T(8,128)(2,1)}, u32[]{:S(2)}, u32[]{:S(2)}) collective-permute-start(bf16[256,896]{1,0:T(8,128)(2,1)S(1)} %concatenate.70.refs_8_.refs_9_), channel_id=1, source_target_pairs={{0,4},{4,0},{8,12},{12,8},{1,5},{5,1},{9,13},{13,9},{2,6},{6,2},{1... | collective-permute-start | bytes 1376264 | tf_op jit(solution)/shard_map/ppermute | solution.py:1137
  63.1 42.3 %collective-permute-start.17 = (bf16[512,1024]{1,0:T(8,128)(2,1)}, bf16[512,1024]{1,0:T(8,128)(2,1)}, u32[]{:S(2)}, u32[]{:S(2)}) collective-permute-start(bf16[512,1024]{1,0:T(8,128)(2,1)} %pad_maximum_fusion.refs_26_.refs_27_), channel_id=1, source_target_pairs={{0,4},{4,0},{8,12},{12,8},{1,5},{5,1},{9,13},{13,9},{2,6},{6,2},{1... | collective-permute-start | bytes 3145736 | tf_op jit(solution)/shard_map/ppermute | solution.py:1137
  121.9 31.7 %collective-permute-start.32 = (bf16[512,1024]{1,0:T(8,128)(2,1)S(1)}, bf16[512,1024]{1,0:T(8,128)(2,1)S(1)}, u32[]{:S(2)}, u32[]{:S(2)}) collective-permute-start(bf16[512,1024]{1,0:T(8,128)(2,1)S(1)} %bitcast.231), channel_id=1, source_target_pairs={{0,8},{4,12},{8,0},{12,4},{1,9},{5,13},{9,1},{13,5},{2,10},{6,14},... | collective-permute-start | bytes 3145736 | tf_op jit(solution)/shard_map/ppermute | solution.py:1137
  123.8 45.0 %collective-permute-start.23 = (bf16[256,2048]{1,0:T(8,128)(2,1)S(1)}, bf16[256,2048]{1,0:T(8,128)(2,1)S(1)}, u32[]{:S(2)}, u32[]{:S(2)}) collective-permute-start(bf16[256,2048]{1,0:T(8,128)(2,1)S(1)} %bitcast.203), channel_id=1, source_target_pairs={{0,4},{4,0},{8,12},{12,8},{1,5},{5,1},{9,13},{13,9},{2,6},{6,2},{1... | collective-permute-start | bytes 3145736 | tf_op jit(solution)/shard_map/ppermute | solution.py:1137
  123.9 45.0 %collective-permute-start.26 = (bf16[128,2048]{1,0:T(8,128)(2,1)}, bf16[128,2048]{1,0:T(8,128)(2,1)S(1)}, u32[]{:S(2)}, u32[]{:S(2)}) collective-permute-start(bf16[128,2048]{1,0:T(8,128)(2,1)} %collective-permute-done.24.refs_7_.refs_34_.refs_35_.refs_9_), channel_id=1, source_target_pairs={{0,4},{4,0},{8,12},{12,8},{1,5},{5,1},{9,13},{13,9},{2,6},{6,2},{1... | collective-permute-start | bytes 1572872 | tf_op jit(solution)/shard_map/ppermute | solution.py:1137
  137.0 31.9 %collective-permute-start.27 = (bf16[128,2048]{1,0:T(8,128)(2,1)S(1)}, bf16[128,2048]{1,0:T(8,128)(2,1)S(1)}, u32[]{:S(2)}, u32[]{:S(2)}) collective-permute-start(bf16[128,2048]{1,0:T(8,128)(2,1)S(1)} %collective-permute-done.25.refs_8_.refs_35_.refs_36_.refs_10_), channel_id=1, source_target_pairs={{0,4},{4,0},{8,12},{12,8},{1,5},{5,1},{9,13},{13,9},{2,6},{6,2},{1... | collective-permute-start | bytes 1572872 | tf_op jit(solution)/shard_map/ppermute | solution.py:1137
  137.0 31.9 %collective-permute-start.30 = (bf16[256,2048]{1,0:T(8,128)(2,1)S(1)}, bf16[256,2048]{1,0:T(8,128)(2,1)S(1)}, u32[]{:S(2)}, u32[]{:S(2)}) collective-permute-start(bf16[256,2048]{1,0:T(8,128)(2,1)S(1)} %collective-permute-done.29.refs_13_.refs_40_.refs_41_.refs_15_), channel_id=1, source_target_pairs={{0,4},{4,0},{8,12},{12,8},{1,5},{5,1},{9,13},{13,9},{2,6},{6,2},{1... | collective-permute-start | bytes 3145736 | tf_op jit(solution)/shard_map/ppermute | solution.py:1137
  184.8 37.8 %collective-permute-start.22 = (bf16[256,1024]{1,0:T(8,128)(2,1)S(1)}, bf16[256,1024]{1,0:T(8,128)(2,1)S(1)}, u32[]{:S(2)}, u32[]{:S(2)}) collective-permute-start(bf16[256,1024]{1,0:T(8,128)(2,1)S(1)} %copy-done.82), channel_id=1, source_target_pairs={{0,3},{1,2},{2,1},{3,0},{4,7},{5,6},{6,5},{7,4},{8,11},{9,10},{10,... | collective-permute-start | bytes 1572872 | tf_op jit(solution)/shard_map/ppermute | solution.py:1137
  320.8 32.6 %collective-permute-start.39 = (bf16[256,1024]{1,0:T(8,128)(2,1)}, bf16[256,1024]{1,0:T(8,128)(2,1)S(1)}, u32[]{:S(2)}, u32[]{:S(2)}) collective-permute-start(bf16[256,1024]{1,0:T(8,128)(2,1)} %get-tuple-element.491), channel_id=1, source_target_pairs={{16,0},{17,1},{18,2},{19,3},{20,4},{21,5},{22,6},{23,7},{24,8},{25... | collective-permute-start | bytes 1572872 | tf_op jit(solution)/shard_map/ppermute | solution.py:1569
  350.5 35.8 %collective-permute-start.38 = (bf16[256,1024]{1,0:T(8,128)(2,1)}, bf16[256,1024]{1,0:T(8,128)(2,1)S(1)}, u32[]{:S(2)}, u32[]{:S(2)}) collective-permute-start(bf16[256,1024]{1,0:T(8,128)(2,1)} %get-tuple-element.503), channel_id=1, source_target_pairs={{16,0},{17,1},{18,2},{19,3},{20,4},{21,5},{22,6},{23,7},{24,8},{25... | collective-permute-start | bytes 1572872 | tf_op jit(solution)/shard_map/ppermute | solution.py:1569
  383.4 34.6 %collective-permute-start.41 = (bf16[256,1024]{1,0:T(8,128)(2,1)}, bf16[256,1024]{1,0:T(8,128)(2,1)S(1)}, u32[]{:S(2)}, u32[]{:S(2)}) collective-permute-start(bf16[256,1024]{1,0:T(8,128)(2,1)} %get-tuple-element.516), channel_id=1, source_target_pairs={{16,0},{17,1},{18,2},{19,3},{20,4},{21,5},{22,6},{23,7},{24,8},{25... | collective-permute-start | bytes 1572872 | tf_op jit(solution)/shard_map/ppermute | solution.py:1569
  478.9 38.0 %collective-permute-start.47 = (bf16[256,1024]{1,0:T(8,128)(2,1)S(1)}, bf16[256,1024]{1,0:T(8,128)(2,1)S(1)}, u32[]{:S(2)}, u32[]{:S(2)}) collective-permute-start(bf16[256,1024]{1,0:T(8,128)(2,1)S(1)} %bitcast_select_fusion.2), channel_id=1, source_target_pairs={{0,3},{1,2},{2,1},{3,0},{4,7},{5,6},{6,5},{7,4},{8,11},{9,10},{10,... | collective-permute-start | bytes 1572872 | tf_op jit(solution)/shard_map/ppermute | solution.py:1137
  482.3 44.3 %collective-permute-start.46 = (bf16[256,1024]{1,0:T(8,128)(2,1)S(1)}, bf16[256,1024]{1,0:T(8,128)(2,1)S(1)}, u32[]{:S(2)}, u32[]{:S(2)}) collective-permute-start(bf16[256,1024]{1,0:T(8,128)(2,1)S(1)} %bitcast_select_fusion.3), channel_id=1, source_target_pairs={{0,2},{1,3},{2,0},{3,1},{4,6},{5,7},{6,4},{7,5},{8,10},{9,11},{10,... | collective-permute-start | bytes 1572872 | tf_op jit(solution)/shard_map/ppermute | solution.py:1137
  486.4 61.4 %collective-permute-start.50 = (bf16[256,2048]{1,0:T(8,128)(2,1)S(1)}, bf16[256,2048]{1,0:T(8,128)(2,1)S(1)}, u32[]{:S(2)}, u32[]{:S(2)}) collective-permute-start(bf16[256,2048]{1,0:T(8,128)(2,1)S(1)} %fusion.7), channel_id=1, source_target_pairs={{0,8},{4,12},{8,0},{12,4},{1,9},{5,13},{9,1},{13,5},{2,10},{6,14},... | collective-permute-start | bytes 3145736 | tf_op jit(solution)/shard_map/ppermute | solution.py:1137
  512.8 37.9 %collective-permute-start.49 = (bf16[256,2048]{1,0:T(8,128)(2,1)S(1)}, bf16[256,2048]{1,0:T(8,128)(2,1)S(1)}, u32[]{:S(2)}, u32[]{:S(2)}) collective-permute-start(bf16[256,2048]{1,0:T(8,128)(2,1)S(1)} %fusion.2), channel_id=1, source_target_pairs={{0,1},{3,2},{4,5},{7,6},{8,9},{11,10},{12,13},{15,14},{16,17},{19,... | collective-permute-start | bytes 3145736 | tf_op jit(solution)/shard_map/ppermute | solution.py:1216
  561.3 48.7 %collective-permute-start.53 = (bf16[2,256,1792]{2,1,0:T(8,128)(2,1)}, bf16[2,256,1792]{2,1,0:T(8,128)(2,1)}, u32[]{:S(2)}, u32[]{:S(2)}) collective-permute-start(bf16[2,256,1792]{2,1,0:T(8,128)(2,1)} %get-tuple-element.619), channel_id=1, source_target_pairs={{0,4},{4,0},{8,12},{12,8},{1,5},{5,1},{9,13},{13,9},{2,6},{6,2},{1... | collective-permute-start | bytes 5505032 | tf_op jit(solution)/shard_map/ppermute | solution.py:1137
  565.8 45.8 %collective-permute-start.52 = (bf16[512,1024]{1,0:T(8,128)(2,1)}, bf16[512,1024]{1,0:T(8,128)(2,1)}, u32[]{:S(2)}, u32[]{:S(2)}) collective-permute-start(bf16[512,1024]{1,0:T(8,128)(2,1)} %copy-done.76), channel_id=1, source_target_pairs={{0,8},{4,12},{8,0},{12,4},{1,9},{5,13},{9,1},{13,5},{2,10},{6,14},... | collective-permute-start | bytes 3145736 | tf_op jit(solution)/shard_map/ppermute | solution.py:1137
  568.3 97.9 %collective-permute-start.48 = (bf16[256,1024]{1,0:T(8,128)(2,1)}, bf16[256,1024]{1,0:T(8,128)(2,1)}, u32[]{:S(2)}, u32[]{:S(2)}) collective-permute-start(bf16[256,1024]{1,0:T(8,128)(2,1)} %bitcast_select_fusion), channel_id=1, source_target_pairs={{0,1},{1,0},{2,3},{3,2},{4,5},{5,4},{6,7},{7,6},{8,9},{9,8},{10,11... | collective-permute-start | bytes 1572872 | tf_op jit(solution)/shard_map/ppermute | solution.py:1137
  569.4 44.8 %collective-permute-start.58 = (bf16[256,2048]{1,0:T(8,128)(2,1)}, bf16[256,2048]{1,0:T(8,128)(2,1)}, u32[]{:S(2)}, u32[]{:S(2)}) collective-permute-start(bf16[256,2048]{1,0:T(8,128)(2,1)} %fusion.1), channel_id=1, source_target_pairs={{0,1},{3,2},{4,5},{7,6},{8,9},{11,10},{12,13},{15,14},{16,17},{19,... | collective-permute-start | bytes 3145736 | tf_op jit(solution)/shard_map/ppermute | solution.py:1216
  578.1 39.3 %collective-permute-start.57 = (bf16[256,2048]{1,0:T(8,128)(2,1)}, bf16[256,2048]{1,0:T(8,128)(2,1)}, u32[]{:S(2)}, u32[]{:S(2)}) collective-permute-start(bf16[256,2048]{1,0:T(8,128)(2,1)} %add_convert_fusion.5), channel_id=1, source_target_pairs={{1,2},{2,1},{5,6},{6,5},{9,10},{10,9},{13,14},{14,13},{17,18},{18,... | collective-permute-start | bytes 3145736 | tf_op jit(solution)/shard_map/ppermute | solution.py:1222
  611.6 54.5 %collective-permute-start.62 = (bf16[2,384,1024]{2,1,0:T(8,128)(2,1)S(1)}, bf16[2,384,1024]{2,1,0:T(8,128)(2,1)S(1)}, u32[]{:S(2)}, u32[]{:S(2)}) collective-permute-start(bf16[2,384,1024]{2,1,0:T(8,128)(2,1)S(1)} %copy-done.39), channel_id=1, source_target_pairs={{0,4},{4,0},{8,12},{12,8},{1,5},{5,1},{9,13},{13,9},{2,6},{6,2},{1... | collective-permute-start | bytes 4718600 | tf_op jit(solution)/shard_map/ppermute | solution.py:1137
  641.7 56.2 %collective-permute-start.69 = (bf16[2,256,896]{2,1,0:T(8,128)(2,1)S(1)}, bf16[2,256,896]{2,1,0:T(8,128)(2,1)S(1)}, u32[]{:S(2)}, u32[]{:S(2)}) collective-permute-start(bf16[2,256,896]{2,1,0:T(8,128)(2,1)S(1)} %copy-done.46), channel_id=1, source_target_pairs={{0,4},{4,0},{8,12},{12,8},{1,5},{5,1},{9,13},{13,9},{2,6},{6,2},{1... | collective-permute-start | bytes 2752520 | tf_op jit(solution)/shard_map/ppermute | solution.py:1137
  666.1 60.9 %collective-permute-start.51 = (bf16[2,128,1024]{2,1,0:T(8,128)(2,1)S(1)}, bf16[2,128,1024]{2,1,0:T(8,128)(2,1)S(1)}, u32[]{:S(2)}, u32[]{:S(2)}) collective-permute-start(bf16[2,128,1024]{2,1,0:T(8,128)(2,1)S(1)} %get-tuple-element.618), channel_id=1, source_target_pairs={{0,4},{4,0},{8,12},{12,8},{1,5},{5,1},{9,13},{13,9},{2,6},{6,2},{1... | collective-permute-start | bytes 1572872 | tf_op jit(solution)/shard_map/ppermute | solution.py:1137
  734.7 31.6 %collective-permute-start.77 = (bf16[256,1536]{1,0:T(8,128)(2,1)S(1)}, bf16[256,1536]{1,0:T(8,128)(2,1)S(1)}, u32[]{:S(2)}, u32[]{:S(2)}) collective-permute-start(bf16[256,1536]{1,0:T(8,128)(2,1)S(1)} %add_convert_fusion.13), channel_id=1, source_target_pairs={{1,0},{2,3},{5,4},{6,7},{9,8},{10,11},{13,12},{14,15},{17,16},{18,... | collective-permute-start | bytes 2359304 | tf_op jit(solution)/shard_map/ppermute | solution.py:1228
  (162 other events, 2758.8 us)

commit v3 on v2

--- a/solution.py
+++ b/solution.py
@@ -1005,12 +1005,8 @@
 def weight_kernel(core_ref, away_ref, stay_ref, right_ref, out_away, out_stay, turned):
     rows = away_ref.shape[2]
     tokens = away_ref.shape[0] * away_ref.shape[1]
-
-    @pl.when(pl.program_id(1) == 0)
-    def _():
-        turned[:rows, :] = away_ref[...].reshape(tokens, rows).T
-        turned[rows:, :] = stay_ref[...].reshape(tokens, rows).T
-
+    turned[:rows, :] = away_ref[...].reshape(tokens, rows).T
+    turned[rows:, :] = stay_ref[...].reshape(tokens, rows).T
     right = right_ref[...].reshape(tokens, right_ref.shape[2])
     out_away[0] = dot(turned[:rows, :], right).astype(BF)
     out_stay[0] = dot(turned[rows:, :], right).astype(BF)
@@ -1020,19 +1016,18 @@
     count, length, depth = left.shape
     columns = right.shape[2]
     rows = depth // 4
-    tile = max(t for t in (896, 768, 512, 256, 128) if columns % t == 0)
     grid = pltpu.PrefetchScalarGridSpec(
         num_scalar_prefetch=1,
-        grid=(2, columns // tile),
+        grid=(2,),
         in_specs=[
-            pl.BlockSpec((count, length, rows), lambda c, n, core: (0, 0, 2 * c + 1 - core[0])),
-            pl.BlockSpec((count, length, rows), lambda c, n, core: (0, 0, 2 * c + core[0])),
-            pl.BlockSpec((count, length, tile), lambda c, n, core: (0, 0, n)),
+            pl.BlockSpec((count, length, rows), lambda c, core: (0, 0, 2 * c + 1 - core[0])),
+            pl.BlockSpec((count, length, rows), lambda c, core: (0, 0, 2 * c + core[0])),
+            pl.BlockSpec((count, length, columns), lambda c, core: (0, 0, 0)),
         ],
-        out_specs=[pl.BlockSpec((1, rows, tile), lambda c, n, core: (c, 0, n))] * 2,
+        out_specs=[pl.BlockSpec((1, rows, columns), lambda c, core: (c, 0, 0))] * 2,
         scratch_shapes=[pltpu.VMEM((2 * rows, count * length), BF)],
     )
-    shape = jax.ShapeDtypeStruct((2, rows, columns), BF)
+    shape = pltpu.HBM((2, rows, columns), BF)
     return pl.pallas_call(
         weight_kernel,
         out_shape=[shape, shape],
@@ -1042,7 +1037,7 @@
             flops=100000000, bytes_accessed=1000000, transcendentals=0
         ),
         name="weight_gradient",
-    )(core, left, left, right)
+    )(core, in_hbm(left), in_hbm(left), in_hbm(right))
 
 
 def layer_forward_call(
@@ -1159,12 +1154,15 @@
     near = swap(shard, "fsdp", 1)
     far_one = swap(after(mine, *before_y), "fsdp", 2)
     far_two = swap(after(far_one, *before_z), "rep", 1)
-    return [shard, near, far_one, far_two, swap(far_one, "fsdp", 1), swap(far_two, "fsdp", 1)]
+    return [shard, near, far_one, far_two]
 
 
 def gather_wholes(shard, *before_y):
-    far = swap(after(shard, *before_y), "fsdp", 2)
-    return [shard, swap(shard, "fsdp", 1), far, swap(far, "fsdp", 1)]
+    return [shard, swap(shard, "fsdp", 1), swap(after(shard, *before_y), "fsdp", 2)]
+
+
+def share_far(pieces, *before):
+    return pieces + [swap(after(piece, *before), "fsdp", 1) for piece in pieces[2:]]
 
 
 def plus(a, b):
@@ -1305,8 +1303,6 @@
     def deal(j, *earlier):
         dealt.append(swap(after(outgoing[j], *earlier), "rep", j))
 
-    for j in range(1, count - 1):
-        deal(j)
 
     def columns(flat):
         wide = -(-flat.size // rows)
@@ -1332,13 +1328,16 @@
     at = qw + 2 * kw + heads
     parity = rank % 2
     if quick:
-        g_gate = gather_halves(w_ssm_gate[0], 0, (), dealt[1:2])
-        g_conv = gather_halves(w_conv_in[0], 0, (), dealt[2:3])
+        g_gate = gather_halves(w_ssm_gate[0], 0)
+        g_conv = gather_halves(w_conv_in[0], 0)
         g_first = gather_halves(shard_first, 0, g_gate[2:3], g_gate[3:4])
         shard_out = jnp.concatenate([w_ssm_out[0], w_attn_out[0]], axis=0)
         g_out = gather_halves(shard_out, 1, g_conv[2:3], g_conv[3:4])
         g_g = gather_halves(w_gate[0], 0, g_first[2:3], g_first[3:4])
         g_u = gather_wholes(w_up[0], g_out[2], g_g[2])
+        deal(1, g_out[3])
+        deal(2, dealt[1])
+        g_gate, g_conv, g_first, g_out = (share_far(g) for g in (g_gate, g_conv, g_first, g_out))
         spots = [2 * fsdp, 2 * (fsdp ^ 1)]
         spots += [2 * (fsdp ^ k) + b for k in (2, 3) for b in (parity, 1 - parity)]
         spots = jnp.stack(spots).astype(jnp.int32)
@@ -1351,6 +1350,9 @@
         )
         ridden = jnp.take(blocks, jnp.arange(4, dtype=jnp.int32) ^ fsdp, axis=0)
     else:
+
+        for j in range(1, count - 1):
+            deal(j)
 
         def whole(shard):
             return lax.all_gather(shard, "fsdp", axis=0, tiled=True)
@@ -1442,6 +1444,8 @@
 
     received, hiddens = [], []
 
+    blank = jnp.zeros((8, HALF), F32)
+
     def number(i):
         return jnp.full((1,), i, jnp.int32)
 
@@ -1466,6 +1470,8 @@
 
     def mlp_tick(tick, mlp_stacks):
         (hidden,) = chained(hiddens[tick])
+        if tick == 1:
+            hidden = after(hidden, dealt[2])
         mlp_stacks, low = mlp_forward_call(
             number(tick), plan, spots, hidden, vec, mlp_weights, mlp_stacks, ff
         )
@@ -1485,7 +1491,7 @@
             vec,
             cosine,
             sine,
-            corner(turn),
+            corner(turn) if tick < steps - 1 else blank,
             mixer_weights + mlp_weights,
             stacks,
             widths,
@@ -1495,9 +1501,11 @@
 
     mix_stacks = mixer_tick(0, dealt[0], mix_stacks)
     if quick:
-        mlp_weights = [g_g, g_u, gather_wholes(w_down[0], hiddens[0])]
+        g_down = gather_wholes(w_down[0], hiddens[0])
     deal(count - 1, hiddens[0])
     mix_stacks = mixer_tick(1, hiddens[0], mix_stacks)
+    if quick:
+        mlp_weights = [share_far(g, hiddens[1]) for g in (g_g, g_u, g_down)]
     for tick in range(steps):
         if tick < skew:
             mlp_stacks, low = mlp_tick(tick, mlp_stacks)
@@ -1530,6 +1538,8 @@
     hiddens = []
 
     def mlp_turn(turn, mlp_grads):
+        if turn == count:
+            token.append(returned[3])
         (seed,) = chained(incoming[turn - skew])
         return mlp_backward_call(
             number(steps + turn),
@@ -1538,7 +1548,7 @@
             spots,
             seed,
             vec,
-            corner(hiddens[-1]) if turn > count else jnp.zeros((8, HALF), F32),
+            corner(hiddens[-1]) if turn > count else blank,
             mlp_weights,
             reads,
             mlp_grads,
@@ -1591,7 +1601,7 @@
             vec,
             cosine,
             sine,
-            corner(d_input),
+            corner(d_input) if turn else blank,
             mixer_weights + mlp_weights,
             reads + mix_reads,
             mlp_grads + mix_grads,
@@ -1611,23 +1621,28 @@
     early = [(s_normed2, s_dg), (s_normed2, s_du), (s_act, s_dmlp)]
     chunks = [Reduction(*pair) for pair in early]
 
+    names = dict(W="begin", A="chips", L="line_in", M="middle", O="line_out", F="finish")
+    state = [mix_grads]
+
     def stages(*words):
         for word in words:
-            chain(getattr(chunks[int(word[1])], names[word[0]])(chained))
-
-    names = dict(W="begin", A="chips", L="line_in", M="middle", O="line_out", F="finish")
+            letter, place = word[0], int(word[1:])
+            if letter == "B":
+                before = token[0] if quick else hiddens[place - count]
+                state[0], made = mixer_turn(place, hiddens[place - count], before, state[0])
+            else:
+                made = getattr(chunks[place], names[letter])(chained)
+            chain(made)
+
     if quick:
-        stages("W0", "W1", "W2", "A0", "A1", "A2")
-    for turn in range(count, steps):
-        d_hidden = hiddens[turn - count]
-        before = d_hidden
-        if quick:
-            before = after(token[0], *returned[2:]) if turn > count else token[0]
-        mix_grads, d_input = mixer_turn(turn, d_hidden, before, mix_grads)
-        if quick:
-            chain(d_input)
-            if turn == count:
-                stages("L0")
+        stages("W1")
+        token.append(returned[2])
+        stages(
+            "W2", "W0", "A2", "B4", "A0", "A1", "L2", "B5"
+        )
+    else:
+        stages("B4", "B5")
+    mix_grads = state[0]
     s_dbranch, s_dfirst, s_dconv, s_dgate, s_dinput, small_mix = mix_grads
     late = [
         (s_normed, s_dconv),
@@ -1668,14 +1683,14 @@
         column = tail - HALF + heads
         chunks += [Reduction(*pair) for pair in late]
         chunks[6].riders = (riders, column)
-        stages("L1", "M0", "W3", "W4", "W5", "W6", "W7")
-        stages("A3", "L2", "M1", "O0")
-        stages("A4", "L3", "M2", "O1", "F0")
+        stages(
+            "W4", "M2", "L0", "W5", "W3", "W7", "O2", "A4", "L1", "M0", "A5", "A3", "W6", "A7"
+        )
         token.append(returned[1])
-        stages("A5", "L4", "M3", "O2", "F1")
-        stages("A6", "L5", "M4", "O3", "F2")
-        stages("A7", "L6", "M5", "O4", "F3")
-        stages("L7", "M6", "O5", "F4", "M7", "O6", "F5", "O7", "F6", "F7")
+        stages(
+            "L4", "M1", "O0", "F2", "A6", "L3", "M4", "L7", "O1", "F0", "L6", "M3", "L5", "M7",
+            "O4", "F1", "M6", "O3", "M5", "F4", "O7", "O6", "F3", "O5", "F7", "F6", "F5"
+        )
         reduced = [chunk.result for chunk in chunks]
         flat = reduced[6][:, column : column + spare].reshape(-1)
         ends = chained(*returned, s_dinput, s_low)

time: 823 us -> 809 us (0.983)
  waiting for transfers between devices: 200 us -> 170 us
  other arithmetic: 66.5 us -> 82.3 us
  local copies, waits for them, and re-layouts: 61.2 us -> 46.7 us
  starting transfers between devices: 95 us -> 106 us
    ppermute x8, waiting for transfers between devices: 72.7 us -> 54.2 us  [line_out(): self.moved = lax.ppermute(self.stay, 'rep', [(1, 0), (2, 3)])]
    unnamed x203 -> x141, local copies, waits for them, and re-layouts: 23.6 us -> 6.28 us
    convert_element_type x24, other arithmetic: 15 us -> 27.3 us  [plus(): return (a.astype(F32) + b.astype(F32)).astype(BF)]
    ppermute x53, waiting for transfers between devices: 95.7 us -> 87 us  [swap(): lax.ppermute(block, axis, [(i, i ^ bit) for i in range(lax.axis_size(axis...]
  transfers between devices with their start and end apart: 86 -> 86, of which waited for: 22 -> 25; matrix products, arithmetic and copies ran while one was open for 13% -> 15% of each run, Pallas kernels for 34% -> 38%
where the time goes in v3:
time: 809 us; the launch traced here: 797 us
  Pallas kernels  361 us (45%)
  waiting for transfers between devices  170 us (21%)
  starting transfers between devices  106 us (13%)
  other arithmetic  82.3 us (10%)
  local copies, waits for them, and re-layouts  46.7 us (6%)
  between operations  22.1 us (3%)
  matrix products  8.39 us (1%)
    pallas_call x16, Pallas kernels, call(): pl.pallas_call(kernel, out_shape=[pltpu.HBM(s.shape, s.dtype) for s in st...  306 us
    ppermute x53, waiting for transfers between devices, swap(): lax.ppermute(block, axis, [(i, i ^ bit) for i in range(lax.axis_size(axis...  87 us
    pallas_call x8, Pallas kernels, weight_grad_halves(): pl.pallas_call(weight_kernel, out_shape=[shape, shape], grid_spec=grid, c...  55.5 us
    ppermute x8, waiting for transfers between devices, line_out(): self.moved = lax.ppermute(self.stay, 'rep', [(1, 0), (2, 3)])  54.2 us
    ppermute x53, starting transfers between devices, swap(): lax.ppermute(block, axis, [(i, i ^ bit) for i in range(lax.axis_size(axis...  38.4 us
    ppermute x8, starting transfers between devices, line_in(): self.moved = lax.ppermute(self.stay, 'rep', [(0, 1), (3, 2)])  33.4 us
    ppermute x8, waiting for transfers between devices, line_in(): self.moved = lax.ppermute(self.stay, 'rep', [(0, 1), (3, 2)])  28.5 us
    convert_element_type x24, other arithmetic, plus(): return (a.astype(F32) + b.astype(F32)).astype(BF)  27.3 us
  transfers between devices with their start and end apart: 86, of which 25 were waited for; matrix products, arithmetic and copies ran while one was open for 15% of the time, Pallas kernels for 38%

profile of v3, /device:TPU:0, one launch (start us, length us, event | category | flops | bytes accessed | tf_op | source)
XLA Modules:
  0.0 796.6 jit_solution(1561448194705526569)
XLA Ops:
  73.0 11.5 %collective-permute-done.3.refs_29_.refs_30_ = bf16[512,512]{1,0:T(8,128)(2,1)} collective-permute-done((bf16[512,512]{1,0:T(8,128)(2,1)}, bf16[512,512]{1,0:T(8,128)(2,1)}, u32[]{:S(2)}, u32[]{:S(2)}) %collective-permute-start.3) | collective-permute-done | bytes 524320 | tf_op jit(solution)/shard_map/ppermute | solution.py:1132
  89.6 15.2 %mixer_forward.2 = (bf16[4,256,1024]{2,1,0:T(8,128)(2,1)}, bf16[4,256,1792]{2,1,0:T(8,128)(2,1)}, bf16[4,256,1792]{2,1,0:T(8,128)(2,1)}, bf16[4,256,1536]{2,1,0:...) custom-call(s32[1]{0:T(128)} %constant.359.clone.1.refs_0_, ...), custom_call_target="tpu_custom_call" | custom-call | flops 20000000000 | bytes 1000000 | tf_op jit(solution)/shard_map/mixer_forward/pallas_call | solution.py:177
  114.6 15.0 %mixer_forward.3 = (bf16[4,256,1024]{2,1,0:T(8,128)(2,1)}, bf16[4,256,1792]{2,1,0:T(8,128)(2,1)}, bf16[4,256,1792]{2,1,0:T(8,128)(2,1)}, bf16[4,256,1536]{2,1,0:...) custom-call(s32[1]{0:T(128)} %constant.364.clone.1.refs_0_, ...), custom_call_target="tpu_custom_call", output_to_operand_aliasing={{0}: (32, {}), {1}: (33, {}), {2}: (34, {}), {3}: (35, {}),... | custom-call | flops 20000000000 | bytes 1000000 | tf_op jit(solution)/shard_map/mixer_forward/pallas_call | solution.py:177
  163.4 24.2 %collective-permute-done.5.refs_4_ = bf16[256,1024]{1,0:T(8,128)(2,1)S(1)} collective-permute-done((bf16[256,1024]{1,0:T(8,128)(2,1)}, bf16[256,1024]{1,0:T(8,128)(2,1)S(1)}, u32[]{:S(2)}, u32[]{:S(2)}) %collective-permute-start.5) | collective-permute-done | bytes 524320 | tf_op jit(solution)/shard_map/ppermute | solution.py:1132
  187.6 8.3 %mlp_forward.3 = (bf16[4,256,1024]{2,1,0:T(8,128)(2,1)}, bf16[4,256,2048]{2,1,0:T(8,128)(2,1)}, bf16[4,256,2048]{2,1,0:T(8,128)(2,1)}, bf16[4,256,2048]{2,1,0:T(...) custom-call(s32[1]{0:T(128)} %constant.364.clone.1.refs_0_, ...), custom_call_target="tpu_custom_call", output_to_operand_aliasing={{0}: (19, {}), {1}: (20, {}), {2}: (21, {}), {3}: (22, {}),... | custom-call | flops 300000000 | bytes 1000000 | tf_op jit(solution)/shard_map/mlp_forward/pallas_call | solution.py:177
  199.9 21.3 %layer_forward.4 = (bf16[4,256,1024]{2,1,0:T(8,128)(2,1)}, bf16[4,256,1792]{2,1,0:T(8,128)(2,1)}, bf16[4,256,1792]{2,1,0:T(8,128)(2,1)}, bf16[4,256,1536]{2,1,0:...) custom-call(s32[1]{0:T(128)} %constant.367.clone.1.refs_0_, ...), custom_call_target="tpu_custom_call", output_to_operand_aliasing={{0}: (46, {}), {1}: (47, {}), {2}: (48, {}), {3}: (49, {}),... | custom-call | flops 20000000000 | bytes 1000000 | tf_op jit(solution)/shard_map/layer_forward/pallas_call | solution.py:177
  225.8 21.0 %layer_forward.5 = (bf16[4,256,1024]{2,1,0:T(8,128)(2,1)}, bf16[4,256,1792]{2,1,0:T(8,128)(2,1)}, bf16[4,256,1792]{2,1,0:T(8,128)(2,1)}, bf16[4,256,1536]{2,1,0:...) custom-call(s32[1]{0:T(128)} %constant.366.clone.1.refs_0_, ...), custom_call_target="tpu_custom_call", output_to_operand_aliasing={{0}: (46, {}), {1}: (47, {}), {2}: (48, {}), {3}: (49, {}),... | custom-call | flops 20000000000 | bytes 1000000 | tf_op jit(solution)/shard_map/layer_forward/pallas_call | solution.py:177
  250.4 19.9 %layer_forward.6 = (bf16[4,256,1024]{2,1,0:T(8,128)(2,1)}, bf16[4,256,1792]{2,1,0:T(8,128)(2,1)}, bf16[4,256,1792]{2,1,0:T(8,128)(2,1)}, bf16[4,256,1536]{2,1,0:...) custom-call(s32[1]{0:T(128)} %constant.368.clone.1.refs_0_, ...), custom_call_target="tpu_custom_call", output_to_operand_aliasing={{0}: (46, {}), {1}: (47, {}), {2}: (48, {}), {3}: (49, {}),... | custom-call | flops 20000000000 | bytes 1000000 | tf_op jit(solution)/shard_map/layer_forward/pallas_call | solution.py:177
  271.1 19.7 %layer_forward.7 = (bf16[4,256,1024]{2,1,0:T(8,128)(2,1)}, bf16[4,256,1792]{2,1,0:T(8,128)(2,1)}, bf16[4,256,1792]{2,1,0:T(8,128)(2,1)}, bf16[4,256,1536]{2,1,0:...) custom-call(s32[1]{0:T(128)} %constant.365.clone.1.refs_0_, ...), custom_call_target="tpu_custom_call", output_to_operand_aliasing={{0}: (46, {}), {1}: (47, {}), {2}: (48, {}), {3}: (49, {}),... | custom-call | flops 20000000000 | bytes 1000000 | tf_op jit(solution)/shard_map/layer_forward/pallas_call | solution.py:177
  290.9 28.0 %layer_backward.4 = (bf16[4,256,1024]{2,1,0:T(8,128)(2,1)}, bf16[4,256,2048]{2,1,0:T(8,128)(2,1)}, bf16[4,256,2048]{2,1,0:T(8,128)(2,1)}, f32[4,8,1024]{2,1,0:T(...) custom-call(s32[1]{0:T(128)} %constant.358.clone.1.refs_0_, ...), custom_call_target="tpu_custom_call" | custom-call | flops 24999999488 | bytes 1000000 | tf_op jit(solution)/shard_map/layer_backward/pallas_call | solution.py:177
  322.0 28.1 %layer_backward.5 = (bf16[4,256,1024]{2,1,0:T(8,128)(2,1)}, bf16[4,256,2048]{2,1,0:T(8,128)(2,1)}, bf16[4,256,2048]{2,1,0:T(8,128)(2,1)}, f32[4,8,1024]{2,1,0:T(...) custom-call(s32[1]{0:T(128)} %constant.353.clone.1.refs_0_, ...), custom_call_target="tpu_custom_call", output_to_operand_aliasing={{0}: (59, {}), {1}: (60, {}), {2}: (61, {}), {3}: (62, {}),... | custom-call | flops 24999999488 | bytes 1000000 | tf_op jit(solution)/shard_map/layer_backward/pallas_call | solution.py:177
  353.9 29.3 %layer_backward.6 = (bf16[4,256,1024]{2,1,0:T(8,128)(2,1)}, bf16[4,256,2048]{2,1,0:T(8,128)(2,1)}, bf16[4,256,2048]{2,1,0:T(8,128)(2,1)}, f32[4,8,1024]{2,1,0:T(...) custom-call(s32[1]{0:T(128)} %constant.369.clone.1.refs_0_, ...), custom_call_target="tpu_custom_call", output_to_operand_aliasing={{0}: (59, {}), {1}: (60, {}), {2}: (61, {}), {3}: (62, {}),... | custom-call | flops 24999999488 | bytes 1000000 | tf_op jit(solution)/shard_map/layer_backward/pallas_call | solution.py:177
  392.5 29.1 %layer_backward.7 = (bf16[4,256,1024]{2,1,0:T(8,128)(2,1)}, bf16[4,256,2048]{2,1,0:T(8,128)(2,1)}, bf16[4,256,2048]{2,1,0:T(8,128)(2,1)}, f32[4,8,1024]{2,1,0:T(...) custom-call(s32[1]{0:T(128)} %constant.352.clone.1.refs_0_, ...), custom_call_target="tpu_custom_call", output_to_operand_aliasing={{0}: (59, {}), {1}: (60, {}), {2}: (61, {}), {3}: (62, {}),... | custom-call | flops 24999999488 | bytes 1000000 | tf_op jit(solution)/shard_map/layer_backward/pallas_call | solution.py:177
  427.2 10.1 %mlp_backward.2 = (bf16[4,256,1024]{2,1,0:T(8,128)(2,1)}, bf16[4,256,2048]{2,1,0:T(8,128)(2,1)}, bf16[4,256,2048]{2,1,0:T(8,128)(2,1)}, f32[4,8,1024]{2,1,0:T(8,128)}, f32[256,1024]{1,0:T(8,128)S(1)}) custom-call(s32[1]{0:T(128)} %constant.370.clone.1.refs_0_, ...), custom_call_target="tpu_custom_call", output_to_operand_aliasing={{0}: (25, {}), {1}: (26, {}), {2}: (27, {}), {3}: (28, {})} | custom-call | flops 300000000 | bytes 1000000 | tf_op jit(solution)/shard_map/mlp_backward/pallas_call | solution.py:177
  437.4 10.0 %mlp_backward.3 = (bf16[4,256,1024]{2,1,0:T(8,128)(2,1)}, bf16[4,256,2048]{2,1,0:T(8,128)(2,1)}, bf16[4,256,2048]{2,1,0:T(8,128)(2,1)}, f32[4,8,1024]{2,1,0:T(8,128)}, f32[256,1024]{1,0:T(8,128)S(1)}) custom-call(s32[1]{0:T(128)} %constant.337.clone.1.refs_0_, ...), custom_call_target="tpu_custom_call", output_to_operand_aliasing={{0}: (25, {}), {1}: (26, {}), {2}: (27, {}), {3}: (28, {})} | custom-call | flops 300000000 | bytes 1000000 | tf_op jit(solution)/shard_map/mlp_backward/pallas_call | solution.py:177
  447.4 8.4 %weight_gradient.8 = (bf16[2,256,2048]{2,1,0:T(8,128)(2,1)}, bf16[2,256,2048]{2,1,0:T(8,128)(2,1)}) custom-call(s32[1]{0:T(128)} %bitcast.53.core_ref, bf16[4,256,1024]{2,1,0:T(8,128)(2,1)} %get-tuple-element.560.away_ref.stay_ref, bf16[4,256,1024]{2,1,0:T(8,128)(2,1)} %get-tuple-element.560.away_ref.stay_ref, bf16[4,256,2048]{2,1,0:T(8,128)(2,1)} %get-tuple-element.552.right_ref), custom_call_target="tpu_custom_call" | custom-call | flops 100000000 | bytes 1000000 | tf_op jit(solution)/shard_map/weight_gradient/pallas_call | solution.py:1031
  467.8 8.5 %weight_gradient.10 = (bf16[2,256,2048]{2,1,0:T(8,128)(2,1)}, bf16[2,256,2048]{2,1,0:T(8,128)(2,1)}) custom-call(s32[1]{0:T(128)} %bitcast.53.core_ref, bf16[4,256,1024]{2,1,0:T(8,128)(2,1)} %get-tuple-element.560.away_ref.stay_ref, bf16[4,256,1024]{2,1,0:T(8,128)(2,1)} %get-tuple-element.560.away_ref.stay_ref, ...), custom_call_target="tpu_custom_call" | custom-call | flops 100000000 | bytes 1000000 | tf_op jit(solution)/shard_map/weight_gradient/pallas_call | solution.py:1031
  481.3 21.2 %mixer_backward.2 = (bf16[4,256,1024]{2,1,0:T(8,128)(2,1)}, bf16[4,256,896]{2,1,0:T(8,128)(2,1)}, bf16[4,256,1792]{2,1,0:T(8,128)(2,1)}, bf16[4,256,1536]{2,1,0:...) custom-call(s32[1]{0:T(128)} %constant.370.clone.1.refs_0_, ...), custom_call_target="tpu_custom_call", output_to_operand_aliasing={{0}: (40, {}), {1}: (41, {}), {2}: (42, {}), {3}: (43, {}),... | custom-call | flops 24999999488 | bytes 1000000 | tf_op jit(solution)/shard_map/mixer_backward/pallas_call | solution.py:177
  518.4 20.9 %mixer_backward.3 = (bf16[4,256,1024]{2,1,0:T(8,128)(2,1)}, bf16[4,256,896]{2,1,0:T(8,128)(2,1)}, bf16[4,256,1792]{2,1,0:T(8,128)(2,1)}, bf16[4,256,1536]{2,1,0:...) custom-call(s32[1]{0:T(128)} %constant.337.clone.1.refs_0_, ...), custom_call_target="tpu_custom_call", output_to_operand_aliasing={{0}: (40, {}), {1}: (41, {}), {2}: (42, {}), {3}: (43, {}),... | custom-call | flops 24999999488 | bytes 1000000 | tf_op jit(solution)/shard_map/mixer_backward/pallas_call | solution.py:177
  587.5 14.9 %collective-permute-done.52 = bf16[256,2048]{1,0:T(8,128)(2,1)S(1)} collective-permute-done((bf16[256,2048]{1,0:T(8,128)(2,1)S(1)}, bf16[256,2048]{1,0:T(8,128)(2,1)S(1)}, u32[]{:S(2)}, u32[]{:S(2)}) %collective-permute-start.52) | collective-permute-done | bytes 1048608 | tf_op jit(solution)/shard_map/ppermute | solution.py:1214
  651.8 12.9 %collective-permute-done.58 = bf16[256,1792]{1,0:T(8,128)(2,1)} collective-permute-done((bf16[256,1792]{1,0:T(8,128)(2,1)}, bf16[256,1792]{1,0:T(8,128)(2,1)}, u32[]{:S(2)}, u32[]{:S(2)}) %collective-permute-start.58) | collective-permute-done | bytes 917536 | tf_op jit(solution)/shard_map/ppermute | solution.py:1132
  722.4 12.2 %collective-permute-done.81 = bf16[256,1536]{1,0:T(8,128)(2,1)S(1)} collective-permute-done((bf16[256,1536]{1,0:T(8,128)(2,1)S(1)}, bf16[256,1536]{1,0:T(8,128)(2,1)S(1)}, u32[]{:S(2)}, u32[]{:S(2)}) %collective-permute-start.81) | collective-permute-done | bytes 786464 | tf_op jit(solution)/shard_map/ppermute | solution.py:1226
  738.6 15.6 %collective-permute-done.78 = bf16[256,1792]{1,0:T(8,128)(2,1)S(1)} collective-permute-done((bf16[256,1792]{1,0:T(8,128)(2,1)S(1)}, bf16[256,1792]{1,0:T(8,128)(2,1)S(1)}, u32[]{:S(2)}, u32[]{:S(2)}) %collective-permute-start.78) | collective-permute-done | bytes 917536 | tf_op jit(solution)/shard_map/ppermute | solution.py:1226
  760.7 9.0 %collective-permute-done.83 = bf16[256,896]{1,0:T(8,128)(2,1)S(1)} collective-permute-done((bf16[256,896]{1,0:T(8,128)(2,1)S(1)}, bf16[256,896]{1,0:T(8,128)(2,1)S(1)}, u32[]{:S(2)}, u32[]{:S(2)}) %collective-permute-start.83) | collective-permute-done | bytes 458784 | tf_op jit(solution)/shard_map/ppermute | solution.py:1226
  (503 shorter events, 359.9 us)
Async XLA Ops:
  11.3 35.5 %collective-permute-start.6 = (bf16[256,896]{1,0:T(8,128)(2,1)S(1)}, bf16[256,896]{1,0:T(8,128)(2,1)}, u32[]{:S(2)}, u32[]{:S(2)}) collective-permute-start(bf16[256,896]{1,0:T(8,128)(2,1)S(1)} %concatenate.71.refs_8_.refs_9_), channel_id=1, source_target_pairs={{0,4},{4,0},{8,12},{12,8},{1,5},{5,1},{9,13},{13,9},{2,6},{6,2},{1... | collective-permute-start | bytes 1376264 | tf_op jit(solution)/shard_map/ppermute | solution.py:1132
  42.9 42.5 %collective-permute-start.19 = (bf16[512,1024]{1,0:T(8,128)(2,1)}, bf16[512,1024]{1,0:T(8,128)(2,1)}, u32[]{:S(2)}, u32[]{:S(2)}) collective-permute-start(bf16[512,1024]{1,0:T(8,128)(2,1)} %pad_maximum_fusion.refs_26_.refs_27_), channel_id=1, source_target_pairs={{0,4},{4,0},{8,12},{12,8},{1,5},{5,1},{9,13},{13,9},{2,6},{6,2},{1... | collective-permute-start | bytes 3145736 | tf_op jit(solution)/shard_map/ppermute | solution.py:1132
  85.4 52.5 %collective-permute-start.28 = (bf16[256,2048]{1,0:T(8,128)(2,1)}, bf16[256,2048]{1,0:T(8,128)(2,1)S(1)}, u32[]{:S(2)}, u32[]{:S(2)}) collective-permute-start(bf16[256,2048]{1,0:T(8,128)(2,1)} %bitcast.204), channel_id=1, source_target_pairs={{0,4},{4,0},{8,12},{12,8},{1,5},{5,1},{9,13},{13,9},{2,6},{6,2},{1... | collective-permute-start | bytes 3145736 | tf_op jit(solution)/shard_map/ppermute | solution.py:1132
  87.1 51.3 %collective-permute-start.31 = (bf16[512,1024]{1,0:T(8,128)(2,1)}, bf16[512,1024]{1,0:T(8,128)(2,1)S(1)}, u32[]{:S(2)}, u32[]{:S(2)}) collective-permute-start(bf16[512,1024]{1,0:T(8,128)(2,1)} %bitcast.218), channel_id=1, source_target_pairs={{0,4},{4,0},{8,12},{12,8},{1,5},{5,1},{9,13},{13,9},{2,6},{6,2},{1... | collective-permute-start | bytes 3145736 | tf_op jit(solution)/shard_map/ppermute | solution.py:1132
  87.3 51.7 %collective-permute-start.23 = (bf16[256,2048]{1,0:T(8,128)(2,1)S(1)}, bf16[256,2048]{1,0:T(8,128)(2,1)S(1)}, u32[]{:S(2)}, u32[]{:S(2)}) collective-permute-start(bf16[256,2048]{1,0:T(8,128)(2,1)S(1)} %bitcast.203), channel_id=1, source_target_pairs={{0,4},{4,0},{8,12},{12,8},{1,5},{5,1},{9,13},{13,9},{2,6},{6,2},{1... | collective-permute-start | bytes 3145736 | tf_op jit(solution)/shard_map/ppermute | solution.py:1132
  105.0 32.4 %collective-permute-start.25 = (bf16[128,2048]{1,0:T(8,128)(2,1)S(1)}, bf16[128,2048]{1,0:T(8,128)(2,1)S(1)}, u32[]{:S(2)}, u32[]{:S(2)}) collective-permute-start(bf16[128,2048]{1,0:T(8,128)(2,1)S(1)} %collective-permute-done.24.refs_7_.refs_34_.refs_35_.refs_9_), channel_id=1, source_target_pairs={{0,1},{1,0},{2,3},{3,2},{4,5},{5,4},{6,7},{7,6},{8,9},{9,8},{10,11... | collective-permute-start | bytes 1572872 | tf_op jit(solution)/shard_map/ppermute | solution.py:1132
  142.4 45.3 %collective-permute-start.5 = (bf16[256,1024]{1,0:T(8,128)(2,1)}, bf16[256,1024]{1,0:T(8,128)(2,1)S(1)}, u32[]{:S(2)}, u32[]{:S(2)}) collective-permute-start(bf16[256,1024]{1,0:T(8,128)(2,1)} %get-tuple-element.367), channel_id=1, source_target_pairs={{0,2},{1,3},{2,0},{3,1},{4,6},{5,7},{6,4},{7,5},{8,10},{9,11},{10,... | collective-permute-start | bytes 1572872 | tf_op jit(solution)/shard_map/ppermute | solution.py:1132
  155.4 43.6 %collective-permute-start.35 = (bf16[256,1024]{1,0:T(8,128)(2,1)S(1)}, bf16[256,1024]{1,0:T(8,128)(2,1)}, u32[]{:S(2)}, u32[]{:S(2)}) collective-permute-start(bf16[256,1024]{1,0:T(8,128)(2,1)S(1)} %get-tuple-element.394), channel_id=1, source_target_pairs={{0,16},{1,17},{2,18},{3,19},{4,20},{5,21},{6,22},{7,23},{8,24},{9,... | collective-permute-start | bytes 1572872 | tf_op jit(solution)/shard_map/ppermute | solution.py:1517
  320.3 32.7 %collective-permute-start.39 = (bf16[256,1024]{1,0:T(8,128)(2,1)}, bf16[256,1024]{1,0:T(8,128)(2,1)S(1)}, u32[]{:S(2)}, u32[]{:S(2)}) collective-permute-start(bf16[256,1024]{1,0:T(8,128)(2,1)} %get-tuple-element.494), channel_id=1, source_target_pairs={{16,0},{17,1},{18,2},{19,3},{20,4},{21,5},{22,6},{23,7},{24,8},{25... | collective-permute-start | bytes 1572872 | tf_op jit(solution)/shard_map/ppermute | solution.py:1579
  350.1 35.9 %collective-permute-start.38 = (bf16[256,1024]{1,0:T(8,128)(2,1)}, bf16[256,1024]{1,0:T(8,128)(2,1)}, u32[]{:S(2)}, u32[]{:S(2)}) collective-permute-start(bf16[256,1024]{1,0:T(8,128)(2,1)} %get-tuple-element.506), channel_id=1, source_target_pairs={{16,0},{17,1},{18,2},{19,3},{20,4},{21,5},{22,6},{23,7},{24,8},{25... | collective-permute-start | bytes 1572872 | tf_op jit(solution)/shard_map/ppermute | solution.py:1579
  383.1 44.0 %collective-permute-start.41 = (bf16[256,1024]{1,0:T(8,128)(2,1)}, bf16[256,1024]{1,0:T(8,128)(2,1)S(1)}, u32[]{:S(2)}, u32[]{:S(2)}) collective-permute-start(bf16[256,1024]{1,0:T(8,128)(2,1)} %get-tuple-element.519), channel_id=1, source_target_pairs={{16,0},{17,1},{18,2},{19,3},{20,4},{21,5},{22,6},{23,7},{24,8},{25... | collective-permute-start | bytes 1572872 | tf_op jit(solution)/shard_map/ppermute | solution.py:1579
  387.9 39.2 %collective-permute-start.42 = (bf16[256,1024]{1,0:T(8,128)(2,1)}, bf16[256,1024]{1,0:T(8,128)(2,1)}, u32[]{:S(2)}, u32[]{:S(2)}) collective-permute-start(bf16[256,1024]{1,0:T(8,128)(2,1)} %bitcast_select_fusion.3), channel_id=1, source_target_pairs={{0,3},{1,2},{2,1},{3,0},{4,7},{5,6},{6,5},{7,4},{8,11},{9,10},{10,... | collective-permute-start | bytes 1572872 | tf_op jit(solution)/shard_map/ppermute | solution.py:1132
  505.3 46.4 %collective-permute-start.49 = (bf16[256,2048]{1,0:T(8,128)(2,1)}, bf16[256,2048]{1,0:T(8,128)(2,1)}, u32[]{:S(2)}, u32[]{:S(2)}) collective-permute-start(bf16[256,2048]{1,0:T(8,128)(2,1)} %fusion.7), channel_id=1, source_target_pairs={{0,8},{4,12},{8,0},{12,4},{1,9},{5,13},{9,1},{13,5},{2,10},{6,14},... | collective-permute-start | bytes 3145736 | tf_op jit(solution)/shard_map/ppermute | solution.py:1132
  508.5 75.8 %collective-permute-start.53 = (bf16[256,2048]{1,0:T(8,128)(2,1)}, bf16[256,2048]{1,0:T(8,128)(2,1)}, u32[]{:S(2)}, u32[]{:S(2)}) collective-permute-start(bf16[256,2048]{1,0:T(8,128)(2,1)} %fusion.8), channel_id=1, source_target_pairs={{0,8},{4,12},{8,0},{12,4},{1,9},{5,13},{9,1},{13,5},{2,10},{6,14},... | collective-permute-start | bytes 3145736 | tf_op jit(solution)/shard_map/ppermute | solution.py:1132
  513.8 33.5 %collective-permute-start.50 = (bf16[512,1024]{1,0:T(8,128)(2,1)S(1)}, bf16[512,1024]{1,0:T(8,128)(2,1)}, u32[]{:S(2)}, u32[]{:S(2)}) collective-permute-start(bf16[512,1024]{1,0:T(8,128)(2,1)S(1)} %fusion.2), channel_id=1, source_target_pairs={{0,1},{3,2},{4,5},{7,6},{8,9},{11,10},{12,13},{15,14},{16,17},{19,... | collective-permute-start | bytes 3145736 | tf_op jit(solution)/shard_map/ppermute | solution.py:1214
  547.2 34.9 %collective-permute-start.54 = (bf16[2,256,1536]{2,1,0:T(8,128)(2,1)}, bf16[2,256,1536]{2,1,0:T(8,128)(2,1)}, u32[]{:S(2)}, u32[]{:S(2)}) collective-permute-start(bf16[2,256,1536]{2,1,0:T(8,128)(2,1)} %get-tuple-element.607), channel_id=1, source_target_pairs={{0,4},{4,0},{8,12},{12,8},{1,5},{5,1},{9,13},{13,9},{2,6},{6,2},{1... | collective-permute-start | bytes 4718600 | tf_op jit(solution)/shard_map/ppermute | solution.py:1132
  561.5 41.6 %collective-permute-start.51 = (bf16[2,384,1024]{2,1,0:T(8,128)(2,1)}, bf16[2,384,1024]{2,1,0:T(8,128)(2,1)}, u32[]{:S(2)}, u32[]{:S(2)}) collective-permute-start(bf16[2,384,1024]{2,1,0:T(8,128)(2,1)} %get-tuple-element.606), channel_id=1, source_target_pairs={{0,4},{4,0},{8,12},{12,8},{1,5},{5,1},{9,13},{13,9},{2,6},{6,2},{1... | collective-permute-start | bytes 4718600 | tf_op jit(solution)/shard_map/ppermute | solution.py:1132
  571.3 40.2 %collective-permute-start.57 = (bf16[2,256,1792]{2,1,0:T(8,128)(2,1)}, bf16[2,256,1792]{2,1,0:T(8,128)(2,1)S(1)}, u32[]{:S(2)}, u32[]{:S(2)}) collective-permute-start(bf16[2,256,1792]{2,1,0:T(8,128)(2,1)} %get-tuple-element.627), channel_id=1, source_target_pairs={{0,4},{4,0},{8,12},{12,8},{1,5},{5,1},{9,13},{13,9},{2,6},{6,2},{1... | collective-permute-start | bytes 5505032 | tf_op jit(solution)/shard_map/ppermute | solution.py:1132
  582.1 42.6 %collective-permute-start.48 = (bf16[256,1024]{1,0:T(8,128)(2,1)}, bf16[256,1024]{1,0:T(8,128)(2,1)}, u32[]{:S(2)}, u32[]{:S(2)}) collective-permute-start(bf16[256,1024]{1,0:T(8,128)(2,1)} %bitcast_select_fusion), channel_id=1, source_target_pairs={{0,1},{1,0},{2,3},{3,2},{4,5},{5,4},{6,7},{7,6},{8,9},{9,8},{10,11... | collective-permute-start | bytes 1572872 | tf_op jit(solution)/shard_map/ppermute | solution.py:1132
  584.3 37.3 %collective-permute-start.64 = (bf16[2,128,1024]{2,1,0:T(8,128)(2,1)}, bf16[2,128,1024]{2,1,0:T(8,128)(2,1)}, u32[]{:S(2)}, u32[]{:S(2)}) collective-permute-start(bf16[2,128,1024]{2,1,0:T(8,128)(2,1)} %get-tuple-element.637), channel_id=1, source_target_pairs={{0,4},{4,0},{8,12},{12,8},{1,5},{5,1},{9,13},{13,9},{2,6},{6,2},{1... | collective-permute-start | bytes 1572872 | tf_op jit(solution)/shard_map/ppermute | solution.py:1132
  624.7 74.9 %collective-permute-start.56 = (bf16[384,1024]{1,0:T(8,128)(2,1)S(1)}, bf16[384,1024]{1,0:T(8,128)(2,1)}, u32[]{:S(2)}, u32[]{:S(2)}) collective-permute-start(bf16[384,1024]{1,0:T(8,128)(2,1)S(1)} %fusion.12), channel_id=1, source_target_pairs={{0,8},{4,12},{8,0},{12,4},{1,9},{5,13},{9,1},{13,5},{2,10},{6,14},... | collective-permute-start | bytes 2359304 | tf_op jit(solution)/shard_map/ppermute | solution.py:1132
  626.1 38.6 %collective-permute-start.58 = (bf16[256,1792]{1,0:T(8,128)(2,1)}, bf16[256,1792]{1,0:T(8,128)(2,1)}, u32[]{:S(2)}, u32[]{:S(2)}) collective-permute-start(bf16[256,1792]{1,0:T(8,128)(2,1)} %fusion.9), channel_id=1, source_target_pairs={{0,8},{4,12},{8,0},{12,4},{1,9},{5,13},{9,1},{13,5},{2,10},{6,14},... | collective-permute-start | bytes 2752520 | tf_op jit(solution)/shard_map/ppermute | solution.py:1132
  716.0 38.2 %collective-permute-start.78 = (bf16[256,1792]{1,0:T(8,128)(2,1)S(1)}, bf16[256,1792]{1,0:T(8,128)(2,1)S(1)}, u32[]{:S(2)}, u32[]{:S(2)}) collective-permute-start(bf16[256,1792]{1,0:T(8,128)(2,1)S(1)} %add_convert_fusion.9), channel_id=1, source_target_pairs={{1,0},{2,3},{5,4},{6,7},{9,8},{10,11},{13,12},{14,15},{17,16},{18,... | collective-permute-start | bytes 2752520 | tf_op jit(solution)/shard_map/ppermute | solution.py:1226
  721.7 33.9 %collective-permute-start.77 = (bf16[384,1024]{1,0:T(8,128)(2,1)S(1)}, bf16[384,1024]{1,0:T(8,128)(2,1)S(1)}, u32[]{:S(2)}, u32[]{:S(2)}) collective-permute-start(bf16[384,1024]{1,0:T(8,128)(2,1)S(1)} %add_convert_fusion.13), channel_id=1, source_target_pairs={{1,2},{2,1},{5,6},{6,5},{9,10},{10,9},{13,14},{14,13},{17,18},{18,... | collective-permute-start | bytes 2359304 | tf_op jit(solution)/shard_map/ppermute | solution.py:1220
  (131 other events, 2723.0 us)

commit v4 on v3

--- a/solution.py
+++ b/solution.py
@@ -1278,32 +1278,6 @@
     tail = qw + 2 * kw + HALF
     total = ci + mi + tail
 
-    turns = jnp.arange(count, dtype=jnp.int32)
-    numbers = jnp.arange(order.shape[0], dtype=jnp.int32)
-    mine = device * count + turns
-    sources = jnp.sum(jnp.where(order[None, :] == mine[:, None], numbers[None, :], 0), axis=1)
-    target = lax.dynamic_slice_in_dim(order, device * count, count) // count % n_rep
-    anchor = sources // count % n_rep
-
-    def inverse(key):
-        return jnp.sum(jnp.where((key ^ rank)[None, :] == turns[:, None], turns[None, :], 0), axis=1)
-
-    send_at, keep_at = inverse(target), inverse(anchor)
-    own_lengths = jnp.take(lengths, jnp.take(sources, keep_at))
-    outgoing = [
-        jnp.where(
-            first,
-            lax.dynamic_index_in_dim(inputs, send_at[j], 0, keepdims=False),
-            lax.dynamic_index_in_dim(teacher, send_at[j], 0, keepdims=False),
-        )
-        for j in range(count)
-    ]
-    dealt = [outgoing[0]]
-
-    def deal(j, *earlier):
-        dealt.append(swap(after(outgoing[j], *earlier), "rep", j))
-
-
     def columns(flat):
         wide = -(-flat.size // rows)
         return jnp.pad(flat, (0, wide * rows - flat.size)).reshape(rows, wide)
@@ -1321,38 +1295,28 @@
     used = riders.shape[1]
     wide = -(-convs.size // rows)
     shard_first = jnp.concatenate(
-        [w_query[0], w_key[0], w_value[0], w_step[0], riders]
-        + [jnp.zeros((rows, HALF - heads - used), BF)],
+        [w_query[0], w_key[0], w_value[0], w_step[0]] + [jnp.zeros((rows, HALF - heads), BF)],
         axis=1,
     )
-    at = qw + 2 * kw + heads
     parity = rank % 2
     if quick:
         g_gate = gather_halves(w_ssm_gate[0], 0)
         g_conv = gather_halves(w_conv_in[0], 0)
-        g_first = gather_halves(shard_first, 0, g_gate[2:3], g_gate[3:4])
+        g_first = gather_halves(shard_first, 0, (), g_gate[3:4])
         shard_out = jnp.concatenate([w_ssm_out[0], w_attn_out[0]], axis=0)
-        g_out = gather_halves(shard_out, 1, g_conv[2:3], g_conv[3:4])
-        g_g = gather_halves(w_gate[0], 0, g_first[2:3], g_first[3:4])
+        g_out = gather_halves(shard_out, 1, g_gate[2:3], g_conv[3:4])
+        g_g = gather_halves(w_gate[0], 0, g_conv[2:3], g_first[3:4])
         g_u = gather_wholes(w_up[0], g_out[2], g_g[2])
-        deal(1, g_out[3])
-        deal(2, dealt[1])
-        g_gate, g_conv, g_first, g_out = (share_far(g) for g in (g_gate, g_conv, g_first, g_out))
+        g_gate, g_conv, g_first, g_out = (
+            share_far(g, g_out[3]) for g in (g_gate, g_conv, g_first, g_out)
+        )
         spots = [2 * fsdp, 2 * (fsdp ^ 1)]
         spots += [2 * (fsdp ^ k) + b for k in (2, 3) for b in (parity, 1 - parity)]
         spots = jnp.stack(spots).astype(jnp.int32)
-        cut = [piece[:, at : at + used] for piece in g_first]
-        swapped = [jnp.where(parity == 0, cut[i], cut[i + 1]) for i in (2, 4)]
-        swapped2 = [jnp.where(parity == 0, cut[i + 1], cut[i]) for i in (2, 4)]
-        blocks = jnp.stack(
-            [cut[0], cut[1]]
-            + [jnp.concatenate([a, b], axis=0) for a, b in zip(swapped, swapped2)]
-        )
+        far = swap(riders, "fsdp", 2)
+        blocks = jnp.stack([riders, swap(riders, "fsdp", 1), far, swap(far, "fsdp", 1)])
         ridden = jnp.take(blocks, jnp.arange(4, dtype=jnp.int32) ^ fsdp, axis=0)
     else:
-
-        for j in range(1, count - 1):
-            deal(j)
 
         def whole(shard):
             return lax.all_gather(shard, "fsdp", axis=0, tiled=True)
@@ -1363,7 +1327,43 @@
         )
         g_out = [jnp.concatenate([whole(w_ssm_out[0]), whole(w_attn_out[0])], axis=0)]
         spots = jnp.zeros((1,), jnp.int32)
-        ridden = g_first[0][:, at : at + used].reshape(n_fsdp, rows, used)
+        ridden = whole(riders).reshape(n_fsdp, rows, used)
+    if quick:
+        order = after(order, g_gate[3])
+
+    turns = jnp.arange(count, dtype=jnp.int32)
+    numbers = jnp.arange(order.shape[0], dtype=jnp.int32)
+    mine = device * count + turns
+    sources = jnp.sum(jnp.where(order[None, :] == mine[:, None], numbers[None, :], 0), axis=1)
+    target = lax.dynamic_slice_in_dim(order, device * count, count) // count % n_rep
+    anchor = sources // count % n_rep
+
+    def inverse(key):
+        return jnp.sum(jnp.where((key ^ rank)[None, :] == turns[:, None], turns[None, :], 0), axis=1)
+
+    send_at, keep_at = inverse(target), inverse(anchor)
+    own_lengths = jnp.take(lengths, jnp.take(sources, keep_at))
+    outgoing = [
+        jnp.where(
+            first,
+            lax.dynamic_index_in_dim(inputs, send_at[j], 0, keepdims=False),
+            lax.dynamic_index_in_dim(teacher, send_at[j], 0, keepdims=False),
+        )
+        for j in range(count)
+    ]
+    dealt = [outgoing[0]]
+
+    def deal(j, *earlier):
+        dealt.append(swap(after(outgoing[j], *earlier), "rep", j))
+
+
+    if quick:
+        deal(1, g_out[3])
+        deal(2, dealt[1])
+    else:
+        for j in range(1, count - 1):
+            deal(j)
+
     mixer_weights = [g_first, g_conv, g_gate, g_out]
     mlp_weights = None if quick else [g_g, g_u, g_down]
 
@@ -1470,8 +1470,6 @@
 
     def mlp_tick(tick, mlp_stacks):
         (hidden,) = chained(hiddens[tick])
-        if tick == 1:
-            hidden = after(hidden, dealt[2])
         mlp_stacks, low = mlp_forward_call(
             number(tick), plan, spots, hidden, vec, mlp_weights, mlp_stacks, ff
         )
@@ -1502,13 +1500,14 @@
     mix_stacks = mixer_tick(0, dealt[0], mix_stacks)
     if quick:
         g_down = gather_wholes(w_down[0], hiddens[0])
-    deal(count - 1, hiddens[0])
     mix_stacks = mixer_tick(1, hiddens[0], mix_stacks)
     if quick:
-        mlp_weights = [share_far(g, hiddens[1]) for g in (g_g, g_u, g_down)]
+        mlp_weights = [share_far(g, hiddens[1], dealt[2]) for g in (g_g, g_u, g_down)]
     for tick in range(steps):
         if tick < skew:
             mlp_stacks, low = mlp_tick(tick, mlp_stacks)
+            if tick == 0:
+                deal(count - 1, low)
         else:
             stacks, low = layer_tick(tick, low, mix_stacks + mlp_stacks)
             mix_stacks, mlp_stacks = stacks[: len(mix_stacks)], stacks[len(mix_stacks) :]
@@ -1635,11 +1634,9 @@
             chain(made)
 
     if quick:
-        stages("W1")
+        stages("W0", "W1", "A0", "W2", "B4")
         token.append(returned[2])
-        stages(
-            "W2", "W0", "A2", "B4", "A0", "A1", "L2", "B5"
-        )
+        stages("A2", "A1", "L0", "B5")
     else:
         stages("B4", "B5")
     mix_grads = state[0]
@@ -1684,12 +1681,12 @@
         chunks += [Reduction(*pair) for pair in late]
         chunks[6].riders = (riders, column)
         stages(
-            "W4", "M2", "L0", "W5", "W3", "W7", "O2", "A4", "L1", "M0", "A5", "A3", "W6", "A7"
+            "L1", "M0", "W4", "W7", "W3", "L2", "M1", "O0", "A4", "A7", "A3", "W6", "W5", "F0"
         )
         token.append(returned[1])
         stages(
-            "L4", "M1", "O0", "F2", "A6", "L3", "M4", "L7", "O1", "F0", "L6", "M3", "L5", "M7",
-            "O4", "F1", "M6", "O3", "M5", "F4", "O7", "O6", "F3", "O5", "F7", "F6", "F5"
+            "O1", "L3", "M2", "L7", "A5", "L4", "A6", "M3", "O2", "F1", "L5", "M4", "L6", "O3",
+            "F2", "M7", "M5", "O4", "M6", "F3", "O7", "O5", "F4", "O6", "F7", "F5", "F6"
         )
         reduced = [chunk.result for chunk in chunks]
         flat = reduced[6][:, column : column + spare].reshape(-1)

time: 809 us -> 762 us (0.942)
  waiting for transfers between devices: 170 us -> 154 us
  other arithmetic: 82.3 us -> 67.5 us
  local copies, waits for them, and re-layouts: 46.7 us -> 33 us
    ppermute x8, waiting for transfers between devices: 28.5 us -> 17.1 us  [line_in(): self.moved = lax.ppermute(self.stay, 'rep', [(0, 1), (3, 2)])]
    ppermute x53 -> x56, waiting for transfers between devices: 87 us -> 80 us  [swap(): lax.ppermute(block, axis, [(i, i ^ bit) for i in range(lax.axis_size(axis...]
    ppermute x53 -> x56, starting transfers between devices: 38.4 us -> 39.9 us  [swap(): lax.ppermute(block, axis, [(i, i ^ bit) for i in range(lax.axis_size(axis...]
  transfers between devices with their start and end apart: 86 -> 89, of which waited for: 25 -> 26; matrix products, arithmetic and copies ran while one was open for 15% -> 12% of each run, Pallas kernels for 38% -> 38%
where the time goes in v4:
time: 762 us; the launch traced here: 751 us
  Pallas kernels  362 us (48%)
  waiting for transfers between devices  154 us (20%)
  starting transfers between devices  104 us (14%)
  other arithmetic  67.5 us (9%)
  local copies, waits for them, and re-layouts  33 us (4%)
  between operations  22.2 us (3%)
  matrix products  9.05 us (1%)
    pallas_call x16, Pallas kernels, call(): pl.pallas_call(kernel, out_shape=[pltpu.HBM(s.shape, s.dtype) for s in st...  306 us
    ppermute x56, waiting for transfers between devices, swap(): lax.ppermute(block, axis, [(i, i ^ bit) for i in range(lax.axis_size(axis...  80 us
    pallas_call x8, Pallas kernels, weight_grad_halves(): pl.pallas_call(weight_kernel, out_shape=[shape, shape], grid_spec=grid, c...  55.9 us
    ppermute x8, waiting for transfers between devices, line_out(): self.moved = lax.ppermute(self.stay, 'rep', [(1, 0), (2, 3)])  53.3 us
    ppermute x56, starting transfers between devices, swap(): lax.ppermute(block, axis, [(i, i ^ bit) for i in range(lax.axis_size(axis...  39.9 us
    ppermute x8, starting transfers between devices, line_in(): self.moved = lax.ppermute(self.stay, 'rep', [(0, 1), (3, 2)])  33 us
    convert_element_type x24, other arithmetic, plus(): return (a.astype(F32) + b.astype(F32)).astype(BF)  20.9 us
    ppermute x8, waiting for transfers between devices, line_in(): self.moved = lax.ppermute(self.stay, 'rep', [(0, 1), (3, 2)])  17.1 us
  transfers between devices with their start and end apart: 89, of which 26 were waited for; matrix products, arithmetic and copies ran while one was open for 12% of the time, Pallas kernels for 38%

profile of v4, /device:TPU:0, one launch (start us, length us, event | category | flops | bytes accessed | tf_op | source)
XLA Modules:
  0.0 751.3 jit_solution(9978131715737651392)
XLA Ops:
  36.3 10.0 %collective-permute-done.2.refs_28_.refs_29_ = bf16[512,512]{1,0:T(8,128)(2,1)} collective-permute-done((bf16[512,512]{1,0:T(8,128)(2,1)}, bf16[512,512]{1,0:T(8,128)(2,1)}, u32[]{:S(2)}, u32[]{:S(2)}) %collective-permute-start.2) | collective-permute-done | bytes 524320 | tf_op jit(solution)/shard_map/ppermute | solution.py:1132
  49.0 12.3 %collective-permute-done.5.refs_29_.refs_30_ = bf16[512,512]{1,0:T(8,128)(2,1)} collective-permute-done((bf16[512,512]{1,0:T(8,128)(2,1)}, bf16[512,512]{1,0:T(8,128)(2,1)}, u32[]{:S(2)}, u32[]{:S(2)}) %collective-permute-start.5) | collective-permute-done | bytes 524320 | tf_op jit(solution)/shard_map/ppermute | solution.py:1132
  92.0 15.2 %mixer_forward.2 = (bf16[4,256,1024]{2,1,0:T(8,128)(2,1)}, bf16[4,256,1792]{2,1,0:T(8,128)(2,1)}, bf16[4,256,1792]{2,1,0:T(8,128)(2,1)}, bf16[4,256,1536]{2,1,0:...) custom-call(s32[1]{0:T(128)} %constant.359.clone.1.refs_0_, ...), custom_call_target="tpu_custom_call" | custom-call | flops 20000000000 | bytes 1000000 | tf_op jit(solution)/shard_map/mixer_forward/pallas_call | solution.py:177
  119.3 15.5 %mixer_forward.3 = (bf16[4,256,1024]{2,1,0:T(8,128)(2,1)}, bf16[4,256,1792]{2,1,0:T(8,128)(2,1)}, bf16[4,256,1792]{2,1,0:T(8,128)(2,1)}, bf16[4,256,1536]{2,1,0:...) custom-call(s32[1]{0:T(128)} %constant.364.clone.1.refs_0_, ...), custom_call_target="tpu_custom_call", output_to_operand_aliasing={{0}: (32, {}), {1}: (33, {}), {2}: (34, {}), {3}: (35, {}),... | custom-call | flops 20000000000 | bytes 1000000 | tf_op jit(solution)/shard_map/mixer_forward/pallas_call | solution.py:177
  167.3 8.3 %mlp_forward.3 = (bf16[4,256,1024]{2,1,0:T(8,128)(2,1)}, bf16[4,256,2048]{2,1,0:T(8,128)(2,1)}, bf16[4,256,2048]{2,1,0:T(8,128)(2,1)}, bf16[4,256,2048]{2,1,0:T(...) custom-call(s32[1]{0:T(128)} %constant.364.clone.1.refs_0_, ...), custom_call_target="tpu_custom_call", output_to_operand_aliasing={{0}: (19, {}), {1}: (20, {}), {2}: (21, {}), {3}: (22, {}),... | custom-call | flops 300000000 | bytes 1000000 | tf_op jit(solution)/shard_map/mlp_forward/pallas_call | solution.py:177
  182.4 21.3 %layer_forward.4 = (bf16[4,256,1024]{2,1,0:T(8,128)(2,1)}, bf16[4,256,1792]{2,1,0:T(8,128)(2,1)}, bf16[4,256,1792]{2,1,0:T(8,128)(2,1)}, bf16[4,256,1536]{2,1,0:...) custom-call(s32[1]{0:T(128)} %constant.367.clone.1.refs_0_, ...), custom_call_target="tpu_custom_call", output_to_operand_aliasing={{0}: (46, {}), {1}: (47, {}), {2}: (48, {}), {3}: (49, {}),... | custom-call | flops 20000000000 | bytes 1000000 | tf_op jit(solution)/shard_map/layer_forward/pallas_call | solution.py:177
  207.4 21.1 %layer_forward.5 = (bf16[4,256,1024]{2,1,0:T(8,128)(2,1)}, bf16[4,256,1792]{2,1,0:T(8,128)(2,1)}, bf16[4,256,1792]{2,1,0:T(8,128)(2,1)}, bf16[4,256,1536]{2,1,0:...) custom-call(s32[1]{0:T(128)} %constant.366.clone.1.refs_0_, ...), custom_call_target="tpu_custom_call", output_to_operand_aliasing={{0}: (46, {}), {1}: (47, {}), {2}: (48, {}), {3}: (49, {}),... | custom-call | flops 20000000000 | bytes 1000000 | tf_op jit(solution)/shard_map/layer_forward/pallas_call | solution.py:177
  232.0 19.9 %layer_forward.6 = (bf16[4,256,1024]{2,1,0:T(8,128)(2,1)}, bf16[4,256,1792]{2,1,0:T(8,128)(2,1)}, bf16[4,256,1792]{2,1,0:T(8,128)(2,1)}, bf16[4,256,1536]{2,1,0:...) custom-call(s32[1]{0:T(128)} %constant.368.clone.1.refs_0_, ...), custom_call_target="tpu_custom_call", output_to_operand_aliasing={{0}: (46, {}), {1}: (47, {}), {2}: (48, {}), {3}: (49, {}),... | custom-call | flops 20000000000 | bytes 1000000 | tf_op jit(solution)/shard_map/layer_forward/pallas_call | solution.py:177
  252.7 19.7 %layer_forward.7 = (bf16[4,256,1024]{2,1,0:T(8,128)(2,1)}, bf16[4,256,1792]{2,1,0:T(8,128)(2,1)}, bf16[4,256,1792]{2,1,0:T(8,128)(2,1)}, bf16[4,256,1536]{2,1,0:...) custom-call(s32[1]{0:T(128)} %constant.365.clone.1.refs_0_, ...), custom_call_target="tpu_custom_call", output_to_operand_aliasing={{0}: (46, {}), {1}: (47, {}), {2}: (48, {}), {3}: (49, {}),... | custom-call | flops 20000000000 | bytes 1000000 | tf_op jit(solution)/shard_map/layer_forward/pallas_call | solution.py:177
  272.5 28.1 %layer_backward.4 = (bf16[4,256,1024]{2,1,0:T(8,128)(2,1)}, bf16[4,256,2048]{2,1,0:T(8,128)(2,1)}, bf16[4,256,2048]{2,1,0:T(8,128)(2,1)}, f32[4,8,1024]{2,1,0:T(...) custom-call(s32[1]{0:T(128)} %constant.358.clone.1.refs_0_, ...), custom_call_target="tpu_custom_call" | custom-call | flops 24999999488 | bytes 1000000 | tf_op jit(solution)/shard_map/layer_backward/pallas_call | solution.py:177
  303.6 28.0 %layer_backward.5 = (bf16[4,256,1024]{2,1,0:T(8,128)(2,1)}, bf16[4,256,2048]{2,1,0:T(8,128)(2,1)}, bf16[4,256,2048]{2,1,0:T(8,128)(2,1)}, f32[4,8,1024]{2,1,0:T(...) custom-call(s32[1]{0:T(128)} %constant.355.clone.1.refs_0_, ...), custom_call_target="tpu_custom_call", output_to_operand_aliasing={{0}: (59, {}), {1}: (60, {}), {2}: (61, {}), {3}: (62, {}),... | custom-call | flops 24999999488 | bytes 1000000 | tf_op jit(solution)/shard_map/layer_backward/pallas_call | solution.py:177
  335.4 29.2 %layer_backward.6 = (bf16[4,256,1024]{2,1,0:T(8,128)(2,1)}, bf16[4,256,2048]{2,1,0:T(8,128)(2,1)}, bf16[4,256,2048]{2,1,0:T(8,128)(2,1)}, f32[4,8,1024]{2,1,0:T(...) custom-call(s32[1]{0:T(128)} %constant.369.clone.1.refs_0_, ...), custom_call_target="tpu_custom_call", output_to_operand_aliasing={{0}: (59, {}), {1}: (60, {}), {2}: (61, {}), {3}: (62, {}),... | custom-call | flops 24999999488 | bytes 1000000 | tf_op jit(solution)/shard_map/layer_backward/pallas_call | solution.py:177
  370.1 29.1 %layer_backward.7 = (bf16[4,256,1024]{2,1,0:T(8,128)(2,1)}, bf16[4,256,2048]{2,1,0:T(8,128)(2,1)}, bf16[4,256,2048]{2,1,0:T(8,128)(2,1)}, f32[4,8,1024]{2,1,0:T(...) custom-call(s32[1]{0:T(128)} %constant.354.clone.1.refs_0_, ...), custom_call_target="tpu_custom_call", output_to_operand_aliasing={{0}: (59, {}), {1}: (60, {}), {2}: (61, {}), {3}: (62, {}),... | custom-call | flops 24999999488 | bytes 1000000 | tf_op jit(solution)/shard_map/layer_backward/pallas_call | solution.py:177
  401.6 10.1 %mlp_backward.2 = (bf16[4,256,1024]{2,1,0:T(8,128)(2,1)}, bf16[4,256,2048]{2,1,0:T(8,128)(2,1)}, bf16[4,256,2048]{2,1,0:T(8,128)(2,1)}, f32[4,8,1024]{2,1,0:T(8,128)}, f32[256,1024]{1,0:T(8,128)S(1)}) custom-call(s32[1]{0:T(128)} %constant.370.clone.1.refs_0_, ...), custom_call_target="tpu_custom_call", output_to_operand_aliasing={{0}: (25, {}), {1}: (26, {}), {2}: (27, {}), {3}: (28, {})} | custom-call | flops 300000000 | bytes 1000000 | tf_op jit(solution)/shard_map/mlp_backward/pallas_call | solution.py:177
  415.4 10.0 %mlp_backward.3 = (bf16[4,256,1024]{2,1,0:T(8,128)(2,1)}, bf16[4,256,2048]{2,1,0:T(8,128)(2,1)}, bf16[4,256,2048]{2,1,0:T(8,128)(2,1)}, f32[4,8,1024]{2,1,0:T(8,128)}, f32[256,1024]{1,0:T(8,128)S(1)}) custom-call(s32[1]{0:T(128)} %constant.337.clone.1.refs_0_, ...), custom_call_target="tpu_custom_call", output_to_operand_aliasing={{0}: (25, {}), {1}: (26, {}), {2}: (27, {}), {3}: (28, {})} | custom-call | flops 300000000 | bytes 1000000 | tf_op jit(solution)/shard_map/mlp_backward/pallas_call | solution.py:177
  425.4 8.8 %weight_gradient.8 = (bf16[2,256,2048]{2,1,0:T(8,128)(2,1)}, bf16[2,256,2048]{2,1,0:T(8,128)(2,1)}) custom-call(s32[1]{0:T(128)} %bitcast.53.core_ref, bf16[4,256,1024]{2,1,0:T(8,128)(2,1)} %get-tuple-element.568.away_ref.stay_ref, bf16[4,256,1024]{2,1,0:T(8,128)(2,1)} %get-tuple-element.568.away_ref.stay_ref, bf16[4,256,2048]{2,1,0:T(8,128)(2,1)} %get-tuple-element.564.right_ref), custom_call_target="tpu_custom_call" | custom-call | flops 100000000 | bytes 1000000 | tf_op jit(solution)/shard_map/weight_gradient/pallas_call | solution.py:1031
  441.3 8.4 %weight_gradient.9 = (bf16[2,256,2048]{2,1,0:T(8,128)(2,1)}, bf16[2,256,2048]{2,1,0:T(8,128)(2,1)}) custom-call(s32[1]{0:T(128)} %bitcast.53.core_ref, bf16[4,256,1024]{2,1,0:T(8,128)(2,1)} %get-tuple-element.568.away_ref.stay_ref, bf16[4,256,1024]{2,1,0:T(8,128)(2,1)} %get-tuple-element.568.away_ref.stay_ref, bf16[4,256,2048]{2,1,0:T(8,128)(2,1)} %get-tuple-element.569.right_ref), custom_call_target="tpu_custom_call" | custom-call | flops 100000000 | bytes 1000000 | tf_op jit(solution)/shard_map/weight_gradient/pallas_call | solution.py:1031
  462.3 21.2 %mixer_backward.2 = (bf16[4,256,1024]{2,1,0:T(8,128)(2,1)}, bf16[4,256,896]{2,1,0:T(8,128)(2,1)}, bf16[4,256,1792]{2,1,0:T(8,128)(2,1)}, bf16[4,256,1536]{2,1,0:...) custom-call(s32[1]{0:T(128)} %constant.370.clone.1.refs_0_, ...), custom_call_target="tpu_custom_call", output_to_operand_aliasing={{0}: (40, {}), {1}: (41, {}), {2}: (42, {}), {3}: (43, {}),... | custom-call | flops 24999999488 | bytes 1000000 | tf_op jit(solution)/shard_map/mixer_backward/pallas_call | solution.py:177
  500.5 21.0 %mixer_backward.3 = (bf16[4,256,1024]{2,1,0:T(8,128)(2,1)}, bf16[4,256,896]{2,1,0:T(8,128)(2,1)}, bf16[4,256,1792]{2,1,0:T(8,128)(2,1)}, bf16[4,256,1536]{2,1,0:...) custom-call(s32[1]{0:T(128)} %constant.337.clone.1.refs_0_, ...), custom_call_target="tpu_custom_call", output_to_operand_aliasing={{0}: (40, {}), {1}: (41, {}), {2}: (42, {}), {3}: (43, {}),... | custom-call | flops 24999999488 | bytes 1000000 | tf_op jit(solution)/shard_map/mixer_backward/pallas_call | solution.py:177
  560.2 8.9 %collective-permute-start.64 = (bf16[512,1024]{1,0:T(8,128)(2,1)S(1)}, bf16[512,1024]{1,0:T(8,128)(2,1)}, u32[]{:S(2)}, u32[]{:S(2)}) collective-permute-start(bf16[512,1024]{1,0:T(8,128)(2,1)S(1)} %fusion), channel_id=1, source_target_pairs={{0,1},{3,2},{4,5},{7,6},{8,9},{11,10},{12,13},{15,14},{16,17},{19,... | collective-permute-start | bytes 3145736 | tf_op jit(solution)/shard_map/ppermute | solution.py:1214
  607.1 11.0 %collective-permute-done.61 = bf16[256,1536]{1,0:T(8,128)(2,1)S(1)} collective-permute-done((bf16[256,1536]{1,0:T(8,128)(2,1)S(1)}, bf16[256,1536]{1,0:T(8,128)(2,1)S(1)}, u32[]{:S(2)}, u32[]{:S(2)}) %collective-permute-start.61) | collective-permute-done | bytes 786464 | tf_op jit(solution)/shard_map/ppermute | solution.py:1132
  679.6 11.4 %collective-permute-done.84 = bf16[256,1792]{1,0:T(8,128)(2,1)S(1)} collective-permute-done((bf16[256,1792]{1,0:T(8,128)(2,1)S(1)}, bf16[256,1792]{1,0:T(8,128)(2,1)S(1)}, u32[]{:S(2)}, u32[]{:S(2)}) %collective-permute-start.84) | collective-permute-done | bytes 917536 | tf_op jit(solution)/shard_map/ppermute | solution.py:1226
  695.4 12.5 %collective-permute-done.81 = bf16[256,1536]{1,0:T(8,128)(2,1)S(1)} collective-permute-done((bf16[256,1536]{1,0:T(8,128)(2,1)S(1)}, bf16[256,1536]{1,0:T(8,128)(2,1)S(1)}, u32[]{:S(2)}, u32[]{:S(2)}) %collective-permute-start.81) | collective-permute-done | bytes 786464 | tf_op jit(solution)/shard_map/ppermute | solution.py:1226
  714.3 16.0 %collective-permute-done.86 = bf16[384,1024]{1,0:T(8,128)(2,1)S(1)} collective-permute-done((bf16[384,1024]{1,0:T(8,128)(2,1)S(1)}, bf16[384,1024]{1,0:T(8,128)(2,1)S(1)}, u32[]{:S(2)}, u32[]{:S(2)}) %collective-permute-start.86) | collective-permute-done | bytes 786464 | tf_op jit(solution)/shard_map/ppermute | solution.py:1226
  (525 shorter events, 332.1 us)
Async XLA Ops:
  12.6 35.9 %collective-permute-start.11 = (bf16[256,896]{1,0:T(8,128)(2,1)S(1)}, bf16[256,896]{1,0:T(8,128)(2,1)}, u32[]{:S(2)}, u32[]{:S(2)}) collective-permute-start(bf16[256,896]{1,0:T(8,128)(2,1)S(1)} %concatenate.67.refs_8_.refs_9_), channel_id=1, source_target_pairs={{0,4},{4,0},{8,12},{12,8},{1,5},{5,1},{9,13},{13,9},{2,6},{6,2},{1... | collective-permute-start | bytes 1376264 | tf_op jit(solution)/shard_map/ppermute | solution.py:1132
  20.4 47.3 %collective-permute-start.16 = (bf16[256,1792]{1,0:T(8,128)(2,1)}, bf16[256,1792]{1,0:T(8,128)(2,1)}, u32[]{:S(2)}, u32[]{:S(2)}) collective-permute-start(bf16[256,1792]{1,0:T(8,128)(2,1)} %bitcast.229), channel_id=1, source_target_pairs={{0,4},{4,0},{8,12},{12,8},{1,5},{5,1},{9,13},{13,9},{2,6},{6,2},{1... | collective-permute-start | bytes 2752520 | tf_op jit(solution)/shard_map/ppermute | solution.py:1132
  36.2 38.5 %collective-permute-start.22 = (bf16[512,1024]{1,0:T(8,128)(2,1)S(1)}, bf16[512,1024]{1,0:T(8,128)(2,1)}, u32[]{:S(2)}, u32[]{:S(2)}) collective-permute-start(bf16[512,1024]{1,0:T(8,128)(2,1)S(1)} %pad_maximum_fusion.refs_26_.refs_27_), channel_id=1, source_target_pairs={{0,4},{4,0},{8,12},{12,8},{1,5},{5,1},{9,13},{13,9},{2,6},{6,2},{1... | collective-permute-start | bytes 3145736 | tf_op jit(solution)/shard_map/ppermute | solution.py:1132
  88.7 54.5 %collective-permute-start.30 = (bf16[256,2048]{1,0:T(8,128)(2,1)S(1)}, bf16[256,2048]{1,0:T(8,128)(2,1)S(1)}, u32[]{:S(2)}, u32[]{:S(2)}) collective-permute-start(bf16[256,2048]{1,0:T(8,128)(2,1)S(1)} %bitcast.213), channel_id=1, source_target_pairs={{0,4},{4,0},{8,12},{12,8},{1,5},{5,1},{9,13},{13,9},{2,6},{6,2},{1... | collective-permute-start | bytes 3145736 | tf_op jit(solution)/shard_map/ppermute | solution.py:1132
  89.2 54.5 %collective-permute-start.33 = (bf16[512,1024]{1,0:T(8,128)(2,1)S(1)}, bf16[512,1024]{1,0:T(8,128)(2,1)S(1)}, u32[]{:S(2)}, u32[]{:S(2)}) collective-permute-start(bf16[512,1024]{1,0:T(8,128)(2,1)S(1)} %bitcast.227), channel_id=1, source_target_pairs={{0,4},{4,0},{8,12},{12,8},{1,5},{5,1},{9,13},{13,9},{2,6},{6,2},{1... | collective-permute-start | bytes 3145736 | tf_op jit(solution)/shard_map/ppermute | solution.py:1132
  89.6 53.5 %collective-permute-start.27 = (bf16[128,2048]{1,0:T(8,128)(2,1)S(1)}, bf16[128,2048]{1,0:T(8,128)(2,1)S(1)}, u32[]{:S(2)}, u32[]{:S(2)}) collective-permute-start(bf16[128,2048]{1,0:T(8,128)(2,1)S(1)} %collective-permute-done.26.refs_7_.refs_34_.refs_35_.refs_9_), channel_id=1, source_target_pairs={{0,1},{1,0},{2,3},{3,2},{4,5},{5,4},{6,7},{7,6},{8,9},{9,8},{10,11... | collective-permute-start | bytes 1572872 | tf_op jit(solution)/shard_map/ppermute | solution.py:1132
  175.7 30.7 %collective-permute-start.37 = (bf16[256,1024]{1,0:T(8,128)(2,1)S(1)}, bf16[256,1024]{1,0:T(8,128)(2,1)S(1)}, u32[]{:S(2)}, u32[]{:S(2)}) collective-permute-start(bf16[256,1024]{1,0:T(8,128)(2,1)S(1)} %get-tuple-element.417), channel_id=1, source_target_pairs={{0,16},{1,17},{2,18},{3,19},{4,20},{5,21},{6,22},{7,23},{8,24},{9,... | collective-permute-start | bytes 1572872 | tf_op jit(solution)/shard_map/ppermute | solution.py:1516
  301.9 32.7 %collective-permute-start.42 = (bf16[256,1024]{1,0:T(8,128)(2,1)}, bf16[256,1024]{1,0:T(8,128)(2,1)S(1)}, u32[]{:S(2)}, u32[]{:S(2)}) collective-permute-start(bf16[256,1024]{1,0:T(8,128)(2,1)} %get-tuple-element.508), channel_id=1, source_target_pairs={{16,0},{17,1},{18,2},{19,3},{20,4},{21,5},{22,6},{23,7},{24,8},{25... | collective-permute-start | bytes 1572872 | tf_op jit(solution)/shard_map/ppermute | solution.py:1578
  331.7 35.9 %collective-permute-start.41 = (bf16[256,1024]{1,0:T(8,128)(2,1)}, bf16[256,1024]{1,0:T(8,128)(2,1)S(1)}, u32[]{:S(2)}, u32[]{:S(2)}) collective-permute-start(bf16[256,1024]{1,0:T(8,128)(2,1)} %get-tuple-element.520), channel_id=1, source_target_pairs={{16,0},{17,1},{18,2},{19,3},{20,4},{21,5},{22,6},{23,7},{24,8},{25... | collective-permute-start | bytes 1572872 | tf_op jit(solution)/shard_map/ppermute | solution.py:1578
  364.7 36.1 %collective-permute-start.44 = (bf16[256,1024]{1,0:T(8,128)(2,1)}, bf16[256,1024]{1,0:T(8,128)(2,1)S(1)}, u32[]{:S(2)}, u32[]{:S(2)}) collective-permute-start(bf16[256,1024]{1,0:T(8,128)(2,1)} %get-tuple-element.533), channel_id=1, source_target_pairs={{16,0},{17,1},{18,2},{19,3},{20,4},{21,5},{22,6},{23,7},{24,8},{25... | collective-permute-start | bytes 1572872 | tf_op jit(solution)/shard_map/ppermute | solution.py:1578
  368.8 32.0 %collective-permute-start.45 = (bf16[256,1024]{1,0:T(8,128)(2,1)S(1)}, bf16[256,1024]{1,0:T(8,128)(2,1)S(1)}, u32[]{:S(2)}, u32[]{:S(2)}) collective-permute-start(bf16[256,1024]{1,0:T(8,128)(2,1)S(1)} %bitcast_select_fusion.3), channel_id=1, source_target_pairs={{0,3},{1,2},{2,1},{3,0},{4,7},{5,6},{6,5},{7,4},{8,11},{9,10},{10,... | collective-permute-start | bytes 1572872 | tf_op jit(solution)/shard_map/ppermute | solution.py:1132
  441.2 48.3 %collective-permute-start.50 = (bf16[256,1024]{1,0:T(8,128)(2,1)S(1)}, bf16[256,1024]{1,0:T(8,128)(2,1)S(1)}, u32[]{:S(2)}, u32[]{:S(2)}) collective-permute-start(bf16[256,1024]{1,0:T(8,128)(2,1)S(1)} %bitcast_select_fusion.2), channel_id=1, source_target_pairs={{0,2},{1,3},{2,0},{3,1},{4,6},{5,7},{6,4},{7,5},{8,10},{9,11},{10,... | collective-permute-start | bytes 1572872 | tf_op jit(solution)/shard_map/ppermute | solution.py:1132
  449.6 41.6 %collective-permute-start.48 = (bf16[2,256,2048]{2,1,0:T(8,128)(2,1)}, bf16[2,256,2048]{2,1,0:T(8,128)(2,1)}, u32[]{:S(2)}, u32[]{:S(2)}) collective-permute-start(bf16[2,256,2048]{2,1,0:T(8,128)(2,1)} %get-tuple-element.573), channel_id=1, source_target_pairs={{0,4},{4,0},{8,12},{12,8},{1,5},{5,1},{9,13},{13,9},{2,6},{6,2},{1... | collective-permute-start | bytes 6291464 | tf_op jit(solution)/shard_map/ppermute | solution.py:1132
  452.7 42.7 %collective-permute-start.47 = (bf16[256,2048]{1,0:T(8,128)(2,1)S(1)}, bf16[256,2048]{1,0:T(8,128)(2,1)S(1)}, u32[]{:S(2)}, u32[]{:S(2)}) collective-permute-start(bf16[256,2048]{1,0:T(8,128)(2,1)S(1)} %fusion.6), channel_id=1, source_target_pairs={{0,8},{4,12},{8,0},{12,4},{1,9},{5,13},{9,1},{13,5},{2,10},{6,14},... | collective-permute-start | bytes 3145736 | tf_op jit(solution)/shard_map/ppermute | solution.py:1132
  485.6 106.6 %collective-permute-start.51 = (bf16[256,1024]{1,0:T(8,128)(2,1)}, bf16[256,1024]{1,0:T(8,128)(2,1)}, u32[]{:S(2)}, u32[]{:S(2)}) collective-permute-start(bf16[256,1024]{1,0:T(8,128)(2,1)} %bitcast_select_fusion), channel_id=1, source_target_pairs={{0,1},{1,0},{2,3},{3,2},{4,5},{5,4},{6,7},{7,6},{8,9},{9,8},{10,11... | collective-permute-start | bytes 1572872 | tf_op jit(solution)/shard_map/ppermute | solution.py:1132
  500.1 47.5 %collective-permute-start.59 = (bf16[512,1024]{1,0:T(8,128)(2,1)}, bf16[512,1024]{1,0:T(8,128)(2,1)}, u32[]{:S(2)}, u32[]{:S(2)}) collective-permute-start(bf16[512,1024]{1,0:T(8,128)(2,1)} %fusion.7), channel_id=1, source_target_pairs={{0,8},{4,12},{8,0},{12,4},{1,9},{5,13},{9,1},{13,5},{2,10},{6,14},... | collective-permute-start | bytes 3145736 | tf_op jit(solution)/shard_map/ppermute | solution.py:1132
  551.9 37.6 %collective-permute-start.67 = (bf16[256,2048]{1,0:T(8,128)(2,1)}, bf16[256,2048]{1,0:T(8,128)(2,1)}, u32[]{:S(2)}, u32[]{:S(2)}) collective-permute-start(bf16[256,2048]{1,0:T(8,128)(2,1)} %add_convert_fusion.3), channel_id=1, source_target_pairs={{1,0},{2,3},{5,4},{6,7},{9,8},{10,11},{13,12},{14,15},{17,16},{18,... | collective-permute-start | bytes 3145736 | tf_op jit(solution)/shard_map/ppermute | solution.py:1226
  556.2 36.7 %collective-permute-start.66 = (bf16[256,2048]{1,0:T(8,128)(2,1)S(1)}, bf16[256,2048]{1,0:T(8,128)(2,1)}, u32[]{:S(2)}, u32[]{:S(2)}) collective-permute-start(bf16[256,2048]{1,0:T(8,128)(2,1)S(1)} %add_convert_fusion.4), channel_id=1, source_target_pairs={{1,2},{2,1},{5,6},{6,5},{9,10},{10,9},{13,14},{14,13},{17,18},{18,... | collective-permute-start | bytes 3145736 | tf_op jit(solution)/shard_map/ppermute | solution.py:1220
  560.2 37.8 %collective-permute-start.64 = (bf16[512,1024]{1,0:T(8,128)(2,1)S(1)}, bf16[512,1024]{1,0:T(8,128)(2,1)}, u32[]{:S(2)}, u32[]{:S(2)}) collective-permute-start(bf16[512,1024]{1,0:T(8,128)(2,1)S(1)} %fusion), channel_id=1, source_target_pairs={{0,1},{3,2},{4,5},{7,6},{8,9},{11,10},{12,13},{15,14},{16,17},{19,... | collective-permute-start | bytes 3145736 | tf_op jit(solution)/shard_map/ppermute | solution.py:1214
  598.0 34.2 %collective-permute-start.71 = (bf16[256,2048]{1,0:T(8,128)(2,1)S(1)}, bf16[256,2048]{1,0:T(8,128)(2,1)S(1)}, u32[]{:S(2)}, u32[]{:S(2)}) collective-permute-start(bf16[256,2048]{1,0:T(8,128)(2,1)S(1)} %add_convert_fusion.2), channel_id=1, source_target_pairs={{1,0},{2,3},{5,4},{6,7},{9,8},{10,11},{13,12},{14,15},{17,16},{18,... | collective-permute-start | bytes 3145736 | tf_op jit(solution)/shard_map/ppermute | solution.py:1226
  618.1 50.5 %collective-permute-start.77 = (bf16[128,1024]{1,0:T(8,128)(2,1)S(1)}, bf16[128,1024]{1,0:T(8,128)(2,1)S(1)}, u32[]{:S(2)}, u32[]{:S(2)}) collective-permute-start(bf16[128,1024]{1,0:T(8,128)(2,1)S(1)} %fusion.14), channel_id=1, source_target_pairs={{0,1},{3,2},{4,5},{7,6},{8,9},{11,10},{12,13},{15,14},{16,17},{19,... | collective-permute-start | bytes 786440 | tf_op jit(solution)/shard_map/ppermute | solution.py:1214
  671.9 36.0 %collective-permute-start.81 = (bf16[256,1536]{1,0:T(8,128)(2,1)S(1)}, bf16[256,1536]{1,0:T(8,128)(2,1)S(1)}, u32[]{:S(2)}, u32[]{:S(2)}) collective-permute-start(bf16[256,1536]{1,0:T(8,128)(2,1)S(1)} %add_convert_fusion.13), channel_id=1, source_target_pairs={{1,0},{2,3},{5,4},{6,7},{9,8},{10,11},{13,12},{14,15},{17,16},{18,... | collective-permute-start | bytes 2359304 | tf_op jit(solution)/shard_map/ppermute | solution.py:1226
  678.9 30.2 %collective-permute-start.80 = (bf16[256,896]{1,0:T(8,128)(2,1)S(1)}, bf16[256,896]{1,0:T(8,128)(2,1)S(1)}, u32[]{:S(2)}, u32[]{:S(2)}) collective-permute-start(bf16[256,896]{1,0:T(8,128)(2,1)S(1)} %add_convert_fusion.19), channel_id=1, source_target_pairs={{1,2},{2,1},{5,6},{6,5},{9,10},{10,9},{13,14},{14,13},{17,18},{18,... | collective-permute-start | bytes 1376264 | tf_op jit(solution)/shard_map/ppermute | solution.py:1220
  694.1 36.3 %collective-permute-start.86 = (bf16[384,1024]{1,0:T(8,128)(2,1)S(1)}, bf16[384,1024]{1,0:T(8,128)(2,1)S(1)}, u32[]{:S(2)}, u32[]{:S(2)}) collective-permute-start(bf16[384,1024]{1,0:T(8,128)(2,1)S(1)} %add_convert_fusion.12), channel_id=1, source_target_pairs={{1,0},{2,3},{5,4},{6,7},{9,8},{10,11},{13,12},{14,15},{17,16},{18,... | collective-permute-start | bytes 2359304 | tf_op jit(solution)/shard_map/ppermute | solution.py:1226
  (145 other events, 2668.4 us)

commit v5 on v4

--- a/solution.py
+++ b/solution.py
@@ -1306,7 +1306,7 @@
         shard_out = jnp.concatenate([w_ssm_out[0], w_attn_out[0]], axis=0)
         g_out = gather_halves(shard_out, 1, g_gate[2:3], g_conv[3:4])
         g_g = gather_halves(w_gate[0], 0, g_conv[2:3], g_first[3:4])
-        g_u = gather_wholes(w_up[0], g_out[2], g_g[2])
+        g_u = gather_wholes(w_up[0], g_out[2])
         g_gate, g_conv, g_first, g_out = (
             share_far(g, g_out[3]) for g in (g_gate, g_conv, g_first, g_out)
         )
@@ -1497,6 +1497,8 @@
             ff,
         )
 
+    if quick:
+        dealt[0] = after(dealt[0], dealt[1])
     mix_stacks = mixer_tick(0, dealt[0], mix_stacks)
     if quick:
         g_down = gather_wholes(w_down[0], hiddens[0])
@@ -1612,6 +1614,9 @@
         chain(d_input)
         send_back(turn, d_input)
 
+    loss_part = jnp.sum(mlp_grads[3][:, 1])[None]
+    loss_part = jnp.where(first, lax.ppermute(loss_part, "section", [(1, 0)]), loss_part)
+
     for turn in range(count, steps):
         mlp_grads, d_hidden = mlp_turn(turn, mlp_grads)
         chain(d_hidden)
@@ -1634,9 +1639,13 @@
             chain(made)
 
     if quick:
-        stages("W0", "W1", "A0", "W2", "B4")
+        stages(
+            "W2", "W0", "W1", "A0", "B4"
+        )
         token.append(returned[2])
-        stages("A2", "A1", "L0", "B5")
+        stages(
+            "A1", "A2", "L0", "B5"
+        )
     else:
         stages("B4", "B5")
     mix_grads = state[0]
@@ -1656,7 +1665,7 @@
             mix_sum[V_SBIAS, :heads],
             mix_sum[V_DECAY, :heads],
             jnp.sum(mix_sum[V_SKIP, :mi].reshape(heads, HD), axis=1),
-            jnp.sum(mlp_sum[1])[None],
+            loss_part,
         ]
     )
 
@@ -1681,12 +1690,12 @@
         chunks += [Reduction(*pair) for pair in late]
         chunks[6].riders = (riders, column)
         stages(
-            "L1", "M0", "W4", "W7", "W3", "L2", "M1", "O0", "A4", "A7", "A3", "W6", "W5", "F0"
+            "L1", "M0", "W7", "W4", "W3", "L2", "M1", "O0", "A4", "A3", "A7", "W6", "O1", "W5"
         )
         token.append(returned[1])
         stages(
-            "O1", "L3", "M2", "L7", "A5", "L4", "A6", "M3", "O2", "F1", "L5", "M4", "L6", "O3",
-            "F2", "M7", "M5", "O4", "M6", "F3", "O7", "O5", "F4", "O6", "F7", "F5", "F6"
+            "F0", "M2", "L3", "A6", "A5", "L4", "O2", "F1", "M3", "L5", "M4", "F2", "L7", "O3",
+            "M5", "L6", "O4", "F3", "O5", "M7", "F4", "M6", "F5", "O7", "O6", "F7", "F6"
         )
         reduced = [chunk.result for chunk in chunks]
         flat = reduced[6][:, column : column + spare].reshape(-1)
@@ -1708,7 +1717,7 @@
         parts.append(flat[begin : begin + cut])
         begin += cut
     convs = parts[0].reshape(taps + 1, -1)
-    loss = jnp.where(first, lax.ppermute(parts[-1], "section", [(1, 0)]), parts[-1])[0]
+    loss = parts[-1][0]
 
     restored = jnp.zeros((count, length, width), BF)
     for j in range(count):

time: 762 us -> 787 us (1.033)
  starting transfers between devices: 104 us -> 124 us
  waiting for transfers between devices: 154 us -> 138 us
  other arithmetic: 67.5 us -> 81.7 us
    ppermute x8, starting transfers between devices: 33 us -> 54.5 us  [line_in(): self.moved = lax.ppermute(self.stay, 'rep', [(0, 1), (3, 2)])]
    ppermute x56, waiting for transfers between devices: 80 us -> 70.2 us  [swap(): lax.ppermute(block, axis, [(i, i ^ bit) for i in range(lax.axis_size(axis...]
  transfers between devices with their start and end apart: 89 -> 89, of which waited for: 26 -> 21; matrix products, arithmetic and copies ran while one was open for 12% -> 14% of each run, Pallas kernels for 38% -> 36%
where the time goes in v5:
time: 787 us; the launch traced here: 776 us
  Pallas kernels  361 us (46%)
  waiting for transfers between devices  138 us (18%)
  starting transfers between devices  124 us (16%)
  other arithmetic  81.7 us (10%)
  local copies, waits for them, and re-layouts  37.8 us (5%)
  between operations  22.8 us (3%)
  matrix products  9.04 us (1%)
    pallas_call x16, Pallas kernels, call(): pl.pallas_call(kernel, out_shape=[pltpu.HBM(s.shape, s.dtype) for s in st...  306 us
    ppermute x56, waiting for transfers between devices, swap(): lax.ppermute(block, axis, [(i, i ^ bit) for i in range(lax.axis_size(axis...  70.2 us
    pallas_call x8, Pallas kernels, weight_grad_halves(): pl.pallas_call(weight_kernel, out_shape=[shape, shape], grid_spec=grid, c...  55.4 us
    ppermute x8, starting transfers between devices, line_in(): self.moved = lax.ppermute(self.stay, 'rep', [(0, 1), (3, 2)])  54.5 us
    ppermute x8, waiting for transfers between devices, line_out(): self.moved = lax.ppermute(self.stay, 'rep', [(1, 0), (2, 3)])  53.7 us
    ppermute x56, starting transfers between devices, swap(): lax.ppermute(block, axis, [(i, i ^ bit) for i in range(lax.axis_size(axis...  38 us
    convert_element_type x24, other arithmetic, plus(): return (a.astype(F32) + b.astype(F32)).astype(BF)  27.7 us
  transfers between devices with their start and end apart: 89, of which 21 were waited for; matrix products, arithmetic and copies ran while one was open for 14% of the time, Pallas kernels for 36%

profile of v5, /device:TPU:0, one launch (start us, length us, event | category | flops | bytes accessed | tf_op | source)
XLA Modules:
  0.0 775.5 jit_solution(8570824522482704233)
XLA Ops:
  87.2 15.2 %mixer_forward.2 = (bf16[4,256,1024]{2,1,0:T(8,128)(2,1)}, bf16[4,256,1792]{2,1,0:T(8,128)(2,1)}, bf16[4,256,1792]{2,1,0:T(8,128)(2,1)}, bf16[4,256,1536]{2,1,0:...) custom-call(s32[1]{0:T(128)} %constant.359.clone.1.refs_0_, ...), custom_call_target="tpu_custom_call" | custom-call | flops 20000000000 | bytes 1000000 | tf_op jit(solution)/shard_map/mixer_forward/pallas_call | solution.py:177
  113.7 15.5 %mixer_forward.3 = (bf16[4,256,1024]{2,1,0:T(8,128)(2,1)}, bf16[4,256,1792]{2,1,0:T(8,128)(2,1)}, bf16[4,256,1792]{2,1,0:T(8,128)(2,1)}, bf16[4,256,1536]{2,1,0:...) custom-call(s32[1]{0:T(128)} %constant.364.clone.1.refs_0_, ...), custom_call_target="tpu_custom_call", output_to_operand_aliasing={{0}: (32, {}), {1}: (33, {}), {2}: (34, {}), {3}: (35, {}),... | custom-call | flops 20000000000 | bytes 1000000 | tf_op jit(solution)/shard_map/mixer_forward/pallas_call | solution.py:177
  176.1 21.3 %layer_forward.4 = (bf16[4,256,1024]{2,1,0:T(8,128)(2,1)}, bf16[4,256,1792]{2,1,0:T(8,128)(2,1)}, bf16[4,256,1792]{2,1,0:T(8,128)(2,1)}, bf16[4,256,1536]{2,1,0:...) custom-call(s32[1]{0:T(128)} %constant.367.clone.1.refs_0_, ...), custom_call_target="tpu_custom_call", output_to_operand_aliasing={{0}: (46, {}), {1}: (47, {}), {2}: (48, {}), {3}: (49, {}),... | custom-call | flops 20000000000 | bytes 1000000 | tf_op jit(solution)/shard_map/layer_forward/pallas_call | solution.py:177
  201.1 21.1 %layer_forward.5 = (bf16[4,256,1024]{2,1,0:T(8,128)(2,1)}, bf16[4,256,1792]{2,1,0:T(8,128)(2,1)}, bf16[4,256,1792]{2,1,0:T(8,128)(2,1)}, bf16[4,256,1536]{2,1,0:...) custom-call(s32[1]{0:T(128)} %constant.366.clone.1.refs_0_, ...), custom_call_target="tpu_custom_call", output_to_operand_aliasing={{0}: (46, {}), {1}: (47, {}), {2}: (48, {}), {3}: (49, {}),... | custom-call | flops 20000000000 | bytes 1000000 | tf_op jit(solution)/shard_map/layer_forward/pallas_call | solution.py:177
  225.8 19.9 %layer_forward.6 = (bf16[4,256,1024]{2,1,0:T(8,128)(2,1)}, bf16[4,256,1792]{2,1,0:T(8,128)(2,1)}, bf16[4,256,1792]{2,1,0:T(8,128)(2,1)}, bf16[4,256,1536]{2,1,0:...) custom-call(s32[1]{0:T(128)} %constant.368.clone.1.refs_0_, ...), custom_call_target="tpu_custom_call", output_to_operand_aliasing={{0}: (46, {}), {1}: (47, {}), {2}: (48, {}), {3}: (49, {}),... | custom-call | flops 20000000000 | bytes 1000000 | tf_op jit(solution)/shard_map/layer_forward/pallas_call | solution.py:177
  246.5 19.7 %layer_forward.7 = (bf16[4,256,1024]{2,1,0:T(8,128)(2,1)}, bf16[4,256,1792]{2,1,0:T(8,128)(2,1)}, bf16[4,256,1792]{2,1,0:T(8,128)(2,1)}, bf16[4,256,1536]{2,1,0:...) custom-call(s32[1]{0:T(128)} %constant.365.clone.1.refs_0_, ...), custom_call_target="tpu_custom_call", output_to_operand_aliasing={{0}: (46, {}), {1}: (47, {}), {2}: (48, {}), {3}: (49, {}),... | custom-call | flops 20000000000 | bytes 1000000 | tf_op jit(solution)/shard_map/layer_forward/pallas_call | solution.py:177
  266.3 28.1 %layer_backward.4 = (bf16[4,256,1024]{2,1,0:T(8,128)(2,1)}, bf16[4,256,2048]{2,1,0:T(8,128)(2,1)}, bf16[4,256,2048]{2,1,0:T(8,128)(2,1)}, f32[4,8,1024]{2,1,0:T(...) custom-call(s32[1]{0:T(128)} %constant.358.clone.1.refs_0_, ...), custom_call_target="tpu_custom_call" | custom-call | flops 24999999488 | bytes 1000000 | tf_op jit(solution)/shard_map/layer_backward/pallas_call | solution.py:177
  297.4 28.0 %layer_backward.5 = (bf16[4,256,1024]{2,1,0:T(8,128)(2,1)}, bf16[4,256,2048]{2,1,0:T(8,128)(2,1)}, bf16[4,256,2048]{2,1,0:T(8,128)(2,1)}, f32[4,8,1024]{2,1,0:T(...) custom-call(s32[1]{0:T(128)} %constant.355.clone.1.refs_0_, ...), custom_call_target="tpu_custom_call", output_to_operand_aliasing={{0}: (59, {}), {1}: (60, {}), {2}: (61, {}), {3}: (62, {}),... | custom-call | flops 24999999488 | bytes 1000000 | tf_op jit(solution)/shard_map/layer_backward/pallas_call | solution.py:177
  329.2 29.1 %layer_backward.6 = (bf16[4,256,1024]{2,1,0:T(8,128)(2,1)}, bf16[4,256,2048]{2,1,0:T(8,128)(2,1)}, bf16[4,256,2048]{2,1,0:T(8,128)(2,1)}, f32[4,8,1024]{2,1,0:T(...) custom-call(s32[1]{0:T(128)} %constant.369.clone.1.refs_0_, ...), custom_call_target="tpu_custom_call", output_to_operand_aliasing={{0}: (59, {}), {1}: (60, {}), {2}: (61, {}), {3}: (62, {}),... | custom-call | flops 24999999488 | bytes 1000000 | tf_op jit(solution)/shard_map/layer_backward/pallas_call | solution.py:177
  364.6 29.1 %layer_backward.7 = (bf16[4,256,1024]{2,1,0:T(8,128)(2,1)}, bf16[4,256,2048]{2,1,0:T(8,128)(2,1)}, bf16[4,256,2048]{2,1,0:T(8,128)(2,1)}, f32[4,8,1024]{2,1,0:T(...) custom-call(s32[1]{0:T(128)} %constant.354.clone.1.refs_0_, ...), custom_call_target="tpu_custom_call", output_to_operand_aliasing={{0}: (59, {}), {1}: (60, {}), {2}: (61, {}), {3}: (62, {}),... | custom-call | flops 24999999488 | bytes 1000000 | tf_op jit(solution)/shard_map/layer_backward/pallas_call | solution.py:177
  397.0 10.1 %mlp_backward.2 = (bf16[4,256,1024]{2,1,0:T(8,128)(2,1)}, bf16[4,256,2048]{2,1,0:T(8,128)(2,1)}, bf16[4,256,2048]{2,1,0:T(8,128)(2,1)}, f32[4,8,1024]{2,1,0:T(8,128)}, f32[256,1024]{1,0:T(8,128)S(1)}) custom-call(s32[1]{0:T(128)} %constant.370.clone.1.refs_0_, ...), custom_call_target="tpu_custom_call", output_to_operand_aliasing={{0}: (25, {}), {1}: (26, {}), {2}: (27, {}), {3}: (28, {})} | custom-call | flops 300000000 | bytes 1000000 | tf_op jit(solution)/shard_map/mlp_backward/pallas_call | solution.py:177
  409.9 10.0 %mlp_backward.3 = (bf16[4,256,1024]{2,1,0:T(8,128)(2,1)}, bf16[4,256,2048]{2,1,0:T(8,128)(2,1)}, bf16[4,256,2048]{2,1,0:T(8,128)(2,1)}, f32[4,8,1024]{2,1,0:T(8,128)}, f32[256,1024]{1,0:T(8,128)S(1)}) custom-call(s32[1]{0:T(128)} %constant.337.clone.1.refs_0_, ...), custom_call_target="tpu_custom_call", output_to_operand_aliasing={{0}: (25, {}), {1}: (26, {}), {2}: (27, {}), {3}: (28, {})} | custom-call | flops 300000000 | bytes 1000000 | tf_op jit(solution)/shard_map/mlp_backward/pallas_call | solution.py:177
  447.2 8.5 %weight_gradient.10 = (bf16[2,256,2048]{2,1,0:T(8,128)(2,1)}, bf16[2,256,2048]{2,1,0:T(8,128)(2,1)}) custom-call(s32[1]{0:T(128)} %bitcast.53.core_ref, bf16[4,256,1024]{2,1,0:T(8,128)(2,1)} %get-tuple-element.575.away_ref.stay_ref, bf16[4,256,1024]{2,1,0:T(8,128)(2,1)} %get-tuple-element.575.away_ref.stay_ref, ...), custom_call_target="tpu_custom_call" | custom-call | flops 100000000 | bytes 1000000 | tf_op jit(solution)/shard_map/weight_gradient/pallas_call | solution.py:1031
  459.5 21.2 %mixer_backward.2 = (bf16[4,256,1024]{2,1,0:T(8,128)(2,1)}, bf16[4,256,896]{2,1,0:T(8,128)(2,1)}, bf16[4,256,1792]{2,1,0:T(8,128)(2,1)}, bf16[4,256,1536]{2,1,0:...) custom-call(s32[1]{0:T(128)} %constant.370.clone.1.refs_0_, ...), custom_call_target="tpu_custom_call", output_to_operand_aliasing={{0}: (40, {}), {1}: (41, {}), {2}: (42, {}), {3}: (43, {}),... | custom-call | flops 24999999488 | bytes 1000000 | tf_op jit(solution)/shard_map/mixer_backward/pallas_call | solution.py:177
  497.3 20.9 %mixer_backward.3 = (bf16[4,256,1024]{2,1,0:T(8,128)(2,1)}, bf16[4,256,896]{2,1,0:T(8,128)(2,1)}, bf16[4,256,1792]{2,1,0:T(8,128)(2,1)}, bf16[4,256,1536]{2,1,0:...) custom-call(s32[1]{0:T(128)} %constant.337.clone.1.refs_0_, ...), custom_call_target="tpu_custom_call", output_to_operand_aliasing={{0}: (40, {}), {1}: (41, {}), {2}: (42, {}), {3}: (43, {}),... | custom-call | flops 24999999488 | bytes 1000000 | tf_op jit(solution)/shard_map/mixer_backward/pallas_call | solution.py:177
  599.9 11.5 %collective-permute-done.62 = bf16[256,1792]{1,0:T(8,128)(2,1)} collective-permute-done((bf16[256,1792]{1,0:T(8,128)(2,1)S(1)}, bf16[256,1792]{1,0:T(8,128)(2,1)}, u32[]{:S(2)}, u32[]{:S(2)}) %collective-permute-start.62) | collective-permute-done | bytes 917536 | tf_op jit(solution)/shard_map/ppermute | solution.py:1132
  615.2 8.7 %collective-permute-start.69 = (bf16[256,1792]{1,0:T(8,128)(2,1)S(1)}, bf16[256,1792]{1,0:T(8,128)(2,1)S(1)}, u32[]{:S(2)}, u32[]{:S(2)}) collective-permute-start(bf16[256,1792]{1,0:T(8,128)(2,1)S(1)} %fusion.3), channel_id=1, source_target_pairs={{0,1},{3,2},{4,5},{7,6},{8,9},{11,10},{12,13},{15,14},{16,17},{19,... | collective-permute-start | bytes 2752520 | tf_op jit(solution)/shard_map/ppermute | solution.py:1214
  632.1 14.1 %collective-permute-start.77 = (bf16[256,1536]{1,0:T(8,128)(2,1)S(1)}, bf16[256,1536]{1,0:T(8,128)(2,1)S(1)}, u32[]{:S(2)}, u32[]{:S(2)}) collective-permute-start(bf16[256,1536]{1,0:T(8,128)(2,1)S(1)} %fusion.5), channel_id=1, source_target_pairs={{0,1},{3,2},{4,5},{7,6},{8,9},{11,10},{12,13},{15,14},{16,17},{19,... | collective-permute-start | bytes 2359304 | tf_op jit(solution)/shard_map/ppermute | solution.py:1214
  649.1 10.9 %collective-permute-done.68 = bf16[384,1024]{1,0:T(8,128)(2,1)S(1)} collective-permute-done((bf16[384,1024]{1,0:T(8,128)(2,1)S(1)}, bf16[384,1024]{1,0:T(8,128)(2,1)S(1)}, u32[]{:S(2)}, u32[]{:S(2)}) %collective-permute-start.68) | collective-permute-done | bytes 786464 | tf_op jit(solution)/shard_map/ppermute | solution.py:1132
  662.3 8.7 %collective-permute-start.73 = (bf16[384,1024]{1,0:T(8,128)(2,1)S(1)}, bf16[384,1024]{1,0:T(8,128)(2,1)S(1)}, u32[]{:S(2)}, u32[]{:S(2)}) collective-permute-start(bf16[384,1024]{1,0:T(8,128)(2,1)S(1)} %fusion.4), channel_id=1, source_target_pairs={{0,1},{3,2},{4,5},{7,6},{8,9},{11,10},{12,13},{15,14},{16,17},{19,... | collective-permute-start | bytes 2359304 | tf_op jit(solution)/shard_map/ppermute | solution.py:1214
  679.5 9.4 %collective-permute-done.73 = bf16[384,1024]{1,0:T(8,128)(2,1)S(1)} collective-permute-done((bf16[384,1024]{1,0:T(8,128)(2,1)S(1)}, bf16[384,1024]{1,0:T(8,128)(2,1)S(1)}, u32[]{:S(2)}, u32[]{:S(2)}) %collective-permute-start.73) | collective-permute-done | bytes 786464 | tf_op jit(solution)/shard_map/ppermute | solution.py:1214
  698.9 13.7 %collective-permute-done.83 = bf16[256,1792]{1,0:T(8,128)(2,1)S(1)} collective-permute-done((bf16[256,1792]{1,0:T(8,128)(2,1)S(1)}, bf16[256,1792]{1,0:T(8,128)(2,1)S(1)}, u32[]{:S(2)}, u32[]{:S(2)}) %collective-permute-start.83) | collective-permute-done | bytes 917536 | tf_op jit(solution)/shard_map/ppermute | solution.py:1226
  716.4 13.0 %collective-permute-done.80 = bf16[256,1536]{1,0:T(8,128)(2,1)S(1)} collective-permute-done((bf16[256,1536]{1,0:T(8,128)(2,1)S(1)}, bf16[256,1536]{1,0:T(8,128)(2,1)S(1)}, u32[]{:S(2)}, u32[]{:S(2)}) %collective-permute-start.80) | collective-permute-done | bytes 786464 | tf_op jit(solution)/shard_map/ppermute | solution.py:1226
  731.6 12.0 %collective-permute-done.86 = bf16[384,1024]{1,0:T(8,128)(2,1)S(1)} collective-permute-done((bf16[384,1024]{1,0:T(8,128)(2,1)S(1)}, bf16[384,1024]{1,0:T(8,128)(2,1)S(1)}, u32[]{:S(2)}, u32[]{:S(2)}) %collective-permute-start.86) | collective-permute-done | bytes 786464 | tf_op jit(solution)/shard_map/ppermute | solution.py:1226
  (511 shorter events, 353.1 us)
Async XLA Ops:
  12.6 39.9 %collective-permute-start.11 = (bf16[256,896]{1,0:T(8,128)(2,1)S(1)}, bf16[256,896]{1,0:T(8,128)(2,1)}, u32[]{:S(2)}, u32[]{:S(2)}) collective-permute-start(bf16[256,896]{1,0:T(8,128)(2,1)S(1)} %concatenate.67.refs_8_.refs_9_), channel_id=1, source_target_pairs={{0,4},{4,0},{8,12},{12,8},{1,5},{5,1},{9,13},{13,9},{2,6},{6,2},{1... | collective-permute-start | bytes 1376264 | tf_op jit(solution)/shard_map/ppermute | solution.py:1132
  84.4 53.4 %collective-permute-start.30 = (bf16[256,2048]{1,0:T(8,128)(2,1)}, bf16[256,2048]{1,0:T(8,128)(2,1)S(1)}, u32[]{:S(2)}, u32[]{:S(2)}) collective-permute-start(bf16[256,2048]{1,0:T(8,128)(2,1)} %bitcast.49.refs_11_.refs_38_.refs_39_.refs_13_), channel_id=1, source_target_pairs={{0,4},{4,0},{8,12},{12,8},{1,5},{5,1},{9,13},{13,9},{2,6},{6,2},{1... | collective-permute-start | bytes 3145736 | tf_op jit(solution)/shard_map/ppermute | solution.py:1132
  84.9 53.3 %collective-permute-start.33 = (bf16[512,1024]{1,0:T(8,128)(2,1)}, bf16[512,1024]{1,0:T(8,128)(2,1)S(1)}, u32[]{:S(2)}, u32[]{:S(2)}) collective-permute-start(bf16[512,1024]{1,0:T(8,128)(2,1)} %bitcast.50.refs_15_.refs_42_.refs_43_.refs_17_), channel_id=1, source_target_pairs={{0,4},{4,0},{8,12},{12,8},{1,5},{5,1},{9,13},{13,9},{2,6},{6,2},{1... | collective-permute-start | bytes 3145736 | tf_op jit(solution)/shard_map/ppermute | solution.py:1132
  86.0 51.7 %collective-permute-start.27 = (bf16[128,2048]{1,0:T(8,128)(2,1)}, bf16[128,2048]{1,0:T(8,128)(2,1)S(1)}, u32[]{:S(2)}, u32[]{:S(2)}) collective-permute-start(bf16[128,2048]{1,0:T(8,128)(2,1)} %collective-permute-done.26.refs_7_.refs_34_.refs_35_.refs_9_), channel_id=1, source_target_pairs={{0,1},{1,0},{2,3},{3,2},{4,5},{5,4},{6,7},{7,6},{8,9},{9,8},{10,11... | collective-permute-start | bytes 1572872 | tf_op jit(solution)/shard_map/ppermute | solution.py:1132
  102.5 34.6 %collective-permute-start.34 = (bf16[512,1024]{1,0:T(8,128)(2,1)}, bf16[512,1024]{1,0:T(8,128)(2,1)S(1)}, u32[]{:S(2)}, u32[]{:S(2)}) collective-permute-start(bf16[512,1024]{1,0:T(8,128)(2,1)} %bitcast.50.refs_15_.refs_42_.refs_43_.refs_17_), channel_id=1, source_target_pairs={{0,8},{4,12},{8,0},{12,4},{1,9},{5,13},{9,1},{13,5},{2,10},{6,14},... | collective-permute-start | bytes 3145736 | tf_op jit(solution)/shard_map/ppermute | solution.py:1132
  295.7 32.6 %collective-permute-start.42 = (bf16[256,1024]{1,0:T(8,128)(2,1)}, bf16[256,1024]{1,0:T(8,128)(2,1)S(1)}, u32[]{:S(2)}, u32[]{:S(2)}) collective-permute-start(bf16[256,1024]{1,0:T(8,128)(2,1)} %get-tuple-element.510), channel_id=1, source_target_pairs={{16,0},{17,1},{18,2},{19,3},{20,4},{21,5},{22,6},{23,7},{24,8},{25... | collective-permute-start | bytes 1572872 | tf_op jit(solution)/shard_map/ppermute | solution.py:1580
  325.4 35.8 %collective-permute-start.41 = (bf16[256,1024]{1,0:T(8,128)(2,1)}, bf16[256,1024]{1,0:T(8,128)(2,1)S(1)}, u32[]{:S(2)}, u32[]{:S(2)}) collective-permute-start(bf16[256,1024]{1,0:T(8,128)(2,1)} %get-tuple-element.522), channel_id=1, source_target_pairs={{16,0},{17,1},{18,2},{19,3},{20,4},{21,5},{22,6},{23,7},{24,8},{25... | collective-permute-start | bytes 1572872 | tf_op jit(solution)/shard_map/ppermute | solution.py:1580
  358.3 38.7 %collective-permute-start.44 = (bf16[256,1024]{1,0:T(8,128)(2,1)}, bf16[256,1024]{1,0:T(8,128)(2,1)S(1)}, u32[]{:S(2)}, u32[]{:S(2)}) collective-permute-start(bf16[256,1024]{1,0:T(8,128)(2,1)} %get-tuple-element.535), channel_id=1, source_target_pairs={{16,0},{17,1},{18,2},{19,3},{20,4},{21,5},{22,6},{23,7},{24,8},{25... | collective-permute-start | bytes 1572872 | tf_op jit(solution)/shard_map/ppermute | solution.py:1580
  362.4 34.6 %collective-permute-start.45 = (bf16[256,1024]{1,0:T(8,128)(2,1)S(1)}, bf16[256,1024]{1,0:T(8,128)(2,1)S(1)}, u32[]{:S(2)}, u32[]{:S(2)}) collective-permute-start(bf16[256,1024]{1,0:T(8,128)(2,1)S(1)} %bitcast_select_fusion.3), channel_id=1, source_target_pairs={{0,3},{1,2},{2,1},{3,0},{4,7},{5,6},{6,5},{7,4},{8,11},{9,10},{10,... | collective-permute-start | bytes 1572872 | tf_op jit(solution)/shard_map/ppermute | solution.py:1132
  443.5 37.3 %collective-permute-start.50 = (bf16[256,1024]{1,0:T(8,128)(2,1)}, bf16[256,1024]{1,0:T(8,128)(2,1)S(1)}, u32[]{:S(2)}, u32[]{:S(2)}) collective-permute-start(bf16[256,1024]{1,0:T(8,128)(2,1)} %bitcast_select_fusion.2), channel_id=1, source_target_pairs={{0,2},{1,3},{2,0},{3,1},{4,6},{5,7},{6,4},{7,5},{8,10},{9,11},{10,... | collective-permute-start | bytes 1572872 | tf_op jit(solution)/shard_map/ppermute | solution.py:1132
  483.6 35.6 %collective-permute-start.53 = (bf16[256,2048]{1,0:T(8,128)(2,1)}, bf16[256,2048]{1,0:T(8,128)(2,1)}, u32[]{:S(2)}, u32[]{:S(2)}) collective-permute-start(bf16[256,2048]{1,0:T(8,128)(2,1)} %fusion.7), channel_id=1, source_target_pairs={{0,8},{4,12},{8,0},{12,4},{1,9},{5,13},{9,1},{13,5},{2,10},{6,14},... | collective-permute-start | bytes 3145736 | tf_op jit(solution)/shard_map/ppermute | solution.py:1132
  487.3 62.1 %collective-permute-start.59 = (bf16[512,1024]{1,0:T(8,128)(2,1)}, bf16[512,1024]{1,0:T(8,128)(2,1)}, u32[]{:S(2)}, u32[]{:S(2)}) collective-permute-start(bf16[512,1024]{1,0:T(8,128)(2,1)} %fusion.8), channel_id=1, source_target_pairs={{0,8},{4,12},{8,0},{12,4},{1,9},{5,13},{9,1},{13,5},{2,10},{6,14},... | collective-permute-start | bytes 3145736 | tf_op jit(solution)/shard_map/ppermute | solution.py:1132
  549.4 43.8 %collective-permute-start.51 = (bf16[256,1024]{1,0:T(8,128)(2,1)}, bf16[256,1024]{1,0:T(8,128)(2,1)}, u32[]{:S(2)}, u32[]{:S(2)}) collective-permute-start(bf16[256,1024]{1,0:T(8,128)(2,1)} %bitcast_select_fusion), channel_id=1, source_target_pairs={{0,1},{1,0},{2,3},{3,2},{4,5},{5,4},{6,7},{7,6},{8,9},{9,8},{10,11... | collective-permute-start | bytes 1572872 | tf_op jit(solution)/shard_map/ppermute | solution.py:1132
  559.4 34.7 %collective-permute-start.64 = (bf16[256,2048]{1,0:T(8,128)(2,1)}, bf16[256,2048]{1,0:T(8,128)(2,1)}, u32[]{:S(2)}, u32[]{:S(2)}) collective-permute-start(bf16[256,2048]{1,0:T(8,128)(2,1)} %add_convert_fusion.3), channel_id=1, source_target_pairs={{1,0},{2,3},{5,4},{6,7},{9,8},{10,11},{13,12},{14,15},{17,16},{18,... | collective-permute-start | bytes 3145736 | tf_op jit(solution)/shard_map/ppermute | solution.py:1226
  563.1 33.7 %collective-permute-start.63 = (bf16[512,1024]{1,0:T(8,128)(2,1)S(1)}, bf16[512,1024]{1,0:T(8,128)(2,1)}, u32[]{:S(2)}, u32[]{:S(2)}) collective-permute-start(bf16[512,1024]{1,0:T(8,128)(2,1)S(1)} %fusion), channel_id=1, source_target_pairs={{0,1},{3,2},{4,5},{7,6},{8,9},{11,10},{12,13},{15,14},{16,17},{19,... | collective-permute-start | bytes 3145736 | tf_op jit(solution)/shard_map/ppermute | solution.py:1214
  593.1 35.0 %collective-permute-start.72 = (bf16[256,1536]{1,0:T(8,128)(2,1)}, bf16[256,1536]{1,0:T(8,128)(2,1)S(1)}, u32[]{:S(2)}, u32[]{:S(2)}) collective-permute-start(bf16[256,1536]{1,0:T(8,128)(2,1)} %fusion.11), channel_id=1, source_target_pairs={{0,8},{4,12},{8,0},{12,4},{1,9},{5,13},{9,1},{13,5},{2,10},{6,14},... | collective-permute-start | bytes 2359304 | tf_op jit(solution)/shard_map/ppermute | solution.py:1132
  596.8 35.3 %collective-permute-start.70 = (bf16[256,2048]{1,0:T(8,128)(2,1)S(1)}, bf16[256,2048]{1,0:T(8,128)(2,1)S(1)}, u32[]{:S(2)}, u32[]{:S(2)}) collective-permute-start(bf16[256,2048]{1,0:T(8,128)(2,1)S(1)} %add_convert_fusion.2), channel_id=1, source_target_pairs={{1,0},{2,3},{5,4},{6,7},{9,8},{10,11},{13,12},{14,15},{17,16},{18,... | collective-permute-start | bytes 3145736 | tf_op jit(solution)/shard_map/ppermute | solution.py:1226
  614.0 60.6 %collective-permute-start.75 = (bf16[128,1024]{1,0:T(8,128)(2,1)S(1)}, bf16[128,1024]{1,0:T(8,128)(2,1)S(1)}, u32[]{:S(2)}, u32[]{:S(2)}) collective-permute-start(bf16[128,1024]{1,0:T(8,128)(2,1)S(1)} %copy-done.60), channel_id=1, source_target_pairs={{0,8},{4,12},{8,0},{12,4},{1,9},{5,13},{9,1},{13,5},{2,10},{6,14},... | collective-permute-start | bytes 786440 | tf_op jit(solution)/shard_map/ppermute | solution.py:1132
  615.2 32.4 %collective-permute-start.69 = (bf16[256,1792]{1,0:T(8,128)(2,1)S(1)}, bf16[256,1792]{1,0:T(8,128)(2,1)S(1)}, u32[]{:S(2)}, u32[]{:S(2)}) collective-permute-start(bf16[256,1792]{1,0:T(8,128)(2,1)S(1)} %fusion.3), channel_id=1, source_target_pairs={{0,1},{3,2},{4,5},{7,6},{8,9},{11,10},{12,13},{15,14},{16,17},{19,... | collective-permute-start | bytes 2752520 | tf_op jit(solution)/shard_map/ppermute | solution.py:1214
  628.1 61.8 %collective-permute-start.66 = (bf16[256,896]{1,0:T(8,128)(2,1)S(1)}, bf16[256,896]{1,0:T(8,128)(2,1)S(1)}, u32[]{:S(2)}, u32[]{:S(2)}) collective-permute-start(bf16[256,896]{1,0:T(8,128)(2,1)S(1)} %fusion.15), channel_id=1, source_target_pairs={{0,8},{4,12},{8,0},{12,4},{1,9},{5,13},{9,1},{13,5},{2,10},{6,14},... | collective-permute-start | bytes 1376264 | tf_op jit(solution)/shard_map/ppermute | solution.py:1132
  674.7 40.8 %collective-permute-start.81 = (bf16[128,1024]{1,0:T(8,128)(2,1)S(1)}, bf16[128,1024]{1,0:T(8,128)(2,1)S(1)}, u32[]{:S(2)}, u32[]{:S(2)}) collective-permute-start(bf16[128,1024]{1,0:T(8,128)(2,1)S(1)} %fusion.14), channel_id=1, source_target_pairs={{0,1},{3,2},{4,5},{7,6},{8,9},{11,10},{12,13},{15,14},{16,17},{19,... | collective-permute-start | bytes 786440 | tf_op jit(solution)/shard_map/ppermute | solution.py:1214
  678.2 34.4 %collective-permute-start.83 = (bf16[256,1792]{1,0:T(8,128)(2,1)S(1)}, bf16[256,1792]{1,0:T(8,128)(2,1)S(1)}, u32[]{:S(2)}, u32[]{:S(2)}) collective-permute-start(bf16[256,1792]{1,0:T(8,128)(2,1)S(1)} %add_convert_fusion.9), channel_id=1, source_target_pairs={{1,0},{2,3},{5,4},{6,7},{9,8},{10,11},{13,12},{14,15},{17,16},{18,... | collective-permute-start | bytes 2752520 | tf_op jit(solution)/shard_map/ppermute | solution.py:1226
  690.2 40.4 %collective-permute-start.78 = (bf16[256,896]{1,0:T(8,128)(2,1)S(1)}, bf16[256,896]{1,0:T(8,128)(2,1)S(1)}, u32[]{:S(2)}, u32[]{:S(2)}) collective-permute-start(bf16[256,896]{1,0:T(8,128)(2,1)S(1)} %fusion.10), channel_id=1, source_target_pairs={{0,1},{3,2},{4,5},{7,6},{8,9},{11,10},{12,13},{15,14},{16,17},{19,... | collective-permute-start | bytes 1376264 | tf_op jit(solution)/shard_map/ppermute | solution.py:1214
  697.6 31.7 %collective-permute-start.80 = (bf16[256,1536]{1,0:T(8,128)(2,1)S(1)}, bf16[256,1536]{1,0:T(8,128)(2,1)S(1)}, u32[]{:S(2)}, u32[]{:S(2)}) collective-permute-start(bf16[256,1536]{1,0:T(8,128)(2,1)S(1)} %add_convert_fusion.13), channel_id=1, source_target_pairs={{1,0},{2,3},{5,4},{6,7},{9,8},{10,11},{13,12},{14,15},{17,16},{18,... | collective-permute-start | bytes 2359304 | tf_op jit(solution)/shard_map/ppermute | solution.py:1226
  (138 other events, 2496.2 us)

commit v6 on v5

--- a/solution.py
+++ b/solution.py
@@ -1640,11 +1640,11 @@
 
     if quick:
         stages(
-            "W2", "W0", "W1", "A0", "B4"
+            "W0", "W1", "A0", "W2", "B4"
         )
         token.append(returned[2])
         stages(
-            "A1", "A2", "L0", "B5"
+            "A2", "A1", "L0", "B5"
         )
     else:
         stages("B4", "B5")
@@ -1682,6 +1682,15 @@
     cuts = [v.shape[1] for v in shares]
     flat = jnp.concatenate(shares, axis=1)
 
+    def split_ends(values):
+        return values[:count], values[-2], values[-1]
+
+    def own_outputs(returned, s_dinput, s_low):
+        restored = jnp.zeros((count, length, width), BF)
+        for j in range(count):
+            restored = lax.dynamic_update_index_in_dim(restored, returned[j], send_at[j], 0)
+        return jnp.where(first, s_low, restored)[None], jnp.where(first, restored, s_dinput)[None]
+
     if quick:
         spare = -(-flat.shape[1] // rows)
         flat = jnp.pad(flat, ((0, 0), (0, spare * rows - flat.shape[1])))
@@ -1690,17 +1699,21 @@
         chunks += [Reduction(*pair) for pair in late]
         chunks[6].riders = (riders, column)
         stages(
-            "L1", "M0", "W7", "W4", "W3", "L2", "M1", "O0", "A4", "A3", "A7", "W6", "O1", "W5"
+            "L1", "M0", "W4", "W7", "W3", "L2", "M1", "O0", "A4", "A7", "A3", "W6", "W5", "F0"
         )
         token.append(returned[1])
         stages(
-            "F0", "M2", "L3", "A6", "A5", "L4", "O2", "F1", "M3", "L5", "M4", "F2", "L7", "O3",
-            "M5", "L6", "O4", "F3", "O5", "M7", "F4", "M6", "F5", "O7", "O6", "F7", "F6"
+            "O1", "L3", "M2", "L7", "A5", "L4", "A6", "M3", "O2", "F1", "L5", "M4", "L6", "O3",
+            "F2", "M7", "M5", "O4"
+        )
+        returned, s_dinput, s_low = split_ends(chained(*returned, s_dinput, s_low))
+        activations, gradients = own_outputs(returned, s_dinput, s_low)
+        token.extend([activations, gradients])
+        stages(
+            "M6", "F3", "O7", "O5", "F4", "O6", "F7", "F5", "F6"
         )
         reduced = [chunk.result for chunk in chunks]
         flat = reduced[6][:, column : column + spare].reshape(-1)
-        ends = chained(*returned, s_dinput, s_low)
-        returned, s_dinput, s_low = ends[:count], ends[-2], ends[-1]
     else:
 
         def reduce_all(pair):
@@ -1719,11 +1732,8 @@
     convs = parts[0].reshape(taps + 1, -1)
     loss = parts[-1][0]
 
-    restored = jnp.zeros((count, length, width), BF)
-    for j in range(count):
-        restored = lax.dynamic_update_index_in_dim(restored, returned[j], send_at[j], 0)
-    activations = jnp.where(first, s_low, restored)[None]
-    gradients = jnp.where(first, restored, s_dinput)[None]
+    if not quick:
+        activations, gradients = own_outputs(returned, s_dinput, s_low)
     s0 = qw + 2 * kw
     return (
         activations,

time: 787 us -> 752 us (0.956)
  starting transfers between devices: 124 us -> 104 us
  other arithmetic: 81.7 us -> 71 us
    ppermute x8, starting transfers between devices: 54.5 us -> 34.7 us  [line_in(): self.moved = lax.ppermute(self.stay, 'rep', [(0, 1), (3, 2)])]
  transfers between devices with their start and end apart: 89 -> 89, of which waited for: 21 -> 25; matrix products, arithmetic and copies ran while one was open for 14% -> 13% of each run, Pallas kernels for 36% -> 39%
where the time goes in v6:
time: 752 us; the launch traced here: 741 us
  Pallas kernels  361 us (48%)
  waiting for transfers between devices  142 us (19%)
  starting transfers between devices  104 us (14%)
  other arithmetic  71 us (9%)
  local copies, waits for them, and re-layouts  31.2 us (4%)
  between operations  22.9 us (3%)
  matrix products  8.96 us (1%)
    pallas_call x16, Pallas kernels, call(): pl.pallas_call(kernel, out_shape=[pltpu.HBM(s.shape, s.dtype) for s in st...  306 us
    ppermute x56, waiting for transfers between devices, swap(): lax.ppermute(block, axis, [(i, i ^ bit) for i in range(lax.axis_size(axis...  71.3 us
    pallas_call x8, Pallas kernels, weight_grad_halves(): pl.pallas_call(weight_kernel, out_shape=[shape, shape], grid_spec=grid, c...  55.5 us
    ppermute x8, waiting for transfers between devices, line_out(): self.moved = lax.ppermute(self.stay, 'rep', [(1, 0), (2, 3)])  51.7 us
    ppermute x56, starting transfers between devices, swap(): lax.ppermute(block, axis, [(i, i ^ bit) for i in range(lax.axis_size(axis...  36.8 us
    ppermute x8, starting transfers between devices, line_in(): self.moved = lax.ppermute(self.stay, 'rep', [(0, 1), (3, 2)])  34.7 us
    convert_element_type x24, other arithmetic, plus(): return (a.astype(F32) + b.astype(F32)).astype(BF)  22 us
  transfers between devices with their start and end apart: 89, of which 25 were waited for; matrix products, arithmetic and copies ran while one was open for 13% of the time, Pallas kernels for 39%

profile of v6, /device:TPU:0, one launch (start us, length us, event | category | flops | bytes accessed | tf_op | source)
XLA Modules:
  0.0 741.0 jit_solution(2683502128019036197)
XLA Ops:
  32.7 13.5 %collective-permute-done.2.refs_28_.refs_29_ = bf16[512,512]{1,0:T(8,128)(2,1)S(1)} collective-permute-done((bf16[512,512]{1,0:T(8,128)(2,1)S(1)}, bf16[512,512]{1,0:T(8,128)(2,1)S(1)}, u32[]{:S(2)}, u32[]{:S(2)}) %collective-permute-start.2) | collective-permute-done | bytes 524320 | tf_op jit(solution)/shard_map/ppermute | solution.py:1132
  85.5 15.3 %mixer_forward.2 = (bf16[4,256,1024]{2,1,0:T(8,128)(2,1)}, bf16[4,256,1792]{2,1,0:T(8,128)(2,1)}, bf16[4,256,1792]{2,1,0:T(8,128)(2,1)}, bf16[4,256,1536]{2,1,0:...) custom-call(s32[1]{0:T(128)} %constant.359.clone.1.refs_0_, ...), custom_call_target="tpu_custom_call" | custom-call | flops 20000000000 | bytes 1000000 | tf_op jit(solution)/shard_map/mixer_forward/pallas_call | solution.py:177
  113.4 15.5 %mixer_forward.3 = (bf16[4,256,1024]{2,1,0:T(8,128)(2,1)}, bf16[4,256,1792]{2,1,0:T(8,128)(2,1)}, bf16[4,256,1792]{2,1,0:T(8,128)(2,1)}, bf16[4,256,1536]{2,1,0:...) custom-call(s32[1]{0:T(128)} %constant.364.clone.1.refs_0_, ...), custom_call_target="tpu_custom_call", output_to_operand_aliasing={{0}: (32, {}), {1}: (33, {}), {2}: (34, {}), {3}: (35, {}),... | custom-call | flops 20000000000 | bytes 1000000 | tf_op jit(solution)/shard_map/mixer_forward/pallas_call | solution.py:177
  162.3 8.3 %mlp_forward.3 = (bf16[4,256,1024]{2,1,0:T(8,128)(2,1)}, bf16[4,256,2048]{2,1,0:T(8,128)(2,1)}, bf16[4,256,2048]{2,1,0:T(8,128)(2,1)}, bf16[4,256,2048]{2,1,0:T(...) custom-call(s32[1]{0:T(128)} %constant.364.clone.1.refs_0_, ...), custom_call_target="tpu_custom_call", output_to_operand_aliasing={{0}: (19, {}), {1}: (20, {}), {2}: (21, {}), {3}: (22, {}),... | custom-call | flops 300000000 | bytes 1000000 | tf_op jit(solution)/shard_map/mlp_forward/pallas_call | solution.py:177
  176.4 21.3 %layer_forward.4 = (bf16[4,256,1024]{2,1,0:T(8,128)(2,1)}, bf16[4,256,1792]{2,1,0:T(8,128)(2,1)}, bf16[4,256,1792]{2,1,0:T(8,128)(2,1)}, bf16[4,256,1536]{2,1,0:...) custom-call(s32[1]{0:T(128)} %constant.367.clone.1.refs_0_, ...), custom_call_target="tpu_custom_call", output_to_operand_aliasing={{0}: (46, {}), {1}: (47, {}), {2}: (48, {}), {3}: (49, {}),... | custom-call | flops 20000000000 | bytes 1000000 | tf_op jit(solution)/shard_map/layer_forward/pallas_call | solution.py:177
  201.3 21.1 %layer_forward.5 = (bf16[4,256,1024]{2,1,0:T(8,128)(2,1)}, bf16[4,256,1792]{2,1,0:T(8,128)(2,1)}, bf16[4,256,1792]{2,1,0:T(8,128)(2,1)}, bf16[4,256,1536]{2,1,0:...) custom-call(s32[1]{0:T(128)} %constant.366.clone.1.refs_0_, ...), custom_call_target="tpu_custom_call", output_to_operand_aliasing={{0}: (46, {}), {1}: (47, {}), {2}: (48, {}), {3}: (49, {}),... | custom-call | flops 20000000000 | bytes 1000000 | tf_op jit(solution)/shard_map/layer_forward/pallas_call | solution.py:177
  225.9 19.9 %layer_forward.6 = (bf16[4,256,1024]{2,1,0:T(8,128)(2,1)}, bf16[4,256,1792]{2,1,0:T(8,128)(2,1)}, bf16[4,256,1792]{2,1,0:T(8,128)(2,1)}, bf16[4,256,1536]{2,1,0:...) custom-call(s32[1]{0:T(128)} %constant.368.clone.1.refs_0_, ...), custom_call_target="tpu_custom_call", output_to_operand_aliasing={{0}: (46, {}), {1}: (47, {}), {2}: (48, {}), {3}: (49, {}),... | custom-call | flops 20000000000 | bytes 1000000 | tf_op jit(solution)/shard_map/layer_forward/pallas_call | solution.py:177
  246.7 19.7 %layer_forward.7 = (bf16[4,256,1024]{2,1,0:T(8,128)(2,1)}, bf16[4,256,1792]{2,1,0:T(8,128)(2,1)}, bf16[4,256,1792]{2,1,0:T(8,128)(2,1)}, bf16[4,256,1536]{2,1,0:...) custom-call(s32[1]{0:T(128)} %constant.365.clone.1.refs_0_, ...), custom_call_target="tpu_custom_call", output_to_operand_aliasing={{0}: (46, {}), {1}: (47, {}), {2}: (48, {}), {3}: (49, {}),... | custom-call | flops 20000000000 | bytes 1000000 | tf_op jit(solution)/shard_map/layer_forward/pallas_call | solution.py:177
  266.4 28.0 %layer_backward.4 = (bf16[4,256,1024]{2,1,0:T(8,128)(2,1)}, bf16[4,256,2048]{2,1,0:T(8,128)(2,1)}, bf16[4,256,2048]{2,1,0:T(8,128)(2,1)}, f32[4,8,1024]{2,1,0:T(...) custom-call(s32[1]{0:T(128)} %constant.358.clone.1.refs_0_, ...), custom_call_target="tpu_custom_call" | custom-call | flops 24999999488 | bytes 1000000 | tf_op jit(solution)/shard_map/layer_backward/pallas_call | solution.py:177
  297.6 28.0 %layer_backward.5 = (bf16[4,256,1024]{2,1,0:T(8,128)(2,1)}, bf16[4,256,2048]{2,1,0:T(8,128)(2,1)}, bf16[4,256,2048]{2,1,0:T(8,128)(2,1)}, f32[4,8,1024]{2,1,0:T(...) custom-call(s32[1]{0:T(128)} %constant.355.clone.1.refs_0_, ...), custom_call_target="tpu_custom_call", output_to_operand_aliasing={{0}: (59, {}), {1}: (60, {}), {2}: (61, {}), {3}: (62, {}),... | custom-call | flops 24999999488 | bytes 1000000 | tf_op jit(solution)/shard_map/layer_backward/pallas_call | solution.py:177
  329.4 29.1 %layer_backward.6 = (bf16[4,256,1024]{2,1,0:T(8,128)(2,1)}, bf16[4,256,2048]{2,1,0:T(8,128)(2,1)}, bf16[4,256,2048]{2,1,0:T(8,128)(2,1)}, f32[4,8,1024]{2,1,0:T(...) custom-call(s32[1]{0:T(128)} %constant.369.clone.1.refs_0_, ...), custom_call_target="tpu_custom_call", output_to_operand_aliasing={{0}: (59, {}), {1}: (60, {}), {2}: (61, {}), {3}: (62, {}),... | custom-call | flops 24999999488 | bytes 1000000 | tf_op jit(solution)/shard_map/layer_backward/pallas_call | solution.py:177
  364.9 29.1 %layer_backward.7 = (bf16[4,256,1024]{2,1,0:T(8,128)(2,1)}, bf16[4,256,2048]{2,1,0:T(8,128)(2,1)}, bf16[4,256,2048]{2,1,0:T(8,128)(2,1)}, f32[4,8,1024]{2,1,0:T(...) custom-call(s32[1]{0:T(128)} %constant.354.clone.1.refs_0_, ...), custom_call_target="tpu_custom_call", output_to_operand_aliasing={{0}: (59, {}), {1}: (60, {}), {2}: (61, {}), {3}: (62, {}),... | custom-call | flops 24999999488 | bytes 1000000 | tf_op jit(solution)/shard_map/layer_backward/pallas_call | solution.py:177
  398.0 10.1 %mlp_backward.2 = (bf16[4,256,1024]{2,1,0:T(8,128)(2,1)}, bf16[4,256,2048]{2,1,0:T(8,128)(2,1)}, bf16[4,256,2048]{2,1,0:T(8,128)(2,1)}, f32[4,8,1024]{2,1,0:T(8,128)}, f32[256,1024]{1,0:T(8,128)S(1)}) custom-call(s32[1]{0:T(128)} %constant.370.clone.1.refs_0_, ...), custom_call_target="tpu_custom_call", output_to_operand_aliasing={{0}: (25, {}), {1}: (26, {}), {2}: (27, {}), {3}: (28, {})} | custom-call | flops 300000000 | bytes 1000000 | tf_op jit(solution)/shard_map/mlp_backward/pallas_call | solution.py:177
  410.1 10.0 %mlp_backward.3 = (bf16[4,256,1024]{2,1,0:T(8,128)(2,1)}, bf16[4,256,2048]{2,1,0:T(8,128)(2,1)}, bf16[4,256,2048]{2,1,0:T(8,128)(2,1)}, f32[4,8,1024]{2,1,0:T(8,128)}, f32[256,1024]{1,0:T(8,128)S(1)}) custom-call(s32[1]{0:T(128)} %constant.337.clone.1.refs_0_, ...), custom_call_target="tpu_custom_call", output_to_operand_aliasing={{0}: (25, {}), {1}: (26, {}), {2}: (27, {}), {3}: (28, {})} | custom-call | flops 300000000 | bytes 1000000 | tf_op jit(solution)/shard_map/mlp_backward/pallas_call | solution.py:177
  420.2 8.4 %weight_gradient.8 = (bf16[2,256,2048]{2,1,0:T(8,128)(2,1)}, bf16[2,256,2048]{2,1,0:T(8,128)(2,1)}) custom-call(s32[1]{0:T(128)} %bitcast.53.core_ref, bf16[4,256,1024]{2,1,0:T(8,128)(2,1)} %get-tuple-element.570.away_ref.stay_ref, bf16[4,256,1024]{2,1,0:T(8,128)(2,1)} %get-tuple-element.570.away_ref.stay_ref, bf16[4,256,2048]{2,1,0:T(8,128)(2,1)} %get-tuple-element.566.right_ref), custom_call_target="tpu_custom_call" | custom-call | flops 100000000 | bytes 1000000 | tf_op jit(solution)/shard_map/weight_gradient/pallas_call | solution.py:1031
  441.3 8.4 %weight_gradient.9 = (bf16[2,256,2048]{2,1,0:T(8,128)(2,1)}, bf16[2,256,2048]{2,1,0:T(8,128)(2,1)}) custom-call(s32[1]{0:T(128)} %bitcast.53.core_ref, bf16[4,256,1024]{2,1,0:T(8,128)(2,1)} %get-tuple-element.570.away_ref.stay_ref, bf16[4,256,1024]{2,1,0:T(8,128)(2,1)} %get-tuple-element.570.away_ref.stay_ref, bf16[4,256,2048]{2,1,0:T(8,128)(2,1)} %get-tuple-element.571.right_ref), custom_call_target="tpu_custom_call" | custom-call | flops 100000000 | bytes 1000000 | tf_op jit(solution)/shard_map/weight_gradient/pallas_call | solution.py:1031
  452.2 8.3 %weight_gradient.10 = (bf16[2,512,1024]{2,1,0:T(8,128)(2,1)}, bf16[2,512,1024]{2,1,0:T(8,128)(2,1)}) custom-call(s32[1]{0:T(128)} %bitcast.53.core_ref, bf16[4,256,2048]{2,1,0:T(8,128)(2,1)} %get-tuple-element.578.away_ref.stay_ref, bf16[4,256,2048]{2,1,0:T(8,128)(2,1)} %get-tuple-element.578.away_ref.stay_ref, ...), custom_call_target="tpu_custom_call" | custom-call | flops 100000000 | bytes 1000000 | tf_op jit(solution)/shard_map/weight_gradient/pallas_call | solution.py:1031
  461.5 21.2 %mixer_backward.2 = (bf16[4,256,1024]{2,1,0:T(8,128)(2,1)}, bf16[4,256,896]{2,1,0:T(8,128)(2,1)}, bf16[4,256,1792]{2,1,0:T(8,128)(2,1)}, bf16[4,256,1536]{2,1,0:...) custom-call(s32[1]{0:T(128)} %constant.370.clone.1.refs_0_, ...), custom_call_target="tpu_custom_call", output_to_operand_aliasing={{0}: (40, {}), {1}: (41, {}), {2}: (42, {}), {3}: (43, {}),... | custom-call | flops 24999999488 | bytes 1000000 | tf_op jit(solution)/shard_map/mixer_backward/pallas_call | solution.py:177
  498.1 20.8 %mixer_backward.3 = (bf16[4,256,1024]{2,1,0:T(8,128)(2,1)}, bf16[4,256,896]{2,1,0:T(8,128)(2,1)}, bf16[4,256,1792]{2,1,0:T(8,128)(2,1)}, bf16[4,256,1536]{2,1,0:...) custom-call(s32[1]{0:T(128)} %constant.337.clone.1.refs_0_, ...), custom_call_target="tpu_custom_call", output_to_operand_aliasing={{0}: (40, {}), {1}: (41, {}), {2}: (42, {}), {3}: (43, {}),... | custom-call | flops 24999999488 | bytes 1000000 | tf_op jit(solution)/shard_map/mixer_backward/pallas_call | solution.py:177
  557.8 8.8 %collective-permute-start.64 = (bf16[512,1024]{1,0:T(8,128)(2,1)}, bf16[512,1024]{1,0:T(8,128)(2,1)}, u32[]{:S(2)}, u32[]{:S(2)}) collective-permute-start(bf16[512,1024]{1,0:T(8,128)(2,1)} %fusion), channel_id=1, source_target_pairs={{0,1},{3,2},{4,5},{7,6},{8,9},{11,10},{12,13},{15,14},{16,17},{19,... | collective-permute-start | bytes 3145736 | tf_op jit(solution)/shard_map/ppermute | solution.py:1214
  604.7 10.2 %collective-permute-done.58 = bf16[256,1536]{1,0:T(8,128)(2,1)S(1)} collective-permute-done((bf16[256,1536]{1,0:T(8,128)(2,1)S(1)}, bf16[256,1536]{1,0:T(8,128)(2,1)S(1)}, u32[]{:S(2)}, u32[]{:S(2)}) %collective-permute-start.58) | collective-permute-done | bytes 786464 | tf_op jit(solution)/shard_map/ppermute | solution.py:1132
  677.1 10.6 %collective-permute-done.85 = bf16[256,1792]{1,0:T(8,128)(2,1)S(1)} collective-permute-done((bf16[256,1792]{1,0:T(8,128)(2,1)S(1)}, bf16[256,1792]{1,0:T(8,128)(2,1)S(1)}, u32[]{:S(2)}, u32[]{:S(2)}) %collective-permute-start.85) | collective-permute-done | bytes 917536 | tf_op jit(solution)/shard_map/ppermute | solution.py:1226
  692.1 12.5 %collective-permute-done.82 = bf16[256,1536]{1,0:T(8,128)(2,1)S(1)} collective-permute-done((bf16[256,1536]{1,0:T(8,128)(2,1)S(1)}, bf16[256,1536]{1,0:T(8,128)(2,1)S(1)}, u32[]{:S(2)}, u32[]{:S(2)}) %collective-permute-start.82) | collective-permute-done | bytes 786464 | tf_op jit(solution)/shard_map/ppermute | solution.py:1226
  711.0 16.0 %collective-permute-done.87 = bf16[384,1024]{1,0:T(8,128)(2,1)S(1)} collective-permute-done((bf16[384,1024]{1,0:T(8,128)(2,1)S(1)}, bf16[384,1024]{1,0:T(8,128)(2,1)S(1)}, u32[]{:S(2)}, u32[]{:S(2)}) %collective-permute-start.87) | collective-permute-done | bytes 786464 | tf_op jit(solution)/shard_map/ppermute | solution.py:1226
  (517 shorter events, 324.1 us)
Async XLA Ops:
  12.6 35.7 %collective-permute-start.11 = (bf16[256,896]{1,0:T(8,128)(2,1)S(1)}, bf16[256,896]{1,0:T(8,128)(2,1)}, u32[]{:S(2)}, u32[]{:S(2)}) collective-permute-start(bf16[256,896]{1,0:T(8,128)(2,1)S(1)} %concatenate.67.refs_8_.refs_9_), channel_id=1, source_target_pairs={{0,4},{4,0},{8,12},{12,8},{1,5},{5,1},{9,13},{13,9},{2,6},{6,2},{1... | collective-permute-start | bytes 1376264 | tf_op jit(solution)/shard_map/ppermute | solution.py:1132
  32.5 36.9 %collective-permute-start.16 = (bf16[256,1792]{1,0:T(8,128)(2,1)}, bf16[256,1792]{1,0:T(8,128)(2,1)}, u32[]{:S(2)}, u32[]{:S(2)}) collective-permute-start(bf16[256,1792]{1,0:T(8,128)(2,1)} %bitcast.45.refs_14_.refs_15_), channel_id=1, source_target_pairs={{0,4},{4,0},{8,12},{12,8},{1,5},{5,1},{9,13},{13,9},{2,6},{6,2},{1... | collective-permute-start | bytes 2752520 | tf_op jit(solution)/shard_map/ppermute | solution.py:1132
  84.0 53.3 %collective-permute-start.30 = (bf16[256,2048]{1,0:T(8,128)(2,1)}, bf16[256,2048]{1,0:T(8,128)(2,1)S(1)}, u32[]{:S(2)}, u32[]{:S(2)}) collective-permute-start(bf16[256,2048]{1,0:T(8,128)(2,1)} %bitcast.49.refs_11_.refs_38_.refs_39_.refs_13_), channel_id=1, source_target_pairs={{0,4},{4,0},{8,12},{12,8},{1,5},{5,1},{9,13},{13,9},{2,6},{6,2},{1... | collective-permute-start | bytes 3145736 | tf_op jit(solution)/shard_map/ppermute | solution.py:1132
  84.5 53.2 %collective-permute-start.33 = (bf16[512,1024]{1,0:T(8,128)(2,1)}, bf16[512,1024]{1,0:T(8,128)(2,1)S(1)}, u32[]{:S(2)}, u32[]{:S(2)}) collective-permute-start(bf16[512,1024]{1,0:T(8,128)(2,1)} %bitcast.50.refs_15_.refs_42_.refs_43_.refs_17_), channel_id=1, source_target_pairs={{0,4},{4,0},{8,12},{12,8},{1,5},{5,1},{9,13},{13,9},{2,6},{6,2},{1... | collective-permute-start | bytes 3145736 | tf_op jit(solution)/shard_map/ppermute | solution.py:1132
  85.1 52.1 %collective-permute-start.27 = (bf16[128,2048]{1,0:T(8,128)(2,1)S(1)}, bf16[128,2048]{1,0:T(8,128)(2,1)S(1)}, u32[]{:S(2)}, u32[]{:S(2)}) collective-permute-start(bf16[128,2048]{1,0:T(8,128)(2,1)S(1)} %collective-permute-done.26.refs_7_.refs_34_.refs_35_.refs_9_), channel_id=1, source_target_pairs={{0,1},{1,0},{2,3},{3,2},{4,5},{5,4},{6,7},{7,6},{8,9},{9,8},{10,11... | collective-permute-start | bytes 1572872 | tf_op jit(solution)/shard_map/ppermute | solution.py:1132
  100.8 35.9 %collective-permute-start.34 = (bf16[512,1024]{1,0:T(8,128)(2,1)}, bf16[512,1024]{1,0:T(8,128)(2,1)S(1)}, u32[]{:S(2)}, u32[]{:S(2)}) collective-permute-start(bf16[512,1024]{1,0:T(8,128)(2,1)} %bitcast.50.refs_15_.refs_42_.refs_43_.refs_17_), channel_id=1, source_target_pairs={{0,8},{4,12},{8,0},{12,4},{1,9},{5,13},{9,1},{13,5},{2,10},{6,14},... | collective-permute-start | bytes 3145736 | tf_op jit(solution)/shard_map/ppermute | solution.py:1132
  295.9 32.6 %collective-permute-start.42 = (bf16[256,1024]{1,0:T(8,128)(2,1)}, bf16[256,1024]{1,0:T(8,128)(2,1)S(1)}, u32[]{:S(2)}, u32[]{:S(2)}) collective-permute-start(bf16[256,1024]{1,0:T(8,128)(2,1)} %get-tuple-element.510), channel_id=1, source_target_pairs={{16,0},{17,1},{18,2},{19,3},{20,4},{21,5},{22,6},{23,7},{24,8},{25... | collective-permute-start | bytes 1572872 | tf_op jit(solution)/shard_map/ppermute | solution.py:1580
  325.6 35.8 %collective-permute-start.41 = (bf16[256,1024]{1,0:T(8,128)(2,1)}, bf16[256,1024]{1,0:T(8,128)(2,1)S(1)}, u32[]{:S(2)}, u32[]{:S(2)}) collective-permute-start(bf16[256,1024]{1,0:T(8,128)(2,1)} %get-tuple-element.522), channel_id=1, source_target_pairs={{16,0},{17,1},{18,2},{19,3},{20,4},{21,5},{22,6},{23,7},{24,8},{25... | collective-permute-start | bytes 1572872 | tf_op jit(solution)/shard_map/ppermute | solution.py:1580
  358.5 38.7 %collective-permute-start.44 = (bf16[256,1024]{1,0:T(8,128)(2,1)}, bf16[256,1024]{1,0:T(8,128)(2,1)S(1)}, u32[]{:S(2)}, u32[]{:S(2)}) collective-permute-start(bf16[256,1024]{1,0:T(8,128)(2,1)} %get-tuple-element.535), channel_id=1, source_target_pairs={{16,0},{17,1},{18,2},{19,3},{20,4},{21,5},{22,6},{23,7},{24,8},{25... | collective-permute-start | bytes 1572872 | tf_op jit(solution)/shard_map/ppermute | solution.py:1580
  362.7 34.6 %collective-permute-start.45 = (bf16[256,1024]{1,0:T(8,128)(2,1)S(1)}, bf16[256,1024]{1,0:T(8,128)(2,1)S(1)}, u32[]{:S(2)}, u32[]{:S(2)}) collective-permute-start(bf16[256,1024]{1,0:T(8,128)(2,1)S(1)} %bitcast_select_fusion.3), channel_id=1, source_target_pairs={{0,3},{1,2},{2,1},{3,0},{4,7},{5,6},{6,5},{7,4},{8,11},{9,10},{10,... | collective-permute-start | bytes 1572872 | tf_op jit(solution)/shard_map/ppermute | solution.py:1132
  437.6 47.9 %collective-permute-start.50 = (bf16[256,1024]{1,0:T(8,128)(2,1)}, bf16[256,1024]{1,0:T(8,128)(2,1)S(1)}, u32[]{:S(2)}, u32[]{:S(2)}) collective-permute-start(bf16[256,1024]{1,0:T(8,128)(2,1)} %bitcast_select_fusion.2), channel_id=1, source_target_pairs={{0,2},{1,3},{2,0},{3,1},{4,6},{5,7},{6,4},{7,5},{8,10},{9,11},{10,... | collective-permute-start | bytes 1572872 | tf_op jit(solution)/shard_map/ppermute | solution.py:1132
  449.7 37.5 %collective-permute-start.48 = (bf16[2,256,2048]{2,1,0:T(8,128)(2,1)}, bf16[2,256,2048]{2,1,0:T(8,128)(2,1)}, u32[]{:S(2)}, u32[]{:S(2)}) collective-permute-start(bf16[2,256,2048]{2,1,0:T(8,128)(2,1)} %get-tuple-element.575), channel_id=1, source_target_pairs={{0,4},{4,0},{8,12},{12,8},{1,5},{5,1},{9,13},{13,9},{2,6},{6,2},{1... | collective-permute-start | bytes 6291464 | tf_op jit(solution)/shard_map/ppermute | solution.py:1132
  451.7 39.8 %collective-permute-start.47 = (bf16[256,2048]{1,0:T(8,128)(2,1)S(1)}, bf16[256,2048]{1,0:T(8,128)(2,1)S(1)}, u32[]{:S(2)}, u32[]{:S(2)}) collective-permute-start(bf16[256,2048]{1,0:T(8,128)(2,1)S(1)} %fusion.6), channel_id=1, source_target_pairs={{0,8},{4,12},{8,0},{12,4},{1,9},{5,13},{9,1},{13,5},{2,10},{6,14},... | collective-permute-start | bytes 3145736 | tf_op jit(solution)/shard_map/ppermute | solution.py:1132
  484.8 104.4 %collective-permute-start.51 = (bf16[256,1024]{1,0:T(8,128)(2,1)}, bf16[256,1024]{1,0:T(8,128)(2,1)}, u32[]{:S(2)}, u32[]{:S(2)}) collective-permute-start(bf16[256,1024]{1,0:T(8,128)(2,1)} %bitcast_select_fusion), channel_id=1, source_target_pairs={{0,1},{1,0},{2,3},{3,2},{4,5},{5,4},{6,7},{7,6},{8,9},{9,8},{10,11... | collective-permute-start | bytes 1572872 | tf_op jit(solution)/shard_map/ppermute | solution.py:1132
  490.0 30.3 %collective-permute-start.53 = (bf16[256,2048]{1,0:T(8,128)(2,1)}, bf16[256,2048]{1,0:T(8,128)(2,1)}, u32[]{:S(2)}, u32[]{:S(2)}) collective-permute-start(bf16[256,2048]{1,0:T(8,128)(2,1)} %fusion.8), channel_id=1, source_target_pairs={{0,8},{4,12},{8,0},{12,4},{1,9},{5,13},{9,1},{13,5},{2,10},{6,14},... | collective-permute-start | bytes 3145736 | tf_op jit(solution)/shard_map/ppermute | solution.py:1132
  493.3 30.8 %collective-permute-start.52 = (bf16[256,2048]{1,0:T(8,128)(2,1)S(1)}, bf16[256,2048]{1,0:T(8,128)(2,1)}, u32[]{:S(2)}, u32[]{:S(2)}) collective-permute-start(bf16[256,2048]{1,0:T(8,128)(2,1)S(1)} %fusion.2), channel_id=1, source_target_pairs={{0,1},{3,2},{4,5},{7,6},{8,9},{11,10},{12,13},{15,14},{16,17},{19,... | collective-permute-start | bytes 3145736 | tf_op jit(solution)/shard_map/ppermute | solution.py:1214
  497.6 47.5 %collective-permute-start.57 = (bf16[512,1024]{1,0:T(8,128)(2,1)}, bf16[512,1024]{1,0:T(8,128)(2,1)}, u32[]{:S(2)}, u32[]{:S(2)}) collective-permute-start(bf16[512,1024]{1,0:T(8,128)(2,1)} %fusion.7), channel_id=1, source_target_pairs={{0,8},{4,12},{8,0},{12,4},{1,9},{5,13},{9,1},{13,5},{2,10},{6,14},... | collective-permute-start | bytes 3145736 | tf_op jit(solution)/shard_map/ppermute | solution.py:1132
  551.3 35.1 %collective-permute-start.67 = (bf16[256,2048]{1,0:T(8,128)(2,1)}, bf16[256,2048]{1,0:T(8,128)(2,1)}, u32[]{:S(2)}, u32[]{:S(2)}) collective-permute-start(bf16[256,2048]{1,0:T(8,128)(2,1)} %add_convert_fusion.3), channel_id=1, source_target_pairs={{1,0},{2,3},{5,4},{6,7},{9,8},{10,11},{13,12},{14,15},{17,16},{18,... | collective-permute-start | bytes 3145736 | tf_op jit(solution)/shard_map/ppermute | solution.py:1226
  553.8 36.0 %collective-permute-start.66 = (bf16[256,2048]{1,0:T(8,128)(2,1)}, bf16[256,2048]{1,0:T(8,128)(2,1)}, u32[]{:S(2)}, u32[]{:S(2)}) collective-permute-start(bf16[256,2048]{1,0:T(8,128)(2,1)} %add_convert_fusion.4), channel_id=1, source_target_pairs={{1,2},{2,1},{5,6},{6,5},{9,10},{10,9},{13,14},{14,13},{17,18},{18,... | collective-permute-start | bytes 3145736 | tf_op jit(solution)/shard_map/ppermute | solution.py:1220
  557.8 37.4 %collective-permute-start.64 = (bf16[512,1024]{1,0:T(8,128)(2,1)}, bf16[512,1024]{1,0:T(8,128)(2,1)}, u32[]{:S(2)}, u32[]{:S(2)}) collective-permute-start(bf16[512,1024]{1,0:T(8,128)(2,1)} %fusion), channel_id=1, source_target_pairs={{0,1},{3,2},{4,5},{7,6},{8,9},{11,10},{12,13},{15,14},{16,17},{19,... | collective-permute-start | bytes 3145736 | tf_op jit(solution)/shard_map/ppermute | solution.py:1214
  595.2 34.5 %collective-permute-start.70 = (bf16[256,2048]{1,0:T(8,128)(2,1)S(1)}, bf16[256,2048]{1,0:T(8,128)(2,1)S(1)}, u32[]{:S(2)}, u32[]{:S(2)}) collective-permute-start(bf16[256,2048]{1,0:T(8,128)(2,1)S(1)} %add_convert_fusion.2), channel_id=1, source_target_pairs={{1,0},{2,3},{5,4},{6,7},{9,8},{10,11},{13,12},{14,15},{17,16},{18,... | collective-permute-start | bytes 3145736 | tf_op jit(solution)/shard_map/ppermute | solution.py:1226
  614.8 50.5 %collective-permute-start.76 = (bf16[128,1024]{1,0:T(8,128)(2,1)S(1)}, bf16[128,1024]{1,0:T(8,128)(2,1)S(1)}, u32[]{:S(2)}, u32[]{:S(2)}) collective-permute-start(bf16[128,1024]{1,0:T(8,128)(2,1)S(1)} %fusion.14), channel_id=1, source_target_pairs={{0,1},{3,2},{4,5},{7,6},{8,9},{11,10},{12,13},{15,14},{16,17},{19,... | collective-permute-start | bytes 786440 | tf_op jit(solution)/shard_map/ppermute | solution.py:1214
  669.4 35.2 %collective-permute-start.82 = (bf16[256,1536]{1,0:T(8,128)(2,1)S(1)}, bf16[256,1536]{1,0:T(8,128)(2,1)S(1)}, u32[]{:S(2)}, u32[]{:S(2)}) collective-permute-start(bf16[256,1536]{1,0:T(8,128)(2,1)S(1)} %add_convert_fusion.13), channel_id=1, source_target_pairs={{1,0},{2,3},{5,4},{6,7},{9,8},{10,11},{13,12},{14,15},{17,16},{18,... | collective-permute-start | bytes 2359304 | tf_op jit(solution)/shard_map/ppermute | solution.py:1226
  690.8 36.3 %collective-permute-start.87 = (bf16[384,1024]{1,0:T(8,128)(2,1)S(1)}, bf16[384,1024]{1,0:T(8,128)(2,1)S(1)}, u32[]{:S(2)}, u32[]{:S(2)}) collective-permute-start(bf16[384,1024]{1,0:T(8,128)(2,1)S(1)} %add_convert_fusion.12), channel_id=1, source_target_pairs={{1,0},{2,3},{5,4},{6,7},{9,8},{10,11},{13,12},{14,15},{17,16},{18,... | collective-permute-start | bytes 2359304 | tf_op jit(solution)/shard_map/ppermute | solution.py:1226
  (141 other events, 2486.0 us)

commit v7 on v6

--- a/solution.py
+++ b/solution.py
@@ -1614,9 +1614,6 @@
         chain(d_input)
         send_back(turn, d_input)
 
-    loss_part = jnp.sum(mlp_grads[3][:, 1])[None]
-    loss_part = jnp.where(first, lax.ppermute(loss_part, "section", [(1, 0)]), loss_part)
-
     for turn in range(count, steps):
         mlp_grads, d_hidden = mlp_turn(turn, mlp_grads)
         chain(d_hidden)
@@ -1660,6 +1657,8 @@
 
     mix_sum = jnp.sum(small_mix, axis=0)
     mlp_sum = jnp.sum(small_mlp, axis=0)
+    loss_part = jnp.sum(mlp_sum[1])[None]
+    loss_part = jnp.where(first, lax.ppermute(loss_part, "section", [(1, 0)]), loss_part)
     singles = jnp.concatenate(
         [
             mix_sum[V_SBIAS, :heads],

time: 752 us -> 750 us (level)
  transfers between devices with their start and end apart: 89 -> 89, of which waited for: 25 -> 24; matrix products, arithmetic and copies ran while one was open for 13% -> 13% of each run, Pallas kernels for 39% -> 39%
where the time goes in v7:
time: 750 us; the launch traced here: 740 us
  Pallas kernels  361 us (48%)
  waiting for transfers between devices  141 us (19%)
  starting transfers between devices  104 us (14%)
  other arithmetic  70.1 us (9%)
  local copies, waits for them, and re-layouts  31.2 us (4%)
  between operations  23 us (3%)
  matrix products  8.96 us (1%)
    pallas_call x16, Pallas kernels, call(): pl.pallas_call(kernel, out_shape=[pltpu.HBM(s.shape, s.dtype) for s in st...  306 us
    ppermute x56, waiting for transfers between devices, swap(): lax.ppermute(block, axis, [(i, i ^ bit) for i in range(lax.axis_size(axis...  71.3 us
    pallas_call x8, Pallas kernels, weight_grad_halves(): pl.pallas_call(weight_kernel, out_shape=[shape, shape], grid_spec=grid, c...  55.5 us
    ppermute x8, waiting for transfers between devices, line_out(): self.moved = lax.ppermute(self.stay, 'rep', [(1, 0), (2, 3)])  51.8 us
    ppermute x56, starting transfers between devices, swap(): lax.ppermute(block, axis, [(i, i ^ bit) for i in range(lax.axis_size(axis...  39.3 us
    ppermute x8, starting transfers between devices, line_in(): self.moved = lax.ppermute(self.stay, 'rep', [(0, 1), (3, 2)])  32.5 us
    convert_element_type x24, other arithmetic, plus(): return (a.astype(F32) + b.astype(F32)).astype(BF)  22 us
  transfers between devices with their start and end apart: 89, of which 24 were waited for; matrix products, arithmetic and copies ran while one was open for 13% of the time, Pallas kernels for 39%

profile of v7, /device:TPU:0, one launch (start us, length us, event | category | flops | bytes accessed | tf_op | source)
XLA Modules:
  0.0 739.5 jit_solution(17854203142470404012)
XLA Ops:
  32.7 13.5 %collective-permute-done.2.refs_28_.refs_29_ = bf16[512,512]{1,0:T(8,128)(2,1)S(1)} collective-permute-done((bf16[512,512]{1,0:T(8,128)(2,1)S(1)}, bf16[512,512]{1,0:T(8,128)(2,1)S(1)}, u32[]{:S(2)}, u32[]{:S(2)}) %collective-permute-start.2) | collective-permute-done | bytes 524320 | tf_op jit(solution)/shard_map/ppermute | solution.py:1132
  85.5 15.3 %mixer_forward.2 = (bf16[4,256,1024]{2,1,0:T(8,128)(2,1)}, bf16[4,256,1792]{2,1,0:T(8,128)(2,1)}, bf16[4,256,1792]{2,1,0:T(8,128)(2,1)}, bf16[4,256,1536]{2,1,0:...) custom-call(s32[1]{0:T(128)} %constant.359.clone.1.refs_0_, ...), custom_call_target="tpu_custom_call" | custom-call | flops 20000000000 | bytes 1000000 | tf_op jit(solution)/shard_map/mixer_forward/pallas_call | solution.py:177
  113.4 15.5 %mixer_forward.3 = (bf16[4,256,1024]{2,1,0:T(8,128)(2,1)}, bf16[4,256,1792]{2,1,0:T(8,128)(2,1)}, bf16[4,256,1792]{2,1,0:T(8,128)(2,1)}, bf16[4,256,1536]{2,1,0:...) custom-call(s32[1]{0:T(128)} %constant.364.clone.1.refs_0_, ...), custom_call_target="tpu_custom_call", output_to_operand_aliasing={{0}: (32, {}), {1}: (33, {}), {2}: (34, {}), {3}: (35, {}),... | custom-call | flops 20000000000 | bytes 1000000 | tf_op jit(solution)/shard_map/mixer_forward/pallas_call | solution.py:177
  145.9 8.3 %mlp_forward.2 = (bf16[4,256,1024]{2,1,0:T(8,128)(2,1)}, bf16[4,256,2048]{2,1,0:T(8,128)(2,1)}, bf16[4,256,2048]{2,1,0:T(8,128)(2,1)}, bf16[4,256,2048]{2,1,0:T(...) custom-call(s32[1]{0:T(128)} %constant.359.clone.1.refs_0_, ...), custom_call_target="tpu_custom_call" | custom-call | flops 300000000 | bytes 1000000 | tf_op jit(solution)/shard_map/mlp_forward/pallas_call | solution.py:177
  162.3 8.3 %mlp_forward.3 = (bf16[4,256,1024]{2,1,0:T(8,128)(2,1)}, bf16[4,256,2048]{2,1,0:T(8,128)(2,1)}, bf16[4,256,2048]{2,1,0:T(8,128)(2,1)}, bf16[4,256,2048]{2,1,0:T(...) custom-call(s32[1]{0:T(128)} %constant.364.clone.1.refs_0_, ...), custom_call_target="tpu_custom_call", output_to_operand_aliasing={{0}: (19, {}), {1}: (20, {}), {2}: (21, {}), {3}: (22, {}),... | custom-call | flops 300000000 | bytes 1000000 | tf_op jit(solution)/shard_map/mlp_forward/pallas_call | solution.py:177
  176.4 21.3 %layer_forward.4 = (bf16[4,256,1024]{2,1,0:T(8,128)(2,1)}, bf16[4,256,1792]{2,1,0:T(8,128)(2,1)}, bf16[4,256,1792]{2,1,0:T(8,128)(2,1)}, bf16[4,256,1536]{2,1,0:...) custom-call(s32[1]{0:T(128)} %constant.367.clone.1.refs_0_, ...), custom_call_target="tpu_custom_call", output_to_operand_aliasing={{0}: (46, {}), {1}: (47, {}), {2}: (48, {}), {3}: (49, {}),... | custom-call | flops 20000000000 | bytes 1000000 | tf_op jit(solution)/shard_map/layer_forward/pallas_call | solution.py:177
  201.3 21.1 %layer_forward.5 = (bf16[4,256,1024]{2,1,0:T(8,128)(2,1)}, bf16[4,256,1792]{2,1,0:T(8,128)(2,1)}, bf16[4,256,1792]{2,1,0:T(8,128)(2,1)}, bf16[4,256,1536]{2,1,0:...) custom-call(s32[1]{0:T(128)} %constant.366.clone.1.refs_0_, ...), custom_call_target="tpu_custom_call", output_to_operand_aliasing={{0}: (46, {}), {1}: (47, {}), {2}: (48, {}), {3}: (49, {}),... | custom-call | flops 20000000000 | bytes 1000000 | tf_op jit(solution)/shard_map/layer_forward/pallas_call | solution.py:177
  225.9 19.9 %layer_forward.6 = (bf16[4,256,1024]{2,1,0:T(8,128)(2,1)}, bf16[4,256,1792]{2,1,0:T(8,128)(2,1)}, bf16[4,256,1792]{2,1,0:T(8,128)(2,1)}, bf16[4,256,1536]{2,1,0:...) custom-call(s32[1]{0:T(128)} %constant.368.clone.1.refs_0_, ...), custom_call_target="tpu_custom_call", output_to_operand_aliasing={{0}: (46, {}), {1}: (47, {}), {2}: (48, {}), {3}: (49, {}),... | custom-call | flops 20000000000 | bytes 1000000 | tf_op jit(solution)/shard_map/layer_forward/pallas_call | solution.py:177
  246.7 19.7 %layer_forward.7 = (bf16[4,256,1024]{2,1,0:T(8,128)(2,1)}, bf16[4,256,1792]{2,1,0:T(8,128)(2,1)}, bf16[4,256,1792]{2,1,0:T(8,128)(2,1)}, bf16[4,256,1536]{2,1,0:...) custom-call(s32[1]{0:T(128)} %constant.365.clone.1.refs_0_, ...), custom_call_target="tpu_custom_call", output_to_operand_aliasing={{0}: (46, {}), {1}: (47, {}), {2}: (48, {}), {3}: (49, {}),... | custom-call | flops 20000000000 | bytes 1000000 | tf_op jit(solution)/shard_map/layer_forward/pallas_call | solution.py:177
  266.4 28.0 %layer_backward.4 = (bf16[4,256,1024]{2,1,0:T(8,128)(2,1)}, bf16[4,256,2048]{2,1,0:T(8,128)(2,1)}, bf16[4,256,2048]{2,1,0:T(8,128)(2,1)}, f32[4,8,1024]{2,1,0:T(...) custom-call(s32[1]{0:T(128)} %constant.358.clone.1.refs_0_, ...), custom_call_target="tpu_custom_call" | custom-call | flops 24999999488 | bytes 1000000 | tf_op jit(solution)/shard_map/layer_backward/pallas_call | solution.py:177
  297.6 28.0 %layer_backward.5 = (bf16[4,256,1024]{2,1,0:T(8,128)(2,1)}, bf16[4,256,2048]{2,1,0:T(8,128)(2,1)}, bf16[4,256,2048]{2,1,0:T(8,128)(2,1)}, f32[4,8,1024]{2,1,0:T(...) custom-call(s32[1]{0:T(128)} %constant.355.clone.1.refs_0_, ...), custom_call_target="tpu_custom_call", output_to_operand_aliasing={{0}: (59, {}), {1}: (60, {}), {2}: (61, {}), {3}: (62, {}),... | custom-call | flops 24999999488 | bytes 1000000 | tf_op jit(solution)/shard_map/layer_backward/pallas_call | solution.py:177
  329.4 29.2 %layer_backward.6 = (bf16[4,256,1024]{2,1,0:T(8,128)(2,1)}, bf16[4,256,2048]{2,1,0:T(8,128)(2,1)}, bf16[4,256,2048]{2,1,0:T(8,128)(2,1)}, f32[4,8,1024]{2,1,0:T(...) custom-call(s32[1]{0:T(128)} %constant.369.clone.1.refs_0_, ...), custom_call_target="tpu_custom_call", output_to_operand_aliasing={{0}: (59, {}), {1}: (60, {}), {2}: (61, {}), {3}: (62, {}),... | custom-call | flops 24999999488 | bytes 1000000 | tf_op jit(solution)/shard_map/layer_backward/pallas_call | solution.py:177
  364.9 29.1 %layer_backward.7 = (bf16[4,256,1024]{2,1,0:T(8,128)(2,1)}, bf16[4,256,2048]{2,1,0:T(8,128)(2,1)}, bf16[4,256,2048]{2,1,0:T(8,128)(2,1)}, f32[4,8,1024]{2,1,0:T(...) custom-call(s32[1]{0:T(128)} %constant.354.clone.1.refs_0_, ...), custom_call_target="tpu_custom_call", output_to_operand_aliasing={{0}: (59, {}), {1}: (60, {}), {2}: (61, {}), {3}: (62, {}),... | custom-call | flops 24999999488 | bytes 1000000 | tf_op jit(solution)/shard_map/layer_backward/pallas_call | solution.py:177
  396.5 10.1 %mlp_backward.2 = (bf16[4,256,1024]{2,1,0:T(8,128)(2,1)}, bf16[4,256,2048]{2,1,0:T(8,128)(2,1)}, bf16[4,256,2048]{2,1,0:T(8,128)(2,1)}, f32[4,8,1024]{2,1,0:T(8,128)}, f32[256,1024]{1,0:T(8,128)S(1)}) custom-call(s32[1]{0:T(128)} %constant.370.clone.1.refs_0_, ...), custom_call_target="tpu_custom_call", output_to_operand_aliasing={{0}: (25, {}), {1}: (26, {}), {2}: (27, {}), {3}: (28, {})} | custom-call | flops 300000000 | bytes 1000000 | tf_op jit(solution)/shard_map/mlp_backward/pallas_call | solution.py:177
  410.1 10.0 %mlp_backward.3 = (bf16[4,256,1024]{2,1,0:T(8,128)(2,1)}, bf16[4,256,2048]{2,1,0:T(8,128)(2,1)}, bf16[4,256,2048]{2,1,0:T(8,128)(2,1)}, f32[4,8,1024]{2,1,0:T(8,128)}, f32[256,1024]{1,0:T(8,128)S(1)}) custom-call(s32[1]{0:T(128)} %constant.337.clone.1.refs_0_, ...), custom_call_target="tpu_custom_call", output_to_operand_aliasing={{0}: (25, {}), {1}: (26, {}), {2}: (27, {}), {3}: (28, {})} | custom-call | flops 300000000 | bytes 1000000 | tf_op jit(solution)/shard_map/mlp_backward/pallas_call | solution.py:177
  420.2 8.4 %weight_gradient.8 = (bf16[2,256,2048]{2,1,0:T(8,128)(2,1)}, bf16[2,256,2048]{2,1,0:T(8,128)(2,1)}) custom-call(s32[1]{0:T(128)} %bitcast.53.core_ref, bf16[4,256,1024]{2,1,0:T(8,128)(2,1)} %get-tuple-element.570.away_ref.stay_ref, bf16[4,256,1024]{2,1,0:T(8,128)(2,1)} %get-tuple-element.570.away_ref.stay_ref, bf16[4,256,2048]{2,1,0:T(8,128)(2,1)} %get-tuple-element.566.right_ref), custom_call_target="tpu_custom_call" | custom-call | flops 100000000 | bytes 1000000 | tf_op jit(solution)/shard_map/weight_gradient/pallas_call | solution.py:1031
  438.2 8.3 %weight_gradient.9 = (bf16[2,256,2048]{2,1,0:T(8,128)(2,1)}, bf16[2,256,2048]{2,1,0:T(8,128)(2,1)}) custom-call(s32[1]{0:T(128)} %bitcast.53.core_ref, bf16[4,256,1024]{2,1,0:T(8,128)(2,1)} %get-tuple-element.570.away_ref.stay_ref, bf16[4,256,1024]{2,1,0:T(8,128)(2,1)} %get-tuple-element.570.away_ref.stay_ref, bf16[4,256,2048]{2,1,0:T(8,128)(2,1)} %get-tuple-element.571.right_ref), custom_call_target="tpu_custom_call" | custom-call | flops 100000000 | bytes 1000000 | tf_op jit(solution)/shard_map/weight_gradient/pallas_call | solution.py:1031
  451.0 8.3 %weight_gradient.10 = (bf16[2,512,1024]{2,1,0:T(8,128)(2,1)}, bf16[2,512,1024]{2,1,0:T(8,128)(2,1)}) custom-call(s32[1]{0:T(128)} %bitcast.53.core_ref, bf16[4,256,2048]{2,1,0:T(8,128)(2,1)} %get-tuple-element.578.away_ref.stay_ref, bf16[4,256,2048]{2,1,0:T(8,128)(2,1)} %get-tuple-element.578.away_ref.stay_ref, ...), custom_call_target="tpu_custom_call" | custom-call | flops 100000000 | bytes 1000000 | tf_op jit(solution)/shard_map/weight_gradient/pallas_call | solution.py:1031
  460.0 21.2 %mixer_backward.2 = (bf16[4,256,1024]{2,1,0:T(8,128)(2,1)}, bf16[4,256,896]{2,1,0:T(8,128)(2,1)}, bf16[4,256,1792]{2,1,0:T(8,128)(2,1)}, bf16[4,256,1536]{2,1,0:...) custom-call(s32[1]{0:T(128)} %constant.370.clone.1.refs_0_, ...), custom_call_target="tpu_custom_call", output_to_operand_aliasing={{0}: (40, {}), {1}: (41, {}), {2}: (42, {}), {3}: (43, {}),... | custom-call | flops 24999999488 | bytes 1000000 | tf_op jit(solution)/shard_map/mixer_backward/pallas_call | solution.py:177
  497.4 20.9 %mixer_backward.3 = (bf16[4,256,1024]{2,1,0:T(8,128)(2,1)}, bf16[4,256,896]{2,1,0:T(8,128)(2,1)}, bf16[4,256,1792]{2,1,0:T(8,128)(2,1)}, bf16[4,256,1536]{2,1,0:...) custom-call(s32[1]{0:T(128)} %constant.337.clone.1.refs_0_, ...), custom_call_target="tpu_custom_call", output_to_operand_aliasing={{0}: (40, {}), {1}: (41, {}), {2}: (42, {}), {3}: (43, {}),... | custom-call | flops 24999999488 | bytes 1000000 | tf_op jit(solution)/shard_map/mixer_backward/pallas_call | solution.py:177
  603.2 10.2 %collective-permute-done.58 = bf16[256,1536]{1,0:T(8,128)(2,1)S(1)} collective-permute-done((bf16[256,1536]{1,0:T(8,128)(2,1)S(1)}, bf16[256,1536]{1,0:T(8,128)(2,1)S(1)}, u32[]{:S(2)}, u32[]{:S(2)}) %collective-permute-start.58) | collective-permute-done | bytes 786464 | tf_op jit(solution)/shard_map/ppermute | solution.py:1132
  675.7 10.6 %collective-permute-done.85 = bf16[256,1792]{1,0:T(8,128)(2,1)S(1)} collective-permute-done((bf16[256,1792]{1,0:T(8,128)(2,1)S(1)}, bf16[256,1792]{1,0:T(8,128)(2,1)S(1)}, u32[]{:S(2)}, u32[]{:S(2)}) %collective-permute-start.85) | collective-permute-done | bytes 917536 | tf_op jit(solution)/shard_map/ppermute | solution.py:1226
  690.6 12.5 %collective-permute-done.82 = bf16[256,1536]{1,0:T(8,128)(2,1)S(1)} collective-permute-done((bf16[256,1536]{1,0:T(8,128)(2,1)S(1)}, bf16[256,1536]{1,0:T(8,128)(2,1)S(1)}, u32[]{:S(2)}, u32[]{:S(2)}) %collective-permute-start.82) | collective-permute-done | bytes 786464 | tf_op jit(solution)/shard_map/ppermute | solution.py:1226
  709.5 16.0 %collective-permute-done.87 = bf16[384,1024]{1,0:T(8,128)(2,1)S(1)} collective-permute-done((bf16[384,1024]{1,0:T(8,128)(2,1)S(1)}, bf16[384,1024]{1,0:T(8,128)(2,1)S(1)}, u32[]{:S(2)}, u32[]{:S(2)}) %collective-permute-start.87) | collective-permute-done | bytes 786464 | tf_op jit(solution)/shard_map/ppermute | solution.py:1226
  (517 shorter events, 322.9 us)
Async XLA Ops:
  12.6 35.7 %collective-permute-start.11 = (bf16[256,896]{1,0:T(8,128)(2,1)S(1)}, bf16[256,896]{1,0:T(8,128)(2,1)}, u32[]{:S(2)}, u32[]{:S(2)}) collective-permute-start(bf16[256,896]{1,0:T(8,128)(2,1)S(1)} %concatenate.67.refs_8_.refs_9_), channel_id=1, source_target_pairs={{0,4},{4,0},{8,12},{12,8},{1,5},{5,1},{9,13},{13,9},{2,6},{6,2},{1... | collective-permute-start | bytes 1376264 | tf_op jit(solution)/shard_map/ppermute | solution.py:1132
  18.6 29.5 %collective-permute-start.12 = (bf16[128,896]{1,0:T(8,128)(2,1)S(1)}, bf16[128,896]{1,0:T(8,128)(2,1)}, u32[]{:S(2)}, u32[]{:S(2)}) collective-permute-start(bf16[128,896]{1,0:T(8,128)(2,1)S(1)} %constant_dynamic-slice_fusion), channel_id=1, source_target_pairs={{0,8},{4,12},{8,0},{12,4},{1,9},{5,13},{9,1},{13,5},{2,10},{6,14},... | collective-permute-start | bytes 688136 | tf_op jit(solution)/shard_map/ppermute | solution.py:1132
  32.5 36.9 %collective-permute-start.16 = (bf16[256,1792]{1,0:T(8,128)(2,1)}, bf16[256,1792]{1,0:T(8,128)(2,1)}, u32[]{:S(2)}, u32[]{:S(2)}) collective-permute-start(bf16[256,1792]{1,0:T(8,128)(2,1)} %bitcast.45.refs_14_.refs_15_), channel_id=1, source_target_pairs={{0,4},{4,0},{8,12},{12,8},{1,5},{5,1},{9,13},{13,9},{2,6},{6,2},{1... | collective-permute-start | bytes 2752520 | tf_op jit(solution)/shard_map/ppermute | solution.py:1132
  84.0 53.3 %collective-permute-start.30 = (bf16[256,2048]{1,0:T(8,128)(2,1)}, bf16[256,2048]{1,0:T(8,128)(2,1)S(1)}, u32[]{:S(2)}, u32[]{:S(2)}) collective-permute-start(bf16[256,2048]{1,0:T(8,128)(2,1)} %bitcast.49.refs_11_.refs_38_.refs_39_.refs_13_), channel_id=1, source_target_pairs={{0,4},{4,0},{8,12},{12,8},{1,5},{5,1},{9,13},{13,9},{2,6},{6,2},{1... | collective-permute-start | bytes 3145736 | tf_op jit(solution)/shard_map/ppermute | solution.py:1132
  84.5 53.2 %collective-permute-start.33 = (bf16[512,1024]{1,0:T(8,128)(2,1)}, bf16[512,1024]{1,0:T(8,128)(2,1)S(1)}, u32[]{:S(2)}, u32[]{:S(2)}) collective-permute-start(bf16[512,1024]{1,0:T(8,128)(2,1)} %bitcast.50.refs_15_.refs_42_.refs_43_.refs_17_), channel_id=1, source_target_pairs={{0,4},{4,0},{8,12},{12,8},{1,5},{5,1},{9,13},{13,9},{2,6},{6,2},{1... | collective-permute-start | bytes 3145736 | tf_op jit(solution)/shard_map/ppermute | solution.py:1132
  85.1 52.1 %collective-permute-start.27 = (bf16[128,2048]{1,0:T(8,128)(2,1)S(1)}, bf16[128,2048]{1,0:T(8,128)(2,1)S(1)}, u32[]{:S(2)}, u32[]{:S(2)}) collective-permute-start(bf16[128,2048]{1,0:T(8,128)(2,1)S(1)} %collective-permute-done.26.refs_7_.refs_34_.refs_35_.refs_9_), channel_id=1, source_target_pairs={{0,1},{1,0},{2,3},{3,2},{4,5},{5,4},{6,7},{7,6},{8,9},{9,8},{10,11... | collective-permute-start | bytes 1572872 | tf_op jit(solution)/shard_map/ppermute | solution.py:1132
  100.8 35.9 %collective-permute-start.34 = (bf16[512,1024]{1,0:T(8,128)(2,1)}, bf16[512,1024]{1,0:T(8,128)(2,1)S(1)}, u32[]{:S(2)}, u32[]{:S(2)}) collective-permute-start(bf16[512,1024]{1,0:T(8,128)(2,1)} %bitcast.50.refs_15_.refs_42_.refs_43_.refs_17_), channel_id=1, source_target_pairs={{0,8},{4,12},{8,0},{12,4},{1,9},{5,13},{9,1},{13,5},{2,10},{6,14},... | collective-permute-start | bytes 3145736 | tf_op jit(solution)/shard_map/ppermute | solution.py:1132
  170.6 29.8 %collective-permute-start.37 = (bf16[256,1024]{1,0:T(8,128)(2,1)S(1)}, bf16[256,1024]{1,0:T(8,128)(2,1)S(1)}, u32[]{:S(2)}, u32[]{:S(2)}) collective-permute-start(bf16[256,1024]{1,0:T(8,128)(2,1)S(1)} %get-tuple-element.419), channel_id=1, source_target_pairs={{0,16},{1,17},{2,18},{3,19},{4,20},{5,21},{6,22},{7,23},{8,24},{9,... | collective-permute-start | bytes 1572872 | tf_op jit(solution)/shard_map/ppermute | solution.py:1518
  295.9 32.6 %collective-permute-start.42 = (bf16[256,1024]{1,0:T(8,128)(2,1)}, bf16[256,1024]{1,0:T(8,128)(2,1)S(1)}, u32[]{:S(2)}, u32[]{:S(2)}) collective-permute-start(bf16[256,1024]{1,0:T(8,128)(2,1)} %get-tuple-element.510), channel_id=1, source_target_pairs={{16,0},{17,1},{18,2},{19,3},{20,4},{21,5},{22,6},{23,7},{24,8},{25... | collective-permute-start | bytes 1572872 | tf_op jit(solution)/shard_map/ppermute | solution.py:1580
  325.6 38.4 %collective-permute-start.41 = (bf16[256,1024]{1,0:T(8,128)(2,1)}, bf16[256,1024]{1,0:T(8,128)(2,1)S(1)}, u32[]{:S(2)}, u32[]{:S(2)}) collective-permute-start(bf16[256,1024]{1,0:T(8,128)(2,1)} %get-tuple-element.522), channel_id=1, source_target_pairs={{16,0},{17,1},{18,2},{19,3},{20,4},{21,5},{22,6},{23,7},{24,8},{25... | collective-permute-start | bytes 1572872 | tf_op jit(solution)/shard_map/ppermute | solution.py:1580
  358.5 37.2 %collective-permute-start.44 = (bf16[256,1024]{1,0:T(8,128)(2,1)}, bf16[256,1024]{1,0:T(8,128)(2,1)S(1)}, u32[]{:S(2)}, u32[]{:S(2)}) collective-permute-start(bf16[256,1024]{1,0:T(8,128)(2,1)} %get-tuple-element.535), channel_id=1, source_target_pairs={{16,0},{17,1},{18,2},{19,3},{20,4},{21,5},{22,6},{23,7},{24,8},{25... | collective-permute-start | bytes 1572872 | tf_op jit(solution)/shard_map/ppermute | solution.py:1580
  361.3 34.4 %collective-permute-start.45 = (bf16[256,1024]{1,0:T(8,128)(2,1)S(1)}, bf16[256,1024]{1,0:T(8,128)(2,1)S(1)}, u32[]{:S(2)}, u32[]{:S(2)}) collective-permute-start(bf16[256,1024]{1,0:T(8,128)(2,1)S(1)} %bitcast_select_fusion.3), channel_id=1, source_target_pairs={{0,3},{1,2},{2,1},{3,0},{4,7},{5,6},{6,5},{7,4},{8,11},{9,10},{10,... | collective-permute-start | bytes 1572872 | tf_op jit(solution)/shard_map/ppermute | solution.py:1132
  436.3 49.8 %collective-permute-start.50 = (bf16[256,1024]{1,0:T(8,128)(2,1)}, bf16[256,1024]{1,0:T(8,128)(2,1)S(1)}, u32[]{:S(2)}, u32[]{:S(2)}) collective-permute-start(bf16[256,1024]{1,0:T(8,128)(2,1)} %bitcast_select_fusion.2), channel_id=1, source_target_pairs={{0,2},{1,3},{2,0},{3,1},{4,6},{5,7},{6,4},{7,5},{8,10},{9,11},{10,... | collective-permute-start | bytes 1572872 | tf_op jit(solution)/shard_map/ppermute | solution.py:1132
  446.6 41.3 %collective-permute-start.48 = (bf16[2,256,2048]{2,1,0:T(8,128)(2,1)}, bf16[2,256,2048]{2,1,0:T(8,128)(2,1)}, u32[]{:S(2)}, u32[]{:S(2)}) collective-permute-start(bf16[2,256,2048]{2,1,0:T(8,128)(2,1)} %get-tuple-element.575), channel_id=1, source_target_pairs={{0,4},{4,0},{8,12},{12,8},{1,5},{5,1},{9,13},{13,9},{2,6},{6,2},{1... | collective-permute-start | bytes 6291464 | tf_op jit(solution)/shard_map/ppermute | solution.py:1132
  450.4 41.7 %collective-permute-start.47 = (bf16[256,2048]{1,0:T(8,128)(2,1)S(1)}, bf16[256,2048]{1,0:T(8,128)(2,1)S(1)}, u32[]{:S(2)}, u32[]{:S(2)}) collective-permute-start(bf16[256,2048]{1,0:T(8,128)(2,1)S(1)} %fusion.6), channel_id=1, source_target_pairs={{0,8},{4,12},{8,0},{12,4},{1,9},{5,13},{9,1},{13,5},{2,10},{6,14},... | collective-permute-start | bytes 3145736 | tf_op jit(solution)/shard_map/ppermute | solution.py:1132
  483.3 104.4 %collective-permute-start.51 = (bf16[256,1024]{1,0:T(8,128)(2,1)}, bf16[256,1024]{1,0:T(8,128)(2,1)}, u32[]{:S(2)}, u32[]{:S(2)}) collective-permute-start(bf16[256,1024]{1,0:T(8,128)(2,1)} %bitcast_select_fusion), channel_id=1, source_target_pairs={{0,1},{1,0},{2,3},{3,2},{4,5},{5,4},{6,7},{7,6},{8,9},{9,8},{10,11... | collective-permute-start | bytes 1572872 | tf_op jit(solution)/shard_map/ppermute | solution.py:1132
  496.9 47.5 %collective-permute-start.57 = (bf16[512,1024]{1,0:T(8,128)(2,1)}, bf16[512,1024]{1,0:T(8,128)(2,1)}, u32[]{:S(2)}, u32[]{:S(2)}) collective-permute-start(bf16[512,1024]{1,0:T(8,128)(2,1)} %fusion.7), channel_id=1, source_target_pairs={{0,8},{4,12},{8,0},{12,4},{1,9},{5,13},{9,1},{13,5},{2,10},{6,14},... | collective-permute-start | bytes 3145736 | tf_op jit(solution)/shard_map/ppermute | solution.py:1132
  550.7 34.2 %collective-permute-start.67 = (bf16[256,2048]{1,0:T(8,128)(2,1)}, bf16[256,2048]{1,0:T(8,128)(2,1)}, u32[]{:S(2)}, u32[]{:S(2)}) collective-permute-start(bf16[256,2048]{1,0:T(8,128)(2,1)} %add_convert_fusion.3), channel_id=1, source_target_pairs={{1,0},{2,3},{5,4},{6,7},{9,8},{10,11},{13,12},{14,15},{17,16},{18,... | collective-permute-start | bytes 3145736 | tf_op jit(solution)/shard_map/ppermute | solution.py:1226
  553.2 35.1 %collective-permute-start.66 = (bf16[256,2048]{1,0:T(8,128)(2,1)}, bf16[256,2048]{1,0:T(8,128)(2,1)}, u32[]{:S(2)}, u32[]{:S(2)}) collective-permute-start(bf16[256,2048]{1,0:T(8,128)(2,1)} %add_convert_fusion.4), channel_id=1, source_target_pairs={{1,2},{2,1},{5,6},{6,5},{9,10},{10,9},{13,14},{14,13},{17,18},{18,... | collective-permute-start | bytes 3145736 | tf_op jit(solution)/shard_map/ppermute | solution.py:1220
  557.2 36.6 %collective-permute-start.64 = (bf16[512,1024]{1,0:T(8,128)(2,1)}, bf16[512,1024]{1,0:T(8,128)(2,1)}, u32[]{:S(2)}, u32[]{:S(2)}) collective-permute-start(bf16[512,1024]{1,0:T(8,128)(2,1)} %fusion), channel_id=1, source_target_pairs={{0,1},{3,2},{4,5},{7,6},{8,9},{11,10},{12,13},{15,14},{16,17},{19,... | collective-permute-start | bytes 3145736 | tf_op jit(solution)/shard_map/ppermute | solution.py:1214
  593.7 34.5 %collective-permute-start.70 = (bf16[256,2048]{1,0:T(8,128)(2,1)S(1)}, bf16[256,2048]{1,0:T(8,128)(2,1)S(1)}, u32[]{:S(2)}, u32[]{:S(2)}) collective-permute-start(bf16[256,2048]{1,0:T(8,128)(2,1)S(1)} %add_convert_fusion.2), channel_id=1, source_target_pairs={{1,0},{2,3},{5,4},{6,7},{9,8},{10,11},{13,12},{14,15},{17,16},{18,... | collective-permute-start | bytes 3145736 | tf_op jit(solution)/shard_map/ppermute | solution.py:1226
  613.3 50.5 %collective-permute-start.76 = (bf16[128,1024]{1,0:T(8,128)(2,1)S(1)}, bf16[128,1024]{1,0:T(8,128)(2,1)S(1)}, u32[]{:S(2)}, u32[]{:S(2)}) collective-permute-start(bf16[128,1024]{1,0:T(8,128)(2,1)S(1)} %fusion.14), channel_id=1, source_target_pairs={{0,1},{3,2},{4,5},{7,6},{8,9},{11,10},{12,13},{15,14},{16,17},{19,... | collective-permute-start | bytes 786440 | tf_op jit(solution)/shard_map/ppermute | solution.py:1214
  667.9 35.2 %collective-permute-start.82 = (bf16[256,1536]{1,0:T(8,128)(2,1)S(1)}, bf16[256,1536]{1,0:T(8,128)(2,1)S(1)}, u32[]{:S(2)}, u32[]{:S(2)}) collective-permute-start(bf16[256,1536]{1,0:T(8,128)(2,1)S(1)} %add_convert_fusion.13), channel_id=1, source_target_pairs={{1,0},{2,3},{5,4},{6,7},{9,8},{10,11},{13,12},{14,15},{17,16},{18,... | collective-permute-start | bytes 2359304 | tf_op jit(solution)/shard_map/ppermute | solution.py:1226
  689.3 36.3 %collective-permute-start.87 = (bf16[384,1024]{1,0:T(8,128)(2,1)S(1)}, bf16[384,1024]{1,0:T(8,128)(2,1)S(1)}, u32[]{:S(2)}, u32[]{:S(2)}) collective-permute-start(bf16[384,1024]{1,0:T(8,128)(2,1)S(1)} %add_convert_fusion.12), channel_id=1, source_target_pairs={{1,0},{2,3},{5,4},{6,7},{9,8},{10,11},{13,12},{14,15},{17,16},{18,... | collective-permute-start | bytes 2359304 | tf_op jit(solution)/shard_map/ppermute | solution.py:1226
  (141 other events, 2489.5 us)
